TPU v7x, 256 devices: a whole 4x4x8 slice. The times are simulated.
256 devices in a mesh: row: 16 (over y, x), col: 16 (over z, core).
Axes of the slice: x: 4, y: 4, z: 8, core: 2. Of those that a mesh axis runs over, the one named last changes fastest.
Arguments:
- image: bfloat16 [1024, 1024, 256], P('row', 'col'), may hold values from -6 to 6
- vert_rate: float32 [8, 256], replicated, may hold values from 0.00029296875 to 0.065625
- vert_coef: float32 [8, 256], replicated, may hold values from -28.8 to 28.8
- horiz_rate: float32 [8, 256], replicated, may hold values from 0.00029296875 to 0.065625
- horiz_coef: float32 [8, 256], replicated, may hold values from -28.8 to 28.8
- w_in: bfloat16 [256, 1024], replicated, may hold values from -0.375 to 0.375
- w_out: bfloat16 [1024, 256], replicated, may hold values from -0.1875 to 0.1875
Outputs:
- mixed: bfloat16 [1024, 1024, 256], P('row', 'col')
All inputs are finite; a program needn't handle non-finite values.
Results may differ from a plain program's by a relative error of at most 0.006.
Values sent between devices are 32-bit elements; how exact they have to be, the bound alone decides.
No kernel may reach another device: no remote copies, remote signals or barrier semaphores. Data moves between devices by JAX's collectives and lax.ppermute only.
A program may use at most 128 MiB of HBM per device.

v0:
```python
import jax
import jax.numpy as jnp
from jax import lax
from jax.sharding import PartitionSpec as P

HIGH = lax.Precision.HIGHEST


def from_behind(block, axis, distance):
    devices = range(lax.axis_size(axis))
    route = [(i - distance, i) for i in devices if i - distance in devices]
    return lax.ppermute(block, axis, route)


def tables(rate, coef, length):
    gain = jnp.sqrt(1.0 - jnp.exp(-2.0 * rate))
    steps = jnp.arange(length, dtype=jnp.float32)
    powers = jnp.exp(-rate[:, None, :] * steps[None, :, None])
    impulse = jnp.sum((coef * gain)[:, None, :] * powers, axis=0)
    offset = steps[:, None] - steps[None, :]
    index = jnp.clip(offset, 0, length - 1).astype(jnp.int32)
    toeplitz = jnp.where((offset >= 0)[:, :, None], impulse[index], 0.0)
    tail = gain[:, None, :] * jnp.exp(-rate[:, None, :] * (length - 1 - steps)[None, :, None])
    lead = coef[:, None, :] * jnp.exp(-rate[:, None, :] * (steps + 1.0)[None, :, None])
    decay = jnp.exp(-rate * length)[:, None, :]
    return (toeplitz, tail, lead, decay)


def chain_rows(decay, edge):

    def relay(step, incoming):
        return from_behind(decay * incoming + edge, "row", 1)

    incoming = lax.fori_loop(0, lax.axis_size("row") - 1, relay, jnp.zeros_like(edge))
    return incoming


def chain_cols(decay, edge):

    def relay(step, incoming):
        return from_behind(decay * incoming + edge, "col", 1)

    incoming = lax.fori_loop(0, lax.axis_size("col") - 1, relay, jnp.zeros_like(edge))
    return incoming


def on_device(image, vert_rate, vert_coef, horiz_rate, horiz_coef, w_in, w_out):
    rows_here, cols_here, channels = image.shape
    field = image.astype(jnp.float32)
    toeplitz, tail, lead, decay = tables(vert_rate, vert_coef, rows_here)
    edge = jnp.einsum("msc,swc->mwc", tail, field, precision=HIGH)
    incoming = chain_rows(decay, edge)
    local = jnp.einsum("tsc,swc->twc", toeplitz, field, precision=HIGH)
    vert = local + jnp.einsum("mtc,mwc->twc", lead, incoming, precision=HIGH)
    act = jax.nn.gelu(vert).astype(jnp.bfloat16)
    field = act.astype(jnp.float32)
    toeplitz, tail, lead, decay = tables(horiz_rate, horiz_coef, cols_here)
    edge = jnp.einsum("msc,hsc->mhc", tail, field, precision=HIGH)
    incoming = chain_cols(decay, edge)
    local = jnp.einsum("tsc,hsc->htc", toeplitz, field, precision=HIGH)
    horiz = local + jnp.einsum("mtc,mhc->htc", lead, incoming, precision=HIGH)
    flat = horiz.reshape(rows_here * cols_here, channels)
    normed = (flat * lax.rsqrt(jnp.mean(flat * flat, axis=-1, keepdims=True) + 1e-06)).astype(
        jnp.bfloat16
    )
    hidden = jax.nn.gelu(jnp.dot(normed, w_in, preferred_element_type=jnp.float32)).astype(
        jnp.bfloat16
    )
    mixed = flat + jnp.dot(hidden, w_out, preferred_element_type=jnp.float32)
    return mixed.astype(jnp.bfloat16).reshape(rows_here, cols_here, channels)


def solution(mesh):
    placed = (P("row", "col", None), P(), P(), P(), P(), P(), P())
    return jax.shard_map(
        on_device, mesh=mesh, in_specs=placed, out_specs=P("row", "col", None), check_vma=False
    )
```

profile of v0, /device:TPU:136, one launch (start us, length us, event | category | flops | bytes accessed | tf_op | source)
XLA Modules:
  0.0 576.2 jit_solution(9094469814854956873)
XLA Ops:
  1.1 7.5 %copy.42 = bf16[64,64,256]{1,0,2:T(8,128)(2,1)} copy(bf16[64,64,256]{2,1,0:T(8,128)(2,1)} %param.11) | data formatting | bytes 4194304 | tf_op args[0]
  8.5 5.2 convolution_bitcast_fusion.1
  14.2 238.2 %while.20 = (s32[]{:T(128)}, f32[8,64,256]{2,1,0:T(8,128)S(1)}, f32[8,1,256]{2,0,1:T(8,128)S(1)}, f32[8,64,256]{2,1,0:T(8,128)S(1)}, s32[]{:T(128)}) while((s32[]{:T(128)}, f32[8,64,256]{2,1,0:T(8,128)S(1)}, f32[8,1,256]{2,0,1:T(8,128)S(1)}, f32[8,64,256]{2,1,0:T(8,128)S(1)}, s32[]{:T(128)}) %tuple.40), condition=%wide.region_2.3_spmd, body=%wide.region_1.2_spmd.sunk | while | flops 262146 | bytes 3678309 | solution.py:34
  14.3 3.4 collective-permute-start
  17.7 14.3 %collective-permute-done = f32[8,64,256]{2,1,0:T(8,128)S(1)} collective-permute-done((f32[8,64,256]{2,1,0:T(8,128)S(1)}, f32[8,64,256]{2,1,0:T(8,128)S(1)}, u32[]{:S(2)}, u32[]{:S(2)}) %collective-permute-start) | collective-permute-done | bytes 524320 | tf_op jit(solution)/shard_map/while/body/eval_jaxpr/ppermute | solution.py:12
  34.0 14.9 %collective-permute-done = f32[8,64,256]{2,1,0:T(8,128)S(1)} collective-permute-done((f32[8,64,256]{2,1,0:T(8,128)S(1)}, f32[8,64,256]{2,1,0:T(8,128)S(1)}, u32[]{:S(2)}, u32[]{:S(2)}) %collective-permute-start) | collective-permute-done | bytes 524320 | tf_op jit(solution)/shard_map/while/body/eval_jaxpr/ppermute | solution.py:12
  50.8 13.9 %collective-permute-done = f32[8,64,256]{2,1,0:T(8,128)S(1)} collective-permute-done((f32[8,64,256]{2,1,0:T(8,128)S(1)}, f32[8,64,256]{2,1,0:T(8,128)S(1)}, u32[]{:S(2)}, u32[]{:S(2)}) %collective-permute-start) | collective-permute-done | bytes 524320 | tf_op jit(solution)/shard_map/while/body/eval_jaxpr/ppermute | solution.py:12
  66.8 13.0 %collective-permute-done = f32[8,64,256]{2,1,0:T(8,128)S(1)} collective-permute-done((f32[8,64,256]{2,1,0:T(8,128)S(1)}, f32[8,64,256]{2,1,0:T(8,128)S(1)}, u32[]{:S(2)}, u32[]{:S(2)}) %collective-permute-start) | collective-permute-done | bytes 524320 | tf_op jit(solution)/shard_map/while/body/eval_jaxpr/ppermute | solution.py:12
  81.8 12.1 %collective-permute-done = f32[8,64,256]{2,1,0:T(8,128)S(1)} collective-permute-done((f32[8,64,256]{2,1,0:T(8,128)S(1)}, f32[8,64,256]{2,1,0:T(8,128)S(1)}, u32[]{:S(2)}, u32[]{:S(2)}) %collective-permute-start) | collective-permute-done | bytes 524320 | tf_op jit(solution)/shard_map/while/body/eval_jaxpr/ppermute | solution.py:12
  95.9 11.3 %collective-permute-done = f32[8,64,256]{2,1,0:T(8,128)S(1)} collective-permute-done((f32[8,64,256]{2,1,0:T(8,128)S(1)}, f32[8,64,256]{2,1,0:T(8,128)S(1)}, u32[]{:S(2)}, u32[]{:S(2)}) %collective-permute-start) | collective-permute-done | bytes 524320 | tf_op jit(solution)/shard_map/while/body/eval_jaxpr/ppermute | solution.py:12
  107.2 1.9 collective-permute-start
  109.2 11.5 %collective-permute-done = f32[8,64,256]{2,1,0:T(8,128)S(1)} collective-permute-done((f32[8,64,256]{2,1,0:T(8,128)S(1)}, f32[8,64,256]{2,1,0:T(8,128)S(1)}, u32[]{:S(2)}, u32[]{:S(2)}) %collective-permute-start) | collective-permute-done | bytes 524320 | tf_op jit(solution)/shard_map/while/body/eval_jaxpr/ppermute | solution.py:12
  122.7 12.6 %collective-permute-done = f32[8,64,256]{2,1,0:T(8,128)S(1)} collective-permute-done((f32[8,64,256]{2,1,0:T(8,128)S(1)}, f32[8,64,256]{2,1,0:T(8,128)S(1)}, u32[]{:S(2)}, u32[]{:S(2)}) %collective-permute-start) | collective-permute-done | bytes 524320 | tf_op jit(solution)/shard_map/while/body/eval_jaxpr/ppermute | solution.py:12
  137.3 13.7 %collective-permute-done = f32[8,64,256]{2,1,0:T(8,128)S(1)} collective-permute-done((f32[8,64,256]{2,1,0:T(8,128)S(1)}, f32[8,64,256]{2,1,0:T(8,128)S(1)}, u32[]{:S(2)}, u32[]{:S(2)}) %collective-permute-start) | collective-permute-done | bytes 524320 | tf_op jit(solution)/shard_map/while/body/eval_jaxpr/ppermute | solution.py:12
  153.0 14.8 %collective-permute-done = f32[8,64,256]{2,1,0:T(8,128)S(1)} collective-permute-done((f32[8,64,256]{2,1,0:T(8,128)S(1)}, f32[8,64,256]{2,1,0:T(8,128)S(1)}, u32[]{:S(2)}, u32[]{:S(2)}) %collective-permute-start) | collective-permute-done | bytes 524320 | tf_op jit(solution)/shard_map/while/body/eval_jaxpr/ppermute | solution.py:12
  169.8 15.9 %collective-permute-done = f32[8,64,256]{2,1,0:T(8,128)S(1)} collective-permute-done((f32[8,64,256]{2,1,0:T(8,128)S(1)}, f32[8,64,256]{2,1,0:T(8,128)S(1)}, u32[]{:S(2)}, u32[]{:S(2)}) %collective-permute-start) | collective-permute-done | bytes 524320 | tf_op jit(solution)/shard_map/while/body/eval_jaxpr/ppermute | solution.py:12
  187.8 16.7 %collective-permute-done = f32[8,64,256]{2,1,0:T(8,128)S(1)} collective-permute-done((f32[8,64,256]{2,1,0:T(8,128)S(1)}, f32[8,64,256]{2,1,0:T(8,128)S(1)}, u32[]{:S(2)}, u32[]{:S(2)}) %collective-permute-start) | collective-permute-done | bytes 524320 | tf_op jit(solution)/shard_map/while/body/eval_jaxpr/ppermute | solution.py:12
  206.4 15.8 %collective-permute-done = f32[8,64,256]{2,1,0:T(8,128)S(1)} collective-permute-done((f32[8,64,256]{2,1,0:T(8,128)S(1)}, f32[8,64,256]{2,1,0:T(8,128)S(1)}, u32[]{:S(2)}, u32[]{:S(2)}) %collective-permute-start) | collective-permute-done | bytes 524320 | tf_op jit(solution)/shard_map/while/body/eval_jaxpr/ppermute | solution.py:12
  224.2 14.9 %collective-permute-done = f32[8,64,256]{2,1,0:T(8,128)S(1)} collective-permute-done((f32[8,64,256]{2,1,0:T(8,128)S(1)}, f32[8,64,256]{2,1,0:T(8,128)S(1)}, u32[]{:S(2)}, u32[]{:S(2)}) %collective-permute-start) | collective-permute-done | bytes 524320 | tf_op jit(solution)/shard_map/while/body/eval_jaxpr/ppermute | solution.py:12
  241.2 11.3 %collective-permute-done = f32[8,64,256]{2,1,0:T(8,128)S(1)} collective-permute-done((f32[8,64,256]{2,1,0:T(8,128)S(1)}, f32[8,64,256]{2,1,0:T(8,128)S(1)}, u32[]{:S(2)}, u32[]{:S(2)}) %collective-permute-start) | collective-permute-done | bytes 524320 | tf_op jit(solution)/shard_map/while/body/eval_jaxpr/ppermute | solution.py:12
  253.8 16.1 %gather_fusion = f32[4096,256]{1,0:T(8,128)} fusion(f32[64,256]{1,0:T(8,128)S(1)} %copy.40, s32[4096]{0:T(1024)S(1)} %broadcast_clamp_fusion), kind=kCustom, calls=%fused_computation | custom fusion | bytes 8404992 | tf_op jit(solution)/shard_map/gather | solution.py:22
  269.9 9.2 %copy.41 = f32[64,64,256]{1,0,2:T(8,128)} copy(f32[64,64,256]{2,1,0:T(8,128)} %bitcast.42) | data formatting | bytes 8388608 | tf_op jit(solution)/shard_map/gather | solution.py:22
  279.1 12.2 %fusion.18 = f32[256,64,64]{2,1,0:T(8,128)} fusion(bf16[64,64,256]{1,0,2:T(8,128)(2,1)} %copy.42, f32[64,64,256]{1,0,2:T(8,128)} %copy.41, pred[64,64]{1,0:T(8,128)(4,1)S(1)} %subtract_compare_fusion), kind=kOutput, calls=%fused_computation.27 | convolution fusion | flops 806354944 | bytes 10489856 | tf_op jit(solution)/shard_map/tsc,swc->twc/dot_general | solution.py:53
  291.4 19.0 %fusion.15 = bf16[64,64,256]{1,0,2:T(8,128)(2,1)} fusion(f32[256,64,64]{2,1,0:T(8,128)} %fusion.18, f32[8,64,256]{1,0,2:T(8,128)S(1)} %copy.47, f32[64]{0:T(128)S(1)} %iota_add_fusion, f32[8,256]{0,1:T(8,128)S(1)} %copy.46, f32[8,256]{0,1:T(8,128)S(1)} %copy.39), kind=kOutput, calls=%fused_computation.21 | convolution fusion | flops 111411200 | bytes 6832384 | tf_op jit(solution)/shard_map/mtc,mwc->twc/dot_general | solution.py:54
  310.8 8.4 %convolution_bitcast_fusion = f32[8,64,256]{1,0,2:T(8,128)S(1)} fusion(bf16[64,64,256]{1,0,2:T(8,128)(2,1)} %fusion.15, f32[8,256]{0,1:T(8,128)S(1)} %copy.53, f32[8,256]{0,1:T(8,128)S(1)} %copy.50, f32[64]{0:T(128)S(1)} %iota_subtract_fusion), kind=kOutput, calls=%fused_computation.39 | convolution fusion | flops 100925440 | bytes 2638080 | tf_op jit(solution)/shard_map/msc,hsc->mhc/dot_general | solution.py:58
  319.6 176.8 %while.21 = (s32[]{:T(128)}, f32[8,64,256]{2,1,0:T(8,128)S(1)}, f32[8,1,256]{2,0,1:T(8,128)S(1)}, f32[8,64,256]{2,1,0:T(8,128)S(1)}, s32[]{:T(128)}) while((s32[]{:T(128)}, f32[8,64,256]{2,1,0:T(8,128)S(1)}, f32[8,1,256]{2,0,1:T(8,128)S(1)}, f32[8,64,256]{2,1,0:T(8,128)S(1)}, s32[]{:T(128)}) %tuple.43), condition=%wide.region_5.6_spmd, body=%wide.region_4.5_spmd.sunk | while | flops 262146 | bytes 3678309 | solution.py:43
  321.7 9.8 %collective-permute-done.1 = f32[8,64,256]{2,1,0:T(8,128)S(1)} collective-permute-done((f32[8,64,256]{2,1,0:T(8,128)S(1)}, f32[8,64,256]{2,1,0:T(8,128)S(1)}, u32[]{:S(2)}, u32[]{:S(2)}) %collective-permute-start.1) | collective-permute-done | bytes 524320 | tf_op jit(solution)/shard_map/while/body/eval_jaxpr/ppermute | solution.py:12
  333.4 9.8 %collective-permute-done.1 = f32[8,64,256]{2,1,0:T(8,128)S(1)} collective-permute-done((f32[8,64,256]{2,1,0:T(8,128)S(1)}, f32[8,64,256]{2,1,0:T(8,128)S(1)}, u32[]{:S(2)}, u32[]{:S(2)}) %collective-permute-start.1) | collective-permute-done | bytes 524320 | tf_op jit(solution)/shard_map/while/body/eval_jaxpr/ppermute | solution.py:12
  345.2 9.8 %collective-permute-done.1 = f32[8,64,256]{2,1,0:T(8,128)S(1)} collective-permute-done((f32[8,64,256]{2,1,0:T(8,128)S(1)}, f32[8,64,256]{2,1,0:T(8,128)S(1)}, u32[]{:S(2)}, u32[]{:S(2)}) %collective-permute-start.1) | collective-permute-done | bytes 524320 | tf_op jit(solution)/shard_map/while/body/eval_jaxpr/ppermute | solution.py:12
  357.0 9.8 %collective-permute-done.1 = f32[8,64,256]{2,1,0:T(8,128)S(1)} collective-permute-done((f32[8,64,256]{2,1,0:T(8,128)S(1)}, f32[8,64,256]{2,1,0:T(8,128)S(1)}, u32[]{:S(2)}, u32[]{:S(2)}) %collective-permute-start.1) | collective-permute-done | bytes 524320 | tf_op jit(solution)/shard_map/while/body/eval_jaxpr/ppermute | solution.py:12
  368.8 9.8 %collective-permute-done.1 = f32[8,64,256]{2,1,0:T(8,128)S(1)} collective-permute-done((f32[8,64,256]{2,1,0:T(8,128)S(1)}, f32[8,64,256]{2,1,0:T(8,128)S(1)}, u32[]{:S(2)}, u32[]{:S(2)}) %collective-permute-start.1) | collective-permute-done | bytes 524320 | tf_op jit(solution)/shard_map/while/body/eval_jaxpr/ppermute | solution.py:12
  380.6 9.8 %collective-permute-done.1 = f32[8,64,256]{2,1,0:T(8,128)S(1)} collective-permute-done((f32[8,64,256]{2,1,0:T(8,128)S(1)}, f32[8,64,256]{2,1,0:T(8,128)S(1)}, u32[]{:S(2)}, u32[]{:S(2)}) %collective-permute-start.1) | collective-permute-done | bytes 524320 | tf_op jit(solution)/shard_map/while/body/eval_jaxpr/ppermute | solution.py:12
  392.4 9.8 %collective-permute-done.1 = f32[8,64,256]{2,1,0:T(8,128)S(1)} collective-permute-done((f32[8,64,256]{2,1,0:T(8,128)S(1)}, f32[8,64,256]{2,1,0:T(8,128)S(1)}, u32[]{:S(2)}, u32[]{:S(2)}) %collective-permute-start.1) | collective-permute-done | bytes 524320 | tf_op jit(solution)/shard_map/while/body/eval_jaxpr/ppermute | solution.py:12
  404.2 9.8 %collective-permute-done.1 = f32[8,64,256]{2,1,0:T(8,128)S(1)} collective-permute-done((f32[8,64,256]{2,1,0:T(8,128)S(1)}, f32[8,64,256]{2,1,0:T(8,128)S(1)}, u32[]{:S(2)}, u32[]{:S(2)}) %collective-permute-start.1) | collective-permute-done | bytes 524320 | tf_op jit(solution)/shard_map/while/body/eval_jaxpr/ppermute | solution.py:12
  415.9 9.8 %collective-permute-done.1 = f32[8,64,256]{2,1,0:T(8,128)S(1)} collective-permute-done((f32[8,64,256]{2,1,0:T(8,128)S(1)}, f32[8,64,256]{2,1,0:T(8,128)S(1)}, u32[]{:S(2)}, u32[]{:S(2)}) %collective-permute-start.1) | collective-permute-done | bytes 524320 | tf_op jit(solution)/shard_map/while/body/eval_jaxpr/ppermute | solution.py:12
  427.7 9.8 %collective-permute-done.1 = f32[8,64,256]{2,1,0:T(8,128)S(1)} collective-permute-done((f32[8,64,256]{2,1,0:T(8,128)S(1)}, f32[8,64,256]{2,1,0:T(8,128)S(1)}, u32[]{:S(2)}, u32[]{:S(2)}) %collective-permute-start.1) | collective-permute-done | bytes 524320 | tf_op jit(solution)/shard_map/while/body/eval_jaxpr/ppermute | solution.py:12
  439.5 9.8 %collective-permute-done.1 = f32[8,64,256]{2,1,0:T(8,128)S(1)} collective-permute-done((f32[8,64,256]{2,1,0:T(8,128)S(1)}, f32[8,64,256]{2,1,0:T(8,128)S(1)}, u32[]{:S(2)}, u32[]{:S(2)}) %collective-permute-start.1) | collective-permute-done | bytes 524320 | tf_op jit(solution)/shard_map/while/body/eval_jaxpr/ppermute | solution.py:12
  451.3 9.8 %collective-permute-done.1 = f32[8,64,256]{2,1,0:T(8,128)S(1)} collective-permute-done((f32[8,64,256]{2,1,0:T(8,128)S(1)}, f32[8,64,256]{2,1,0:T(8,128)S(1)}, u32[]{:S(2)}, u32[]{:S(2)}) %collective-permute-start.1) | collective-permute-done | bytes 524320 | tf_op jit(solution)/shard_map/while/body/eval_jaxpr/ppermute | solution.py:12
  463.1 9.8 %collective-permute-done.1 = f32[8,64,256]{2,1,0:T(8,128)S(1)} collective-permute-done((f32[8,64,256]{2,1,0:T(8,128)S(1)}, f32[8,64,256]{2,1,0:T(8,128)S(1)}, u32[]{:S(2)}, u32[]{:S(2)}) %collective-permute-start.1) | collective-permute-done | bytes 524320 | tf_op jit(solution)/shard_map/while/body/eval_jaxpr/ppermute | solution.py:12
  474.9 9.8 %collective-permute-done.1 = f32[8,64,256]{2,1,0:T(8,128)S(1)} collective-permute-done((f32[8,64,256]{2,1,0:T(8,128)S(1)}, f32[8,64,256]{2,1,0:T(8,128)S(1)}, u32[]{:S(2)}, u32[]{:S(2)}) %collective-permute-start.1) | collective-permute-done | bytes 524320 | tf_op jit(solution)/shard_map/while/body/eval_jaxpr/ppermute | solution.py:12
  486.7 9.8 %collective-permute-done.1 = f32[8,64,256]{2,1,0:T(8,128)S(1)} collective-permute-done((f32[8,64,256]{2,1,0:T(8,128)S(1)}, f32[8,64,256]{2,1,0:T(8,128)S(1)}, u32[]{:S(2)}, u32[]{:S(2)}) %collective-permute-start.1) | collective-permute-done | bytes 524320 | tf_op jit(solution)/shard_map/while/body/eval_jaxpr/ppermute | solution.py:12
  497.0 16.1 %fusion.37 = f32[256,64,64]{2,1,0:T(8,128)} fusion(f32[8,64,256]{1,0,2:T(8,128)S(1)} %copy.56, f32[8,256]{0,1:T(8,128)S(1)} %copy.55, f32[8,256]{0,1:T(8,128)S(1)} %copy.50, f32[64]{0:T(128)S(1)} %iota_add_fusion), kind=kOutput, calls=%fused_computation.41 | convolution fusion | flops 100925440 | bytes 4735232 | tf_op jit(solution)/shard_map/mtc,mhc->htc/dot_general | solution.py:61
  513.9 16.1 %gather_fusion.1 = f32[4096,256]{1,0:T(8,128)} fusion(f32[64,256]{1,0:T(8,128)S(1)} %copy.51, s32[4096]{0:T(1024)S(1)} %broadcast_clamp_fusion), kind=kCustom, calls=%fused_computation.1 | custom fusion | bytes 8404992 | tf_op jit(solution)/shard_map/gather | solution.py:22
  530.1 9.3 %copy.52 = f32[64,64,256]{1,0,2:T(8,128)} copy(f32[64,64,256]{2,1,0:T(8,128)} %bitcast.41) | data formatting | bytes 8388608 | tf_op jit(solution)/shard_map/gather | solution.py:22
  539.4 17.2 %multiply_reduce_fusion = (f32[64,64]{1,0:T(8,128)S(1)}, f32[64,64,256]{1,0,2:T(8,128)}) fusion(f32[256,64,64]{2,1,0:T(8,128)} %fusion.37, bf16[64,64,256]{1,0,2:T(8,128)(2,1)} %fusion.15, f32[64,64,256]{1,0,2:T(8,128)} %copy.52, pred[64,64]{1,0:T(8,128)(4,1)S(1)} %subtract_compare_fusion), kind=kOutput, calls=%fused_computation.23 | convolution fusion | flops 809496576 | bytes 14700544 | tf_op jit(solution)/shard_map/tsc,hsc->htc/dot_general | solution.py:60
  556.7 7.8 %copy.57 = f32[64,64,256]{2,1,0:T(8,128)} copy(f32[64,64,256]{1,0,2:T(8,128)} %get-tuple-element.84) | data formatting | bytes 8388608 | tf_op jit(solution)/shard_map/add | solution.py:61
  564.6 2.6 fusion.30
  567.2 8.8 %fusion.27 = bf16[4096,256]{1,0:T(8,128)(2,1)} fusion(f32[4096,256]{1,0:T(8,128)} %bitcast.40, bf16[1024,256]{1,0:T(8,128)(2,1)S(1)} %copy-done, bf16[4096,256]{1,0:T(8,128)(2,1)S(1)} %fusion.30, bf16[256,1024]{1,0:T(8,128)(2,1)S(1)} %copy-done.4), kind=kOutput, calls=%fused_computation.32 | convolution fusion | flops 4334813184 | bytes 9437184 | tf_op jit(solution)/shard_map/dot_general | solution.py:69
  (96 shorter events, 61.0 us)
Async XLA Ops:
  0.0 567.2 %copy-start = (bf16[1024,256]{1,0:T(8,128)(2,1)S(1)}, bf16[1024,256]{1,0:T(8,128)(2,1)}, u32[]{:S(2)}) copy-start(bf16[1024,256]{1,0:T(8,128)(2,1)} %param.17) | copy-start | bytes 1572868
  14.3 17.7 %collective-permute-start = (f32[8,64,256]{2,1,0:T(8,128)S(1)}, f32[8,64,256]{2,1,0:T(8,128)S(1)}, u32[]{:S(2)}, u32[]{:S(2)}) collective-permute-start(f32[8,64,256]{2,1,0:T(8,128)S(1)} %multiply_add_fusion.4), channel_id=1, source_target_pairs={{0,16},{16,32},{32,48},{48,64},{64,80},{80,96},{96,112},{112,128},... | collective-permute-start | bytes 1572872 | tf_op jit(solution)/shard_map/while/body/eval_jaxpr/ppermute | solution.py:12
  32.0 16.8 %collective-permute-start = (f32[8,64,256]{2,1,0:T(8,128)S(1)}, f32[8,64,256]{2,1,0:T(8,128)S(1)}, u32[]{:S(2)}, u32[]{:S(2)}) collective-permute-start(f32[8,64,256]{2,1,0:T(8,128)S(1)} %multiply_add_fusion.4), channel_id=1, source_target_pairs={{0,16},{16,32},{32,48},{48,64},{64,80},{80,96},{96,112},{112,128},... | collective-permute-start | bytes 1572872 | tf_op jit(solution)/shard_map/while/body/eval_jaxpr/ppermute | solution.py:12
  48.9 15.9 %collective-permute-start = (f32[8,64,256]{2,1,0:T(8,128)S(1)}, f32[8,64,256]{2,1,0:T(8,128)S(1)}, u32[]{:S(2)}, u32[]{:S(2)}) collective-permute-start(f32[8,64,256]{2,1,0:T(8,128)S(1)} %multiply_add_fusion.4), channel_id=1, source_target_pairs={{0,16},{16,32},{32,48},{48,64},{64,80},{80,96},{96,112},{112,128},... | collective-permute-start | bytes 1572872 | tf_op jit(solution)/shard_map/while/body/eval_jaxpr/ppermute | solution.py:12
  64.8 15.0 %collective-permute-start = (f32[8,64,256]{2,1,0:T(8,128)S(1)}, f32[8,64,256]{2,1,0:T(8,128)S(1)}, u32[]{:S(2)}, u32[]{:S(2)}) collective-permute-start(f32[8,64,256]{2,1,0:T(8,128)S(1)} %multiply_add_fusion.4), channel_id=1, source_target_pairs={{0,16},{16,32},{32,48},{48,64},{64,80},{80,96},{96,112},{112,128},... | collective-permute-start | bytes 1572872 | tf_op jit(solution)/shard_map/while/body/eval_jaxpr/ppermute | solution.py:12
  79.9 14.0 %collective-permute-start = (f32[8,64,256]{2,1,0:T(8,128)S(1)}, f32[8,64,256]{2,1,0:T(8,128)S(1)}, u32[]{:S(2)}, u32[]{:S(2)}) collective-permute-start(f32[8,64,256]{2,1,0:T(8,128)S(1)} %multiply_add_fusion.4), channel_id=1, source_target_pairs={{0,16},{16,32},{32,48},{48,64},{64,80},{80,96},{96,112},{112,128},... | collective-permute-start | bytes 1572872 | tf_op jit(solution)/shard_map/while/body/eval_jaxpr/ppermute | solution.py:12
  94.0 13.2 %collective-permute-start = (f32[8,64,256]{2,1,0:T(8,128)S(1)}, f32[8,64,256]{2,1,0:T(8,128)S(1)}, u32[]{:S(2)}, u32[]{:S(2)}) collective-permute-start(f32[8,64,256]{2,1,0:T(8,128)S(1)} %multiply_add_fusion.4), channel_id=1, source_target_pairs={{0,16},{16,32},{32,48},{48,64},{64,80},{80,96},{96,112},{112,128},... | collective-permute-start | bytes 1572872 | tf_op jit(solution)/shard_map/while/body/eval_jaxpr/ppermute | solution.py:12
  107.2 13.5 %collective-permute-start = (f32[8,64,256]{2,1,0:T(8,128)S(1)}, f32[8,64,256]{2,1,0:T(8,128)S(1)}, u32[]{:S(2)}, u32[]{:S(2)}) collective-permute-start(f32[8,64,256]{2,1,0:T(8,128)S(1)} %multiply_add_fusion.4), channel_id=1, source_target_pairs={{0,16},{16,32},{32,48},{48,64},{64,80},{80,96},{96,112},{112,128},... | collective-permute-start | bytes 1572872 | tf_op jit(solution)/shard_map/while/body/eval_jaxpr/ppermute | solution.py:12
  120.8 14.6 %collective-permute-start = (f32[8,64,256]{2,1,0:T(8,128)S(1)}, f32[8,64,256]{2,1,0:T(8,128)S(1)}, u32[]{:S(2)}, u32[]{:S(2)}) collective-permute-start(f32[8,64,256]{2,1,0:T(8,128)S(1)} %multiply_add_fusion.4), channel_id=1, source_target_pairs={{0,16},{16,32},{32,48},{48,64},{64,80},{80,96},{96,112},{112,128},... | collective-permute-start | bytes 1572872 | tf_op jit(solution)/shard_map/while/body/eval_jaxpr/ppermute | solution.py:12
  135.4 15.6 %collective-permute-start = (f32[8,64,256]{2,1,0:T(8,128)S(1)}, f32[8,64,256]{2,1,0:T(8,128)S(1)}, u32[]{:S(2)}, u32[]{:S(2)}) collective-permute-start(f32[8,64,256]{2,1,0:T(8,128)S(1)} %multiply_add_fusion.4), channel_id=1, source_target_pairs={{0,16},{16,32},{32,48},{48,64},{64,80},{80,96},{96,112},{112,128},... | collective-permute-start | bytes 1572872 | tf_op jit(solution)/shard_map/while/body/eval_jaxpr/ppermute | solution.py:12
  151.1 16.7 %collective-permute-start = (f32[8,64,256]{2,1,0:T(8,128)S(1)}, f32[8,64,256]{2,1,0:T(8,128)S(1)}, u32[]{:S(2)}, u32[]{:S(2)}) collective-permute-start(f32[8,64,256]{2,1,0:T(8,128)S(1)} %multiply_add_fusion.4), channel_id=1, source_target_pairs={{0,16},{16,32},{32,48},{48,64},{64,80},{80,96},{96,112},{112,128},... | collective-permute-start | bytes 1572872 | tf_op jit(solution)/shard_map/while/body/eval_jaxpr/ppermute | solution.py:12
  167.9 17.9 %collective-permute-start = (f32[8,64,256]{2,1,0:T(8,128)S(1)}, f32[8,64,256]{2,1,0:T(8,128)S(1)}, u32[]{:S(2)}, u32[]{:S(2)}) collective-permute-start(f32[8,64,256]{2,1,0:T(8,128)S(1)} %multiply_add_fusion.4), channel_id=1, source_target_pairs={{0,16},{16,32},{32,48},{48,64},{64,80},{80,96},{96,112},{112,128},... | collective-permute-start | bytes 1572872 | tf_op jit(solution)/shard_map/while/body/eval_jaxpr/ppermute | solution.py:12
  185.8 18.6 %collective-permute-start = (f32[8,64,256]{2,1,0:T(8,128)S(1)}, f32[8,64,256]{2,1,0:T(8,128)S(1)}, u32[]{:S(2)}, u32[]{:S(2)}) collective-permute-start(f32[8,64,256]{2,1,0:T(8,128)S(1)} %multiply_add_fusion.4), channel_id=1, source_target_pairs={{0,16},{16,32},{32,48},{48,64},{64,80},{80,96},{96,112},{112,128},... | collective-permute-start | bytes 1572872 | tf_op jit(solution)/shard_map/while/body/eval_jaxpr/ppermute | solution.py:12
  204.5 17.7 %collective-permute-start = (f32[8,64,256]{2,1,0:T(8,128)S(1)}, f32[8,64,256]{2,1,0:T(8,128)S(1)}, u32[]{:S(2)}, u32[]{:S(2)}) collective-permute-start(f32[8,64,256]{2,1,0:T(8,128)S(1)} %multiply_add_fusion.4), channel_id=1, source_target_pairs={{0,16},{16,32},{32,48},{48,64},{64,80},{80,96},{96,112},{112,128},... | collective-permute-start | bytes 1572872 | tf_op jit(solution)/shard_map/while/body/eval_jaxpr/ppermute | solution.py:12
  222.3 16.9 %collective-permute-start = (f32[8,64,256]{2,1,0:T(8,128)S(1)}, f32[8,64,256]{2,1,0:T(8,128)S(1)}, u32[]{:S(2)}, u32[]{:S(2)}) collective-permute-start(f32[8,64,256]{2,1,0:T(8,128)S(1)} %multiply_add_fusion.4), channel_id=1, source_target_pairs={{0,16},{16,32},{32,48},{48,64},{64,80},{80,96},{96,112},{112,128},... | collective-permute-start | bytes 1572872 | tf_op jit(solution)/shard_map/while/body/eval_jaxpr/ppermute | solution.py:12
  239.2 13.2 %collective-permute-start = (f32[8,64,256]{2,1,0:T(8,128)S(1)}, f32[8,64,256]{2,1,0:T(8,128)S(1)}, u32[]{:S(2)}, u32[]{:S(2)}) collective-permute-start(f32[8,64,256]{2,1,0:T(8,128)S(1)} %multiply_add_fusion.4), channel_id=1, source_target_pairs={{0,16},{16,32},{32,48},{48,64},{64,80},{80,96},{96,112},{112,128},... | collective-permute-start | bytes 1572872 | tf_op jit(solution)/shard_map/while/body/eval_jaxpr/ppermute | solution.py:12
  279.1 12.2 %copy-start.1 = (f32[8,256]{1,0:T(8,128)S(1)}, f32[8,256]{1,0:T(8,128)}, u32[]{:S(2)}) copy-start(f32[8,256]{1,0:T(8,128)} %param.13) | copy-start | bytes 24580
  291.4 19.1 %copy-start.2 = (f32[8,256]{1,0:T(8,128)S(1)}, f32[8,256]{1,0:T(8,128)}, u32[]{:S(2)}) copy-start(f32[8,256]{1,0:T(8,128)} %param.15) | copy-start | bytes 24580
  291.4 19.1 %copy-start.3 = (f32[8,256]{1,0:T(8,128)S(1)}, f32[8,256]{1,0:T(8,128)}, u32[]{:S(2)}) copy-start(f32[8,256]{1,0:T(8,128)} %param.14) | copy-start | bytes 24580
  319.7 11.7 %collective-permute-start.1 = (f32[8,64,256]{2,1,0:T(8,128)S(1)}, f32[8,64,256]{2,1,0:T(8,128)S(1)}, u32[]{:S(2)}, u32[]{:S(2)}) collective-permute-start(f32[8,64,256]{2,1,0:T(8,128)S(1)} %multiply_add_fusion.5), channel_id=1, source_target_pairs={{0,1},{1,2},{2,3},{3,4},{4,5},{5,6},{6,7},{7,8},{8,9},{9,10},{10,1... | collective-permute-start | bytes 1572872 | tf_op jit(solution)/shard_map/while/body/eval_jaxpr/ppermute | solution.py:12
  331.5 11.7 %collective-permute-start.1 = (f32[8,64,256]{2,1,0:T(8,128)S(1)}, f32[8,64,256]{2,1,0:T(8,128)S(1)}, u32[]{:S(2)}, u32[]{:S(2)}) collective-permute-start(f32[8,64,256]{2,1,0:T(8,128)S(1)} %multiply_add_fusion.5), channel_id=1, source_target_pairs={{0,1},{1,2},{2,3},{3,4},{4,5},{5,6},{6,7},{7,8},{8,9},{9,10},{10,1... | collective-permute-start | bytes 1572872 | tf_op jit(solution)/shard_map/while/body/eval_jaxpr/ppermute | solution.py:12
  343.3 11.7 %collective-permute-start.1 = (f32[8,64,256]{2,1,0:T(8,128)S(1)}, f32[8,64,256]{2,1,0:T(8,128)S(1)}, u32[]{:S(2)}, u32[]{:S(2)}) collective-permute-start(f32[8,64,256]{2,1,0:T(8,128)S(1)} %multiply_add_fusion.5), channel_id=1, source_target_pairs={{0,1},{1,2},{2,3},{3,4},{4,5},{5,6},{6,7},{7,8},{8,9},{9,10},{10,1... | collective-permute-start | bytes 1572872 | tf_op jit(solution)/shard_map/while/body/eval_jaxpr/ppermute | solution.py:12
  355.1 11.7 %collective-permute-start.1 = (f32[8,64,256]{2,1,0:T(8,128)S(1)}, f32[8,64,256]{2,1,0:T(8,128)S(1)}, u32[]{:S(2)}, u32[]{:S(2)}) collective-permute-start(f32[8,64,256]{2,1,0:T(8,128)S(1)} %multiply_add_fusion.5), channel_id=1, source_target_pairs={{0,1},{1,2},{2,3},{3,4},{4,5},{5,6},{6,7},{7,8},{8,9},{9,10},{10,1... | collective-permute-start | bytes 1572872 | tf_op jit(solution)/shard_map/while/body/eval_jaxpr/ppermute | solution.py:12
  366.9 11.7 %collective-permute-start.1 = (f32[8,64,256]{2,1,0:T(8,128)S(1)}, f32[8,64,256]{2,1,0:T(8,128)S(1)}, u32[]{:S(2)}, u32[]{:S(2)}) collective-permute-start(f32[8,64,256]{2,1,0:T(8,128)S(1)} %multiply_add_fusion.5), channel_id=1, source_target_pairs={{0,1},{1,2},{2,3},{3,4},{4,5},{5,6},{6,7},{7,8},{8,9},{9,10},{10,1... | collective-permute-start | bytes 1572872 | tf_op jit(solution)/shard_map/while/body/eval_jaxpr/ppermute | solution.py:12
  378.7 11.7 %collective-permute-start.1 = (f32[8,64,256]{2,1,0:T(8,128)S(1)}, f32[8,64,256]{2,1,0:T(8,128)S(1)}, u32[]{:S(2)}, u32[]{:S(2)}) collective-permute-start(f32[8,64,256]{2,1,0:T(8,128)S(1)} %multiply_add_fusion.5), channel_id=1, source_target_pairs={{0,1},{1,2},{2,3},{3,4},{4,5},{5,6},{6,7},{7,8},{8,9},{9,10},{10,1... | collective-permute-start | bytes 1572872 | tf_op jit(solution)/shard_map/while/body/eval_jaxpr/ppermute | solution.py:12
  390.4 11.7 %collective-permute-start.1 = (f32[8,64,256]{2,1,0:T(8,128)S(1)}, f32[8,64,256]{2,1,0:T(8,128)S(1)}, u32[]{:S(2)}, u32[]{:S(2)}) collective-permute-start(f32[8,64,256]{2,1,0:T(8,128)S(1)} %multiply_add_fusion.5), channel_id=1, source_target_pairs={{0,1},{1,2},{2,3},{3,4},{4,5},{5,6},{6,7},{7,8},{8,9},{9,10},{10,1... | collective-permute-start | bytes 1572872 | tf_op jit(solution)/shard_map/while/body/eval_jaxpr/ppermute | solution.py:12
  402.2 11.7 %collective-permute-start.1 = (f32[8,64,256]{2,1,0:T(8,128)S(1)}, f32[8,64,256]{2,1,0:T(8,128)S(1)}, u32[]{:S(2)}, u32[]{:S(2)}) collective-permute-start(f32[8,64,256]{2,1,0:T(8,128)S(1)} %multiply_add_fusion.5), channel_id=1, source_target_pairs={{0,1},{1,2},{2,3},{3,4},{4,5},{5,6},{6,7},{7,8},{8,9},{9,10},{10,1... | collective-permute-start | bytes 1572872 | tf_op jit(solution)/shard_map/while/body/eval_jaxpr/ppermute | solution.py:12
  414.0 11.7 %collective-permute-start.1 = (f32[8,64,256]{2,1,0:T(8,128)S(1)}, f32[8,64,256]{2,1,0:T(8,128)S(1)}, u32[]{:S(2)}, u32[]{:S(2)}) collective-permute-start(f32[8,64,256]{2,1,0:T(8,128)S(1)} %multiply_add_fusion.5), channel_id=1, source_target_pairs={{0,1},{1,2},{2,3},{3,4},{4,5},{5,6},{6,7},{7,8},{8,9},{9,10},{10,1... | collective-permute-start | bytes 1572872 | tf_op jit(solution)/shard_map/while/body/eval_jaxpr/ppermute | solution.py:12
  425.8 11.7 %collective-permute-start.1 = (f32[8,64,256]{2,1,0:T(8,128)S(1)}, f32[8,64,256]{2,1,0:T(8,128)S(1)}, u32[]{:S(2)}, u32[]{:S(2)}) collective-permute-start(f32[8,64,256]{2,1,0:T(8,128)S(1)} %multiply_add_fusion.5), channel_id=1, source_target_pairs={{0,1},{1,2},{2,3},{3,4},{4,5},{5,6},{6,7},{7,8},{8,9},{9,10},{10,1... | collective-permute-start | bytes 1572872 | tf_op jit(solution)/shard_map/while/body/eval_jaxpr/ppermute | solution.py:12
  437.6 11.7 %collective-permute-start.1 = (f32[8,64,256]{2,1,0:T(8,128)S(1)}, f32[8,64,256]{2,1,0:T(8,128)S(1)}, u32[]{:S(2)}, u32[]{:S(2)}) collective-permute-start(f32[8,64,256]{2,1,0:T(8,128)S(1)} %multiply_add_fusion.5), channel_id=1, source_target_pairs={{0,1},{1,2},{2,3},{3,4},{4,5},{5,6},{6,7},{7,8},{8,9},{9,10},{10,1... | collective-permute-start | bytes 1572872 | tf_op jit(solution)/shard_map/while/body/eval_jaxpr/ppermute | solution.py:12
  449.4 11.7 %collective-permute-start.1 = (f32[8,64,256]{2,1,0:T(8,128)S(1)}, f32[8,64,256]{2,1,0:T(8,128)S(1)}, u32[]{:S(2)}, u32[]{:S(2)}) collective-permute-start(f32[8,64,256]{2,1,0:T(8,128)S(1)} %multiply_add_fusion.5), channel_id=1, source_target_pairs={{0,1},{1,2},{2,3},{3,4},{4,5},{5,6},{6,7},{7,8},{8,9},{9,10},{10,1... | collective-permute-start | bytes 1572872 | tf_op jit(solution)/shard_map/while/body/eval_jaxpr/ppermute | solution.py:12
  461.1 11.7 %collective-permute-start.1 = (f32[8,64,256]{2,1,0:T(8,128)S(1)}, f32[8,64,256]{2,1,0:T(8,128)S(1)}, u32[]{:S(2)}, u32[]{:S(2)}) collective-permute-start(f32[8,64,256]{2,1,0:T(8,128)S(1)} %multiply_add_fusion.5), channel_id=1, source_target_pairs={{0,1},{1,2},{2,3},{3,4},{4,5},{5,6},{6,7},{7,8},{8,9},{9,10},{10,1... | collective-permute-start | bytes 1572872 | tf_op jit(solution)/shard_map/while/body/eval_jaxpr/ppermute | solution.py:12
  472.9 11.7 %collective-permute-start.1 = (f32[8,64,256]{2,1,0:T(8,128)S(1)}, f32[8,64,256]{2,1,0:T(8,128)S(1)}, u32[]{:S(2)}, u32[]{:S(2)}) collective-permute-start(f32[8,64,256]{2,1,0:T(8,128)S(1)} %multiply_add_fusion.5), channel_id=1, source_target_pairs={{0,1},{1,2},{2,3},{3,4},{4,5},{5,6},{6,7},{7,8},{8,9},{9,10},{10,1... | collective-permute-start | bytes 1572872 | tf_op jit(solution)/shard_map/while/body/eval_jaxpr/ppermute | solution.py:12
  484.7 11.7 %collective-permute-start.1 = (f32[8,64,256]{2,1,0:T(8,128)S(1)}, f32[8,64,256]{2,1,0:T(8,128)S(1)}, u32[]{:S(2)}, u32[]{:S(2)}) collective-permute-start(f32[8,64,256]{2,1,0:T(8,128)S(1)} %multiply_add_fusion.5), channel_id=1, source_target_pairs={{0,1},{1,2},{2,3},{3,4},{4,5},{5,6},{6,7},{7,8},{8,9},{9,10},{10,1... | collective-permute-start | bytes 1572872 | tf_op jit(solution)/shard_map/while/body/eval_jaxpr/ppermute | solution.py:12
  556.7 10.5 %copy-start.4 = (bf16[256,1024]{1,0:T(8,128)(2,1)S(1)}, bf16[256,1024]{1,0:T(8,128)(2,1)}, u32[]{:S(2)}) copy-start(bf16[256,1024]{1,0:T(8,128)(2,1)} %param.16) | copy-start | bytes 1572868
where the time goes:
time: 585 us; the launch traced here: 576 us
  waiting for transfers between devices  353 us (60%)
  matrix products  87 us (15%)
  local copies, waits for them, and re-layouts  69 us (12%)
  starting transfers between devices  59.1 us (10%)
  other arithmetic  6.85 us (1%)
    ppermute x30, waiting for transfers between devices, from_behind(): return lax.ppermute(block, axis, route)  353 us
    ppermute x30, starting transfers between devices, from_behind(): return lax.ppermute(block, axis, route)  59.1 us
    gather x4, local copies, waits for them, and re-layouts, tables(): toeplitz = jnp.where((offset >= 0)[:, :, None], impulse[index], 0.0)  50.7 us
    dot_general x1, matrix products, on_device(): vert = local + jnp.einsum('mtc,mwc->twc', lead, incoming, precision=HIGH)  19 us
    dot_general x1, matrix products, on_device(): local = jnp.einsum('tsc,hsc->htc', toeplitz, field, precision=HIGH)  17.2 us
    dot_general x1, matrix products, on_device(): horiz = local + jnp.einsum('mtc,mhc->htc', lead, incoming, precision=HIGH)  16.1 us
    dot_general x1, matrix products, on_device(): local = jnp.einsum('tsc,swc->twc', toeplitz, field, precision=HIGH)  12.2 us
  transfers between devices with their start and end apart: 30, of which 30 were waited for; matrix products, arithmetic and copies ran while one was open for 0% of the time, Pallas kernels for 0%

commit v1 on v0

v1 whole, which is shorter than its diff:
```python
import math

import jax
import jax.numpy as jnp
from jax import lax
from jax.experimental import pallas as pl
from jax.experimental.pallas import tpu as pltpu
from jax.sharding import PartitionSpec as P

F32 = jnp.float32
BF16 = jnp.bfloat16
LANES = 128
MODES = 8
SQRT_2_PI = math.sqrt(2.0 / math.pi)


def gelu(x):
    inner = x * (SQRT_2_PI + (SQRT_2_PI * 0.044715) * (x * x))
    half = 0.5 * x
    return half + half * jnp.tanh(inner)


def poles(rate_ref, half, rows):
    lanes = slice(half * LANES, (half + 1) * LANES)
    return [
        jnp.broadcast_to(jnp.exp(-rate_ref[m : m + 1, lanes]), (rows, LANES)) for m in range(MODES)
    ]


def weights(rate_ref, coef_ref, half, rows):
    lanes = slice(half * LANES, (half + 1) * LANES)
    return [
        jnp.broadcast_to(
            coef_ref[m : m + 1, lanes] * jnp.sqrt(1.0 - jnp.exp(-2.0 * rate_ref[m : m + 1, lanes])),
            (rows, LANES),
        )
        for m in range(MODES)
    ]


def tree(terms):
    while len(terms) > 1:
        terms = [a + b for a, b in zip(terms[::2], terms[1::2])]
    return terms[0]


def edge_kernel(image_ref, rate_ref, edge_ref):
    for half in range(2):
        lanes = slice(half * LANES, (half + 1) * LANES)
        pole = poles(rate_ref, half, 16)

        def steps(i, states, lanes=lanes, pole=pole):
            for k in range(8):
                u = image_ref[i * 8 + k, :, lanes].astype(F32)
                states = [p * h + u for p, h in zip(pole, states)]
            return states

        states = lax.fori_loop(0, 8, steps, [jnp.zeros((16, LANES), F32)] * MODES)
        for m in range(MODES):
            edge_ref[half, :, m] = states[m].reshape(2, 8, LANES)


def prefix_kernel(span, edge_ref, rate_ref, out_ref):
    decay = [
        jnp.broadcast_to(jnp.exp(-span * rate_ref[m : m + 1, :]), (8, LANES)) for m in range(MODES)
    ]
    states = [jnp.zeros((8, LANES), F32)] * MODES
    for r in range(edge_ref.shape[0]):
        for m in range(MODES):
            out_ref[r, m] = states[m]
            states[m] = decay[m] * states[m] + edge_ref[r, m]


def act_kernel(image_ref, in_ref, vr_ref, vc_ref, hr_ref, act_ref, edge_ref, state, field):
    @pl.when(pl.program_id(0) == 0)
    def _():
        state[...] = in_ref[...]

    for half in range(2):
        lanes = slice(half * LANES, (half + 1) * LANES)
        pole = poles(vr_ref, half, 16)
        weight = weights(vr_ref, vc_ref, half, 16)

        def block(b, _, half=half, lanes=lanes, pole=pole, weight=weight):
            pair = pl.ds(b * 2, 2)
            cols = pl.ds(pl.multiple_of(b * 16, 16), 16)
            hs = [state[half, pair, m].reshape(16, LANES) for m in range(MODES)]
            for s in range(16):
                u = image_ref[s, cols, lanes].astype(F32)
                hs = [p * h + u for p, h in zip(pole, hs)]
                y = tree([q * h for q, h in zip(weight, hs)])
                a = gelu(y).astype(BF16).astype(F32)
                field[half, pl.ds(pl.multiple_of(s * 64 + b * 16, 16), 16), :] = a
            for m in range(MODES):
                state[half, pair, m] = hs[m].reshape(2, 8, LANES)
            return 0

        lax.fori_loop(0, 4, block, 0)

    for half in range(2):
        lanes = slice(half * LANES, (half + 1) * LANES)
        pole = poles(hr_ref, half, 16)

        def steps(i, states, half=half, lanes=lanes, pole=pole):
            for k in range(8):
                w = i * 8 + k
                u = field[half, pl.ds(w, 16, stride=64), :]
                act_ref[w, :, lanes] = u.astype(BF16)
                states = [p * h + u for p, h in zip(pole, states)]
            return states

        states = lax.fori_loop(0, 8, steps, [jnp.zeros((16, LANES), F32)] * MODES)
        for m in range(MODES):
            edge_ref[half, :, m] = states[m].reshape(2, 8, LANES)


def mix_kernel(core_ref, act_ref, keep_ref, got_ref, hr_ref, hc_ref, w_in_ref, w_out_ref, out_ref, horiz, mixed):
    core = core_ref[0]
    for half in range(2):
        lanes = slice(half * LANES, (half + 1) * LANES)
        pole = poles(hr_ref, half, 16)
        weight = weights(hr_ref, hc_ref, half, 16)
        mine = core == half
        start = [
            jnp.where(mine, keep_ref[:, m], got_ref[:, m]).reshape(16, LANES) for m in range(MODES)
        ]

        def steps(i, states, lanes=lanes, pole=pole, weight=weight):
            for k in range(8):
                w = i * 8 + k
                u = act_ref[w, :, lanes].astype(F32)
                states = [p * h + u for p, h in zip(pole, states)]
                y = tree([q * h for q, h in zip(weight, states)])
                horiz[pl.ds(pl.multiple_of(w * 16, 16), 16), lanes] = y
            return states

        lax.fori_loop(0, 8, steps, start)

    def mlp(i, _):
        y = horiz[pl.ds(pl.multiple_of(i * 256, 256), 256), :]
        scale = lax.rsqrt(jnp.mean(y * y, axis=-1, keepdims=True) + 1e-06)
        normed = (y * scale).astype(BF16)
        hidden = gelu(jnp.dot(normed, w_in_ref[...], preferred_element_type=F32)).astype(BF16)
        out = y + jnp.dot(hidden, w_out_ref[...], preferred_element_type=F32)
        for k in range(16):
            for half in range(2):
                lanes = slice(half * LANES, (half + 1) * LANES)
                mixed[half, pl.ds(i * 16 + k, 16, stride=64), :] = out[k * 16 : (k + 1) * 16, lanes]
        return 0

    lax.fori_loop(0, 4, mlp, 0)
    for half in range(2):
        lanes = slice(half * LANES, (half + 1) * LANES)
        out_ref[:, :, lanes] = mixed[half].astype(BF16).reshape(16, 64, LANES)


def whole(shape):
    return pl.BlockSpec(shape, lambda i: (0,) * len(shape))


def params(mib):
    return pltpu.CompilerParams(vmem_limit_bytes=mib * 1024 * 1024)


def row_edges(image, rate):
    return pl.pallas_call(
        edge_kernel,
        grid=(4,),
        in_specs=[pl.BlockSpec((64, 16, 256), lambda i: (0, i, 0)), whole((8, 256))],
        out_specs=pl.BlockSpec((2, 2, 8, 8, LANES), lambda i: (0, i, 0, 0, 0)),
        out_shape=jax.ShapeDtypeStruct((2, 8, 8, 8, LANES), F32),
        compiler_params=params(16),
        name="row_edges",
    )(image, rate)


def prefix(edges, rate, span):
    def kernel(edge_ref, rate_ref, out_ref):
        prefix_kernel(span, edge_ref, rate_ref, out_ref)

    return pl.pallas_call(
        kernel,
        out_shape=jax.ShapeDtypeStruct(edges.shape, F32),
        compiler_params=params(8),
        name="prefix",
    )(edges, rate)


def act_and_edges(image, incoming, vert_rate, vert_coef, horiz_rate):
    return pl.pallas_call(
        act_kernel,
        grid=(4,),
        in_specs=[
            pl.BlockSpec((16, 64, 256), lambda i: (i, 0, 0)),
            whole((2, 8, 8, 8, LANES)),
            whole((8, 256)),
            whole((8, 256)),
            whole((8, 256)),
        ],
        out_specs=[
            pl.BlockSpec((64, 16, 256), lambda i: (0, i, 0)),
            pl.BlockSpec((2, 2, 8, 8, LANES), lambda i: (0, i, 0, 0, 0)),
        ],
        out_shape=[
            jax.ShapeDtypeStruct((64, 64, 256), BF16),
            jax.ShapeDtypeStruct((2, 8, 8, 8, LANES), F32),
        ],
        scratch_shapes=[
            pltpu.VMEM((2, 8, 8, 8, LANES), F32),
            pltpu.VMEM((2, 1024, LANES), F32),
        ],
        compiler_params=params(16),
        name="act_and_edges",
    )(image, incoming, vert_rate, vert_coef, horiz_rate)


def mix(core, act, keep, got, horiz_rate, horiz_coef, w_in, w_out):
    return pl.pallas_call(
        mix_kernel,
        grid=(4,),
        in_specs=[
            pl.BlockSpec(memory_space=pltpu.SMEM),
            pl.BlockSpec((64, 16, 256), lambda i: (0, i, 0)),
            pl.BlockSpec((2, 8, 8, LANES), lambda i: (i, 0, 0, 0)),
            pl.BlockSpec((2, 8, 8, LANES), lambda i: (i, 0, 0, 0)),
            whole((8, 256)),
            whole((8, 256)),
            whole((256, 1024)),
            whole((1024, 256)),
        ],
        out_specs=pl.BlockSpec((16, 64, 256), lambda i: (i, 0, 0)),
        out_shape=jax.ShapeDtypeStruct((64, 64, 256), BF16),
        scratch_shapes=[pltpu.VMEM((1024, 256), F32), pltpu.VMEM((2, 1024, LANES), F32)],
        compiler_params=params(32),
        name="mix",
    )(core, act, keep, got, horiz_rate, horiz_coef, w_in, w_out)


def swap_cores(block):
    n = lax.axis_size("col")
    return lax.ppermute(block, "col", [(i, i ^ 1) for i in range(n)])


def on_device(image, vert_rate, vert_coef, horiz_rate, horiz_coef, w_in, w_out):
    rows, cols = lax.axis_size("row"), lax.axis_size("col")
    piece = lax.axis_index("row")
    core = lax.axis_index("col") % 2

    edges = row_edges(image, vert_rate).reshape(rows, 8, 8, LANES)
    edges = lax.all_to_all(edges, "row", 0, 0, tiled=True)
    rate_here = lax.dynamic_slice_in_dim(vert_rate, (piece // 8) * LANES, LANES, 1)
    incoming = prefix(edges, rate_here, 64.0)
    incoming = lax.all_to_all(incoming, "row", 0, 0, tiled=True).reshape(2, 8, 8, 8, LANES)

    act, edge = act_and_edges(image, incoming, vert_rate, vert_coef, horiz_rate)

    chips = [[2 * z + c for z in range(cols // 2)] for c in range(2)]
    mine = lax.dynamic_index_in_dim(edge, core, 0, keepdims=False)
    other = swap_cores(lax.dynamic_index_in_dim(edge, 1 - core, 0, keepdims=False))
    rate_here = lax.dynamic_slice_in_dim(horiz_rate, core * LANES, LANES, 1)
    decay = jnp.exp(-64.0 * rate_here)[None, :, None, :]
    first = jnp.where(core == 0, mine, other)
    second = jnp.where(core == 0, other, mine)
    joined = lax.all_to_all(decay * first + second, "col", 0, 0, tiled=True, axis_index_groups=chips)
    chain = prefix(joined, rate_here, 128.0)
    chain = lax.all_to_all(chain, "col", 0, 0, tiled=True, axis_index_groups=chips)
    after = decay * chain + first
    keep = jnp.where(core == 0, chain, after)
    got = swap_cores(jnp.where(core == 0, after, chain))

    return mix(core.reshape(1), act, keep, got, horiz_rate, horiz_coef, w_in, w_out)


def solution(mesh):
    placed = (P("row", "col", None), P(), P(), P(), P(), P(), P())
    return jax.shard_map(
        on_device, mesh=mesh, in_specs=placed, out_specs=P("row", "col", None), check_vma=False
    )
```

time: 585 us -> 112 us (0.19)
  the two profiles are of different devices: /device:TPU:136 before, /device:TPU:1 now
where the time goes in v1:
time: 112 us
  Pallas kernels  34.7 us (31%)
  blocking collectives  31.1 us (28%)
  waiting for transfers between devices  22.4 us (20%)
  starting transfers between devices  17.5 us (16%)
  local copies, waits for them, and re-layouts  5.73 us (5%)
    pallas_call x1, Pallas kernels, mix(): pl.pallas_call(mix_kernel, grid=(4,), in_specs=[pl.BlockSpec(memory_space...  19.9 us
    all_to_all x1, blocking collectives, on_device(): lax.all_to_all(decay * first + second, 'col', 0, 0, tiled=True, axis_inde...  19.1 us
    all_to_all x1, blocking collectives, on_device(): lax.all_to_all(chain, 'col', 0, 0, tiled=True, axis_index_groups=chips)  12.1 us
    pallas_call x1, Pallas kernels, act_and_edges(): pl.pallas_call(act_kernel, grid=(4,), in_specs=[pl.BlockSpec((16, 64, 256...  10.5 us
    all_to_all x1, waiting for transfers between devices, on_device(): edges = lax.all_to_all(edges, 'row', 0, 0, tiled=True)  10.5 us
    all_to_all x1, waiting for transfers between devices, on_device(): lax.all_to_all(incoming, 'row', 0, 0, tiled=True).reshape(2, 8, 8, 8, LANES)  9.65 us
    all_to_all x1, starting transfers between devices, on_device(): edges = lax.all_to_all(edges, 'row', 0, 0, tiled=True)  7.72 us
    ppermute x2, starting transfers between devices, swap_cores(): return lax.ppermute(block, 'col', [(i, i ^ 1) for i in range(n)])  6.18 us
  transfers between devices with their start and end apart: 4, of which 4 were waited for; matrix products, arithmetic and copies ran while one was open for 0% of the time, Pallas kernels for 0%

profile of v1, /device:TPU:1, one launch (start us, length us, event | category | flops | bytes accessed | tf_op | source)
XLA Modules:
  0.0 111.7 jit_solution(7021059100230635407)
XLA Ops:
  0.0 0.0 copy-start
  0.0 1.6 %copy-done = bf16[64,64,256]{2,1,0:T(8,128)(2,1)S(1)} copy-done((bf16[64,64,256]{2,1,0:T(8,128)(2,1)S(1)}, bf16[64,64,256]{2,1,0:T(8,128)(2,1)}, u32[]{:S(2)}) %copy-start) | copy-done | bytes 2097176
  1.6 0.0 copy-start.6
  1.6 0.7 copy-done.6
  2.3 0.0 copy-start.7
  2.3 3.4 %row_edges.1 = f32[2,8,8,8,128]{4,3,2,1,0:T(8,128)} custom-call(bf16[64,64,256]{2,1,0:T(8,128)(2,1)S(1)} %copy-done, f32[8,256]{1,0:T(8,128)S(1)} %copy-done.6), custom_call_target="tpu_custom_call" | custom-call | tf_op jit(solution)/shard_map/row_edges/pallas_call | solution.py:166
  5.7 0.0 copy-start.1
  5.7 0.0 copy-start.8
  5.7 0.0 copy-start.9
  5.7 7.7 %all-to-all-start = ((f32[16,8,8,128]{3,2,1,0:T(8,128)}), f32[16,8,8,128]{3,2,1,0:T(8,128)S(1)}, u32[]{:S(2)}, u32[]{:S(2)}) async-start(f32[16,8,8,128]{3,2,1,0:T(8,128)} %bitcast.1), calls=%async_computation | async-start | bytes 1048576 | tf_op jit(solution)/shard_map/all_to_all | solution.py:250
  13.5 0.0 copy-done.7
  13.5 10.5 %all-to-all-done.edge_ref = f32[16,8,8,128]{3,2,1,0:T(8,128)S(1)} async-done(((f32[16,8,8,128]{3,2,1,0:T(8,128)}), f32[16,8,8,128]{3,2,1,0:T(8,128)S(1)}, u32[]{:S(2)}, u32[]{:S(2)}) %all-to-all-start) | async-done | bytes 524320 | tf_op jit(solution)/shard_map/all_to_all | solution.py:250
  24.0 0.8 prefix.2
  24.8 3.6 %all-to-all-start.1 = ((f32[16,8,8,128]{3,2,1,0:T(8,128)}), f32[16,8,8,128]{3,2,1,0:T(8,128)S(1)}, u32[]{:S(2)}, u32[]{:S(2)}) async-start(f32[16,8,8,128]{3,2,1,0:T(8,128)} %prefix.2), calls=%async_computation.1 | async-start | bytes 1048576 | tf_op jit(solution)/shard_map/all_to_all | solution.py:253
  28.4 9.6 %all-to-all-done.1 = f32[16,8,8,128]{3,2,1,0:T(8,128)S(1)} async-done(((f32[16,8,8,128]{3,2,1,0:T(8,128)}), f32[16,8,8,128]{3,2,1,0:T(8,128)S(1)}, u32[]{:S(2)}, u32[]{:S(2)}) %all-to-all-start.1) | async-done | bytes 524320 | tf_op jit(solution)/shard_map/all_to_all | solution.py:253
  38.1 0.0 copy-done.1
  38.1 0.0 copy-done.8
  38.1 0.0 copy-done.9
  38.1 10.5 %act_and_edges.1 = (bf16[64,64,256]{2,1,0:T(8,128)(2,1)S(1)}, f32[2,8,8,8,128]{4,3,2,1,0:T(8,128)S(1)}) custom-call(bf16[64,64,256]{2,1,0:T(8,128)(2,1)S(1)} %copy-done.1, f32[2,8,8,8,128]{4,3,2,1,0:T(8,128)S(1)} %bitcast.16, f32[8,256]{1,0:T(8,128)S(1)} %copy-done.7, f32[8,256]{1,0:T(8,128)S(1)} %copy-done.9, f32[8,256]{1,0:T(8,128)S(1)} %copy-done.8), custom_call_target="tpu_custom_call" | custom-call | tf_op jit(solution)/shard_map/act_and_edges/pallas_call | solution.py:190
  48.6 0.0 copy-start.2
  48.6 1.3 %copy-done.2 = bf16[64,64,256]{2,1,0:T(8,128)(2,1)} copy-done((bf16[64,64,256]{2,1,0:T(8,128)(2,1)}, bf16[64,64,256]{2,1,0:T(8,128)(2,1)S(1)}, u32[]{:S(2)}) %copy-start.2) | copy-done | bytes 2097176
  49.9 0.0 copy-start.3
  49.9 0.0 copy-start.10
  49.9 2.9 %collective-permute-start = (f32[8,8,8,128]{3,2,1,0:T(8,128)S(1)}, f32[8,8,8,128]{3,2,1,0:T(8,128)S(1)}, u32[]{:S(2)}, u32[]{:S(2)}) collective-permute-start(f32[8,8,8,128]{3,2,1,0:T(8,128)S(1)} %dynamic-slice_bitcast_fusion), channel_id=1, source_target_pairs={{0,1},{1,0},{2,3},{3,2},{4,5},{5,4},{6,7},{7,6},{8,9},{9,8},{10,11... | collective-permute-start | bytes 786440 | tf_op jit(solution)/shard_map/ppermute | solution.py:241
  52.9 1.2 %collective-permute-done = f32[8,8,8,128]{3,2,1,0:T(8,128)S(1)} collective-permute-done((f32[8,8,8,128]{3,2,1,0:T(8,128)S(1)}, f32[8,8,8,128]{3,2,1,0:T(8,128)S(1)}, u32[]{:S(2)}, u32[]{:S(2)}) %collective-permute-start) | collective-permute-done | bytes 262176 | tf_op jit(solution)/shard_map/ppermute | solution.py:241
  54.1 19.1 %all_to_all.20.edge_ref = f32[8,8,8,128]{3,2,1,0:T(8,128)S(1)} all-to-all(f32[8,8,8,128]{3,2,1,0:T(8,128)S(1)} %fusion), channel_id=1, replica_groups={{0,2,4,6,8,10,12,14},{1,3,5,7,9,11,13,15},{16,18,20,22,24,26,28,30},{17..., dimensions={0} | all-to-all | bytes 524288 | tf_op jit(solution)/shard_map/all_to_all | solution.py:264
  73.2 12.1 %all_to_all.21 = f32[8,8,8,128]{3,2,1,0:T(8,128)S(1)} all-to-all(f32[8,8,8,128]{3,2,1,0:T(8,128)S(1)} %prefix.3), channel_id=1, replica_groups={{0,2,4,6,8,10,12,14},{1,3,5,7,9,11,13,15},{16,18,20,22,24,26,28,30},{17..., dimensions={0} | all-to-all | bytes 524288 | tf_op jit(solution)/shard_map/all_to_all | solution.py:266
  85.2 0.1 fusion.1
  85.3 3.3 %collective-permute-start.1 = (f32[8,8,8,128]{3,2,1,0:T(8,128)S(1)}, f32[8,8,8,128]{3,2,1,0:T(8,128)S(1)}, u32[]{:S(2)}, u32[]{:S(2)}) collective-permute-start(f32[8,8,8,128]{3,2,1,0:T(8,128)S(1)} %get-tuple-element.11), channel_id=1, source_target_pairs={{0,1},{1,0},{2,3},{3,2},{4,5},{5,4},{6,7},{7,6},{8,9},{9,8},{10,11... | collective-permute-start | bytes 786440 | tf_op jit(solution)/shard_map/ppermute | solution.py:241
  88.6 1.2 %collective-permute-done.1.got_ref = f32[8,8,8,128]{3,2,1,0:T(8,128)S(1)} collective-permute-done((f32[8,8,8,128]{3,2,1,0:T(8,128)S(1)}, f32[8,8,8,128]{3,2,1,0:T(8,128)S(1)}, u32[]{:S(2)}, u32[]{:S(2)}) %collective-permute-start.1) | collective-permute-done | bytes 262176 | tf_op jit(solution)/shard_map/ppermute | solution.py:241
  89.7 0.0 copy-done.3
  89.7 0.0 copy-done.10
  89.7 0.0 copy-start.4
  89.7 1.0 copy-done.4
  90.8 0.0 copy-start.5
  90.8 1.0 copy-done.5
  91.8 19.9 %mix.1 = bf16[64,64,256]{2,1,0:T(8,128)(2,1)} custom-call(s32[1]{0:T(128)} %bitcast.core_ref, bf16[64,64,256]{2,1,0:T(8,128)(2,1)S(1)} %copy-done.3, f32[8,8,8,128]{3,2,1,0:T(8,128)S(1)} %get-tuple-element.12.keep_ref, f32[8,8,8,128]{3,2,1,0:T(8,128)S(1)} %collective-permute-done.1.got_ref, f32[8,256]{1,0:T(8,128)S(1)} %copy-done.8, ...), custom_call_target="tpu_custom_call" | custom-call | tf_op jit(solution)/shard_map/mix/pallas_call | solution.py:218
  (5 shorter events, 0.1 us)
Async XLA Ops:
  0.0 1.6 %copy-start = (bf16[64,64,256]{2,1,0:T(8,128)(2,1)S(1)}, bf16[64,64,256]{2,1,0:T(8,128)(2,1)}, u32[]{:S(2)}) copy-start(bf16[64,64,256]{2,1,0:T(8,128)(2,1)} %image_ref.3) | copy-start | bytes 6291460
  1.6 0.7 copy-start.6
  2.3 11.2 %copy-start.7 = (f32[8,256]{1,0:T(8,128)S(1)}, f32[8,256]{1,0:T(8,128)}, u32[]{:S(2)}) copy-start(f32[8,256]{1,0:T(8,128)} %vr_ref.1) | copy-start | bytes 24580
  5.7 32.3 %copy-start.1 = (bf16[64,64,256]{2,1,0:T(8,128)(2,1)S(1)}, bf16[64,64,256]{2,1,0:T(8,128)(2,1)}, u32[]{:S(2)}) copy-start(bf16[64,64,256]{2,1,0:T(8,128)(2,1)} %image_ref.3) | copy-start | bytes 6291460
  5.7 32.3 %copy-start.8 = (f32[8,256]{1,0:T(8,128)S(1)}, f32[8,256]{1,0:T(8,128)}, u32[]{:S(2)}) copy-start(f32[8,256]{1,0:T(8,128)} %hr_ref.3) | copy-start | bytes 24580
  5.7 32.3 %copy-start.9 = (f32[8,256]{1,0:T(8,128)S(1)}, f32[8,256]{1,0:T(8,128)}, u32[]{:S(2)}) copy-start(f32[8,256]{1,0:T(8,128)} %vc_ref.1) | copy-start | bytes 24580
  5.7 18.2 %all-to-all-start = ((f32[16,8,8,128]{3,2,1,0:T(8,128)}), f32[16,8,8,128]{3,2,1,0:T(8,128)S(1)}, u32[]{:S(2)}, u32[]{:S(2)}) async-start(f32[16,8,8,128]{3,2,1,0:T(8,128)} %bitcast.1), calls=%async_computation | async-start | bytes 1048576 | tf_op jit(solution)/shard_map/all_to_all | solution.py:250
  24.8 13.2 %all-to-all-start.1 = ((f32[16,8,8,128]{3,2,1,0:T(8,128)}), f32[16,8,8,128]{3,2,1,0:T(8,128)S(1)}, u32[]{:S(2)}, u32[]{:S(2)}) async-start(f32[16,8,8,128]{3,2,1,0:T(8,128)} %prefix.2), calls=%async_computation.1 | async-start | bytes 1048576 | tf_op jit(solution)/shard_map/all_to_all | solution.py:253
  48.6 1.3 %copy-start.2 = (bf16[64,64,256]{2,1,0:T(8,128)(2,1)}, bf16[64,64,256]{2,1,0:T(8,128)(2,1)S(1)}, u32[]{:S(2)}) copy-start(bf16[64,64,256]{2,1,0:T(8,128)(2,1)S(1)} %get-tuple-element.7.act_ref) | copy-start | bytes 6291460
  49.9 39.8 %copy-start.3 = (bf16[64,64,256]{2,1,0:T(8,128)(2,1)S(1)}, bf16[64,64,256]{2,1,0:T(8,128)(2,1)}, u32[]{:S(2)}) copy-start(bf16[64,64,256]{2,1,0:T(8,128)(2,1)} %copy-done.2) | copy-start | bytes 6291460
  49.9 39.8 %copy-start.10 = (f32[8,256]{1,0:T(8,128)S(1)}, f32[8,256]{1,0:T(8,128)}, u32[]{:S(2)}) copy-start(f32[8,256]{1,0:T(8,128)} %hc_ref.1) | copy-start | bytes 24580
  49.9 4.1 %collective-permute-start = (f32[8,8,8,128]{3,2,1,0:T(8,128)S(1)}, f32[8,8,8,128]{3,2,1,0:T(8,128)S(1)}, u32[]{:S(2)}, u32[]{:S(2)}) collective-permute-start(f32[8,8,8,128]{3,2,1,0:T(8,128)S(1)} %dynamic-slice_bitcast_fusion), channel_id=1, source_target_pairs={{0,1},{1,0},{2,3},{3,2},{4,5},{5,4},{6,7},{7,6},{8,9},{9,8},{10,11... | collective-permute-start | bytes 786440 | tf_op jit(solution)/shard_map/ppermute | solution.py:241
  85.3 4.4 %collective-permute-start.1 = (f32[8,8,8,128]{3,2,1,0:T(8,128)S(1)}, f32[8,8,8,128]{3,2,1,0:T(8,128)S(1)}, u32[]{:S(2)}, u32[]{:S(2)}) collective-permute-start(f32[8,8,8,128]{3,2,1,0:T(8,128)S(1)} %get-tuple-element.11), channel_id=1, source_target_pairs={{0,1},{1,0},{2,3},{3,2},{4,5},{5,4},{6,7},{7,6},{8,9},{9,8},{10,11... | collective-permute-start | bytes 786440 | tf_op jit(solution)/shard_map/ppermute | solution.py:241
  89.7 1.0 copy-start.4
  90.8 1.0 copy-start.5

commit v2 on v1

--- a/solution.py
+++ b/solution.py
@@ -12,11 +12,19 @@
 LANES = 128
 MODES = 8
 SQRT_2_PI = math.sqrt(2.0 / math.pi)
+PITCH = 72
 
 
 def gelu(x):
     inner = x * (SQRT_2_PI + (SQRT_2_PI * 0.044715) * (x * x))
     half = 0.5 * x
+    return half + half * jnp.tanh(inner)
+
+
+def gelu_packed(x):
+    x = x.astype(BF16)
+    inner = x * (BF16(SQRT_2_PI) + BF16(SQRT_2_PI * 0.044715) * (x * x))
+    half = BF16(0.5) * x
     return half + half * jnp.tanh(inner)
 
 
@@ -71,28 +79,46 @@
             states[m] = decay[m] * states[m] + edge_ref[r, m]
 
 
-def act_kernel(image_ref, in_ref, vr_ref, vc_ref, hr_ref, act_ref, edge_ref, state, field):
-    @pl.when(pl.program_id(0) == 0)
-    def _():
-        state[...] = in_ref[...]
-
+def local_kernel(image_ref, rate_ref, coef_ref, out_ref):
+    for half in range(2):
+        lanes = slice(half * LANES, (half + 1) * LANES)
+        pole = poles(rate_ref, half, 16)
+        weight = weights(rate_ref, coef_ref, half, 16)
+
+        def steps(i, states, lanes=lanes, pole=pole, weight=weight):
+            for k in range(8):
+                s = i * 8 + k
+                u = image_ref[s, :, lanes].astype(F32)
+                states = [p * h + u for p, h in zip(pole, states)]
+                out_ref[s, :, lanes] = tree([q * h for q, h in zip(weight, states)])
+            return states
+
+        lax.fori_loop(0, 8, steps, [jnp.zeros((16, LANES), F32)] * MODES)
+
+
+def act_kernel(local_ref, in_ref, vr_ref, vc_ref, hr_ref, act_ref, edge_ref, tails, field):
     for half in range(2):
         lanes = slice(half * LANES, (half + 1) * LANES)
         pole = poles(vr_ref, half, 16)
-        weight = weights(vr_ref, vc_ref, half, 16)
-
-        def block(b, _, half=half, lanes=lanes, pole=pole, weight=weight):
+
+        @pl.when(pl.program_id(0) == 0)
+        def _(half=half, pole=pole):
+            weight = weights(vr_ref, vc_ref, half, 16)
+            for m in range(MODES):
+                factor = (pole[m] * weight[m])[None, :8]
+                tails[half, :, m] = in_ref[half, :, m] * factor
+
+        def block(b, _, half=half, lanes=lanes, pole=pole):
             pair = pl.ds(b * 2, 2)
             cols = pl.ds(pl.multiple_of(b * 16, 16), 16)
-            hs = [state[half, pair, m].reshape(16, LANES) for m in range(MODES)]
+            tail = [tails[half, pair, m].reshape(16, LANES) for m in range(MODES)]
             for s in range(16):
-                u = image_ref[s, cols, lanes].astype(F32)
-                hs = [p * h + u for p, h in zip(pole, hs)]
-                y = tree([q * h for q, h in zip(weight, hs)])
+                y = local_ref[s, cols, lanes] + tree(tail)
+                tail = [p * g for p, g in zip(pole, tail)]
                 a = gelu(y).astype(BF16).astype(F32)
-                field[half, pl.ds(pl.multiple_of(s * 64 + b * 16, 16), 16), :] = a
+                field[half, pl.ds(pl.multiple_of(s * PITCH + b * 16, 8), 16), :] = a
             for m in range(MODES):
-                state[half, pair, m] = hs[m].reshape(2, 8, LANES)
+                tails[half, pair, m] = tail[m].reshape(2, 8, LANES)
             return 0
 
         lax.fori_loop(0, 4, block, 0)
@@ -104,7 +130,7 @@
         def steps(i, states, half=half, lanes=lanes, pole=pole):
             for k in range(8):
                 w = i * 8 + k
-                u = field[half, pl.ds(w, 16, stride=64), :]
+                u = field[half, pl.ds(w, 16, stride=PITCH), :]
                 act_ref[w, :, lanes] = u.astype(BF16)
                 states = [p * h + u for p, h in zip(pole, states)]
             return states
@@ -114,44 +140,44 @@
             edge_ref[half, :, m] = states[m].reshape(2, 8, LANES)
 
 
-def mix_kernel(core_ref, act_ref, keep_ref, got_ref, hr_ref, hc_ref, w_in_ref, w_out_ref, out_ref, horiz, mixed):
+def mix_kernel(core_ref, local_ref, keep_ref, got_ref, hr_ref, hc_ref, w_in_ref, w_out_ref, out_ref, horiz, mixed):
     core = core_ref[0]
     for half in range(2):
         lanes = slice(half * LANES, (half + 1) * LANES)
         pole = poles(hr_ref, half, 16)
         weight = weights(hr_ref, hc_ref, half, 16)
         mine = core == half
-        start = [
-            jnp.where(mine, keep_ref[:, m], got_ref[:, m]).reshape(16, LANES) for m in range(MODES)
+        tail = [
+            jnp.where(mine, keep_ref[:, m], got_ref[:, m]).reshape(16, LANES) * (pole[m] * weight[m])
+            for m in range(MODES)
         ]
 
-        def steps(i, states, lanes=lanes, pole=pole, weight=weight):
+        def steps(i, tail, lanes=lanes, pole=pole):
             for k in range(8):
                 w = i * 8 + k
-                u = act_ref[w, :, lanes].astype(F32)
-                states = [p * h + u for p, h in zip(pole, states)]
-                y = tree([q * h for q, h in zip(weight, states)])
+                y = local_ref[w, :, lanes] + tree(tail)
+                tail = [p * g for p, g in zip(pole, tail)]
                 horiz[pl.ds(pl.multiple_of(w * 16, 16), 16), lanes] = y
-            return states
-
-        lax.fori_loop(0, 8, steps, start)
-
-    def mlp(i, _):
-        y = horiz[pl.ds(pl.multiple_of(i * 256, 256), 256), :]
-        scale = lax.rsqrt(jnp.mean(y * y, axis=-1, keepdims=True) + 1e-06)
-        normed = (y * scale).astype(BF16)
-        hidden = gelu(jnp.dot(normed, w_in_ref[...], preferred_element_type=F32)).astype(BF16)
-        out = y + jnp.dot(hidden, w_out_ref[...], preferred_element_type=F32)
-        for k in range(16):
-            for half in range(2):
-                lanes = slice(half * LANES, (half + 1) * LANES)
-                mixed[half, pl.ds(i * 16 + k, 16, stride=64), :] = out[k * 16 : (k + 1) * 16, lanes]
-        return 0
-
-    lax.fori_loop(0, 4, mlp, 0)
-    for half in range(2):
-        lanes = slice(half * LANES, (half + 1) * LANES)
-        out_ref[:, :, lanes] = mixed[half].astype(BF16).reshape(16, 64, LANES)
+            return tail
+
+        lax.fori_loop(0, 8, steps, tail)
+
+    y = horiz[...]
+    scale = lax.rsqrt(jnp.mean(y * y, axis=-1, keepdims=True) + 1e-06)
+    normed = (y * scale).astype(BF16)
+    hidden = gelu_packed(jnp.dot(normed, w_in_ref[...], preferred_element_type=F32))
+    out = y + jnp.dot(hidden, w_out_ref[...], preferred_element_type=F32)
+    for w in range(64):
+        for half in range(2):
+            lanes = slice(half * LANES, (half + 1) * LANES)
+            mixed[half, pl.ds(w, 16, stride=PITCH), :] = out[w * 16 : (w + 1) * 16, lanes]
+    for half in range(2):
+        lanes = slice(half * LANES, (half + 1) * LANES)
+        for h in range(16):
+            out_ref[h, :, lanes] = mixed[half, h * PITCH : h * PITCH + 64].astype(BF16)
+
+
+LOCAL_COST = pl.CostEstimate(flops=5_000_000_000, bytes_accessed=8_000_000, transcendentals=0)
 
 
 def whole(shape):
@@ -169,24 +195,40 @@
         in_specs=[pl.BlockSpec((64, 16, 256), lambda i: (0, i, 0)), whole((8, 256))],
         out_specs=pl.BlockSpec((2, 2, 8, 8, LANES), lambda i: (0, i, 0, 0, 0)),
         out_shape=jax.ShapeDtypeStruct((2, 8, 8, 8, LANES), F32),
-        compiler_params=params(16),
+        compiler_params=params(56),
         name="row_edges",
     )(image, rate)
 
 
-def prefix(edges, rate, span):
-    def kernel(edge_ref, rate_ref, out_ref):
+def prefix(edges, rate, span, after):
+    def kernel(edge_ref, rate_ref, after_ref, out_ref):
         prefix_kernel(span, edge_ref, rate_ref, out_ref)
 
+    vmem = pl.BlockSpec(memory_space=pltpu.VMEM)
     return pl.pallas_call(
         kernel,
+        in_specs=[vmem, vmem, pl.BlockSpec(memory_space=pltpu.HBM)],
+        out_specs=vmem,
         out_shape=jax.ShapeDtypeStruct(edges.shape, F32),
         compiler_params=params(8),
         name="prefix",
-    )(edges, rate)
-
-
-def act_and_edges(image, incoming, vert_rate, vert_coef, horiz_rate):
+    )(edges, rate, after)
+
+
+def local_scan(block, rate, coef, mib, name):
+    return pl.pallas_call(
+        local_kernel,
+        grid=(4,),
+        in_specs=[pl.BlockSpec((64, 16, 256), lambda i: (0, i, 0)), whole((8, 256)), whole((8, 256))],
+        out_specs=pl.BlockSpec((64, 16, 256), lambda i: (0, i, 0)),
+        out_shape=pltpu.HBM((64, 64, 256), F32),
+        compiler_params=params(mib),
+        cost_estimate=LOCAL_COST,
+        name=name,
+    )(block, rate, coef)
+
+
+def act_and_edges(local, incoming, vert_rate, vert_coef, horiz_rate):
     return pl.pallas_call(
         act_kernel,
         grid=(4,),
@@ -202,19 +244,19 @@
             pl.BlockSpec((2, 2, 8, 8, LANES), lambda i: (0, i, 0, 0, 0)),
         ],
         out_shape=[
-            jax.ShapeDtypeStruct((64, 64, 256), BF16),
+            pltpu.HBM((64, 64, 256), BF16),
             jax.ShapeDtypeStruct((2, 8, 8, 8, LANES), F32),
         ],
         scratch_shapes=[
             pltpu.VMEM((2, 8, 8, 8, LANES), F32),
-            pltpu.VMEM((2, 1024, LANES), F32),
-        ],
-        compiler_params=params(16),
+            pltpu.VMEM((2, 16 * PITCH, LANES), F32),
+        ],
+        compiler_params=params(24),
         name="act_and_edges",
-    )(image, incoming, vert_rate, vert_coef, horiz_rate)
-
-
-def mix(core, act, keep, got, horiz_rate, horiz_coef, w_in, w_out):
+    )(local, incoming, vert_rate, vert_coef, horiz_rate)
+
+
+def mix(core, local, keep, got, horiz_rate, horiz_coef, w_in, w_out):
     return pl.pallas_call(
         mix_kernel,
         grid=(4,),
@@ -230,10 +272,10 @@
         ],
         out_specs=pl.BlockSpec((16, 64, 256), lambda i: (i, 0, 0)),
         out_shape=jax.ShapeDtypeStruct((64, 64, 256), BF16),
-        scratch_shapes=[pltpu.VMEM((1024, 256), F32), pltpu.VMEM((2, 1024, LANES), F32)],
-        compiler_params=params(32),
+        scratch_shapes=[pltpu.VMEM((1024, 256), F32), pltpu.VMEM((2, 16 * PITCH, LANES), F32)],
+        compiler_params=params(40),
         name="mix",
-    )(core, act, keep, got, horiz_rate, horiz_coef, w_in, w_out)
+    )(core, local, keep, got, horiz_rate, horiz_coef, w_in, w_out)
 
 
 def swap_cores(block):
@@ -249,10 +291,13 @@
     edges = row_edges(image, vert_rate).reshape(rows, 8, 8, LANES)
     edges = lax.all_to_all(edges, "row", 0, 0, tiled=True)
     rate_here = lax.dynamic_slice_in_dim(vert_rate, (piece // 8) * LANES, LANES, 1)
-    incoming = prefix(edges, rate_here, 64.0)
+    local = local_scan(image, vert_rate, vert_coef, 56, "vert_local")
+    incoming = prefix(edges, rate_here, 64.0, local)
     incoming = lax.all_to_all(incoming, "row", 0, 0, tiled=True).reshape(2, 8, 8, 8, LANES)
 
-    act, edge = act_and_edges(image, incoming, vert_rate, vert_coef, horiz_rate)
+    act, edge = act_and_edges(local, incoming, vert_rate, vert_coef, horiz_rate)
+
+    horiz = local_scan(act, horiz_rate, horiz_coef, 56, "horiz_local")
 
     chips = [[2 * z + c for z in range(cols // 2)] for c in range(2)]
     mine = lax.dynamic_index_in_dim(edge, core, 0, keepdims=False)
@@ -262,13 +307,13 @@
     first = jnp.where(core == 0, mine, other)
     second = jnp.where(core == 0, other, mine)
     joined = lax.all_to_all(decay * first + second, "col", 0, 0, tiled=True, axis_index_groups=chips)
-    chain = prefix(joined, rate_here, 128.0)
+    chain = prefix(joined, rate_here, 128.0, horiz)
     chain = lax.all_to_all(chain, "col", 0, 0, tiled=True, axis_index_groups=chips)
     after = decay * chain + first
     keep = jnp.where(core == 0, chain, after)
     got = swap_cores(jnp.where(core == 0, after, chain))
 
-    return mix(core.reshape(1), act, keep, got, horiz_rate, horiz_coef, w_in, w_out)
+    return mix(core.reshape(1), horiz, keep, got, horiz_rate, horiz_coef, w_in, w_out)
 
 
 def solution(mesh):

time: 112 us -> 103 us (0.920)
  blocking collectives: 31.1 us -> 12.6 us
  starting transfers between devices: 17.5 us -> 25.4 us
  waiting for transfers between devices: 22.4 us -> 19.1 us
  Pallas kernels: 34.7 us -> 37.7 us
    all_to_all x1 -> x0, blocking collectives: 19.1 us -> none  [on_device(): lax.all_to_all(decay * first + second, 'col', 0, 0, tiled=True, axis_inde...]
    pallas_call x2 -> x4, Pallas kernels: 0.87 us -> 15.3 us  [the longest x2 14.4 us: local_scan(): pl.pallas_call(local_kernel, grid=(4,), in_specs=[pl.BlockSpec((64, 16, 2...]
    pallas_call x1, Pallas kernels: 19.9 us -> 9.9 us  [mix(): pl.pallas_call(mix_kernel, grid=(4,), in_specs=[pl.BlockSpec(memory_space...]
    all_to_all x0 -> x1, starting transfers between devices: none -> 8.19 us  [on_device(): lax.all_to_all(decay * first + second, 'col', 0, 0, tiled=True, axis_inde...]
    all_to_all x1, waiting for transfers between devices: 10.5 us -> 3.25 us  [on_device(): edges = lax.all_to_all(edges, 'row', 0, 0, tiled=True)]
    all_to_all x0 -> x1, waiting for transfers between devices: none -> 3.88 us  [on_device(): lax.all_to_all(decay * first + second, 'col', 0, 0, tiled=True, axis_inde...]
    pallas_call x1, Pallas kernels: 10.5 us -> 7.66 us  [act_and_edges(): pl.pallas_call(act_kernel, grid=(4,), in_specs=[pl.BlockSpec((16, 64, 256...]
    pallas_call x1, Pallas kernels: 3.43 us -> 4.82 us  [row_edges(): pl.pallas_call(edge_kernel, grid=(4,), in_specs=[pl.BlockSpec((64, 16, 25...]
  transfers between devices with their start and end apart: 4 -> 5, of which waited for: 4 -> 5; matrix products, arithmetic and copies ran while one was open for 0% -> 0% of each run, Pallas kernels for 0% -> 14%
where the time goes in v2:
time: 103 us; the launch traced here: 102 us
  Pallas kernels  37.7 us (37%)
  starting transfers between devices  25.4 us (25%)
  waiting for transfers between devices  19.1 us (19%)
  blocking collectives  12.6 us (12%)
  local copies, waits for them, and re-layouts  6.62 us (6%)
    pallas_call x2, Pallas kernels, local_scan(): pl.pallas_call(local_kernel, grid=(4,), in_specs=[pl.BlockSpec((64, 16, 2...  14.4 us
    all_to_all x1, blocking collectives, on_device(): lax.all_to_all(chain, 'col', 0, 0, tiled=True, axis_index_groups=chips)  12.6 us
    pallas_call x1, Pallas kernels, mix(): pl.pallas_call(mix_kernel, grid=(4,), in_specs=[pl.BlockSpec(memory_space...  9.9 us
    all_to_all x1, waiting for transfers between devices, on_device(): lax.all_to_all(incoming, 'row', 0, 0, tiled=True).reshape(2, 8, 8, 8, LANES)  9.65 us
    all_to_all x1, starting transfers between devices, on_device(): lax.all_to_all(decay * first + second, 'col', 0, 0, tiled=True, axis_inde...  8.19 us
    pallas_call x1, Pallas kernels, act_and_edges(): pl.pallas_call(act_kernel, grid=(4,), in_specs=[pl.BlockSpec((16, 64, 256...  7.66 us
    all_to_all x1, starting transfers between devices, on_device(): edges = lax.all_to_all(edges, 'row', 0, 0, tiled=True)  7.58 us
    unnamed x24, local copies, waits for them, and re-layouts  6.6 us
  transfers between devices with their start and end apart: 5, of which 5 were waited for; matrix products, arithmetic and copies ran while one was open for 0% of the time, Pallas kernels for 14%

profile of v2, /device:TPU:1, one launch (start us, length us, event | category | flops | bytes accessed | tf_op | source)
XLA Modules:
  0.0 102.4 jit_solution(10123519181917479197)
XLA Ops:
  0.0 0.0 copy-start.6
  0.0 4.8 %row_edges.1 = f32[2,8,8,8,128]{4,3,2,1,0:T(8,128)} custom-call(bf16[64,64,256]{2,1,0:T(8,128)(2,1)} %image_ref.3, f32[8,256]{1,0:T(8,128)} %vr_ref.1), custom_call_target="tpu_custom_call" | custom-call | tf_op jit(solution)/shard_map/row_edges/pallas_call | solution.py:192
  4.8 7.6 %all-to-all-start = ((f32[16,8,8,128]{3,2,1,0:T(8,128)}), f32[16,8,8,128]{3,2,1,0:T(8,128)S(1)}, u32[]{:S(2)}, u32[]{:S(2)}) async-start(f32[16,8,8,128]{3,2,1,0:T(8,128)} %bitcast.17), calls=%async_computation | async-start | bytes 1048576 | tf_op jit(solution)/shard_map/all_to_all | solution.py:292
  12.4 0.0 copy-done.6
  12.5 7.2 %vert_local.1.after_ref.local_ref = f32[64,64,256]{2,1,0:T(8,128)} custom-call(bf16[64,64,256]{2,1,0:T(8,128)(2,1)} %image_ref.3, f32[8,256]{1,0:T(8,128)} %vr_ref.1, f32[8,256]{1,0:T(8,128)} %vc_ref.1), custom_call_target="tpu_custom_call" | custom-call | flops 5000000000 | bytes 8000000 | tf_op jit(solution)/shard_map/vert_local/pallas_call | solution.py:219
  19.7 3.3 %all-to-all-done.edge_ref = f32[16,8,8,128]{3,2,1,0:T(8,128)S(1)} async-done(((f32[16,8,8,128]{3,2,1,0:T(8,128)}), f32[16,8,8,128]{3,2,1,0:T(8,128)S(1)}, u32[]{:S(2)}, u32[]{:S(2)}) %all-to-all-start) | async-done | bytes 524320 | tf_op jit(solution)/shard_map/all_to_all | solution.py:292
  22.9 0.0 copy-start
  22.9 2.2 %copy-done = f32[64,64,256]{2,1,0:T(8,128)S(1)} copy-done((f32[64,64,256]{2,1,0:T(8,128)S(1)}, f32[64,64,256]{2,1,0:T(8,128)}, u32[]{:S(2)}) %copy-start) | copy-done | bytes 4194328
  25.1 0.0 copy-start.7
  25.1 0.0 copy-start.8
  25.1 0.0 copy-start.10
  25.1 0.8 prefix.2
  26.0 3.6 %all-to-all-start.1 = ((f32[16,8,8,128]{3,2,1,0:T(8,128)}), f32[16,8,8,128]{3,2,1,0:T(8,128)S(1)}, u32[]{:S(2)}, u32[]{:S(2)}) async-start(f32[16,8,8,128]{3,2,1,0:T(8,128)} %prefix.2), calls=%async_computation.1 | async-start | bytes 1048576 | tf_op jit(solution)/shard_map/all_to_all | solution.py:296
  29.6 9.6 %all-to-all-done.1 = f32[16,8,8,128]{3,2,1,0:T(8,128)S(1)} async-done(((f32[16,8,8,128]{3,2,1,0:T(8,128)}), f32[16,8,8,128]{3,2,1,0:T(8,128)S(1)}, u32[]{:S(2)}, u32[]{:S(2)}) %all-to-all-start.1) | async-done | bytes 524320 | tf_op jit(solution)/shard_map/all_to_all | solution.py:296
  39.2 0.0 copy-done.7
  39.2 0.0 copy-done.8
  39.2 0.0 copy-done.10
  39.2 0.0 copy-start.1
  39.2 2.2 %copy-done.1 = f32[64,64,256]{2,1,0:T(8,128)S(1)} copy-done((f32[64,64,256]{2,1,0:T(8,128)S(1)}, f32[64,64,256]{2,1,0:T(8,128)}, u32[]{:S(2)}) %copy-start.1) | copy-done | bytes 4194328
  41.4 7.7 %act_and_edges.1 = (bf16[64,64,256]{2,1,0:T(8,128)(2,1)}, f32[2,8,8,8,128]{4,3,2,1,0:T(8,128)S(1)}) custom-call(f32[64,64,256]{2,1,0:T(8,128)S(1)} %copy-done.1, f32[2,8,8,8,128]{4,3,2,1,0:T(8,128)S(1)} %bitcast.16, f32[8,256]{1,0:T(8,128)S(1)} %copy-done.7, f32[8,256]{1,0:T(8,128)S(1)} %copy-done.10, f32[8,256]{1,0:T(8,128)S(1)} %copy-done.8), custom_call_target="tpu_custom_call" | custom-call | tf_op jit(solution)/shard_map/act_and_edges/pallas_call | solution.py:232
  49.1 2.9 %collective-permute-start = (f32[8,8,8,128]{3,2,1,0:T(8,128)S(1)}, f32[8,8,8,128]{3,2,1,0:T(8,128)S(1)}, u32[]{:S(2)}, u32[]{:S(2)}) collective-permute-start(f32[8,8,8,128]{3,2,1,0:T(8,128)S(1)} %dynamic-slice_bitcast_fusion), channel_id=1, source_target_pairs={{0,1},{1,0},{2,3},{3,2},{4,5},{5,4},{6,7},{7,6},{8,9},{9,8},{10,11... | collective-permute-start | bytes 786440 | tf_op jit(solution)/shard_map/ppermute | solution.py:283
  52.0 1.2 %collective-permute-done = f32[8,8,8,128]{3,2,1,0:T(8,128)S(1)} collective-permute-done((f32[8,8,8,128]{3,2,1,0:T(8,128)S(1)}, f32[8,8,8,128]{3,2,1,0:T(8,128)S(1)}, u32[]{:S(2)}, u32[]{:S(2)}) %collective-permute-start) | collective-permute-done | bytes 262176 | tf_op jit(solution)/shard_map/ppermute | solution.py:283
  53.2 0.8 fusion
  53.9 8.2 %all-to-all-start.2 = ((f32[8,8,8,128]{3,2,1,0:T(8,128)}), f32[8,8,8,128]{3,2,1,0:T(8,128)S(1)}, u32[]{:S(2)}, u32[]{:S(2)}) async-start(f32[8,8,8,128]{3,2,1,0:T(8,128)} %fusion), calls=%async_computation.2 | async-start | bytes 524288 | tf_op jit(solution)/shard_map/all_to_all | solution.py:309
  62.1 7.2 %horiz_local.1.after_ref.local_ref = f32[64,64,256]{2,1,0:T(8,128)} custom-call(bf16[64,64,256]{2,1,0:T(8,128)(2,1)} %get-tuple-element.7.image_ref, f32[8,256]{1,0:T(8,128)} %hr_ref.3, f32[8,256]{1,0:T(8,128)} %hc_ref.1), custom_call_target="tpu_custom_call" | custom-call | flops 5000000000 | bytes 8000000 | tf_op jit(solution)/shard_map/horiz_local/pallas_call | solution.py:219
  69.3 3.9 %all-to-all-done.2.edge_ref = f32[8,8,8,128]{3,2,1,0:T(8,128)S(1)} async-done(((f32[8,8,8,128]{3,2,1,0:T(8,128)}), f32[8,8,8,128]{3,2,1,0:T(8,128)S(1)}, u32[]{:S(2)}, u32[]{:S(2)}) %all-to-all-start.2) | async-done | bytes 262176 | tf_op jit(solution)/shard_map/all_to_all | solution.py:309
  73.2 0.0 copy-start.2
  73.2 2.2 %copy-done.2 = f32[64,64,256]{2,1,0:T(8,128)S(1)} copy-done((f32[64,64,256]{2,1,0:T(8,128)S(1)}, f32[64,64,256]{2,1,0:T(8,128)}, u32[]{:S(2)}) %copy-start.2) | copy-done | bytes 4194328
  75.4 0.0 copy-start.3
  75.4 0.0 copy-start.9
  75.4 0.0 copy-start.11
  75.4 0.0 copy-start.4
  75.5 0.0 copy-start.5
  75.5 12.6 %all_to_all.20 = f32[8,8,8,128]{3,2,1,0:T(8,128)S(1)} all-to-all(f32[8,8,8,128]{3,2,1,0:T(8,128)S(1)} %prefix.3), channel_id=1, replica_groups={{0,2,4,6,8,10,12,14},{1,3,5,7,9,11,13,15},{16,18,20,22,24,26,28,30},{17..., dimensions={0} | all-to-all | bytes 524288 | tf_op jit(solution)/shard_map/all_to_all | solution.py:311
  88.1 0.1 fusion.1
  88.2 3.1 %collective-permute-start.1 = (f32[8,8,8,128]{3,2,1,0:T(8,128)S(1)}, f32[8,8,8,128]{3,2,1,0:T(8,128)S(1)}, u32[]{:S(2)}, u32[]{:S(2)}) collective-permute-start(f32[8,8,8,128]{3,2,1,0:T(8,128)S(1)} %get-tuple-element.11), channel_id=1, source_target_pairs={{0,1},{1,0},{2,3},{3,2},{4,5},{5,4},{6,7},{7,6},{8,9},{9,8},{10,11... | collective-permute-start | bytes 786440 | tf_op jit(solution)/shard_map/ppermute | solution.py:283
  91.3 1.2 %collective-permute-done.1.got_ref = f32[8,8,8,128]{3,2,1,0:T(8,128)S(1)} collective-permute-done((f32[8,8,8,128]{3,2,1,0:T(8,128)S(1)}, f32[8,8,8,128]{3,2,1,0:T(8,128)S(1)}, u32[]{:S(2)}, u32[]{:S(2)}) %collective-permute-start.1) | collective-permute-done | bytes 262176 | tf_op jit(solution)/shard_map/ppermute | solution.py:283
  92.5 0.0 copy-done.3
  92.5 0.0 copy-done.9
  92.5 0.0 copy-done.11
  92.5 0.0 copy-done.4
  92.5 0.0 copy-done.5
  92.5 9.9 %mix.1 = bf16[64,64,256]{2,1,0:T(8,128)(2,1)} custom-call(s32[1]{0:T(128)} %bitcast.core_ref, f32[64,64,256]{2,1,0:T(8,128)S(1)} %copy-done.3, f32[8,8,8,128]{3,2,1,0:T(8,128)S(1)} %get-tuple-element.12.keep_ref, f32[8,8,8,128]{3,2,1,0:T(8,128)S(1)} %collective-permute-done.1.got_ref, f32[8,256]{1,0:T(8,128)S(1)} %copy-done.9, f32[8,256]{1,0:T(8,128)S(1)} %copy-done.11, ...), custom_call_target="tpu_custom_call" | custom-call | tf_op jit(solution)/shard_map/mix/pallas_call | solution.py:260
  (4 shorter events, 0.1 us)
Async XLA Ops:
  0.0 12.4 %copy-start.6 = (f32[8,256]{1,0:T(8,128)S(1)}, f32[8,256]{1,0:T(8,128)}, u32[]{:S(2)}) copy-start(f32[8,256]{1,0:T(8,128)} %vr_ref.1) | copy-start | bytes 24580
  4.8 18.1 %all-to-all-start = ((f32[16,8,8,128]{3,2,1,0:T(8,128)}), f32[16,8,8,128]{3,2,1,0:T(8,128)S(1)}, u32[]{:S(2)}, u32[]{:S(2)}) async-start(f32[16,8,8,128]{3,2,1,0:T(8,128)} %bitcast.17), calls=%async_computation | async-start | bytes 1048576 | tf_op jit(solution)/shard_map/all_to_all | solution.py:292
  22.9 2.2 %copy-start = (f32[64,64,256]{2,1,0:T(8,128)S(1)}, f32[64,64,256]{2,1,0:T(8,128)}, u32[]{:S(2)}) copy-start(f32[64,64,256]{2,1,0:T(8,128)} %vert_local.1.after_ref.local_ref) | copy-start | bytes 12582916
  25.1 14.1 %copy-start.7 = (f32[8,256]{1,0:T(8,128)S(1)}, f32[8,256]{1,0:T(8,128)}, u32[]{:S(2)}) copy-start(f32[8,256]{1,0:T(8,128)} %vr_ref.1) | copy-start | bytes 24580
  25.1 14.1 %copy-start.8 = (f32[8,256]{1,0:T(8,128)S(1)}, f32[8,256]{1,0:T(8,128)}, u32[]{:S(2)}) copy-start(f32[8,256]{1,0:T(8,128)} %hr_ref.3) | copy-start | bytes 24580
  25.1 14.1 %copy-start.10 = (f32[8,256]{1,0:T(8,128)S(1)}, f32[8,256]{1,0:T(8,128)}, u32[]{:S(2)}) copy-start(f32[8,256]{1,0:T(8,128)} %vc_ref.1) | copy-start | bytes 24580
  26.0 13.2 %all-to-all-start.1 = ((f32[16,8,8,128]{3,2,1,0:T(8,128)}), f32[16,8,8,128]{3,2,1,0:T(8,128)S(1)}, u32[]{:S(2)}, u32[]{:S(2)}) async-start(f32[16,8,8,128]{3,2,1,0:T(8,128)} %prefix.2), calls=%async_computation.1 | async-start | bytes 1048576 | tf_op jit(solution)/shard_map/all_to_all | solution.py:296
  39.2 2.2 %copy-start.1 = (f32[64,64,256]{2,1,0:T(8,128)S(1)}, f32[64,64,256]{2,1,0:T(8,128)}, u32[]{:S(2)}) copy-start(f32[64,64,256]{2,1,0:T(8,128)} %vert_local.1.after_ref.local_ref) | copy-start | bytes 12582916
  49.1 4.1 %collective-permute-start = (f32[8,8,8,128]{3,2,1,0:T(8,128)S(1)}, f32[8,8,8,128]{3,2,1,0:T(8,128)S(1)}, u32[]{:S(2)}, u32[]{:S(2)}) collective-permute-start(f32[8,8,8,128]{3,2,1,0:T(8,128)S(1)} %dynamic-slice_bitcast_fusion), channel_id=1, source_target_pairs={{0,1},{1,0},{2,3},{3,2},{4,5},{5,4},{6,7},{7,6},{8,9},{9,8},{10,11... | collective-permute-start | bytes 786440 | tf_op jit(solution)/shard_map/ppermute | solution.py:283
  53.9 19.3 %all-to-all-start.2 = ((f32[8,8,8,128]{3,2,1,0:T(8,128)}), f32[8,8,8,128]{3,2,1,0:T(8,128)S(1)}, u32[]{:S(2)}, u32[]{:S(2)}) async-start(f32[8,8,8,128]{3,2,1,0:T(8,128)} %fusion), calls=%async_computation.2 | async-start | bytes 524288 | tf_op jit(solution)/shard_map/all_to_all | solution.py:309
  73.2 2.2 %copy-start.2 = (f32[64,64,256]{2,1,0:T(8,128)S(1)}, f32[64,64,256]{2,1,0:T(8,128)}, u32[]{:S(2)}) copy-start(f32[64,64,256]{2,1,0:T(8,128)} %horiz_local.1.after_ref.local_ref) | copy-start | bytes 12582916
  75.4 17.0 %copy-start.3 = (f32[64,64,256]{2,1,0:T(8,128)S(1)}, f32[64,64,256]{2,1,0:T(8,128)}, u32[]{:S(2)}) copy-start(f32[64,64,256]{2,1,0:T(8,128)} %horiz_local.1.after_ref.local_ref) | copy-start | bytes 12582916
  75.4 17.0 %copy-start.9 = (f32[8,256]{1,0:T(8,128)S(1)}, f32[8,256]{1,0:T(8,128)}, u32[]{:S(2)}) copy-start(f32[8,256]{1,0:T(8,128)} %hr_ref.3) | copy-start | bytes 24580
  75.4 17.1 %copy-start.11 = (f32[8,256]{1,0:T(8,128)S(1)}, f32[8,256]{1,0:T(8,128)}, u32[]{:S(2)}) copy-start(f32[8,256]{1,0:T(8,128)} %hc_ref.1) | copy-start | bytes 24580
  75.4 17.0 %copy-start.4 = (bf16[256,1024]{1,0:T(8,128)(2,1)S(1)}, bf16[256,1024]{1,0:T(8,128)(2,1)}, u32[]{:S(2)}) copy-start(bf16[256,1024]{1,0:T(8,128)(2,1)} %w_in_ref.1) | copy-start | bytes 1572868
  75.5 17.0 %copy-start.5 = (bf16[1024,256]{1,0:T(8,128)(2,1)S(1)}, bf16[1024,256]{1,0:T(8,128)(2,1)}, u32[]{:S(2)}) copy-start(bf16[1024,256]{1,0:T(8,128)(2,1)} %w_out_ref.1) | copy-start | bytes 1572868
  88.2 4.3 %collective-permute-start.1 = (f32[8,8,8,128]{3,2,1,0:T(8,128)S(1)}, f32[8,8,8,128]{3,2,1,0:T(8,128)S(1)}, u32[]{:S(2)}, u32[]{:S(2)}) collective-permute-start(f32[8,8,8,128]{3,2,1,0:T(8,128)S(1)} %get-tuple-element.11), channel_id=1, source_target_pairs={{0,1},{1,0},{2,3},{3,2},{4,5},{5,4},{6,7},{7,6},{8,9},{9,8},{10,11... | collective-permute-start | bytes 786440 | tf_op jit(solution)/shard_map/ppermute | solution.py:283

commit v3 on v2

--- a/solution.py
+++ b/solution.py
@@ -180,6 +180,10 @@
 LOCAL_COST = pl.CostEstimate(flops=5_000_000_000, bytes_accessed=8_000_000, transcendentals=0)
 
 
+def in_hbm(block):
+    return pltpu.with_memory_space_constraint(block, pltpu.HBM)
+
+
 def whole(shape):
     return pl.BlockSpec(shape, lambda i: (0,) * len(shape))
 
@@ -200,19 +204,16 @@
     )(image, rate)
 
 
-def prefix(edges, rate, span, after):
-    def kernel(edge_ref, rate_ref, after_ref, out_ref):
+def prefix(edges, rate, span):
+    def kernel(edge_ref, rate_ref, out_ref):
         prefix_kernel(span, edge_ref, rate_ref, out_ref)
 
-    vmem = pl.BlockSpec(memory_space=pltpu.VMEM)
     return pl.pallas_call(
         kernel,
-        in_specs=[vmem, vmem, pl.BlockSpec(memory_space=pltpu.HBM)],
-        out_specs=vmem,
         out_shape=jax.ShapeDtypeStruct(edges.shape, F32),
         compiler_params=params(8),
         name="prefix",
-    )(edges, rate, after)
+    )(edges, rate)
 
 
 def local_scan(block, rate, coef, mib, name):
@@ -253,7 +254,7 @@
         ],
         compiler_params=params(24),
         name="act_and_edges",
-    )(local, incoming, vert_rate, vert_coef, horiz_rate)
+    )(in_hbm(local), incoming, vert_rate, vert_coef, horiz_rate)
 
 
 def mix(core, local, keep, got, horiz_rate, horiz_coef, w_in, w_out):
@@ -275,7 +276,7 @@
         scratch_shapes=[pltpu.VMEM((1024, 256), F32), pltpu.VMEM((2, 16 * PITCH, LANES), F32)],
         compiler_params=params(40),
         name="mix",
-    )(core, local, keep, got, horiz_rate, horiz_coef, w_in, w_out)
+    )(core, in_hbm(local), keep, got, horiz_rate, horiz_coef, w_in, w_out)
 
 
 def swap_cores(block):
@@ -292,7 +293,8 @@
     edges = lax.all_to_all(edges, "row", 0, 0, tiled=True)
     rate_here = lax.dynamic_slice_in_dim(vert_rate, (piece // 8) * LANES, LANES, 1)
     local = local_scan(image, vert_rate, vert_coef, 56, "vert_local")
-    incoming = prefix(edges, rate_here, 64.0, local)
+    edges, local = lax.optimization_barrier((edges, local))
+    incoming = prefix(edges, rate_here, 64.0)
     incoming = lax.all_to_all(incoming, "row", 0, 0, tiled=True).reshape(2, 8, 8, 8, LANES)
 
     act, edge = act_and_edges(local, incoming, vert_rate, vert_coef, horiz_rate)
@@ -307,7 +309,8 @@
     first = jnp.where(core == 0, mine, other)
     second = jnp.where(core == 0, other, mine)
     joined = lax.all_to_all(decay * first + second, "col", 0, 0, tiled=True, axis_index_groups=chips)
-    chain = prefix(joined, rate_here, 128.0, horiz)
+    joined, horiz = lax.optimization_barrier((joined, horiz))
+    chain = prefix(joined, rate_here, 128.0)
     chain = lax.all_to_all(chain, "col", 0, 0, tiled=True, axis_index_groups=chips)
     after = decay * chain + first
     keep = jnp.where(core == 0, chain, after)

time: 103 us -> 98.6 us (0.957)
  local copies, waits for them, and re-layouts: 6.62 us -> 0.06 us
  Pallas kernels: 37.7 us -> 40 us
    unnamed x24 -> x16, local copies, waits for them, and re-layouts: 6.6 us -> 0.03 us
    pallas_call x1, Pallas kernels: 7.66 us -> 8.92 us  [act_and_edges(): pl.pallas_call(act_kernel, grid=(4,), in_specs=[pl.BlockSpec((16, 64, 256...]
  transfers between devices with their start and end apart: 5 -> 5, of which waited for: 5 -> 5; matrix products, arithmetic and copies ran while one was open for 0% -> 0% of each run, Pallas kernels for 14% -> 15%
where the time goes in v3:
time: 98.6 us; the launch traced here: 97.9 us
  Pallas kernels  40 us (41%)
  starting transfers between devices  25 us (25%)
  waiting for transfers between devices  19.1 us (19%)
  blocking collectives  12.9 us (13%)
    pallas_call x2, Pallas kernels, local_scan(): pl.pallas_call(local_kernel, grid=(4,), in_specs=[pl.BlockSpec((64, 16, 2...  14.4 us
    all_to_all x1, blocking collectives, on_device(): lax.all_to_all(chain, 'col', 0, 0, tiled=True, axis_index_groups=chips)  12.9 us
    pallas_call x1, Pallas kernels, mix(): pl.pallas_call(mix_kernel, grid=(4,), in_specs=[pl.BlockSpec(memory_space...  10.9 us
    all_to_all x1, waiting for transfers between devices, on_device(): lax.all_to_all(incoming, 'row', 0, 0, tiled=True).reshape(2, 8, 8, 8, LANES)  9.65 us
    pallas_call x1, Pallas kernels, act_and_edges(): pl.pallas_call(act_kernel, grid=(4,), in_specs=[pl.BlockSpec((16, 64, 256...  8.92 us
    all_to_all x1, starting transfers between devices, on_device(): lax.all_to_all(decay * first + second, 'col', 0, 0, tiled=True, axis_inde...  8.19 us
    all_to_all x1, starting transfers between devices, on_device(): edges = lax.all_to_all(edges, 'row', 0, 0, tiled=True)  7.58 us
    ppermute x2, starting transfers between devices, swap_cores(): return lax.ppermute(block, 'col', [(i, i ^ 1) for i in range(n)])  5.66 us
  transfers between devices with their start and end apart: 5, of which 5 were waited for; matrix products, arithmetic and copies ran while one was open for 0% of the time, Pallas kernels for 15%

profile of v3, /device:TPU:1, one launch (start us, length us, event | category | flops | bytes accessed | tf_op | source)
XLA Modules:
  0.0 97.9 jit_solution(12486119322621933893)
XLA Ops:
  0.0 0.0 copy-start.2
  0.0 4.8 %row_edges.1 = f32[2,8,8,8,128]{4,3,2,1,0:T(8,128)} custom-call(bf16[64,64,256]{2,1,0:T(8,128)(2,1)} %image_ref.3, f32[8,256]{1,0:T(8,128)} %vr_ref.1), custom_call_target="tpu_custom_call" | custom-call | tf_op jit(solution)/shard_map/row_edges/pallas_call | solution.py:196
  4.8 7.6 %all-to-all-start = ((f32[16,8,8,128]{3,2,1,0:T(8,128)}), f32[16,8,8,128]{3,2,1,0:T(8,128)S(1)}, u32[]{:S(2)}, u32[]{:S(2)}) async-start(f32[16,8,8,128]{3,2,1,0:T(8,128)} %bitcast.17), calls=%async_computation | async-start | bytes 1048576 | tf_op jit(solution)/shard_map/all_to_all | solution.py:293
  12.4 0.0 copy-done.2
  12.5 7.2 %vert_local.1.local_ref = f32[64,64,256]{2,1,0:T(8,128)} custom-call(bf16[64,64,256]{2,1,0:T(8,128)(2,1)} %image_ref.3, f32[8,256]{1,0:T(8,128)} %vr_ref.1, f32[8,256]{1,0:T(8,128)} %vc_ref.1), custom_call_target="tpu_custom_call" | custom-call | flops 5000000000 | bytes 8000000 | tf_op jit(solution)/shard_map/vert_local/pallas_call | solution.py:220
  19.7 0.0 copy-start.3
  19.7 0.0 copy-start.4
  19.7 0.0 copy-start.6
  19.7 3.2 %all-to-all-done.edge_ref = f32[16,8,8,128]{3,2,1,0:T(8,128)S(1)} async-done(((f32[16,8,8,128]{3,2,1,0:T(8,128)}), f32[16,8,8,128]{3,2,1,0:T(8,128)S(1)}, u32[]{:S(2)}, u32[]{:S(2)}) %all-to-all-start) | async-done | bytes 524320 | tf_op jit(solution)/shard_map/all_to_all | solution.py:293
  22.9 0.8 prefix.2
  23.8 3.6 %all-to-all-start.1 = ((f32[16,8,8,128]{3,2,1,0:T(8,128)}), f32[16,8,8,128]{3,2,1,0:T(8,128)S(1)}, u32[]{:S(2)}, u32[]{:S(2)}) async-start(f32[16,8,8,128]{3,2,1,0:T(8,128)} %prefix.2), calls=%async_computation.1 | async-start | bytes 1048576 | tf_op jit(solution)/shard_map/all_to_all | solution.py:298
  27.4 9.6 %all-to-all-done.1 = f32[16,8,8,128]{3,2,1,0:T(8,128)S(1)} async-done(((f32[16,8,8,128]{3,2,1,0:T(8,128)}), f32[16,8,8,128]{3,2,1,0:T(8,128)S(1)}, u32[]{:S(2)}, u32[]{:S(2)}) %all-to-all-start.1) | async-done | bytes 524320 | tf_op jit(solution)/shard_map/all_to_all | solution.py:298
  37.0 0.0 copy-done.3
  37.0 0.0 copy-done.4
  37.0 0.0 copy-done.6
  37.0 8.9 %act_and_edges.1 = (bf16[64,64,256]{2,1,0:T(8,128)(2,1)}, f32[2,8,8,8,128]{4,3,2,1,0:T(8,128)S(1)}) custom-call(f32[64,64,256]{2,1,0:T(8,128)} %vert_local.1.local_ref, f32[2,8,8,8,128]{4,3,2,1,0:T(8,128)S(1)} %bitcast.16, f32[8,256]{1,0:T(8,128)S(1)} %copy-done.3, f32[8,256]{1,0:T(8,128)S(1)} %copy-done.6, f32[8,256]{1,0:T(8,128)S(1)} %copy-done.4), custom_call_target="tpu_custom_call" | custom-call | tf_op jit(solution)/shard_map/act_and_edges/pallas_call | solution.py:233
  46.0 2.9 %collective-permute-start = (f32[8,8,8,128]{3,2,1,0:T(8,128)S(1)}, f32[8,8,8,128]{3,2,1,0:T(8,128)S(1)}, u32[]{:S(2)}, u32[]{:S(2)}) collective-permute-start(f32[8,8,8,128]{3,2,1,0:T(8,128)S(1)} %dynamic-slice_bitcast_fusion), channel_id=1, source_target_pairs={{0,1},{1,0},{2,3},{3,2},{4,5},{5,4},{6,7},{7,6},{8,9},{9,8},{10,11... | collective-permute-start | bytes 786440 | tf_op jit(solution)/shard_map/ppermute | solution.py:284
  48.9 1.2 %collective-permute-done = f32[8,8,8,128]{3,2,1,0:T(8,128)S(1)} collective-permute-done((f32[8,8,8,128]{3,2,1,0:T(8,128)S(1)}, f32[8,8,8,128]{3,2,1,0:T(8,128)S(1)}, u32[]{:S(2)}, u32[]{:S(2)}) %collective-permute-start) | collective-permute-done | bytes 262176 | tf_op jit(solution)/shard_map/ppermute | solution.py:284
  50.0 0.8 fusion
  50.8 8.2 %all-to-all-start.2 = ((f32[8,8,8,128]{3,2,1,0:T(8,128)}), f32[8,8,8,128]{3,2,1,0:T(8,128)S(1)}, u32[]{:S(2)}, u32[]{:S(2)}) async-start(f32[8,8,8,128]{3,2,1,0:T(8,128)} %fusion), calls=%async_computation.2 | async-start | bytes 524288 | tf_op jit(solution)/shard_map/all_to_all | solution.py:311
  59.0 7.2 %horiz_local.1.local_ref = f32[64,64,256]{2,1,0:T(8,128)} custom-call(bf16[64,64,256]{2,1,0:T(8,128)(2,1)} %get-tuple-element.14.image_ref, f32[8,256]{1,0:T(8,128)} %hr_ref.3, f32[8,256]{1,0:T(8,128)} %hc_ref.1), custom_call_target="tpu_custom_call" | custom-call | flops 5000000000 | bytes 8000000 | tf_op jit(solution)/shard_map/horiz_local/pallas_call | solution.py:220
  66.2 0.0 copy-start
  66.2 0.0 copy-start.1
  66.2 0.0 copy-start.5
  66.2 0.0 copy-start.7
  66.2 3.9 %all-to-all-done.2.edge_ref = f32[8,8,8,128]{3,2,1,0:T(8,128)S(1)} async-done(((f32[8,8,8,128]{3,2,1,0:T(8,128)}), f32[8,8,8,128]{3,2,1,0:T(8,128)S(1)}, u32[]{:S(2)}, u32[]{:S(2)}) %all-to-all-start.2) | async-done | bytes 262176 | tf_op jit(solution)/shard_map/all_to_all | solution.py:311
  70.1 12.9 %all_to_all.20 = f32[8,8,8,128]{3,2,1,0:T(8,128)S(1)} all-to-all(f32[8,8,8,128]{3,2,1,0:T(8,128)S(1)} %prefix.3), channel_id=1, replica_groups={{0,2,4,6,8,10,12,14},{1,3,5,7,9,11,13,15},{16,18,20,22,24,26,28,30},{17..., dimensions={0} | all-to-all | bytes 524288 | tf_op jit(solution)/shard_map/all_to_all | solution.py:314
  83.0 0.1 fusion.1
  83.1 2.7 %collective-permute-start.1 = (f32[8,8,8,128]{3,2,1,0:T(8,128)S(1)}, f32[8,8,8,128]{3,2,1,0:T(8,128)S(1)}, u32[]{:S(2)}, u32[]{:S(2)}) collective-permute-start(f32[8,8,8,128]{3,2,1,0:T(8,128)S(1)} %get-tuple-element.19), channel_id=1, source_target_pairs={{0,1},{1,0},{2,3},{3,2},{4,5},{5,4},{6,7},{7,6},{8,9},{9,8},{10,11... | collective-permute-start | bytes 786440 | tf_op jit(solution)/shard_map/ppermute | solution.py:284
  85.8 1.2 %collective-permute-done.1.got_ref = f32[8,8,8,128]{3,2,1,0:T(8,128)S(1)} collective-permute-done((f32[8,8,8,128]{3,2,1,0:T(8,128)S(1)}, f32[8,8,8,128]{3,2,1,0:T(8,128)S(1)}, u32[]{:S(2)}, u32[]{:S(2)}) %collective-permute-start.1) | collective-permute-done | bytes 262176 | tf_op jit(solution)/shard_map/ppermute | solution.py:284
  87.0 0.0 copy-done
  87.0 0.0 copy-done.1
  87.0 0.0 copy-done.5
  87.0 0.0 copy-done.7
  87.0 10.9 %mix.1 = bf16[64,64,256]{2,1,0:T(8,128)(2,1)} custom-call(s32[1]{0:T(128)} %bitcast.core_ref, f32[64,64,256]{2,1,0:T(8,128)} %horiz_local.1.local_ref, f32[8,8,8,128]{3,2,1,0:T(8,128)S(1)} %get-tuple-element.20.keep_ref, f32[8,8,8,128]{3,2,1,0:T(8,128)S(1)} %collective-permute-done.1.got_ref, f32[8,256]{1,0:T(8,128)S(1)} %copy-done.5, ...), custom_call_target="tpu_custom_call" | custom-call | tf_op jit(solution)/shard_map/mix/pallas_call | solution.py:261
  (4 shorter events, 0.1 us)
Async XLA Ops:
  0.0 12.4 %copy-start.2 = (f32[8,256]{1,0:T(8,128)S(1)}, f32[8,256]{1,0:T(8,128)}, u32[]{:S(2)}) copy-start(f32[8,256]{1,0:T(8,128)} %vr_ref.1) | copy-start | bytes 24580
  4.8 18.1 %all-to-all-start = ((f32[16,8,8,128]{3,2,1,0:T(8,128)}), f32[16,8,8,128]{3,2,1,0:T(8,128)S(1)}, u32[]{:S(2)}, u32[]{:S(2)}) async-start(f32[16,8,8,128]{3,2,1,0:T(8,128)} %bitcast.17), calls=%async_computation | async-start | bytes 1048576 | tf_op jit(solution)/shard_map/all_to_all | solution.py:293
  19.7 17.3 %copy-start.3 = (f32[8,256]{1,0:T(8,128)S(1)}, f32[8,256]{1,0:T(8,128)}, u32[]{:S(2)}) copy-start(f32[8,256]{1,0:T(8,128)} %vr_ref.1) | copy-start | bytes 24580
  19.7 17.3 %copy-start.4 = (f32[8,256]{1,0:T(8,128)S(1)}, f32[8,256]{1,0:T(8,128)}, u32[]{:S(2)}) copy-start(f32[8,256]{1,0:T(8,128)} %hr_ref.3) | copy-start | bytes 24580
  19.7 17.3 %copy-start.6 = (f32[8,256]{1,0:T(8,128)S(1)}, f32[8,256]{1,0:T(8,128)}, u32[]{:S(2)}) copy-start(f32[8,256]{1,0:T(8,128)} %vc_ref.1) | copy-start | bytes 24580
  23.8 13.2 %all-to-all-start.1 = ((f32[16,8,8,128]{3,2,1,0:T(8,128)}), f32[16,8,8,128]{3,2,1,0:T(8,128)S(1)}, u32[]{:S(2)}, u32[]{:S(2)}) async-start(f32[16,8,8,128]{3,2,1,0:T(8,128)} %prefix.2), calls=%async_computation.1 | async-start | bytes 1048576 | tf_op jit(solution)/shard_map/all_to_all | solution.py:298
  46.0 4.1 %collective-permute-start = (f32[8,8,8,128]{3,2,1,0:T(8,128)S(1)}, f32[8,8,8,128]{3,2,1,0:T(8,128)S(1)}, u32[]{:S(2)}, u32[]{:S(2)}) collective-permute-start(f32[8,8,8,128]{3,2,1,0:T(8,128)S(1)} %dynamic-slice_bitcast_fusion), channel_id=1, source_target_pairs={{0,1},{1,0},{2,3},{3,2},{4,5},{5,4},{6,7},{7,6},{8,9},{9,8},{10,11... | collective-permute-start | bytes 786440 | tf_op jit(solution)/shard_map/ppermute | solution.py:284
  50.8 19.3 %all-to-all-start.2 = ((f32[8,8,8,128]{3,2,1,0:T(8,128)}), f32[8,8,8,128]{3,2,1,0:T(8,128)S(1)}, u32[]{:S(2)}, u32[]{:S(2)}) async-start(f32[8,8,8,128]{3,2,1,0:T(8,128)} %fusion), calls=%async_computation.2 | async-start | bytes 524288 | tf_op jit(solution)/shard_map/all_to_all | solution.py:311
  66.2 20.8 %copy-start = (bf16[256,1024]{1,0:T(8,128)(2,1)S(1)}, bf16[256,1024]{1,0:T(8,128)(2,1)}, u32[]{:S(2)}) copy-start(bf16[256,1024]{1,0:T(8,128)(2,1)} %w_in_ref.1) | copy-start | bytes 1572868
  66.2 20.8 %copy-start.1 = (bf16[1024,256]{1,0:T(8,128)(2,1)S(1)}, bf16[1024,256]{1,0:T(8,128)(2,1)}, u32[]{:S(2)}) copy-start(bf16[1024,256]{1,0:T(8,128)(2,1)} %w_out_ref.1) | copy-start | bytes 1572868
  66.2 20.8 %copy-start.5 = (f32[8,256]{1,0:T(8,128)S(1)}, f32[8,256]{1,0:T(8,128)}, u32[]{:S(2)}) copy-start(f32[8,256]{1,0:T(8,128)} %hr_ref.3) | copy-start | bytes 24580
  66.2 20.8 %copy-start.7 = (f32[8,256]{1,0:T(8,128)S(1)}, f32[8,256]{1,0:T(8,128)}, u32[]{:S(2)}) copy-start(f32[8,256]{1,0:T(8,128)} %hc_ref.1) | copy-start | bytes 24580
  83.1 3.9 %collective-permute-start.1 = (f32[8,8,8,128]{3,2,1,0:T(8,128)S(1)}, f32[8,8,8,128]{3,2,1,0:T(8,128)S(1)}, u32[]{:S(2)}, u32[]{:S(2)}) collective-permute-start(f32[8,8,8,128]{3,2,1,0:T(8,128)S(1)} %get-tuple-element.19), channel_id=1, source_target_pairs={{0,1},{1,0},{2,3},{3,2},{4,5},{5,4},{6,7},{7,6},{8,9},{9,8},{10,11... | collective-permute-start | bytes 786440 | tf_op jit(solution)/shard_map/ppermute | solution.py:284

commit v4 on v3

v4 whole, which is shorter than its diff:
```python
import math

import jax
import jax.numpy as jnp
from jax import lax
from jax.experimental import pallas as pl
from jax.experimental.pallas import tpu as pltpu
from jax.sharding import PartitionSpec as P

F32 = jnp.float32
BF16 = jnp.bfloat16
LANES = 128
MODES = 8
SQRT_2_PI = math.sqrt(2.0 / math.pi)
PITCH = 72


def gelu(x):
    inner = x * (SQRT_2_PI + (SQRT_2_PI * 0.044715) * (x * x))
    half = 0.5 * x
    return half + half * jnp.tanh(inner)


def gelu_packed(x):
    x = x.astype(BF16)
    inner = x * (BF16(SQRT_2_PI) + BF16(SQRT_2_PI * 0.044715) * (x * x))
    half = BF16(0.5) * x
    return half + half * jnp.tanh(inner)


def poles(rate_ref, half, rows):
    lanes = slice(half * LANES, (half + 1) * LANES)
    return [
        jnp.broadcast_to(jnp.exp(-rate_ref[m : m + 1, lanes]), (rows, LANES)) for m in range(MODES)
    ]


def weights(rate_ref, coef_ref, half, rows):
    lanes = slice(half * LANES, (half + 1) * LANES)
    return [
        jnp.broadcast_to(
            coef_ref[m : m + 1, lanes] * jnp.sqrt(1.0 - jnp.exp(-2.0 * rate_ref[m : m + 1, lanes])),
            (rows, LANES),
        )
        for m in range(MODES)
    ]


def tree(terms):
    while len(terms) > 1:
        terms = [a + b for a, b in zip(terms[::2], terms[1::2])]
    return terms[0]


def edge_kernel(image_ref, rate_hbm_ref, edge_ref, image, rate_ref, arrived):
    def fetch(i):
        cols = pl.ds(pl.multiple_of(i * 16, 16), 16)
        return pltpu.make_async_copy(image_ref.at[:, cols, :], image.at[:, cols, :], arrived.at[i])

    rates = pltpu.make_async_copy(rate_hbm_ref, rate_ref, arrived.at[4])
    rates.start()
    for i in range(4):
        fetch(i).start()
    rates.wait()

    def chunk(i, _):
        fetch(i).wait()
        cols = pl.ds(pl.multiple_of(i * 16, 16), 16)
        for half in range(2):
            lanes = slice(half * LANES, (half + 1) * LANES)
            pole = poles(rate_ref, half, 16)

            def steps(j, states, lanes=lanes, pole=pole):
                for k in range(16):
                    u = image[j * 16 + k, cols, lanes].astype(F32)
                    states = [p * h + u for p, h in zip(pole, states)]
                return states

            states = lax.fori_loop(0, 4, steps, [jnp.zeros((16, LANES), F32)] * MODES)
            for m in range(MODES):
                edge_ref[half, pl.ds(i * 2, 2), m] = states[m].reshape(2, 8, LANES)
        return 0

    lax.fori_loop(0, 4, chunk, 0)


def prefix_kernel(span, edge_ref, rate_ref, out_ref):
    decay = [
        jnp.broadcast_to(jnp.exp(-span * rate_ref[m : m + 1, :]), (8, LANES)) for m in range(MODES)
    ]
    states = [jnp.zeros((8, LANES), F32)] * MODES
    for r in range(edge_ref.shape[0]):
        for m in range(MODES):
            out_ref[r, m] = states[m]
            states[m] = decay[m] * states[m] + edge_ref[r, m]


def local_kernel(image_ref, rate_ref, coef_ref, out_ref):
    for half in range(2):
        lanes = slice(half * LANES, (half + 1) * LANES)
        pole = poles(rate_ref, half, 16)
        weight = weights(rate_ref, coef_ref, half, 16)

        def steps(i, states, lanes=lanes, pole=pole, weight=weight):
            for k in range(8):
                s = i * 8 + k
                u = image_ref[s, :, lanes].astype(F32)
                states = [p * h + u for p, h in zip(pole, states)]
                out_ref[s, :, lanes] = tree([q * h for q, h in zip(weight, states)])
            return states

        lax.fori_loop(0, 8, steps, [jnp.zeros((16, LANES), F32)] * MODES)


def decays(rate_ref, span):
    return [jnp.broadcast_to(jnp.exp(-span * rate_ref[m : m + 1, :]), (8, LANES)) for m in range(MODES)]


def join_cores_kernel(info_ref, mine_ref, other_ref, rate_ref, first_ref, keep_ref, send_ref):
    even_core, here = info_ref[0] == 0, info_ref[1] * 4
    decay = decays(rate_ref, 64.0)
    for b in range(8):
        for m in range(MODES):
            mine, other = mine_ref[b, m], other_ref[b, m]
            first_ref[b, m] = jnp.where(even_core, mine, other)
    for b in range(4):
        for out_ref, at in ((keep_ref, here + b), (send_ref, 4 - here + b)):
            for m in range(MODES):
                mine, other, first = mine_ref[at, m], other_ref[at, m], first_ref[at, m]
                out_ref[b, m] = decay[m] * first + jnp.where(even_core, other, mine)


def join_chips_kernel(info_ref, keep_ref, came_ref, rate_ref, even_ref, q0_ref, q1_ref, q2_ref, q3_ref):
    even_chip, pair = info_ref[1] == 0, info_ref[2]
    decay = decays(rate_ref, 128.0)
    for d, q_ref in enumerate((q0_ref, q1_ref, q2_ref, q3_ref)):
        b = pair ^ d
        for m in range(MODES):
            keep, came = keep_ref[b, m], came_ref[b, m]
            even = jnp.where(even_chip, keep, came)
            even_ref[b, m] = even
            q_ref[m] = decay[m] * even + jnp.where(even_chip, came, keep)


def prefix_pairs_kernel(info_ref, e0_ref, e1_ref, e2_ref, e3_ref, rate_ref, h0_ref, h1_ref, h2_ref, h3_ref):
    pair = info_ref[2]
    decay = decays(rate_ref, 256.0)
    edges = (e0_ref, e1_ref, e2_ref, e3_ref)
    for m in range(MODES):
        e = [edge[m] for edge in edges]
        state = jnp.zeros((8, LANES), F32)
        states = []
        for p in range(4):
            states.append(state)
            edge = e[3]
            for d in range(3):
                edge = jnp.where((pair ^ d) == p, e[d], edge)
            state = decay[m] * state + edge
        for d, out_ref in enumerate((h0_ref, h1_ref, h2_ref, h3_ref)):
            out = states[3]
            for p in range(3):
                out = jnp.where((pair ^ d) == p, states[p], out)
            out_ref[m] = out


def part_chips_kernel(info_ref, h0_ref, h1_ref, h2_ref, h3_ref, even_ref, rate_ref, keep_ref, send_ref):
    even_chip, pair = info_ref[1] == 0, info_ref[2]
    decay = decays(rate_ref, 128.0)
    for d, h_ref in enumerate((h0_ref, h1_ref, h2_ref, h3_ref)):
        b = pair ^ d
        for m in range(MODES):
            first = h_ref[m]
            second = decay[m] * first + even_ref[b, m]
            keep_ref[b, m] = jnp.where(even_chip, first, second)
            send_ref[b, m] = jnp.where(even_chip, second, first)


def part_cores_kernel(info_ref, own_ref, came_ref, first_ref, rate_ref, keep_ref, send_ref):
    even_core, here = info_ref[0] == 0, info_ref[1] * 4
    decay = decays(rate_ref, 64.0)
    for b in range(4):
        for in_ref, at in ((own_ref, here + b), (came_ref, 4 - here + b)):
            for m in range(MODES):
                chain = in_ref[b, m]
                after = decay[m] * chain + first_ref[at, m]
                keep_ref[at, m] = jnp.where(even_core, chain, after)
                send_ref[at, m] = jnp.where(even_core, after, chain)


def act_kernel(
    info_ref, local_ref, in_ref, vr_ref, vc_ref, hr_ref, act_ref, mine_ref, other_ref,
    local, act, tails, field, arrived, left,
):
    def rows(i):
        return pl.ds(pl.multiple_of(i * 16, 16), 16)

    def fetch(i):
        return pltpu.make_async_copy(local_ref.at[rows(i)], local.at[rows(i)], arrived.at[i])

    def put(i):
        return pltpu.make_async_copy(act.at[:, rows(i), :], act_ref.at[:, rows(i), :], left.at[i])

    fetch(0).start()
    for half in range(2):
        pole = poles(vr_ref, half, 8)
        weight = weights(vr_ref, vc_ref, half, 8)
        for m in range(MODES):
            tails[half, :, m] = in_ref[half, :, m] * (pole[m] * weight[m])[None]

    def chunk(i, _):
        fetch(i).wait()

        @pl.when(i < 3)
        def _():
            fetch(i + 1).start()

        for half in range(2):
            lanes = slice(half * LANES, (half + 1) * LANES)
            pole = poles(vr_ref, half, 16)

            def block(b, _, half=half, lanes=lanes, pole=pole):
                pair = pl.ds(b * 2, 2)
                cols = pl.ds(pl.multiple_of(b * 16, 16), 16)
                tail = [tails[half, pair, m].reshape(16, LANES) for m in range(MODES)]
                for s in range(16):
                    y = local[i * 16 + s, cols, lanes] + tree(tail)
                    tail = [p * g for p, g in zip(pole, tail)]
                    a = gelu(y).astype(BF16).astype(F32)
                    field[half, pl.ds(pl.multiple_of(s * PITCH + b * 16, 8), 16), :] = a
                for m in range(MODES):
                    tails[half, pair, m] = tail[m].reshape(2, 8, LANES)
                return 0

            lax.fori_loop(0, 4, block, 0)

        for half in range(2):
            lanes = slice(half * LANES, (half + 1) * LANES)
            pole = poles(hr_ref, half, 16)

            def steps(j, states, half=half, lanes=lanes, pole=pole):
                for k in range(8):
                    w = j * 8 + k
                    u = field[half, pl.ds(w, 16, stride=PITCH), :]
                    act[w, rows(i), lanes] = u.astype(BF16)
                    states = [p * h + u for p, h in zip(pole, states)]
                return states

            states = lax.fori_loop(0, 8, steps, [jnp.zeros((16, LANES), F32)] * MODES)
            mine = info_ref[0] == half

            @pl.when(mine)
            def _(states=states):
                for m in range(MODES):
                    mine_ref[pl.ds(i * 2, 2), m] = states[m].reshape(2, 8, LANES)

            @pl.when(jnp.logical_not(mine))
            def _(states=states):
                for m in range(MODES):
                    other_ref[pl.ds(i * 2, 2), m] = states[m].reshape(2, 8, LANES)
        put(i).start()
        return 0

    lax.fori_loop(0, 4, chunk, 0)
    for i in range(4):
        put(i).wait()


def mix_kernel(
    info_ref, top_ref, bottom_ref, keep_ref, got_ref, hr_ref, hc_ref, w_in_ref, w_out_ref, out_ref,
    local, result, horiz, mixed, arrived, left,
):
    core = info_ref[0]

    def rows(i):
        return pl.ds(pl.multiple_of(i * 16, 16), 16)

    def fetch(i, part_ref):
        source = part_ref.at[:, rows(i % 2), :]
        return pltpu.make_async_copy(source, local.at[:, rows(i), :], arrived.at[i])

    def put(i):
        return pltpu.make_async_copy(result.at[rows(i)], out_ref.at[rows(i)], left.at[i])

    for i in range(4):
        fetch(i, (top_ref, bottom_ref)[i // 2]).start()

    def chunk(i, _):
        fetch(i, top_ref).wait()
        for half in range(2):
            lanes = slice(half * LANES, (half + 1) * LANES)
            pole = poles(hr_ref, half, 16)
            weight = weights(hr_ref, hc_ref, half, 16)
            mine = core == half
            pair = pl.ds(i * 2, 2)
            tail = [
                jnp.where(mine, keep_ref[pair, m], got_ref[pair, m]).reshape(16, LANES)
                * (pole[m] * weight[m])
                for m in range(MODES)
            ]

            def steps(j, tail, lanes=lanes, pole=pole):
                for k in range(8):
                    w = j * 8 + k
                    y = local[w, rows(i), lanes] + tree(tail)
                    tail = [p * g for p, g in zip(pole, tail)]
                    horiz[pl.ds(pl.multiple_of(w * 16, 16), 16), lanes] = y
                return tail

            lax.fori_loop(0, 8, steps, tail)

        y = horiz[...]
        scale = lax.rsqrt(jnp.mean(y * y, axis=-1, keepdims=True) + 1e-06)
        normed = (y * scale).astype(BF16)
        hidden = gelu_packed(jnp.dot(normed, w_in_ref[...], preferred_element_type=F32))
        out = y + jnp.dot(hidden, w_out_ref[...], preferred_element_type=F32)
        for w in range(64):
            for half in range(2):
                lanes = slice(half * LANES, (half + 1) * LANES)
                mixed[half, pl.ds(w, 16, stride=PITCH), :] = out[w * 16 : (w + 1) * 16, lanes]
        for half in range(2):
            lanes = slice(half * LANES, (half + 1) * LANES)
            for h in range(16):
                result[i * 16 + h, :, lanes] = mixed[half, h * PITCH : h * PITCH + 64].astype(BF16)
        put(i).start()
        return 0

    lax.fori_loop(0, 4, chunk, 0)
    for i in range(4):
        put(i).wait()


LOCAL_COST = {
    1: pl.CostEstimate(flops=5_000_000_000, bytes_accessed=8_000_000, transcendentals=0),
    2: pl.CostEstimate(flops=2_500_000_000, bytes_accessed=4_000_000, transcendentals=0),
}


def in_hbm(block):
    return pltpu.with_memory_space_constraint(block, pltpu.HBM)


def whole(shape):
    return pl.BlockSpec(shape, lambda i: (0,) * len(shape))


def params(mib):
    return pltpu.CompilerParams(vmem_limit_bytes=mib * 1024 * 1024)


VMEM = pl.BlockSpec(memory_space=pltpu.VMEM)
HBM = pl.BlockSpec(memory_space=pltpu.HBM)
SMEM = pl.BlockSpec(memory_space=pltpu.SMEM)


def row_edges(image, rate):
    return pl.pallas_call(
        edge_kernel,
        in_specs=[HBM, HBM],
        out_specs=VMEM,
        out_shape=jax.ShapeDtypeStruct((2, 8, 8, 8, LANES), F32),
        scratch_shapes=[
            pltpu.VMEM((64, 64, 256), BF16),
            pltpu.VMEM((8, 256), F32),
            pltpu.SemaphoreType.DMA((5,)),
        ],
        compiler_params=params(24),
        name="row_edges",
    )(in_hbm(image), in_hbm(rate))


def prefix(edges, rate, span):
    def kernel(edge_ref, rate_ref, out_ref):
        prefix_kernel(span, edge_ref, rate_ref, out_ref)

    return pl.pallas_call(
        kernel,
        out_shape=jax.ShapeDtypeStruct(edges.shape, F32),
        compiler_params=params(8),
        name="prefix",
    )(edges, rate)


def local_scan(block, rate, coef, part, parts, name):
    steps = 4 // parts
    return pl.pallas_call(
        local_kernel,
        grid=(steps,),
        in_specs=[
            pl.BlockSpec((64, 16, 256), lambda i: (0, i + part * steps, 0)),
            whole((8, 256)),
            whole((8, 256)),
        ],
        out_specs=pl.BlockSpec((64, 16, 256), lambda i: (0, i, 0)),
        out_shape=pltpu.HBM((64, 64 // parts, 256), F32),
        compiler_params=params(56),
        cost_estimate=LOCAL_COST[parts],
        name=name,
    )(block, rate, coef)


def small(kernel, name, outs, *operands):
    return pl.pallas_call(
        kernel,
        in_specs=[SMEM] + [VMEM] * (len(operands) - 1),
        out_specs=[VMEM] * len(outs),
        out_shape=[jax.ShapeDtypeStruct(shape, F32) for shape in outs],
        compiler_params=params(8),
        name=name,
    )(*operands)


def act_and_edges(info, local, incoming, vert_rate, vert_coef, horiz_rate):
    return pl.pallas_call(
        act_kernel,
        in_specs=[SMEM, HBM, VMEM, VMEM, VMEM, VMEM],
        out_specs=[HBM, VMEM, VMEM],
        out_shape=[pltpu.HBM((64, 64, 256), BF16)] + [jax.ShapeDtypeStruct((8, 8, 8, LANES), F32)] * 2,
        scratch_shapes=[
            pltpu.VMEM((64, 64, 256), F32),
            pltpu.VMEM((64, 64, 256), BF16),
            pltpu.VMEM((2, 8, 8, 8, LANES), F32),
            pltpu.VMEM((2, 16 * PITCH, LANES), F32),
            pltpu.SemaphoreType.DMA((4,)),
            pltpu.SemaphoreType.DMA((4,)),
        ],
        compiler_params=params(24),
        name="act_and_edges",
    )(info, in_hbm(local), incoming, vert_rate, vert_coef, horiz_rate)


def mix(info, top, bottom, keep, got, horiz_rate, horiz_coef, w_in, w_out):
    return pl.pallas_call(
        mix_kernel,
        in_specs=[SMEM, HBM, HBM, VMEM, VMEM, VMEM, VMEM, VMEM, VMEM],
        out_specs=HBM,
        out_shape=jax.ShapeDtypeStruct((64, 64, 256), BF16),
        scratch_shapes=[
            pltpu.VMEM((64, 64, 256), F32),
            pltpu.VMEM((64, 64, 256), BF16),
            pltpu.VMEM((1024, 256), F32),
            pltpu.VMEM((2, 16 * PITCH, LANES), F32),
            pltpu.SemaphoreType.DMA((4,)),
            pltpu.SemaphoreType.DMA((4,)),
        ],
        compiler_params=params(40),
        name="mix",
    )(info, in_hbm(top), in_hbm(bottom), keep, got, horiz_rate, horiz_coef, w_in, w_out)


def swap(block, bits):
    n = lax.axis_size("col")
    return lax.ppermute(block, "col", [(i, i ^ bits) for i in range(n)])


def on_device(image, vert_rate, vert_coef, horiz_rate, horiz_coef, w_in, w_out):
    rows = lax.axis_size("row")
    piece = lax.axis_index("row")
    col = lax.axis_index("col")
    core = col % 2
    info = jnp.stack([core, col // 2 % 2, col // 4]).astype(jnp.int32)

    edges = row_edges(image, vert_rate).reshape(rows, 8, 8, LANES)
    edges = lax.all_to_all(edges, "row", 0, 0, tiled=True)
    rate_here = lax.dynamic_slice_in_dim(vert_rate, (piece // 8) * LANES, LANES, 1)
    local = local_scan(image, vert_rate, vert_coef, 0, 1, "vert_local")
    edges, local = lax.optimization_barrier((edges, local))
    incoming = prefix(edges, rate_here, 64.0)
    incoming = lax.all_to_all(incoming, "row", 0, 0, tiled=True).reshape(2, 8, 8, 8, LANES)

    act, mine, other = act_and_edges(info, local, incoming, vert_rate, vert_coef, horiz_rate)

    half, quarter, one = (8, 8, 8, LANES), (4, 8, 8, LANES), (8, 8, LANES)
    rate_here = lax.dynamic_slice_in_dim(horiz_rate, core * LANES, LANES, 1)
    came = swap(other, 1)
    first, keep, send = small(
        join_cores_kernel, "join_cores", [half, quarter, quarter], info, mine, came, rate_here
    )
    top = local_scan(act, horiz_rate, horiz_coef, 0, 2, "horiz_top")
    came = swap(send, 2)
    came, top = lax.optimization_barrier((came, top))
    even, *q = small(
        join_chips_kernel, "join_chips", [quarter] + [one] * 4, info, keep, came, rate_here
    )
    e = [q[0]] + [swap(q[d], 4 * d) for d in range(1, 4)]
    h = small(prefix_pairs_kernel, "prefix_pairs", [one] * 4, info, *e, rate_here)
    h = [h[0]] + [swap(h[d], 4 * d) for d in range(1, 4)]
    own, send = small(
        part_chips_kernel, "part_chips", [quarter] * 2, info, *h, even, rate_here
    )
    bottom = local_scan(act, horiz_rate, horiz_coef, 1, 2, "horiz_bottom")
    came = swap(send, 2)
    came, bottom = lax.optimization_barrier((came, bottom))
    keep, send = small(
        part_cores_kernel, "part_cores", [half] * 2, info, own, came, first, rate_here
    )
    got = swap(send, 1)

    return mix(info, top, bottom, keep, got, horiz_rate, horiz_coef, w_in, w_out)


def solution(mesh):
    placed = (P("row", "col", None), P(), P(), P(), P(), P(), P())
    return jax.shard_map(
        on_device, mesh=mesh, in_specs=placed, out_specs=P("row", "col", None), check_vma=False
    )
```

time: 98.6 us -> 103 us (1.045)
  blocking collectives: 12.9 us -> 0 us
  starting transfers between devices: 25 us -> 34.7 us
  Pallas kernels: 40 us -> 45.3 us
  waiting for transfers between devices: 19.1 us -> 22.5 us
    ppermute x2 -> x10, starting transfers between devices: 5.66 us -> 23.5 us  [swap(): return lax.ppermute(block, 'col', [(i, i ^ bits) for i in range(n)])]
    all_to_all x1 -> x0, blocking collectives: 12.9 us -> none  [on_device(): lax.all_to_all(chain, 'col', 0, 0, tiled=True, axis_index_groups=chips)]
    all_to_all x1 -> x0, starting transfers between devices: 8.19 us -> none  [on_device(): lax.all_to_all(decay * first + second, 'col', 0, 0, tiled=True, axis_inde...]
    ppermute x2 -> x10, waiting for transfers between devices: 2.32 us -> 9.74 us  [swap(): return lax.ppermute(block, 'col', [(i, i ^ bits) for i in range(n)])]
    pallas_call x5 -> x11, Pallas kernels: 39.1 us -> 44.5 us  [the longest x3 16.2 us: local_scan(): pl.pallas_call(local_kernel, grid=(steps,), in_specs=[pl.BlockSpec((64, 1...]
    all_to_all x1 -> x0, waiting for transfers between devices: 3.85 us -> none  [on_device(): lax.all_to_all(decay * first + second, 'col', 0, 0, tiled=True, axis_inde...]
  transfers between devices with their start and end apart: 5 -> 12, of which waited for: 5 -> 8; matrix products, arithmetic and copies ran while one was open for 0% -> 0% of each run, Pallas kernels for 15% -> 16%
where the time goes in v4:
time: 103 us
  Pallas kernels  45.3 us (44%)
  starting transfers between devices  34.7 us (34%)
  waiting for transfers between devices  22.5 us (22%)
    ppermute x10, starting transfers between devices, swap(): return lax.ppermute(block, 'col', [(i, i ^ bits) for i in range(n)])  23.5 us
    pallas_call x3, Pallas kernels, local_scan(): pl.pallas_call(local_kernel, grid=(steps,), in_specs=[pl.BlockSpec((64, 1...  16.2 us
    pallas_call x1, Pallas kernels, mix(): pl.pallas_call(mix_kernel, in_specs=[SMEM, HBM, HBM, VMEM, VMEM, VMEM, VM...  11.4 us
    ppermute x10, waiting for transfers between devices, swap(): return lax.ppermute(block, 'col', [(i, i ^ bits) for i in range(n)])  9.74 us
    all_to_all x1, waiting for transfers between devices, on_device(): lax.all_to_all(incoming, 'row', 0, 0, tiled=True).reshape(2, 8, 8, 8, LANES)  9.55 us
    pallas_call x1, Pallas kernels, act_and_edges(): pl.pallas_call(act_kernel, in_specs=[SMEM, HBM, VMEM, VMEM, VMEM, VMEM],...  9.48 us
    all_to_all x1, starting transfers between devices, on_device(): edges = lax.all_to_all(edges, 'row', 0, 0, tiled=True)  7.6 us
    pallas_call x1, Pallas kernels, row_edges(): pl.pallas_call(edge_kernel, in_specs=[HBM, HBM], out_specs=VMEM, out_shap...  4.42 us
  transfers between devices with their start and end apart: 12, of which 8 were waited for; matrix products, arithmetic and copies ran while one was open for 0% of the time, Pallas kernels for 16%

profile of v4, /device:TPU:1, one launch (start us, length us, event | category | flops | bytes accessed | tf_op | source)
XLA Modules:
  0.0 102.8 jit_solution(11393725082498159009)
XLA Ops:
  0.0 4.4 %row_edges.1 = f32[2,8,8,8,128]{4,3,2,1,0:T(8,128)} custom-call(bf16[64,64,256]{2,1,0:T(8,128)(2,1)} %image_ref.3, f32[8,256]{1,0:T(8,128)} %vr_ref.1), custom_call_target="tpu_custom_call" | custom-call | tf_op jit(solution)/shard_map/row_edges/pallas_call | solution.py:356
  4.4 7.6 %all-to-all-start = ((f32[16,8,8,128]{3,2,1,0:T(8,128)}), f32[16,8,8,128]{3,2,1,0:T(8,128)S(1)}, u32[]{:S(2)}, u32[]{:S(2)}) async-start(f32[16,8,8,128]{3,2,1,0:T(8,128)} %bitcast.3), calls=%async_computation | async-start | bytes 1048576 | tf_op jit(solution)/shard_map/all_to_all | solution.py:463
  12.1 0.0 copy-done.2
  12.1 7.2 %vert_local.1.local_ref = f32[64,64,256]{2,1,0:T(8,128)} custom-call(bf16[64,64,256]{2,1,0:T(8,128)(2,1)} %image_ref.3, f32[8,256]{1,0:T(8,128)} %vr_ref.1, f32[8,256]{1,0:T(8,128)} %vc_ref.1), custom_call_target="tpu_custom_call" | custom-call | flops 5000000000 | bytes 8000000 | tf_op jit(solution)/shard_map/vert_local/pallas_call | solution.py:385
  19.3 3.2 %all-to-all-done.edge_ref = f32[16,8,8,128]{3,2,1,0:T(8,128)S(1)} async-done(((f32[16,8,8,128]{3,2,1,0:T(8,128)}), f32[16,8,8,128]{3,2,1,0:T(8,128)S(1)}, u32[]{:S(2)}, u32[]{:S(2)}) %all-to-all-start) | async-done | bytes 524320 | tf_op jit(solution)/shard_map/all_to_all | solution.py:463
  22.5 0.8 prefix.1
  23.4 3.6 %all-to-all-start.1 = ((f32[16,8,8,128]{3,2,1,0:T(8,128)}), f32[16,8,8,128]{3,2,1,0:T(8,128)S(1)}, u32[]{:S(2)}, u32[]{:S(2)}) async-start(f32[16,8,8,128]{3,2,1,0:T(8,128)} %prefix.1), calls=%async_computation.1 | async-start | bytes 1048576 | tf_op jit(solution)/shard_map/all_to_all | solution.py:468
  27.0 0.1 pad_add_fusion.info_ref
  27.1 9.5 %all-to-all-done.1 = f32[16,8,8,128]{3,2,1,0:T(8,128)S(1)} async-done(((f32[16,8,8,128]{3,2,1,0:T(8,128)}), f32[16,8,8,128]{3,2,1,0:T(8,128)S(1)}, u32[]{:S(2)}, u32[]{:S(2)}) %all-to-all-start.1) | async-done | bytes 524320 | tf_op jit(solution)/shard_map/all_to_all | solution.py:468
  36.6 0.0 copy-done.3
  36.6 0.0 copy-done.4
  36.6 0.0 copy-done.6
  36.6 9.5 %act_and_edges.1 = (bf16[64,64,256]{2,1,0:T(8,128)(2,1)}, f32[8,8,8,128]{3,2,1,0:T(8,128)S(1)}, f32[8,8,8,128]{3,2,1,0:T(8,128)S(1)}) custom-call(s32[3]{0:T(128)S(1)} %pad_add_fusion.info_ref, f32[64,64,256]{2,1,0:T(8,128)} %vert_local.1.local_ref, f32[2,8,8,8,128]{4,3,2,1,0:T(8,128)S(1)} %bitcast.5, f32[8,256]{1,0:T(8,128)S(1)} %copy-done.3, ...), custom_call_target="tpu_custom_call" | custom-call | tf_op jit(solution)/shard_map/act_and_edges/pallas_call | solution.py:413
  46.1 2.9 %collective-permute-start = (f32[8,8,8,128]{3,2,1,0:T(8,128)S(1)}, f32[8,8,8,128]{3,2,1,0:T(8,128)S(1)}, u32[]{:S(2)}, u32[]{:S(2)}) collective-permute-start(f32[8,8,8,128]{3,2,1,0:T(8,128)S(1)} %get-tuple-element.33), channel_id=1, source_target_pairs={{0,1},{1,0},{2,3},{3,2},{4,5},{5,4},{6,7},{7,6},{8,9},{9,8},{10,11... | collective-permute-start | bytes 786440 | tf_op jit(solution)/shard_map/ppermute | solution.py:452
  49.1 1.2 %collective-permute-done.other_ref = f32[8,8,8,128]{3,2,1,0:T(8,128)S(1)} collective-permute-done((f32[8,8,8,128]{3,2,1,0:T(8,128)S(1)}, f32[8,8,8,128]{3,2,1,0:T(8,128)S(1)}, u32[]{:S(2)}, u32[]{:S(2)}) %collective-permute-start) | collective-permute-done | bytes 262176 | tf_op jit(solution)/shard_map/ppermute | solution.py:452
  50.2 0.6 join_cores.1
  50.8 1.7 %collective-permute-start.1 = (f32[4,8,8,128]{3,2,1,0:T(8,128)S(1)}, f32[4,8,8,128]{3,2,1,0:T(8,128)S(1)}, u32[]{:S(2)}, u32[]{:S(2)}) collective-permute-start(f32[4,8,8,128]{3,2,1,0:T(8,128)S(1)} %get-tuple-element.34), channel_id=1, source_target_pairs={{0,2},{1,3},{2,0},{3,1},{4,6},{5,7},{6,4},{7,5},{8,10},{9,11},{10,... | collective-permute-start | bytes 393224 | tf_op jit(solution)/shard_map/ppermute | solution.py:452
  52.6 4.5 %horiz_top.1.top_ref = f32[64,32,256]{2,1,0:T(8,128)} custom-call(bf16[64,64,256]{2,1,0:T(8,128)(2,1)} %get-tuple-element.35.image_ref, f32[8,256]{1,0:T(8,128)} %hr_ref.3, f32[8,256]{1,0:T(8,128)} %hc_ref.1), custom_call_target="tpu_custom_call" | custom-call | flops 2500000000 | bytes 4000000 | tf_op jit(solution)/shard_map/horiz_top/pallas_call | solution.py:385
  57.1 0.0 collective-permute-done.1.came_ref
  57.1 0.6 join_chips.1
  57.6 3.1 %collective-permute-start.2 = (f32[8,8,128]{2,1,0:T(8,128)S(1)}, f32[8,8,128]{2,1,0:T(8,128)S(1)}, u32[]{:S(2)}, u32[]{:S(2)}) collective-permute-start(f32[8,8,128]{2,1,0:T(8,128)S(1)} %get-tuple-element.40), channel_id=1, source_target_pairs={{0,4},{1,5},{2,6},{3,7},{4,0},{5,1},{6,2},{7,3},{8,12},{9,13},{10,... | collective-permute-start | bytes 98312 | tf_op jit(solution)/shard_map/ppermute | solution.py:452
  60.7 4.2 %collective-permute-start.3 = (f32[8,8,128]{2,1,0:T(8,128)S(1)}, f32[8,8,128]{2,1,0:T(8,128)S(1)}, u32[]{:S(2)}, u32[]{:S(2)}) collective-permute-start(f32[8,8,128]{2,1,0:T(8,128)S(1)} %get-tuple-element.41), channel_id=1, source_target_pairs={{0,8},{1,9},{2,10},{3,11},{4,12},{5,13},{6,14},{7,15},{8,0},{9,1},... | collective-permute-start | bytes 98312 | tf_op jit(solution)/shard_map/ppermute | solution.py:452
  64.9 0.0 collective-permute-start.4
  64.9 0.0 collective-permute-done.2.e1_ref
  64.9 2.8 %collective-permute-done.3.e2_ref = f32[8,8,128]{2,1,0:T(8,128)S(1)} collective-permute-done((f32[8,8,128]{2,1,0:T(8,128)S(1)}, f32[8,8,128]{2,1,0:T(8,128)S(1)}, u32[]{:S(2)}, u32[]{:S(2)}) %collective-permute-start.3) | collective-permute-done | bytes 32800 | tf_op jit(solution)/shard_map/ppermute | solution.py:452
  67.7 2.1 %collective-permute-done.4.e3_ref = f32[8,8,128]{2,1,0:T(8,128)S(1)} collective-permute-done((f32[8,8,128]{2,1,0:T(8,128)S(1)}, f32[8,8,128]{2,1,0:T(8,128)S(1)}, u32[]{:S(2)}, u32[]{:S(2)}) %collective-permute-start.4) | collective-permute-done | bytes 32800 | tf_op jit(solution)/shard_map/ppermute | solution.py:452
  69.8 0.6 prefix_pairs.1
  70.4 1.3 %collective-permute-start.5 = (f32[8,8,128]{2,1,0:T(8,128)S(1)}, f32[8,8,128]{2,1,0:T(8,128)S(1)}, u32[]{:S(2)}, u32[]{:S(2)}) collective-permute-start(f32[8,8,128]{2,1,0:T(8,128)S(1)} %get-tuple-element.44), channel_id=1, source_target_pairs={{0,4},{1,5},{2,6},{3,7},{4,0},{5,1},{6,2},{7,3},{8,12},{9,13},{10,... | collective-permute-start | bytes 98312 | tf_op jit(solution)/shard_map/ppermute | solution.py:452
  71.7 1.8 %collective-permute-start.6 = (f32[8,8,128]{2,1,0:T(8,128)S(1)}, f32[8,8,128]{2,1,0:T(8,128)S(1)}, u32[]{:S(2)}, u32[]{:S(2)}) collective-permute-start(f32[8,8,128]{2,1,0:T(8,128)S(1)} %get-tuple-element.45), channel_id=1, source_target_pairs={{0,8},{1,9},{2,10},{3,11},{4,12},{5,13},{6,14},{7,15},{8,0},{9,1},... | collective-permute-start | bytes 98312 | tf_op jit(solution)/shard_map/ppermute | solution.py:452
  73.5 2.7 %collective-permute-start.7 = (f32[8,8,128]{2,1,0:T(8,128)S(1)}, f32[8,8,128]{2,1,0:T(8,128)S(1)}, u32[]{:S(2)}, u32[]{:S(2)}) collective-permute-start(f32[8,8,128]{2,1,0:T(8,128)S(1)} %get-tuple-element.46), channel_id=1, source_target_pairs={{0,12},{1,13},{2,14},{3,15},{4,8},{5,9},{6,10},{7,11},{8,4},{9,5},... | collective-permute-start | bytes 98312 | tf_op jit(solution)/shard_map/ppermute | solution.py:452
  76.1 0.0 collective-permute-done.5.h1_ref
  76.1 2.2 %collective-permute-done.6.h2_ref = f32[8,8,128]{2,1,0:T(8,128)S(1)} collective-permute-done((f32[8,8,128]{2,1,0:T(8,128)S(1)}, f32[8,8,128]{2,1,0:T(8,128)S(1)}, u32[]{:S(2)}, u32[]{:S(2)}) %collective-permute-start.6) | collective-permute-done | bytes 32800 | tf_op jit(solution)/shard_map/ppermute | solution.py:452
  78.4 0.3 collective-permute-done.7.h3_ref
  78.7 0.6 part_chips.1
  79.3 0.0 copy-start
  79.3 0.0 copy-start.1
  79.3 0.0 copy-start.5
  79.3 0.0 copy-start.7
  79.3 0.5 collective-permute-start.8
  79.8 4.5 %horiz_bottom.1.bottom_ref = f32[64,32,256]{2,1,0:T(8,128)} custom-call(bf16[64,64,256]{2,1,0:T(8,128)(2,1)} %get-tuple-element.35.image_ref, f32[8,256]{1,0:T(8,128)} %hr_ref.3, f32[8,256]{1,0:T(8,128)} %hc_ref.1), custom_call_target="tpu_custom_call" | custom-call | flops 2500000000 | bytes 4000000 | tf_op jit(solution)/shard_map/horiz_bottom/pallas_call | solution.py:385
  84.4 0.0 collective-permute-done.8.came_ref
  84.4 0.6 part_cores.1
  85.0 5.3 %collective-permute-start.9 = (f32[8,8,8,128]{3,2,1,0:T(8,128)S(1)}, f32[8,8,8,128]{3,2,1,0:T(8,128)S(1)}, u32[]{:S(2)}, u32[]{:S(2)}) collective-permute-start(f32[8,8,8,128]{3,2,1,0:T(8,128)S(1)} %get-tuple-element.54), channel_id=1, source_target_pairs={{0,1},{1,0},{2,3},{3,2},{4,5},{5,4},{6,7},{7,6},{8,9},{9,8},{10,11... | collective-permute-start | bytes 786440 | tf_op jit(solution)/shard_map/ppermute | solution.py:452
  90.3 1.2 %collective-permute-done.9.got_ref = f32[8,8,8,128]{3,2,1,0:T(8,128)S(1)} collective-permute-done((f32[8,8,8,128]{3,2,1,0:T(8,128)S(1)}, f32[8,8,8,128]{3,2,1,0:T(8,128)S(1)}, u32[]{:S(2)}, u32[]{:S(2)}) %collective-permute-start.9) | collective-permute-done | bytes 262176 | tf_op jit(solution)/shard_map/ppermute | solution.py:452
  91.4 0.0 copy-done
  91.4 0.0 copy-done.1
  91.4 0.0 copy-done.5
  91.4 11.4 %mix.1 = bf16[64,64,256]{2,1,0:T(8,128)(2,1)} custom-call(s32[3]{0:T(128)S(1)} %pad_add_fusion.info_ref, f32[64,32,256]{2,1,0:T(8,128)} %horiz_top.1.top_ref, f32[64,32,256]{2,1,0:T(8,128)} %horiz_bottom.1.bottom_ref, f32[8,8,8,128]{3,2,1,0:T(8,128)S(1)} %get-tuple-element.53.keep_ref, f32[8,8,8,128]{3,2,1,0:T(8,128)S(1)} %collective-permute-done.9.got_ref, ...), custom_call_target="tpu_custom_call" | custom-call | tf_op jit(solution)/shard_map/mix/pallas_call | solution.py:432
  (7 shorter events, 0.0 us)
Async XLA Ops:
  0.0 12.1 %copy-start.2 = (f32[8,256]{1,0:T(8,128)S(1)}, f32[8,256]{1,0:T(8,128)}, u32[]{:S(2)}) copy-start(f32[8,256]{1,0:T(8,128)} %vr_ref.1) | copy-start | bytes 24580
  4.4 18.1 %all-to-all-start = ((f32[16,8,8,128]{3,2,1,0:T(8,128)}), f32[16,8,8,128]{3,2,1,0:T(8,128)S(1)}, u32[]{:S(2)}, u32[]{:S(2)}) async-start(f32[16,8,8,128]{3,2,1,0:T(8,128)} %bitcast.3), calls=%async_computation | async-start | bytes 1048576 | tf_op jit(solution)/shard_map/all_to_all | solution.py:463
  19.3 17.3 %copy-start.3 = (f32[8,256]{1,0:T(8,128)S(1)}, f32[8,256]{1,0:T(8,128)}, u32[]{:S(2)}) copy-start(f32[8,256]{1,0:T(8,128)} %vr_ref.1) | copy-start | bytes 24580
  19.3 17.3 %copy-start.4 = (f32[8,256]{1,0:T(8,128)S(1)}, f32[8,256]{1,0:T(8,128)}, u32[]{:S(2)}) copy-start(f32[8,256]{1,0:T(8,128)} %hr_ref.3) | copy-start | bytes 24580
  19.3 17.3 %copy-start.6 = (f32[8,256]{1,0:T(8,128)S(1)}, f32[8,256]{1,0:T(8,128)}, u32[]{:S(2)}) copy-start(f32[8,256]{1,0:T(8,128)} %vc_ref.1) | copy-start | bytes 24580
  23.4 13.2 %all-to-all-start.1 = ((f32[16,8,8,128]{3,2,1,0:T(8,128)}), f32[16,8,8,128]{3,2,1,0:T(8,128)S(1)}, u32[]{:S(2)}, u32[]{:S(2)}) async-start(f32[16,8,8,128]{3,2,1,0:T(8,128)} %prefix.1), calls=%async_computation.1 | async-start | bytes 1048576 | tf_op jit(solution)/shard_map/all_to_all | solution.py:468
  46.1 4.1 %collective-permute-start = (f32[8,8,8,128]{3,2,1,0:T(8,128)S(1)}, f32[8,8,8,128]{3,2,1,0:T(8,128)S(1)}, u32[]{:S(2)}, u32[]{:S(2)}) collective-permute-start(f32[8,8,8,128]{3,2,1,0:T(8,128)S(1)} %get-tuple-element.33), channel_id=1, source_target_pairs={{0,1},{1,0},{2,3},{3,2},{4,5},{5,4},{6,7},{7,6},{8,9},{9,8},{10,11... | collective-permute-start | bytes 786440 | tf_op jit(solution)/shard_map/ppermute | solution.py:452
  50.8 6.2 %collective-permute-start.1 = (f32[4,8,8,128]{3,2,1,0:T(8,128)S(1)}, f32[4,8,8,128]{3,2,1,0:T(8,128)S(1)}, u32[]{:S(2)}, u32[]{:S(2)}) collective-permute-start(f32[4,8,8,128]{3,2,1,0:T(8,128)S(1)} %get-tuple-element.34), channel_id=1, source_target_pairs={{0,2},{1,3},{2,0},{3,1},{4,6},{5,7},{6,4},{7,5},{8,10},{9,11},{10,... | collective-permute-start | bytes 393224 | tf_op jit(solution)/shard_map/ppermute | solution.py:452
  57.6 7.3 %collective-permute-start.2 = (f32[8,8,128]{2,1,0:T(8,128)S(1)}, f32[8,8,128]{2,1,0:T(8,128)S(1)}, u32[]{:S(2)}, u32[]{:S(2)}) collective-permute-start(f32[8,8,128]{2,1,0:T(8,128)S(1)} %get-tuple-element.40), channel_id=1, source_target_pairs={{0,4},{1,5},{2,6},{3,7},{4,0},{5,1},{6,2},{7,3},{8,12},{9,13},{10,... | collective-permute-start | bytes 98312 | tf_op jit(solution)/shard_map/ppermute | solution.py:452
  60.7 7.0 %collective-permute-start.3 = (f32[8,8,128]{2,1,0:T(8,128)S(1)}, f32[8,8,128]{2,1,0:T(8,128)S(1)}, u32[]{:S(2)}, u32[]{:S(2)}) collective-permute-start(f32[8,8,128]{2,1,0:T(8,128)S(1)} %get-tuple-element.41), channel_id=1, source_target_pairs={{0,8},{1,9},{2,10},{3,11},{4,12},{5,13},{6,14},{7,15},{8,0},{9,1},... | collective-permute-start | bytes 98312 | tf_op jit(solution)/shard_map/ppermute | solution.py:452
  64.9 4.9 %collective-permute-start.4 = (f32[8,8,128]{2,1,0:T(8,128)S(1)}, f32[8,8,128]{2,1,0:T(8,128)S(1)}, u32[]{:S(2)}, u32[]{:S(2)}) collective-permute-start(f32[8,8,128]{2,1,0:T(8,128)S(1)} %get-tuple-element.42), channel_id=1, source_target_pairs={{0,12},{1,13},{2,14},{3,15},{4,8},{5,9},{6,10},{7,11},{8,4},{9,5},... | collective-permute-start | bytes 98312 | tf_op jit(solution)/shard_map/ppermute | solution.py:452
  70.4 5.7 %collective-permute-start.5 = (f32[8,8,128]{2,1,0:T(8,128)S(1)}, f32[8,8,128]{2,1,0:T(8,128)S(1)}, u32[]{:S(2)}, u32[]{:S(2)}) collective-permute-start(f32[8,8,128]{2,1,0:T(8,128)S(1)} %get-tuple-element.44), channel_id=1, source_target_pairs={{0,4},{1,5},{2,6},{3,7},{4,0},{5,1},{6,2},{7,3},{8,12},{9,13},{10,... | collective-permute-start | bytes 98312 | tf_op jit(solution)/shard_map/ppermute | solution.py:452
  71.7 6.7 %collective-permute-start.6 = (f32[8,8,128]{2,1,0:T(8,128)S(1)}, f32[8,8,128]{2,1,0:T(8,128)S(1)}, u32[]{:S(2)}, u32[]{:S(2)}) collective-permute-start(f32[8,8,128]{2,1,0:T(8,128)S(1)} %get-tuple-element.45), channel_id=1, source_target_pairs={{0,8},{1,9},{2,10},{3,11},{4,12},{5,13},{6,14},{7,15},{8,0},{9,1},... | collective-permute-start | bytes 98312 | tf_op jit(solution)/shard_map/ppermute | solution.py:452
  73.5 5.2 %collective-permute-start.7 = (f32[8,8,128]{2,1,0:T(8,128)S(1)}, f32[8,8,128]{2,1,0:T(8,128)S(1)}, u32[]{:S(2)}, u32[]{:S(2)}) collective-permute-start(f32[8,8,128]{2,1,0:T(8,128)S(1)} %get-tuple-element.46), channel_id=1, source_target_pairs={{0,12},{1,13},{2,14},{3,15},{4,8},{5,9},{6,10},{7,11},{8,4},{9,5},... | collective-permute-start | bytes 98312 | tf_op jit(solution)/shard_map/ppermute | solution.py:452
  79.3 12.2 %copy-start = (bf16[256,1024]{1,0:T(8,128)(2,1)S(1)}, bf16[256,1024]{1,0:T(8,128)(2,1)}, u32[]{:S(2)}) copy-start(bf16[256,1024]{1,0:T(8,128)(2,1)} %w_in_ref.1) | copy-start | bytes 1572868
  79.3 12.2 %copy-start.1 = (bf16[1024,256]{1,0:T(8,128)(2,1)S(1)}, bf16[1024,256]{1,0:T(8,128)(2,1)}, u32[]{:S(2)}) copy-start(bf16[1024,256]{1,0:T(8,128)(2,1)} %w_out_ref.1) | copy-start | bytes 1572868
  79.3 12.1 %copy-start.5 = (f32[8,256]{1,0:T(8,128)S(1)}, f32[8,256]{1,0:T(8,128)}, u32[]{:S(2)}) copy-start(f32[8,256]{1,0:T(8,128)} %hr_ref.3) | copy-start | bytes 24580
  79.3 12.1 %copy-start.7 = (f32[8,256]{1,0:T(8,128)S(1)}, f32[8,256]{1,0:T(8,128)}, u32[]{:S(2)}) copy-start(f32[8,256]{1,0:T(8,128)} %hc_ref.1) | copy-start | bytes 24580
  79.3 5.1 %collective-permute-start.8 = (f32[4,8,8,128]{3,2,1,0:T(8,128)S(1)}, f32[4,8,8,128]{3,2,1,0:T(8,128)S(1)}, u32[]{:S(2)}, u32[]{:S(2)}) collective-permute-start(f32[4,8,8,128]{3,2,1,0:T(8,128)S(1)} %get-tuple-element.48), channel_id=1, source_target_pairs={{0,2},{1,3},{2,0},{3,1},{4,6},{5,7},{6,4},{7,5},{8,10},{9,11},{10,... | collective-permute-start | bytes 393224 | tf_op jit(solution)/shard_map/ppermute | solution.py:452
  85.0 6.4 %collective-permute-start.9 = (f32[8,8,8,128]{3,2,1,0:T(8,128)S(1)}, f32[8,8,8,128]{3,2,1,0:T(8,128)S(1)}, u32[]{:S(2)}, u32[]{:S(2)}) collective-permute-start(f32[8,8,8,128]{3,2,1,0:T(8,128)S(1)} %get-tuple-element.54), channel_id=1, source_target_pairs={{0,1},{1,0},{2,3},{3,2},{4,5},{5,4},{6,7},{7,6},{8,9},{9,8},{10,11... | collective-permute-start | bytes 786440 | tf_op jit(solution)/shard_map/ppermute | solution.py:452

commit v5 on v3

--- a/solution.py
+++ b/solution.py
@@ -1,3 +1,4 @@
+import functools
 import math
 
 import jax
@@ -52,20 +53,36 @@
     return terms[0]
 
 
-def edge_kernel(image_ref, rate_ref, edge_ref):
-    for half in range(2):
-        lanes = slice(half * LANES, (half + 1) * LANES)
-        pole = poles(rate_ref, half, 16)
-
-        def steps(i, states, lanes=lanes, pole=pole):
-            for k in range(8):
-                u = image_ref[i * 8 + k, :, lanes].astype(F32)
-                states = [p * h + u for p, h in zip(pole, states)]
-            return states
-
-        states = lax.fori_loop(0, 8, steps, [jnp.zeros((16, LANES), F32)] * MODES)
-        for m in range(MODES):
-            edge_ref[half, :, m] = states[m].reshape(2, 8, LANES)
+def edge_kernel(image_ref, rate_hbm_ref, edge_ref, image, rate_ref, arrived):
+    def fetch(i):
+        cols = pl.ds(pl.multiple_of(i * 16, 16), 16)
+        return pltpu.make_async_copy(image_ref.at[:, cols, :], image.at[:, cols, :], arrived.at[i])
+
+    rates = pltpu.make_async_copy(rate_hbm_ref, rate_ref, arrived.at[4])
+    rates.start()
+    for i in range(4):
+        fetch(i).start()
+    rates.wait()
+
+    def chunk(i, _):
+        fetch(i).wait()
+        cols = pl.ds(pl.multiple_of(i * 16, 16), 16)
+        for half in range(2):
+            lanes = slice(half * LANES, (half + 1) * LANES)
+            pole = poles(rate_ref, half, 16)
+
+            def steps(j, states, lanes=lanes, pole=pole):
+                for k in range(16):
+                    u = image[j * 16 + k, cols, lanes].astype(F32)
+                    states = [p * h + u for p, h in zip(pole, states)]
+                return states
+
+            states = lax.fori_loop(0, 4, steps, [jnp.zeros((16, LANES), F32)] * MODES)
+            for m in range(MODES):
+                edge_ref[half, pl.ds(i * 2, 2), m] = states[m].reshape(2, 8, LANES)
+        return 0
+
+    lax.fori_loop(0, 4, chunk, 0)
 
 
 def prefix_kernel(span, edge_ref, rate_ref, out_ref):
@@ -96,7 +113,42 @@
         lax.fori_loop(0, 8, steps, [jnp.zeros((16, LANES), F32)] * MODES)
 
 
-def act_kernel(local_ref, in_ref, vr_ref, vc_ref, hr_ref, act_ref, edge_ref, tails, field):
+def decays(rate_ref, span):
+    return [jnp.broadcast_to(jnp.exp(-span * rate_ref[m : m + 1, :]), (8, LANES)) for m in range(MODES)]
+
+
+def join_kernel(level, span, info_ref, keep_ref, came_ref, rate_ref, first_ref, *out_refs):
+    left_here = info_ref[level] == 0
+    here = info_ref[4 + level] if len(out_refs) == 2 else 0
+    decay = decays(rate_ref, span)
+    part = keep_ref.shape[0] // len(out_refs)
+    for b in range(part):
+        for k, out_ref in enumerate(out_refs):
+            at = b if len(out_refs) == 1 else (here * part if k == 0 else part - here * part) + b
+            for m in range(MODES):
+                keep, came = keep_ref[at, m], came_ref[at, m]
+                first = jnp.where(left_here, keep, came)
+                first_ref[at, m] = first
+                out_ref[b, m] = decay[m] * first + jnp.where(left_here, came, keep)
+
+
+def part_kernel(level, span, info_ref, *refs):
+    *in_refs, first_ref, rate_ref, keep_ref, send_ref = refs
+    left_here = info_ref[level] == 0
+    here = info_ref[4 + level] if len(in_refs) == 2 else 0
+    decay = decays(rate_ref, span)
+    part = first_ref.shape[0] // len(in_refs)
+    for b in range(part):
+        for k, in_ref in enumerate(in_refs):
+            at = b if len(in_refs) == 1 else (here * part if k == 0 else part - here * part) + b
+            for m in range(MODES):
+                chain = in_ref[b, m]
+                after = decay[m] * chain + first_ref[at, m]
+                keep_ref[at, m] = jnp.where(left_here, chain, after)
+                send_ref[at, m] = jnp.where(left_here, after, chain)
+
+
+def act_kernel(info_ref, local_ref, in_ref, vr_ref, vc_ref, hr_ref, act_ref, mine_ref, other_ref, tails, field):
     for half in range(2):
         lanes = slice(half * LANES, (half + 1) * LANES)
         pole = poles(vr_ref, half, 16)
@@ -136,12 +188,21 @@
             return states
 
         states = lax.fori_loop(0, 8, steps, [jnp.zeros((16, LANES), F32)] * MODES)
-        for m in range(MODES):
-            edge_ref[half, :, m] = states[m].reshape(2, 8, LANES)
-
-
-def mix_kernel(core_ref, local_ref, keep_ref, got_ref, hr_ref, hc_ref, w_in_ref, w_out_ref, out_ref, horiz, mixed):
-    core = core_ref[0]
+        mine = info_ref[0] == half
+
+        @pl.when(mine)
+        def _(states=states):
+            for m in range(MODES):
+                mine_ref[:, m] = states[m].reshape(2, 8, LANES)
+
+        @pl.when(jnp.logical_not(mine))
+        def _(states=states):
+            for m in range(MODES):
+                other_ref[:, m] = states[m].reshape(2, 8, LANES)
+
+
+def mix_kernel(info_ref, local_ref, keep_ref, got_ref, hr_ref, hc_ref, w_in_ref, w_out_ref, out_ref, horiz, mixed):
+    core = info_ref[0]
     for half in range(2):
         lanes = slice(half * LANES, (half + 1) * LANES)
         pole = poles(hr_ref, half, 16)
@@ -177,9 +238,6 @@
             out_ref[h, :, lanes] = mixed[half, h * PITCH : h * PITCH + 64].astype(BF16)
 
 
-LOCAL_COST = pl.CostEstimate(flops=5_000_000_000, bytes_accessed=8_000_000, transcendentals=0)
-
-
 def in_hbm(block):
     return pltpu.with_memory_space_constraint(block, pltpu.HBM)
 
@@ -192,16 +250,25 @@
     return pltpu.CompilerParams(vmem_limit_bytes=mib * 1024 * 1024)
 
 
+VMEM = pl.BlockSpec(memory_space=pltpu.VMEM)
+HBM = pl.BlockSpec(memory_space=pltpu.HBM)
+SMEM = pl.BlockSpec(memory_space=pltpu.SMEM)
+
+
 def row_edges(image, rate):
     return pl.pallas_call(
         edge_kernel,
-        grid=(4,),
-        in_specs=[pl.BlockSpec((64, 16, 256), lambda i: (0, i, 0)), whole((8, 256))],
-        out_specs=pl.BlockSpec((2, 2, 8, 8, LANES), lambda i: (0, i, 0, 0, 0)),
+        in_specs=[HBM, HBM],
+        out_specs=VMEM,
         out_shape=jax.ShapeDtypeStruct((2, 8, 8, 8, LANES), F32),
-        compiler_params=params(56),
+        scratch_shapes=[
+            pltpu.VMEM((64, 64, 256), BF16),
+            pltpu.VMEM((8, 256), F32),
+            pltpu.SemaphoreType.DMA((5,)),
+        ],
+        compiler_params=params(24),
         name="row_edges",
-    )(image, rate)
+    )(in_hbm(image), in_hbm(rate))
 
 
 def prefix(edges, rate, span):
@@ -216,56 +283,74 @@
     )(edges, rate)
 
 
-def local_scan(block, rate, coef, mib, name):
-    return pl.pallas_call(
-        local_kernel,
-        grid=(4,),
-        in_specs=[pl.BlockSpec((64, 16, 256), lambda i: (0, i, 0)), whole((8, 256)), whole((8, 256))],
-        out_specs=pl.BlockSpec((64, 16, 256), lambda i: (0, i, 0)),
+def local_scan(block, rate, coef, name, part=0, parts=1, into=None):
+    steps = 4 // parts
+
+    def kernel(*refs):
+        local_kernel(*refs[:3], refs[-1])
+
+    place = pl.BlockSpec((64, 16, 256), lambda i: (0, i + part * steps, 0))
+    more = [] if into is None else [in_hbm(into)]
+    return pl.pallas_call(
+        kernel,
+        grid=(steps,),
+        in_specs=[place, whole((8, 256)), whole((8, 256))] + [HBM] * len(more),
+        out_specs=place,
         out_shape=pltpu.HBM((64, 64, 256), F32),
-        compiler_params=params(mib),
-        cost_estimate=LOCAL_COST,
+        input_output_aliases={3: 0} if more else {},
+        compiler_params=params(56),
+        cost_estimate=pl.CostEstimate(
+            flops=5_000_000_000 // parts, bytes_accessed=8_000_000 // parts, transcendentals=0
+        ),
         name=name,
-    )(block, rate, coef)
-
-
-def act_and_edges(local, incoming, vert_rate, vert_coef, horiz_rate):
+    )(block, rate, coef, *more)
+
+
+def small(kernel, name, outs, *operands):
+    return pl.pallas_call(
+        kernel,
+        in_specs=[SMEM] + [VMEM] * (len(operands) - 1),
+        out_specs=[VMEM] * len(outs),
+        out_shape=[jax.ShapeDtypeStruct(shape, F32) for shape in outs],
+        compiler_params=params(8),
+        name=name,
+    )(*operands)
+
+
+def act_and_edges(info, local, incoming, vert_rate, vert_coef, horiz_rate):
+    edge = pl.BlockSpec((2, 8, 8, LANES), lambda i: (i, 0, 0, 0))
     return pl.pallas_call(
         act_kernel,
         grid=(4,),
         in_specs=[
+            SMEM,
             pl.BlockSpec((16, 64, 256), lambda i: (i, 0, 0)),
             whole((2, 8, 8, 8, LANES)),
             whole((8, 256)),
             whole((8, 256)),
             whole((8, 256)),
         ],
-        out_specs=[
-            pl.BlockSpec((64, 16, 256), lambda i: (0, i, 0)),
-            pl.BlockSpec((2, 2, 8, 8, LANES), lambda i: (0, i, 0, 0, 0)),
-        ],
-        out_shape=[
-            pltpu.HBM((64, 64, 256), BF16),
-            jax.ShapeDtypeStruct((2, 8, 8, 8, LANES), F32),
-        ],
+        out_specs=[pl.BlockSpec((64, 16, 256), lambda i: (0, i, 0)), edge, edge],
+        out_shape=[pltpu.HBM((64, 64, 256), BF16)] + [jax.ShapeDtypeStruct((8, 8, 8, LANES), F32)] * 2,
         scratch_shapes=[
             pltpu.VMEM((2, 8, 8, 8, LANES), F32),
             pltpu.VMEM((2, 16 * PITCH, LANES), F32),
         ],
         compiler_params=params(24),
         name="act_and_edges",
-    )(in_hbm(local), incoming, vert_rate, vert_coef, horiz_rate)
-
-
-def mix(core, local, keep, got, horiz_rate, horiz_coef, w_in, w_out):
+    )(info, in_hbm(local), incoming, vert_rate, vert_coef, horiz_rate)
+
+
+def mix(info, local, keep, got, horiz_rate, horiz_coef, w_in, w_out):
+    state = pl.BlockSpec((2, 8, 8, LANES), lambda i: (i, 0, 0, 0))
     return pl.pallas_call(
         mix_kernel,
         grid=(4,),
         in_specs=[
-            pl.BlockSpec(memory_space=pltpu.SMEM),
+            SMEM,
             pl.BlockSpec((64, 16, 256), lambda i: (0, i, 0)),
-            pl.BlockSpec((2, 8, 8, LANES), lambda i: (i, 0, 0, 0)),
-            pl.BlockSpec((2, 8, 8, LANES), lambda i: (i, 0, 0, 0)),
+            state,
+            state,
             whole((8, 256)),
             whole((8, 256)),
             whole((256, 1024)),
@@ -276,47 +361,65 @@
         scratch_shapes=[pltpu.VMEM((1024, 256), F32), pltpu.VMEM((2, 16 * PITCH, LANES), F32)],
         compiler_params=params(40),
         name="mix",
-    )(core, in_hbm(local), keep, got, horiz_rate, horiz_coef, w_in, w_out)
-
-
-def swap_cores(block):
+    )(info, in_hbm(local), keep, got, horiz_rate, horiz_coef, w_in, w_out)
+
+
+def swap(block, bits):
     n = lax.axis_size("col")
-    return lax.ppermute(block, "col", [(i, i ^ 1) for i in range(n)])
+    return lax.ppermute(block, "col", [(i, i ^ bits) for i in range(n)])
+
+
+def together(arrived, local):
+    return lax.optimization_barrier((arrived, local))
 
 
 def on_device(image, vert_rate, vert_coef, horiz_rate, horiz_coef, w_in, w_out):
-    rows, cols = lax.axis_size("row"), lax.axis_size("col")
+    rows = lax.axis_size("row")
     piece = lax.axis_index("row")
-    core = lax.axis_index("col") % 2
+    col = lax.axis_index("col")
+    core, chip = col % 2, col // 2
+    bits = [chip % 2, chip // 2 % 2, chip // 4]
+    info = jnp.stack([core, bits[0], bits[1], bits[2], bits[0] ^ bits[2], bits[1] ^ bits[2]]).astype(jnp.int32)
 
     edges = row_edges(image, vert_rate).reshape(rows, 8, 8, LANES)
     edges = lax.all_to_all(edges, "row", 0, 0, tiled=True)
     rate_here = lax.dynamic_slice_in_dim(vert_rate, (piece // 8) * LANES, LANES, 1)
-    local = local_scan(image, vert_rate, vert_coef, 56, "vert_local")
-    edges, local = lax.optimization_barrier((edges, local))
+    local = local_scan(image, vert_rate, vert_coef, "vert_local")
+    edges, local = together(edges, local)
     incoming = prefix(edges, rate_here, 64.0)
     incoming = lax.all_to_all(incoming, "row", 0, 0, tiled=True).reshape(2, 8, 8, 8, LANES)
 
-    act, edge = act_and_edges(local, incoming, vert_rate, vert_coef, horiz_rate)
-
-    horiz = local_scan(act, horiz_rate, horiz_coef, 56, "horiz_local")
-
-    chips = [[2 * z + c for z in range(cols // 2)] for c in range(2)]
-    mine = lax.dynamic_index_in_dim(edge, core, 0, keepdims=False)
-    other = swap_cores(lax.dynamic_index_in_dim(edge, 1 - core, 0, keepdims=False))
-    rate_here = lax.dynamic_slice_in_dim(horiz_rate, core * LANES, LANES, 1)
-    decay = jnp.exp(-64.0 * rate_here)[None, :, None, :]
-    first = jnp.where(core == 0, mine, other)
-    second = jnp.where(core == 0, other, mine)
-    joined = lax.all_to_all(decay * first + second, "col", 0, 0, tiled=True, axis_index_groups=chips)
-    joined, horiz = lax.optimization_barrier((joined, horiz))
-    chain = prefix(joined, rate_here, 128.0)
-    chain = lax.all_to_all(chain, "col", 0, 0, tiled=True, axis_index_groups=chips)
-    after = decay * chain + first
-    keep = jnp.where(core == 0, chain, after)
-    got = swap_cores(jnp.where(core == 0, after, chain))
-
-    return mix(core.reshape(1), horiz, keep, got, horiz_rate, horiz_coef, w_in, w_out)
+    act, mine, other = act_and_edges(info, local, incoming, vert_rate, vert_coef, horiz_rate)
+
+    rate = lax.dynamic_slice_in_dim(horiz_rate, core * LANES, LANES, 1)
+    eight, four, two = (8, 8, 8, LANES), (4, 8, 8, LANES), (2, 8, 8, LANES)
+
+    def horiz(part, into):
+        return local_scan(act, horiz_rate, horiz_coef, f"horiz_local_{part}", part, 4, into)
+
+    def join(level, outs, keep, came):
+        kernel = functools.partial(join_kernel, level, 64.0 * 2**level)
+        return small(kernel, f"join_{level}", outs, info, keep, came, rate)
+
+    def part(level, shape, chains, first):
+        kernel = functools.partial(part_kernel, level, 64.0 * 2**level)
+        return small(kernel, f"part_{level}", [shape] * 2, info, *chains, first, rate)
+
+    first_tile, keep, send = join(0, [eight, four, four], mine, swap(other, 1))
+    came, local = together(swap(send, 2), horiz(0, None))
+    first_chip, keep, send = join(1, [four, two, two], keep, came)
+    came, local = together(swap(send, 4), horiz(1, local))
+    first_pair, group = join(2, [two, two], keep, came)
+    n = lax.axis_size("col")
+    chain = lax.ppermute(group, "col", [(i, i ^ (n - 2)) for i in range(n // 2)])
+    chain, local = together(chain, horiz(2, local))
+    keep, send = part(2, two, [chain], first_pair)
+    came, local = together(swap(send, 4), horiz(3, local))
+    keep, send = part(1, four, [keep, came], first_chip)
+    keep, send = part(0, eight, [keep, swap(send, 2)], first_tile)
+    got = swap(send, 1)
+
+    return mix(info, local, keep, got, horiz_rate, horiz_coef, w_in, w_out)
 
 
 def solution(mesh):

time: 98.6 us -> 99.8 us (1.012)
  blocking collectives: 12.9 us -> 0 us
  Pallas kernels: 40 us -> 49.1 us
  starting transfers between devices: 25 us -> 30.6 us
    ppermute x2 -> x7, starting transfers between devices: 5.66 us -> 18.9 us  [the longest x6 13.3 us: swap(): return lax.ppermute(block, 'col', [(i, i ^ bits) for i in range(n)])]
    all_to_all x1 -> x0, blocking collectives: 12.9 us -> none  [on_device(): lax.all_to_all(chain, 'col', 0, 0, tiled=True, axis_index_groups=chips)]
    pallas_call x5 -> x14, Pallas kernels: 39.1 us -> 48.2 us  [the longest x5 20.4 us: local_scan(): pl.pallas_call(kernel, grid=(steps,), in_specs=[place, whole((8, 256)), w...]
    all_to_all x1 -> x0, starting transfers between devices: 8.19 us -> none  [on_device(): lax.all_to_all(decay * first + second, 'col', 0, 0, tiled=True, axis_inde...]
    all_to_all x1 -> x0, waiting for transfers between devices: 3.85 us -> none  [on_device(): lax.all_to_all(decay * first + second, 'col', 0, 0, tiled=True, axis_inde...]
    ppermute x2 -> x7, waiting for transfers between devices: 2.32 us -> 5.99 us  [the longest x6 5.99 us: swap(): return lax.ppermute(block, 'col', [(i, i ^ bits) for i in range(n)])]
  transfers between devices with their start and end apart: 5 -> 9, of which waited for: 5 -> 6; matrix products, arithmetic and copies ran while one was open for 0% -> 1% of each run, Pallas kernels for 15% -> 21%
where the time goes in v5:
time: 99.8 us; the launch traced here: 99.2 us
  Pallas kernels  49.1 us (49%)
  starting transfers between devices  30.6 us (31%)
  waiting for transfers between devices  18.5 us (19%)
    pallas_call x5, Pallas kernels, local_scan(): pl.pallas_call(kernel, grid=(steps,), in_specs=[place, whole((8, 256)), w...  20.4 us
    ppermute x6, starting transfers between devices, swap(): return lax.ppermute(block, 'col', [(i, i ^ bits) for i in range(n)])  13.3 us
    pallas_call x1, Pallas kernels, mix(): pl.pallas_call(mix_kernel, grid=(4,), in_specs=[SMEM, pl.BlockSpec((64, 1...  10.9 us
    all_to_all x1, waiting for transfers between devices, on_device(): lax.all_to_all(incoming, 'row', 0, 0, tiled=True).reshape(2, 8, 8, 8, LANES)  9.97 us
    pallas_call x1, Pallas kernels, act_and_edges(): pl.pallas_call(act_kernel, grid=(4,), in_specs=[SMEM, pl.BlockSpec((16, 6...  9.02 us
    all_to_all x1, starting transfers between devices, on_device(): edges = lax.all_to_all(edges, 'row', 0, 0, tiled=True)  7.6 us
    ppermute x6, waiting for transfers between devices, swap(): return lax.ppermute(block, 'col', [(i, i ^ bits) for i in range(n)])  5.99 us
    ppermute x1, starting transfers between devices, on_device(): chain = lax.ppermute(group, 'col', [(i, i ^ n - 2) for i in range(n // 2)])  5.58 us
  transfers between devices with their start and end apart: 9, of which 6 were waited for; matrix products, arithmetic and copies ran while one was open for 1% of the time, Pallas kernels for 21%

profile of v5, /device:TPU:1, one launch (start us, length us, event | category | flops | bytes accessed | tf_op | source)
XLA Modules:
  0.0 99.2 jit_solution(14655676300218695023)
XLA Ops:
  0.0 4.4 %row_edges.1 = f32[2,8,8,8,128]{4,3,2,1,0:T(8,128)} custom-call(bf16[64,64,256]{2,1,0:T(8,128)(2,1)} %refs_0_.1, f32[8,256]{1,0:T(8,128)} %vr_ref.1), custom_call_target="tpu_custom_call" | custom-call | tf_op jit(solution)/shard_map/row_edges/pallas_call | solution.py:259
  4.4 7.6 %all-to-all-start = ((f32[16,8,8,128]{3,2,1,0:T(8,128)}), f32[16,8,8,128]{3,2,1,0:T(8,128)S(1)}, u32[]{:S(2)}, u32[]{:S(2)}) async-start(f32[16,8,8,128]{3,2,1,0:T(8,128)} %bitcast.6), calls=%async_computation | async-start | bytes 1048576 | tf_op jit(solution)/shard_map/all_to_all | solution.py:385
  12.0 0.7 constant_dynamic-slice_fusion.1.rate_ref
  12.7 0.0 copy-start.2
  12.7 0.0 copy-start.5
  12.7 7.3 %vert_local.1.local_ref = f32[64,64,256]{2,1,0:T(8,128)} custom-call(bf16[64,64,256]{2,1,0:T(8,128)(2,1)} %refs_0_.1, f32[8,256]{1,0:T(8,128)} %vr_ref.1, f32[8,256]{1,0:T(8,128)} %vc_ref.1), custom_call_target="tpu_custom_call" | custom-call | flops 5000000000 | bytes 8000000 | tf_op jit(solution)/shard_map/vert_local/pallas_call | solution.py:294
  20.0 2.5 %all-to-all-done.edge_ref = f32[16,8,8,128]{3,2,1,0:T(8,128)S(1)} async-done(((f32[16,8,8,128]{3,2,1,0:T(8,128)}), f32[16,8,8,128]{3,2,1,0:T(8,128)S(1)}, u32[]{:S(2)}, u32[]{:S(2)}) %all-to-all-start) | async-done | bytes 524320 | tf_op jit(solution)/shard_map/all_to_all | solution.py:385
  22.5 0.8 prefix.1
  23.4 4.1 %all-to-all-start.1 = ((f32[16,8,8,128]{3,2,1,0:T(8,128)}), f32[16,8,8,128]{3,2,1,0:T(8,128)S(1)}, u32[]{:S(2)}, u32[]{:S(2)}) async-start(f32[16,8,8,128]{3,2,1,0:T(8,128)} %prefix.1), calls=%async_computation.1 | async-start | bytes 1048576 | tf_op jit(solution)/shard_map/all_to_all | solution.py:390
  27.6 0.1 stack.27.info_ref
  27.7 10.0 %all-to-all-done.1 = f32[16,8,8,128]{3,2,1,0:T(8,128)S(1)} async-done(((f32[16,8,8,128]{3,2,1,0:T(8,128)}), f32[16,8,8,128]{3,2,1,0:T(8,128)S(1)}, u32[]{:S(2)}, u32[]{:S(2)}) %all-to-all-start.1) | async-done | bytes 524320 | tf_op jit(solution)/shard_map/all_to_all | solution.py:390
  37.6 0.0 copy-done.2
  37.6 0.0 copy-done.5
  37.6 0.0 copy-done.6
  37.6 9.0 %act_and_edges.1 = (bf16[64,64,256]{2,1,0:T(8,128)(2,1)}, f32[8,8,8,128]{3,2,1,0:T(8,128)S(1)}, f32[8,8,8,128]{3,2,1,0:T(8,128)S(1)}) custom-call(s32[6]{0:T(128)S(1)} %stack.27.info_ref, f32[64,64,256]{2,1,0:T(8,128)} %vert_local.1.local_ref, f32[2,8,8,8,128]{4,3,2,1,0:T(8,128)S(1)} %bitcast.8, f32[8,256]{1,0:T(8,128)S(1)} %copy-done.5, ...), custom_call_target="tpu_custom_call" | custom-call | tf_op jit(solution)/shard_map/act_and_edges/pallas_call | solution.py:322
  46.7 2.4 %collective-permute-start = (f32[8,8,8,128]{3,2,1,0:T(8,128)S(1)}, f32[8,8,8,128]{3,2,1,0:T(8,128)S(1)}, u32[]{:S(2)}, u32[]{:S(2)}) collective-permute-start(f32[8,8,8,128]{3,2,1,0:T(8,128)S(1)} %get-tuple-element.35), channel_id=1, source_target_pairs={{0,1},{1,0},{2,3},{3,2},{4,5},{5,4},{6,7},{7,6},{8,9},{9,8},{10,11... | collective-permute-start | bytes 786440 | tf_op jit(solution)/shard_map/ppermute | solution.py:369
  49.0 1.2 %collective-permute-done.came_ref = f32[8,8,8,128]{3,2,1,0:T(8,128)S(1)} collective-permute-done((f32[8,8,8,128]{3,2,1,0:T(8,128)S(1)}, f32[8,8,8,128]{3,2,1,0:T(8,128)S(1)}, u32[]{:S(2)}, u32[]{:S(2)}) %collective-permute-start) | collective-permute-done | bytes 262176 | tf_op jit(solution)/shard_map/ppermute | solution.py:369
  50.2 0.6 join_0.1
  50.8 1.7 %collective-permute-start.1 = (f32[4,8,8,128]{3,2,1,0:T(8,128)S(1)}, f32[4,8,8,128]{3,2,1,0:T(8,128)S(1)}, u32[]{:S(2)}, u32[]{:S(2)}) collective-permute-start(f32[4,8,8,128]{3,2,1,0:T(8,128)S(1)} %get-tuple-element.37), channel_id=1, source_target_pairs={{0,2},{1,3},{2,0},{3,1},{4,6},{5,7},{6,4},{7,5},{8,10},{9,11},{10,... | collective-permute-start | bytes 393224 | tf_op jit(solution)/shard_map/ppermute | solution.py:369
  52.5 3.3 %horiz_local_0.1.refs_3_ = f32[64,64,256]{2,1,0:T(8,128)} custom-call(bf16[64,64,256]{2,1,0:T(8,128)(2,1)} %get-tuple-element.38.refs_0_, f32[8,256]{1,0:T(8,128)} %hr_ref.3, f32[8,256]{1,0:T(8,128)} %hc_ref.1), custom_call_target="tpu_custom_call" | custom-call | flops 1250000000 | bytes 2000000 | tf_op jit(solution)/shard_map/horiz_local_0/pallas_call | solution.py:294
  55.9 0.1 collective-permute-done.1.came_ref
  56.0 0.6 join_1.1
  56.6 3.1 %collective-permute-start.2 = (f32[2,8,8,128]{3,2,1,0:T(8,128)S(1)}, f32[2,8,8,128]{3,2,1,0:T(8,128)S(1)}, u32[]{:S(2)}, u32[]{:S(2)}) collective-permute-start(f32[2,8,8,128]{3,2,1,0:T(8,128)S(1)} %get-tuple-element.41), channel_id=1, source_target_pairs={{0,4},{1,5},{2,6},{3,7},{4,0},{5,1},{6,2},{7,3},{8,12},{9,13},{10,... | collective-permute-start | bytes 196616 | tf_op jit(solution)/shard_map/ppermute | solution.py:369
  59.6 3.2 %horiz_local_1.1.refs_3_ = f32[64,64,256]{2,1,0:T(8,128)} custom-call(bf16[64,64,256]{2,1,0:T(8,128)(2,1)} %get-tuple-element.38.refs_0_, f32[8,256]{1,0:T(8,128)} %hr_ref.3, f32[8,256]{1,0:T(8,128)} %hc_ref.1, f32[64,64,256]{2,1,0:T(8,128)} %horiz_local_0.1.refs_3_), custom_call_target="tpu_custom_call", output_to_operand_aliasing={{}: (3, {})} | custom-call | flops 1250000000 | bytes 2000000 | tf_op jit(solution)/shard_map/horiz_local_1/pallas_call | solution.py:294
  62.9 0.0 collective-permute-done.2.came_ref
  62.9 0.6 join_2.1
  63.5 5.6 %collective-permute-start.3 = (f32[2,8,8,128]{3,2,1,0:T(8,128)S(1)}, f32[2,8,8,128]{3,2,1,0:T(8,128)S(1)}, u32[]{:S(2)}, u32[]{:S(2)}) collective-permute-start(f32[2,8,8,128]{3,2,1,0:T(8,128)S(1)} %get-tuple-element.44), channel_id=1, source_target_pairs={{0,14},{1,15},{2,12},{3,13},{4,10},{5,11},{6,8},{7,9},{16,30},{17,... | collective-permute-start | bytes 196616 | tf_op jit(solution)/shard_map/ppermute | solution.py:414
  69.0 3.3 %horiz_local_2.1.refs_3_ = f32[64,64,256]{2,1,0:T(8,128)} custom-call(bf16[64,64,256]{2,1,0:T(8,128)(2,1)} %get-tuple-element.38.refs_0_, f32[8,256]{1,0:T(8,128)} %hr_ref.3, f32[8,256]{1,0:T(8,128)} %hc_ref.1, f32[64,64,256]{2,1,0:T(8,128)} %horiz_local_1.1.refs_3_), custom_call_target="tpu_custom_call", output_to_operand_aliasing={{}: (3, {})} | custom-call | flops 1250000000 | bytes 2000000 | tf_op jit(solution)/shard_map/horiz_local_2/pallas_call | solution.py:294
  72.3 0.0 collective-permute-done.3.refs_0_
  72.3 0.6 part_2.1
  72.9 0.0 copy-start
  72.9 0.0 copy-start.1
  72.9 0.0 copy-start.3
  72.9 0.0 copy-start.4
  72.9 1.9 %collective-permute-start.4 = (f32[2,8,8,128]{3,2,1,0:T(8,128)S(1)}, f32[2,8,8,128]{3,2,1,0:T(8,128)S(1)}, u32[]{:S(2)}, u32[]{:S(2)}) collective-permute-start(f32[2,8,8,128]{3,2,1,0:T(8,128)S(1)} %get-tuple-element.48), channel_id=1, source_target_pairs={{0,4},{1,5},{2,6},{3,7},{4,0},{5,1},{6,2},{7,3},{8,12},{9,13},{10,... | collective-permute-start | bytes 196616 | tf_op jit(solution)/shard_map/ppermute | solution.py:369
  74.8 3.3 %horiz_local_3.1.local_ref = f32[64,64,256]{2,1,0:T(8,128)} custom-call(bf16[64,64,256]{2,1,0:T(8,128)(2,1)} %get-tuple-element.38.refs_0_, f32[8,256]{1,0:T(8,128)} %hr_ref.3, f32[8,256]{1,0:T(8,128)} %hc_ref.1, f32[64,64,256]{2,1,0:T(8,128)} %horiz_local_2.1.refs_3_), custom_call_target="tpu_custom_call", output_to_operand_aliasing={{}: (3, {})} | custom-call | flops 1250000000 | bytes 2000000 | tf_op jit(solution)/shard_map/horiz_local_3/pallas_call | solution.py:294
  78.1 0.0 collective-permute-done.4.refs_1_
  78.1 0.6 part_1.1
  78.7 0.3 collective-permute-start.5
  79.0 3.6 %collective-permute-done.5.refs_1_ = f32[4,8,8,128]{3,2,1,0:T(8,128)S(1)} collective-permute-done((f32[4,8,8,128]{3,2,1,0:T(8,128)S(1)}, f32[4,8,8,128]{3,2,1,0:T(8,128)S(1)}, u32[]{:S(2)}, u32[]{:S(2)}) %collective-permute-start.5) | collective-permute-done | bytes 131104 | tf_op jit(solution)/shard_map/ppermute | solution.py:369
  82.6 0.6 part_0.1
  83.2 3.9 %collective-permute-start.6 = (f32[8,8,8,128]{3,2,1,0:T(8,128)S(1)}, f32[8,8,8,128]{3,2,1,0:T(8,128)S(1)}, u32[]{:S(2)}, u32[]{:S(2)}) collective-permute-start(f32[8,8,8,128]{3,2,1,0:T(8,128)S(1)} %get-tuple-element.58), channel_id=1, source_target_pairs={{0,1},{1,0},{2,3},{3,2},{4,5},{5,4},{6,7},{7,6},{8,9},{9,8},{10,11... | collective-permute-start | bytes 786440 | tf_op jit(solution)/shard_map/ppermute | solution.py:369
  87.1 1.2 %collective-permute-done.6.got_ref = f32[8,8,8,128]{3,2,1,0:T(8,128)S(1)} collective-permute-done((f32[8,8,8,128]{3,2,1,0:T(8,128)S(1)}, f32[8,8,8,128]{3,2,1,0:T(8,128)S(1)}, u32[]{:S(2)}, u32[]{:S(2)}) %collective-permute-start.6) | collective-permute-done | bytes 262176 | tf_op jit(solution)/shard_map/ppermute | solution.py:369
  88.3 0.0 copy-done
  88.3 0.0 copy-done.1
  88.3 0.0 copy-done.3
  88.3 0.0 copy-done.4
  88.3 10.9 %mix.1 = bf16[64,64,256]{2,1,0:T(8,128)(2,1)} custom-call(s32[6]{0:T(128)S(1)} %stack.27.info_ref, f32[64,64,256]{2,1,0:T(8,128)} %horiz_local_3.1.local_ref, f32[8,8,8,128]{3,2,1,0:T(8,128)S(1)} %get-tuple-element.57.keep_ref, f32[8,8,8,128]{3,2,1,0:T(8,128)S(1)} %collective-permute-done.6.got_ref, f32[8,256]{1,0:T(8,128)S(1)} %copy-done.3, ...), custom_call_target="tpu_custom_call" | custom-call | tf_op jit(solution)/shard_map/mix/pallas_call | solution.py:346
  (2 shorter events, 0.0 us)
Async XLA Ops:
  4.4 18.1 %all-to-all-start = ((f32[16,8,8,128]{3,2,1,0:T(8,128)}), f32[16,8,8,128]{3,2,1,0:T(8,128)S(1)}, u32[]{:S(2)}, u32[]{:S(2)}) async-start(f32[16,8,8,128]{3,2,1,0:T(8,128)} %bitcast.6), calls=%async_computation | async-start | bytes 1048576 | tf_op jit(solution)/shard_map/all_to_all | solution.py:385
  12.7 24.9 %copy-start.2 = (f32[8,256]{1,0:T(8,128)S(1)}, f32[8,256]{1,0:T(8,128)}, u32[]{:S(2)}) copy-start(f32[8,256]{1,0:T(8,128)} %hr_ref.3) | copy-start | bytes 24580
  12.7 24.9 %copy-start.5 = (f32[8,256]{1,0:T(8,128)S(1)}, f32[8,256]{1,0:T(8,128)}, u32[]{:S(2)}) copy-start(f32[8,256]{1,0:T(8,128)} %vr_ref.1) | copy-start | bytes 24580
  12.7 24.9 %copy-start.6 = (f32[8,256]{1,0:T(8,128)S(1)}, f32[8,256]{1,0:T(8,128)}, u32[]{:S(2)}) copy-start(f32[8,256]{1,0:T(8,128)} %vc_ref.1) | copy-start | bytes 24580
  23.4 14.3 %all-to-all-start.1 = ((f32[16,8,8,128]{3,2,1,0:T(8,128)}), f32[16,8,8,128]{3,2,1,0:T(8,128)S(1)}, u32[]{:S(2)}, u32[]{:S(2)}) async-start(f32[16,8,8,128]{3,2,1,0:T(8,128)} %prefix.1), calls=%async_computation.1 | async-start | bytes 1048576 | tf_op jit(solution)/shard_map/all_to_all | solution.py:390
  46.7 3.5 %collective-permute-start = (f32[8,8,8,128]{3,2,1,0:T(8,128)S(1)}, f32[8,8,8,128]{3,2,1,0:T(8,128)S(1)}, u32[]{:S(2)}, u32[]{:S(2)}) collective-permute-start(f32[8,8,8,128]{3,2,1,0:T(8,128)S(1)} %get-tuple-element.35), channel_id=1, source_target_pairs={{0,1},{1,0},{2,3},{3,2},{4,5},{5,4},{6,7},{7,6},{8,9},{9,8},{10,11... | collective-permute-start | bytes 786440 | tf_op jit(solution)/shard_map/ppermute | solution.py:369
  50.8 5.2 %collective-permute-start.1 = (f32[4,8,8,128]{3,2,1,0:T(8,128)S(1)}, f32[4,8,8,128]{3,2,1,0:T(8,128)S(1)}, u32[]{:S(2)}, u32[]{:S(2)}) collective-permute-start(f32[4,8,8,128]{3,2,1,0:T(8,128)S(1)} %get-tuple-element.37), channel_id=1, source_target_pairs={{0,2},{1,3},{2,0},{3,1},{4,6},{5,7},{6,4},{7,5},{8,10},{9,11},{10,... | collective-permute-start | bytes 393224 | tf_op jit(solution)/shard_map/ppermute | solution.py:369
  56.6 6.3 %collective-permute-start.2 = (f32[2,8,8,128]{3,2,1,0:T(8,128)S(1)}, f32[2,8,8,128]{3,2,1,0:T(8,128)S(1)}, u32[]{:S(2)}, u32[]{:S(2)}) collective-permute-start(f32[2,8,8,128]{3,2,1,0:T(8,128)S(1)} %get-tuple-element.41), channel_id=1, source_target_pairs={{0,4},{1,5},{2,6},{3,7},{4,0},{5,1},{6,2},{7,3},{8,12},{9,13},{10,... | collective-permute-start | bytes 196616 | tf_op jit(solution)/shard_map/ppermute | solution.py:369
  63.5 8.8 %collective-permute-start.3 = (f32[2,8,8,128]{3,2,1,0:T(8,128)S(1)}, f32[2,8,8,128]{3,2,1,0:T(8,128)S(1)}, u32[]{:S(2)}, u32[]{:S(2)}) collective-permute-start(f32[2,8,8,128]{3,2,1,0:T(8,128)S(1)} %get-tuple-element.44), channel_id=1, source_target_pairs={{0,14},{1,15},{2,12},{3,13},{4,10},{5,11},{6,8},{7,9},{16,30},{17,... | collective-permute-start | bytes 196616 | tf_op jit(solution)/shard_map/ppermute | solution.py:414
  72.9 15.4 %copy-start = (bf16[256,1024]{1,0:T(8,128)(2,1)S(1)}, bf16[256,1024]{1,0:T(8,128)(2,1)}, u32[]{:S(2)}) copy-start(bf16[256,1024]{1,0:T(8,128)(2,1)} %w_in_ref.1) | copy-start | bytes 1572868
  72.9 15.4 %copy-start.1 = (bf16[1024,256]{1,0:T(8,128)(2,1)S(1)}, bf16[1024,256]{1,0:T(8,128)(2,1)}, u32[]{:S(2)}) copy-start(bf16[1024,256]{1,0:T(8,128)(2,1)} %w_out_ref.1) | copy-start | bytes 1572868
  72.9 15.4 %copy-start.3 = (f32[8,256]{1,0:T(8,128)S(1)}, f32[8,256]{1,0:T(8,128)}, u32[]{:S(2)}) copy-start(f32[8,256]{1,0:T(8,128)} %hr_ref.3) | copy-start | bytes 24580
  72.9 15.4 %copy-start.4 = (f32[8,256]{1,0:T(8,128)S(1)}, f32[8,256]{1,0:T(8,128)}, u32[]{:S(2)}) copy-start(f32[8,256]{1,0:T(8,128)} %hc_ref.1) | copy-start | bytes 24580
  72.9 5.2 %collective-permute-start.4 = (f32[2,8,8,128]{3,2,1,0:T(8,128)S(1)}, f32[2,8,8,128]{3,2,1,0:T(8,128)S(1)}, u32[]{:S(2)}, u32[]{:S(2)}) collective-permute-start(f32[2,8,8,128]{3,2,1,0:T(8,128)S(1)} %get-tuple-element.48), channel_id=1, source_target_pairs={{0,4},{1,5},{2,6},{3,7},{4,0},{5,1},{6,2},{7,3},{8,12},{9,13},{10,... | collective-permute-start | bytes 196616 | tf_op jit(solution)/shard_map/ppermute | solution.py:369
  78.7 3.9 %collective-permute-start.5 = (f32[4,8,8,128]{3,2,1,0:T(8,128)S(1)}, f32[4,8,8,128]{3,2,1,0:T(8,128)S(1)}, u32[]{:S(2)}, u32[]{:S(2)}) collective-permute-start(f32[4,8,8,128]{3,2,1,0:T(8,128)S(1)} %get-tuple-element.55), channel_id=1, source_target_pairs={{0,2},{1,3},{2,0},{3,1},{4,6},{5,7},{6,4},{7,5},{8,10},{9,11},{10,... | collective-permute-start | bytes 393224 | tf_op jit(solution)/shard_map/ppermute | solution.py:369
  83.2 5.1 %collective-permute-start.6 = (f32[8,8,8,128]{3,2,1,0:T(8,128)S(1)}, f32[8,8,8,128]{3,2,1,0:T(8,128)S(1)}, u32[]{:S(2)}, u32[]{:S(2)}) collective-permute-start(f32[8,8,8,128]{3,2,1,0:T(8,128)S(1)} %get-tuple-element.58), channel_id=1, source_target_pairs={{0,1},{1,0},{2,3},{3,2},{4,5},{5,4},{6,7},{7,6},{8,9},{9,8},{10,11... | collective-permute-start | bytes 786440 | tf_op jit(solution)/shard_map/ppermute | solution.py:369

commit v6 on v5

--- a/solution.py
+++ b/solution.py
@@ -14,6 +14,7 @@
 MODES = 8
 SQRT_2_PI = math.sqrt(2.0 / math.pi)
 PITCH = 72
+ACT_ROWS = 32
 
 
 def gelu(x):
@@ -117,88 +118,67 @@
     return [jnp.broadcast_to(jnp.exp(-span * rate_ref[m : m + 1, :]), (8, LANES)) for m in range(MODES)]
 
 
-def join_kernel(level, span, info_ref, keep_ref, came_ref, rate_ref, first_ref, *out_refs):
-    left_here = info_ref[level] == 0
-    here = info_ref[4 + level] if len(out_refs) == 2 else 0
+def join_kernel(span, core_ref, mine_ref, came_ref, rate_ref, first_ref, joined_ref):
+    left_here = core_ref[0] == 0
     decay = decays(rate_ref, span)
-    part = keep_ref.shape[0] // len(out_refs)
-    for b in range(part):
-        for k, out_ref in enumerate(out_refs):
-            at = b if len(out_refs) == 1 else (here * part if k == 0 else part - here * part) + b
-            for m in range(MODES):
-                keep, came = keep_ref[at, m], came_ref[at, m]
-                first = jnp.where(left_here, keep, came)
-                first_ref[at, m] = first
-                out_ref[b, m] = decay[m] * first + jnp.where(left_here, came, keep)
-
-
-def part_kernel(level, span, info_ref, *refs):
-    *in_refs, first_ref, rate_ref, keep_ref, send_ref = refs
-    left_here = info_ref[level] == 0
-    here = info_ref[4 + level] if len(in_refs) == 2 else 0
+    for b in range(8):
+        for m in range(MODES):
+            mine, came = mine_ref[b, m], came_ref[b, m]
+            first = jnp.where(left_here, mine, came)
+            first_ref[b, m] = first
+            joined_ref[b, m] = decay[m] * first + jnp.where(left_here, came, mine)
+
+
+def part_kernel(span, core_ref, chain_ref, first_ref, rate_ref, keep_ref, send_ref):
+    left_here = core_ref[0] == 0
     decay = decays(rate_ref, span)
-    part = first_ref.shape[0] // len(in_refs)
-    for b in range(part):
-        for k, in_ref in enumerate(in_refs):
-            at = b if len(in_refs) == 1 else (here * part if k == 0 else part - here * part) + b
-            for m in range(MODES):
-                chain = in_ref[b, m]
-                after = decay[m] * chain + first_ref[at, m]
-                keep_ref[at, m] = jnp.where(left_here, chain, after)
-                send_ref[at, m] = jnp.where(left_here, after, chain)
-
-
-def act_kernel(info_ref, local_ref, in_ref, vr_ref, vc_ref, hr_ref, act_ref, mine_ref, other_ref, tails, field):
-    for half in range(2):
-        lanes = slice(half * LANES, (half + 1) * LANES)
-        pole = poles(vr_ref, half, 16)
-
-        @pl.when(pl.program_id(0) == 0)
-        def _(half=half, pole=pole):
-            weight = weights(vr_ref, vc_ref, half, 16)
-            for m in range(MODES):
-                factor = (pole[m] * weight[m])[None, :8]
-                tails[half, :, m] = in_ref[half, :, m] * factor
-
-        def block(b, _, half=half, lanes=lanes, pole=pole):
-            pair = pl.ds(b * 2, 2)
-            cols = pl.ds(pl.multiple_of(b * 16, 16), 16)
-            tail = [tails[half, pair, m].reshape(16, LANES) for m in range(MODES)]
-            for s in range(16):
-                y = local_ref[s, cols, lanes] + tree(tail)
-                tail = [p * g for p, g in zip(pole, tail)]
-                a = gelu(y).astype(BF16).astype(F32)
-                field[half, pl.ds(pl.multiple_of(s * PITCH + b * 16, 8), 16), :] = a
-            for m in range(MODES):
-                tails[half, pair, m] = tail[m].reshape(2, 8, LANES)
-            return 0
-
-        lax.fori_loop(0, 4, block, 0)
-
-    for half in range(2):
-        lanes = slice(half * LANES, (half + 1) * LANES)
-        pole = poles(hr_ref, half, 16)
-
-        def steps(i, states, half=half, lanes=lanes, pole=pole):
+    for b in range(8):
+        for m in range(MODES):
+            chain = chain_ref[b, m]
+            after = decay[m] * chain + first_ref[b, m]
+            keep_ref[b, m] = jnp.where(left_here, chain, after)
+            send_ref[b, m] = jnp.where(left_here, after, chain)
+
+
+def act_kernel(side_ref, local_ref, in_ref, vr_ref, vc_ref, hr_ref, *refs):
+    act_ref, edge_ref, tails, field = refs[-4:]
+    rows = local_ref.shape[0]
+    pole = poles(vr_ref, 0, 16)
+
+    @pl.when(pl.program_id(0) == 0)
+    def _():
+        weight = weights(vr_ref, vc_ref, 0, 16)
+        for m in range(MODES):
+            tails[:, m] = in_ref[0, :, m] * (pole[m] * weight[m])[None, :8]
+
+    def block(b, _):
+        pair = pl.ds(b * 2, 2)
+        cols = pl.ds(pl.multiple_of(b * 16, 16), 16)
+        tail = [tails[pair, m].reshape(16, LANES) for m in range(MODES)]
+        for s in range(rows):
+            y = local_ref[s, cols, :] + tree(tail)
+            tail = [p * g for p, g in zip(pole, tail)]
+            a = gelu(y).astype(BF16).astype(F32)
+            field[pl.ds(pl.multiple_of(s * PITCH + b * 16, 8), 16), :] = a
+        for m in range(MODES):
+            tails[pair, m] = tail[m].reshape(2, 8, LANES)
+        return 0
+
+    lax.fori_loop(0, 4, block, 0)
+    pole_along = poles(hr_ref, 0, 16)
+    for r in range(0, rows, 16):
+
+        def steps(i, states, r=r):
             for k in range(8):
                 w = i * 8 + k
-                u = field[half, pl.ds(w, 16, stride=PITCH), :]
-                act_ref[w, :, lanes] = u.astype(BF16)
-                states = [p * h + u for p, h in zip(pole, states)]
+                u = field[pl.ds(w + r * PITCH, 16, stride=PITCH), :]
+                act_ref[w, r : r + 16, :] = u.astype(BF16)
+                states = [p * h + u for p, h in zip(pole_along, states)]
             return states
 
         states = lax.fori_loop(0, 8, steps, [jnp.zeros((16, LANES), F32)] * MODES)
-        mine = info_ref[0] == half
-
-        @pl.when(mine)
-        def _(states=states):
-            for m in range(MODES):
-                mine_ref[:, m] = states[m].reshape(2, 8, LANES)
-
-        @pl.when(jnp.logical_not(mine))
-        def _(states=states):
-            for m in range(MODES):
-                other_ref[:, m] = states[m].reshape(2, 8, LANES)
+        for m in range(MODES):
+            edge_ref[r // 8 : r // 8 + 2, m] = states[m].reshape(2, 8, LANES)
 
 
 def mix_kernel(info_ref, local_ref, keep_ref, got_ref, hr_ref, hc_ref, w_in_ref, w_out_ref, out_ref, horiz, mixed):
@@ -283,27 +263,18 @@
     )(edges, rate)
 
 
-def local_scan(block, rate, coef, name, part=0, parts=1, into=None):
-    steps = 4 // parts
-
-    def kernel(*refs):
-        local_kernel(*refs[:3], refs[-1])
-
-    place = pl.BlockSpec((64, 16, 256), lambda i: (0, i + part * steps, 0))
-    more = [] if into is None else [in_hbm(into)]
-    return pl.pallas_call(
-        kernel,
-        grid=(steps,),
-        in_specs=[place, whole((8, 256)), whole((8, 256))] + [HBM] * len(more),
+def local_scan(block, rate, coef, name):
+    place = pl.BlockSpec((64, 16, 256), lambda i: (0, i, 0))
+    return pl.pallas_call(
+        local_kernel,
+        grid=(4,),
+        in_specs=[place, whole((8, 256)), whole((8, 256))],
         out_specs=place,
         out_shape=pltpu.HBM((64, 64, 256), F32),
-        input_output_aliases={3: 0} if more else {},
         compiler_params=params(56),
-        cost_estimate=pl.CostEstimate(
-            flops=5_000_000_000 // parts, bytes_accessed=8_000_000 // parts, transcendentals=0
-        ),
+        cost_estimate=pl.CostEstimate(flops=5_000_000_000, bytes_accessed=8_000_000, transcendentals=0),
         name=name,
-    )(block, rate, coef, *more)
+    )(block, rate, coef)
 
 
 def small(kernel, name, outs, *operands):
@@ -317,28 +288,37 @@
     )(*operands)
 
 
-def act_and_edges(info, local, incoming, vert_rate, vert_coef, horiz_rate):
-    edge = pl.BlockSpec((2, 8, 8, LANES), lambda i: (i, 0, 0, 0))
+def act_and_edges(side, local, incoming, vert_rate, vert_coef, horiz_rate, into=None):
+    rate = pl.BlockSpec((8, LANES), lambda i, side: (0, side[0]))
+    more = [] if into is None else [in_hbm(into)]
     return pl.pallas_call(
         act_kernel,
-        grid=(4,),
-        in_specs=[
-            SMEM,
-            pl.BlockSpec((16, 64, 256), lambda i: (i, 0, 0)),
-            whole((2, 8, 8, 8, LANES)),
-            whole((8, 256)),
-            whole((8, 256)),
-            whole((8, 256)),
-        ],
-        out_specs=[pl.BlockSpec((64, 16, 256), lambda i: (0, i, 0)), edge, edge],
-        out_shape=[pltpu.HBM((64, 64, 256), BF16)] + [jax.ShapeDtypeStruct((8, 8, 8, LANES), F32)] * 2,
-        scratch_shapes=[
-            pltpu.VMEM((2, 8, 8, 8, LANES), F32),
-            pltpu.VMEM((2, 16 * PITCH, LANES), F32),
-        ],
+        grid_spec=pltpu.PrefetchScalarGridSpec(
+            num_scalar_prefetch=1,
+            grid=(64 // ACT_ROWS,),
+            in_specs=[
+                pl.BlockSpec((ACT_ROWS, 64, LANES), lambda i, side: (i, 0, side[0])),
+                pl.BlockSpec((1, 8, 8, 8, LANES), lambda i, side: (side[0], 0, 0, 0, 0)),
+                rate,
+                rate,
+                rate,
+            ]
+            + [HBM] * len(more),
+            out_specs=[
+                pl.BlockSpec((64, ACT_ROWS, LANES), lambda i, side: (0, i, side[0])),
+                pl.BlockSpec((ACT_ROWS // 8, 8, 8, LANES), lambda i, side: (i, 0, 0, 0)),
+            ],
+            scratch_shapes=[
+                pltpu.VMEM((8, 8, 8, LANES), F32),
+                pltpu.VMEM((ACT_ROWS * PITCH, LANES), F32),
+            ],
+        ),
+        out_shape=[pltpu.HBM((64, 64, 256), BF16), jax.ShapeDtypeStruct((8, 8, 8, LANES), F32)],
+        input_output_aliases={6: 0} if more else {},
         compiler_params=params(24),
+        cost_estimate=pl.CostEstimate(flops=3_000_000_000, bytes_accessed=4_000_000, transcendentals=0),
         name="act_and_edges",
-    )(info, in_hbm(local), incoming, vert_rate, vert_coef, horiz_rate)
+    )(side, in_hbm(local), incoming, vert_rate, vert_coef, horiz_rate, *more)
 
 
 def mix(info, local, keep, got, horiz_rate, horiz_coef, w_in, w_out):
@@ -374,52 +354,39 @@
 
 
 def on_device(image, vert_rate, vert_coef, horiz_rate, horiz_coef, w_in, w_out):
-    rows = lax.axis_size("row")
+    rows, cols = lax.axis_size("row"), lax.axis_size("col")
     piece = lax.axis_index("row")
-    col = lax.axis_index("col")
-    core, chip = col % 2, col // 2
-    bits = [chip % 2, chip // 2 % 2, chip // 4]
-    info = jnp.stack([core, bits[0], bits[1], bits[2], bits[0] ^ bits[2], bits[1] ^ bits[2]]).astype(jnp.int32)
+    core = lax.axis_index("col") % 2
+    mine, other = core.reshape(1), (1 - core).reshape(1)
 
     edges = row_edges(image, vert_rate).reshape(rows, 8, 8, LANES)
     edges = lax.all_to_all(edges, "row", 0, 0, tiled=True)
-    rate_here = lax.dynamic_slice_in_dim(vert_rate, (piece // 8) * LANES, LANES, 1)
+    rate = lax.dynamic_slice_in_dim(vert_rate, (piece // 8) * LANES, LANES, 1)
     local = local_scan(image, vert_rate, vert_coef, "vert_local")
     edges, local = together(edges, local)
-    incoming = prefix(edges, rate_here, 64.0)
+    incoming = prefix(edges, rate, 64.0)
     incoming = lax.all_to_all(incoming, "row", 0, 0, tiled=True).reshape(2, 8, 8, 8, LANES)
 
-    act, mine, other = act_and_edges(info, local, incoming, vert_rate, vert_coef, horiz_rate)
-
+    vert = (incoming, vert_rate, vert_coef, horiz_rate)
+    act, edge = act_and_edges(other, local, *vert)
+    came = swap(edge, 1)
+    act, edge = act_and_edges(mine, local, *vert, act)
+
+    chips = [[2 * z + c for z in range(cols // 2)] for c in range(2)]
     rate = lax.dynamic_slice_in_dim(horiz_rate, core * LANES, LANES, 1)
-    eight, four, two = (8, 8, 8, LANES), (4, 8, 8, LANES), (2, 8, 8, LANES)
-
-    def horiz(part, into):
-        return local_scan(act, horiz_rate, horiz_coef, f"horiz_local_{part}", part, 4, into)
-
-    def join(level, outs, keep, came):
-        kernel = functools.partial(join_kernel, level, 64.0 * 2**level)
-        return small(kernel, f"join_{level}", outs, info, keep, came, rate)
-
-    def part(level, shape, chains, first):
-        kernel = functools.partial(part_kernel, level, 64.0 * 2**level)
-        return small(kernel, f"part_{level}", [shape] * 2, info, *chains, first, rate)
-
-    first_tile, keep, send = join(0, [eight, four, four], mine, swap(other, 1))
-    came, local = together(swap(send, 2), horiz(0, None))
-    first_chip, keep, send = join(1, [four, two, two], keep, came)
-    came, local = together(swap(send, 4), horiz(1, local))
-    first_pair, group = join(2, [two, two], keep, came)
-    n = lax.axis_size("col")
-    chain = lax.ppermute(group, "col", [(i, i ^ (n - 2)) for i in range(n // 2)])
-    chain, local = together(chain, horiz(2, local))
-    keep, send = part(2, two, [chain], first_pair)
-    came, local = together(swap(send, 4), horiz(3, local))
-    keep, send = part(1, four, [keep, came], first_chip)
-    keep, send = part(0, eight, [keep, swap(send, 2)], first_tile)
+    tile = [(8, 8, 8, LANES)] * 2
+    join = functools.partial(join_kernel, 64.0)
+    first, joined = small(join, "join_cores", tile, mine, edge, came, rate)
+    joined = lax.all_to_all(joined, "col", 0, 0, tiled=True, axis_index_groups=chips)
+    local = local_scan(act, horiz_rate, horiz_coef, "horiz_local")
+    joined, local = together(joined, local)
+    chain = prefix(joined, rate, 128.0)
+    chain = lax.all_to_all(chain, "col", 0, 0, tiled=True, axis_index_groups=chips)
+    part = functools.partial(part_kernel, 64.0)
+    keep, send = small(part, "part_cores", tile, mine, chain, first, rate)
     got = swap(send, 1)
 
-    return mix(info, local, keep, got, horiz_rate, horiz_coef, w_in, w_out)
+    return mix(mine, local, keep, got, horiz_rate, horiz_coef, w_in, w_out)
 
 
 def solution(mesh):

time: 99.8 us -> 99.5 us (level)
  blocking collectives: 0 us -> 14.7 us
  starting transfers between devices: 30.6 us -> 22.8 us
  Pallas kernels: 49.1 us -> 42 us
    all_to_all x0 -> x1, blocking collectives: none -> 14.7 us  [on_device(): lax.all_to_all(chain, 'col', 0, 0, tiled=True, axis_index_groups=chips)]
    ppermute x6 -> x2, starting transfers between devices: 13.3 us -> 3.49 us  [swap(): return lax.ppermute(block, 'col', [(i, i ^ bits) for i in range(n)])]
    all_to_all x0 -> x1, starting transfers between devices: none -> 8.19 us  [on_device(): lax.all_to_all(joined, 'col', 0, 0, tiled=True, axis_index_groups=chips)]
    ppermute x1 -> x0, starting transfers between devices: 5.58 us -> none  [on_device(): chain = lax.ppermute(group, 'col', [(i, i ^ n - 2) for i in range(n // 2)])]
    all_to_all x0 -> x1, waiting for transfers between devices: none -> 5.04 us  [on_device(): lax.all_to_all(joined, 'col', 0, 0, tiled=True, axis_index_groups=chips)]
    ppermute x6 -> x2, waiting for transfers between devices: 5.99 us -> 1.16 us  [swap(): return lax.ppermute(block, 'col', [(i, i ^ bits) for i in range(n)])]
    pallas_call x6 -> x4, Pallas kernels: 29.4 us -> 25.1 us  [the longest x2 14.5 us: local_scan(): pl.pallas_call(local_kernel, grid=(4,), in_specs=[place, whole((8, 256)),...]
    pallas_call x6 -> x2, Pallas kernels: 3.48 us -> 0.82 us  [small(): pl.pallas_call(kernel, in_specs=[SMEM] + [VMEM] * (len(operands) - 1), ou...]
  transfers between devices with their start and end apart: 9 -> 5, of which waited for: 6 -> 4; matrix products, arithmetic and copies ran while one was open for 1% -> 0% of each run, Pallas kernels for 21% -> 20%
where the time goes in v6:
time: 99.5 us; the launch traced here: 98.8 us
  Pallas kernels  42 us (42%)
  starting transfers between devices  22.8 us (23%)
  waiting for transfers between devices  19.1 us (19%)
  blocking collectives  14.7 us (15%)
    all_to_all x1, blocking collectives, on_device(): lax.all_to_all(chain, 'col', 0, 0, tiled=True, axis_index_groups=chips)  14.7 us
    pallas_call x2, Pallas kernels, local_scan(): pl.pallas_call(local_kernel, grid=(4,), in_specs=[place, whole((8, 256)),...  14.5 us
    pallas_call x1, Pallas kernels, mix(): pl.pallas_call(mix_kernel, grid=(4,), in_specs=[SMEM, pl.BlockSpec((64, 1...  10.8 us
    pallas_call x2, Pallas kernels, act_and_edges(): pl.pallas_call(act_kernel, grid_spec=pltpu.PrefetchScalarGridSpec(num_sca...  10.6 us
    all_to_all x1, waiting for transfers between devices, on_device(): lax.all_to_all(incoming, 'row', 0, 0, tiled=True).reshape(2, 8, 8, 8, LANES)  9.62 us
    all_to_all x1, starting transfers between devices, on_device(): lax.all_to_all(joined, 'col', 0, 0, tiled=True, axis_index_groups=chips)  8.19 us
    all_to_all x1, starting transfers between devices, on_device(): edges = lax.all_to_all(edges, 'row', 0, 0, tiled=True)  7.6 us
    all_to_all x1, waiting for transfers between devices, on_device(): lax.all_to_all(joined, 'col', 0, 0, tiled=True, axis_index_groups=chips)  5.04 us
  transfers between devices with their start and end apart: 5, of which 4 were waited for; matrix products, arithmetic and copies ran while one was open for 0% of the time, Pallas kernels for 20%

profile of v6, /device:TPU:1, one launch (start us, length us, event | category | flops | bytes accessed | tf_op | source)
XLA Modules:
  0.0 98.8 jit_solution(1688681906709567174)
XLA Ops:
  0.0 0.0 copy-start.2
  0.0 4.4 %row_edges.1 = f32[2,8,8,8,128]{4,3,2,1,0:T(8,128)} custom-call(bf16[64,64,256]{2,1,0:T(8,128)(2,1)} %image_ref.3, f32[8,256]{1,0:T(8,128)} %vr_ref.3), custom_call_target="tpu_custom_call" | custom-call | tf_op jit(solution)/shard_map/row_edges/pallas_call | solution.py:239
  4.4 7.6 %all-to-all-start = ((f32[16,8,8,128]{3,2,1,0:T(8,128)}), f32[16,8,8,128]{3,2,1,0:T(8,128)S(1)}, u32[]{:S(2)}, u32[]{:S(2)}) async-start(f32[16,8,8,128]{3,2,1,0:T(8,128)} %bitcast.1), calls=%async_computation | async-start | bytes 1048576 | tf_op jit(solution)/shard_map/all_to_all | solution.py:363
  12.1 0.0 copy-done.2
  12.1 7.2 %vert_local.1.local_ref = f32[64,64,256]{2,1,0:T(8,128)} custom-call(bf16[64,64,256]{2,1,0:T(8,128)(2,1)} %image_ref.3, f32[8,256]{1,0:T(8,128)} %vr_ref.3, f32[8,256]{1,0:T(8,128)} %vc_ref.3), custom_call_target="tpu_custom_call" | custom-call | flops 5000000000 | bytes 8000000 | tf_op jit(solution)/shard_map/vert_local/pallas_call | solution.py:268
  19.3 0.0 copy-start.4
  19.3 0.0 copy-start.3
  19.3 0.0 copy-start.7
  19.3 3.2 %all-to-all-done.edge_ref = f32[16,8,8,128]{3,2,1,0:T(8,128)S(1)} async-done(((f32[16,8,8,128]{3,2,1,0:T(8,128)}), f32[16,8,8,128]{3,2,1,0:T(8,128)S(1)}, u32[]{:S(2)}, u32[]{:S(2)}) %all-to-all-start) | async-done | bytes 524320 | tf_op jit(solution)/shard_map/all_to_all | solution.py:363
  22.5 0.8 prefix.2
  23.4 3.6 %all-to-all-start.1 = ((f32[16,8,8,128]{3,2,1,0:T(8,128)}), f32[16,8,8,128]{3,2,1,0:T(8,128)S(1)}, u32[]{:S(2)}, u32[]{:S(2)}) async-start(f32[16,8,8,128]{3,2,1,0:T(8,128)} %prefix.2), calls=%async_computation.1 | async-start | bytes 1048576 | tf_op jit(solution)/shard_map/all_to_all | solution.py:368
  27.0 0.0 copy-done.4
  27.0 9.6 %all-to-all-done.1 = f32[16,8,8,128]{3,2,1,0:T(8,128)S(1)} async-done(((f32[16,8,8,128]{3,2,1,0:T(8,128)}), f32[16,8,8,128]{3,2,1,0:T(8,128)S(1)}, u32[]{:S(2)}, u32[]{:S(2)}) %all-to-all-start.1) | async-done | bytes 524320 | tf_op jit(solution)/shard_map/all_to_all | solution.py:368
  36.6 0.0 copy-done.3
  36.6 0.0 copy-done.7
  36.6 5.3 %act_and_edges.2 = (bf16[64,64,256]{2,1,0:T(8,128)(2,1)}, f32[8,8,8,128]{3,2,1,0:T(8,128)S(1)}) custom-call(s32[1]{0:T(128)} %bitcast.3.side_ref, f32[64,64,256]{2,1,0:T(8,128)} %vert_local.1.local_ref, f32[2,8,8,8,128]{4,3,2,1,0:T(8,128)S(1)} %bitcast.4, f32[8,256]{1,0:T(8,128)S(1)} %copy-done.3, f32[8,256]{1,0:T(8,128)S(1)} %copy-done.7, ...), custom_call_target="tpu_custom_call" | custom-call | flops 3000000000 | bytes 4000000 | tf_op jit(solution)/shard_map/act_and_edges/pallas_call | solution.py:294
  41.9 2.8 %collective-permute-start = (f32[8,8,8,128]{3,2,1,0:T(8,128)S(1)}, f32[8,8,8,128]{3,2,1,0:T(8,128)S(1)}, u32[]{:S(2)}, u32[]{:S(2)}) collective-permute-start(f32[8,8,8,128]{3,2,1,0:T(8,128)S(1)} %get-tuple-element.21), channel_id=1, source_target_pairs={{0,1},{1,0},{2,3},{3,2},{4,5},{5,4},{6,7},{7,6},{8,9},{9,8},{10,11... | collective-permute-start | bytes 786440 | tf_op jit(solution)/shard_map/ppermute | solution.py:349
  44.8 5.3 %act_and_edges.3 = (bf16[64,64,256]{2,1,0:T(8,128)(2,1)}, f32[8,8,8,128]{3,2,1,0:T(8,128)S(1)}) custom-call(s32[1]{0:T(128)} %bitcast.side_ref.core_ref.info_ref, f32[64,64,256]{2,1,0:T(8,128)} %vert_local.1.local_ref, f32[2,8,8,8,128]{4,3,2,1,0:T(8,128)S(1)} %bitcast.5, f32[8,256]{1,0:T(8,128)S(1)} %copy-done.3, ...), custom_call_target="tpu_custom_call", output_to_operand_aliasing={{0}: (6, {})} | custom-call | flops 3000000000 | bytes 4000000 | tf_op jit(solution)/shard_map/act_and_edges/pallas_call | solution.py:294
  50.1 0.0 collective-permute-done.came_ref
  50.1 0.8 join_cores.1
  50.8 8.2 %all-to-all-start.2 = ((f32[8,8,8,128]{3,2,1,0:T(8,128)}), f32[8,8,8,128]{3,2,1,0:T(8,128)S(1)}, u32[]{:S(2)}, u32[]{:S(2)}) async-start(f32[8,8,8,128]{3,2,1,0:T(8,128)} %get-tuple-element.22), calls=%async_computation.2 | async-start | bytes 524288 | tf_op jit(solution)/shard_map/all_to_all | solution.py:380
  59.0 0.0 copy-start
  59.0 0.0 copy-start.1
  59.0 0.0 copy-start.5
  59.0 0.0 copy-start.6
  59.1 7.3 %horiz_local.1.local_ref = f32[64,64,256]{2,1,0:T(8,128)} custom-call(bf16[64,64,256]{2,1,0:T(8,128)(2,1)} %get-tuple-element.23.image_ref, f32[8,256]{1,0:T(8,128)} %hr_ref.5, f32[8,256]{1,0:T(8,128)} %hc_ref.1), custom_call_target="tpu_custom_call" | custom-call | flops 5000000000 | bytes 8000000 | tf_op jit(solution)/shard_map/horiz_local/pallas_call | solution.py:268
  66.3 5.0 %all-to-all-done.2.edge_ref = f32[8,8,8,128]{3,2,1,0:T(8,128)S(1)} async-done(((f32[8,8,8,128]{3,2,1,0:T(8,128)}), f32[8,8,8,128]{3,2,1,0:T(8,128)S(1)}, u32[]{:S(2)}, u32[]{:S(2)}) %all-to-all-start.2) | async-done | bytes 262176 | tf_op jit(solution)/shard_map/all_to_all | solution.py:380
  71.4 14.7 %all_to_all.20.chain_ref = f32[8,8,8,128]{3,2,1,0:T(8,128)S(1)} all-to-all(f32[8,8,8,128]{3,2,1,0:T(8,128)S(1)} %prefix.3), channel_id=1, replica_groups={{0,2,4,6,8,10,12,14},{1,3,5,7,9,11,13,15},{16,18,20,22,24,26,28,30},{17..., dimensions={0} | all-to-all | bytes 524288 | tf_op jit(solution)/shard_map/all_to_all | solution.py:384
  86.1 0.1 part_cores.1
  86.1 0.7 collective-permute-start.1
  86.8 1.2 %collective-permute-done.1.got_ref = f32[8,8,8,128]{3,2,1,0:T(8,128)S(1)} collective-permute-done((f32[8,8,8,128]{3,2,1,0:T(8,128)S(1)}, f32[8,8,8,128]{3,2,1,0:T(8,128)S(1)}, u32[]{:S(2)}, u32[]{:S(2)}) %collective-permute-start.1) | collective-permute-done | bytes 262176 | tf_op jit(solution)/shard_map/ppermute | solution.py:349
  88.0 0.0 copy-done
  88.0 0.0 copy-done.1
  88.0 0.0 copy-done.5
  88.0 0.0 copy-done.6
  88.0 10.8 %mix.1 = bf16[64,64,256]{2,1,0:T(8,128)(2,1)} custom-call(s32[1]{0:T(128)} %bitcast.side_ref.core_ref.info_ref, f32[64,64,256]{2,1,0:T(8,128)} %horiz_local.1.local_ref, f32[8,8,8,128]{3,2,1,0:T(8,128)S(1)} %get-tuple-element.27.keep_ref, f32[8,8,8,128]{3,2,1,0:T(8,128)S(1)} %collective-permute-done.1.got_ref, f32[8,256]{1,0:T(8,128)S(1)} %copy-done.5, ...), custom_call_target="tpu_custom_call" | custom-call | tf_op jit(solution)/shard_map/mix/pallas_call | solution.py:326
  (3 shorter events, 0.0 us)
Async XLA Ops:
  0.0 12.1 %copy-start.2 = (f32[8,256]{1,0:T(8,128)S(1)}, f32[8,256]{1,0:T(8,128)}, u32[]{:S(2)}) copy-start(f32[8,256]{1,0:T(8,128)} %vr_ref.3) | copy-start | bytes 24580
  4.4 18.1 %all-to-all-start = ((f32[16,8,8,128]{3,2,1,0:T(8,128)}), f32[16,8,8,128]{3,2,1,0:T(8,128)S(1)}, u32[]{:S(2)}, u32[]{:S(2)}) async-start(f32[16,8,8,128]{3,2,1,0:T(8,128)} %bitcast.1), calls=%async_computation | async-start | bytes 1048576 | tf_op jit(solution)/shard_map/all_to_all | solution.py:363
  19.3 7.7 %copy-start.4 = (f32[8,256]{1,0:T(8,128)S(1)}, f32[8,256]{1,0:T(8,128)}, u32[]{:S(2)}) copy-start(f32[8,256]{1,0:T(8,128)} %hr_ref.5) | copy-start | bytes 24580
  19.3 17.3 %copy-start.3 = (f32[8,256]{1,0:T(8,128)S(1)}, f32[8,256]{1,0:T(8,128)}, u32[]{:S(2)}) copy-start(f32[8,256]{1,0:T(8,128)} %vr_ref.3) | copy-start | bytes 24580
  19.3 17.3 %copy-start.7 = (f32[8,256]{1,0:T(8,128)S(1)}, f32[8,256]{1,0:T(8,128)}, u32[]{:S(2)}) copy-start(f32[8,256]{1,0:T(8,128)} %vc_ref.3) | copy-start | bytes 24580
  23.4 13.2 %all-to-all-start.1 = ((f32[16,8,8,128]{3,2,1,0:T(8,128)}), f32[16,8,8,128]{3,2,1,0:T(8,128)S(1)}, u32[]{:S(2)}, u32[]{:S(2)}) async-start(f32[16,8,8,128]{3,2,1,0:T(8,128)} %prefix.2), calls=%async_computation.1 | async-start | bytes 1048576 | tf_op jit(solution)/shard_map/all_to_all | solution.py:368
  41.9 8.1 %collective-permute-start = (f32[8,8,8,128]{3,2,1,0:T(8,128)S(1)}, f32[8,8,8,128]{3,2,1,0:T(8,128)S(1)}, u32[]{:S(2)}, u32[]{:S(2)}) collective-permute-start(f32[8,8,8,128]{3,2,1,0:T(8,128)S(1)} %get-tuple-element.21), channel_id=1, source_target_pairs={{0,1},{1,0},{2,3},{3,2},{4,5},{5,4},{6,7},{7,6},{8,9},{9,8},{10,11... | collective-permute-start | bytes 786440 | tf_op jit(solution)/shard_map/ppermute | solution.py:349
  50.8 20.6 %all-to-all-start.2 = ((f32[8,8,8,128]{3,2,1,0:T(8,128)}), f32[8,8,8,128]{3,2,1,0:T(8,128)S(1)}, u32[]{:S(2)}, u32[]{:S(2)}) async-start(f32[8,8,8,128]{3,2,1,0:T(8,128)} %get-tuple-element.22), calls=%async_computation.2 | async-start | bytes 524288 | tf_op jit(solution)/shard_map/all_to_all | solution.py:380
  59.0 28.9 %copy-start = (bf16[256,1024]{1,0:T(8,128)(2,1)S(1)}, bf16[256,1024]{1,0:T(8,128)(2,1)}, u32[]{:S(2)}) copy-start(bf16[256,1024]{1,0:T(8,128)(2,1)} %w_in_ref.1) | copy-start | bytes 1572868
  59.0 28.9 %copy-start.1 = (bf16[1024,256]{1,0:T(8,128)(2,1)S(1)}, bf16[1024,256]{1,0:T(8,128)(2,1)}, u32[]{:S(2)}) copy-start(bf16[1024,256]{1,0:T(8,128)(2,1)} %w_out_ref.1) | copy-start | bytes 1572868
  59.0 28.9 %copy-start.5 = (f32[8,256]{1,0:T(8,128)S(1)}, f32[8,256]{1,0:T(8,128)}, u32[]{:S(2)}) copy-start(f32[8,256]{1,0:T(8,128)} %hr_ref.5) | copy-start | bytes 24580
  59.0 28.9 %copy-start.6 = (f32[8,256]{1,0:T(8,128)S(1)}, f32[8,256]{1,0:T(8,128)}, u32[]{:S(2)}) copy-start(f32[8,256]{1,0:T(8,128)} %hc_ref.1) | copy-start | bytes 24580
  86.1 1.8 %collective-permute-start.1 = (f32[8,8,8,128]{3,2,1,0:T(8,128)S(1)}, f32[8,8,8,128]{3,2,1,0:T(8,128)S(1)}, u32[]{:S(2)}, u32[]{:S(2)}) collective-permute-start(f32[8,8,8,128]{3,2,1,0:T(8,128)S(1)} %get-tuple-element.28), channel_id=1, source_target_pairs={{0,1},{1,0},{2,3},{3,2},{4,5},{5,4},{6,7},{7,6},{8,9},{9,8},{10,11... | collective-permute-start | bytes 786440 | tf_op jit(solution)/shard_map/ppermute | solution.py:349

commit v7 on v6

v7 whole, which is shorter than its diff:
```python
import functools
import math

import jax
import jax.numpy as jnp
from jax import lax
from jax.experimental import pallas as pl
from jax.experimental.pallas import tpu as pltpu
from jax.sharding import PartitionSpec as P

F32 = jnp.float32
BF16 = jnp.bfloat16
LANES = 128
MODES = 8
SQRT_2_PI = math.sqrt(2.0 / math.pi)
PITCH = 73
ACT_ROWS = 16
MIX_ROWS = 16


def gelu_of_half(x):
    inner = x * (2.0 * SQRT_2_PI + (8.0 * SQRT_2_PI * 0.044715) * (x * x))
    return x + x * jnp.tanh(inner)


def gelu_packed(x):
    x = x.astype(BF16)
    inner = x * (BF16(SQRT_2_PI) + BF16(SQRT_2_PI * 0.044715) * (x * x))
    half = BF16(0.5) * x
    return half + half * jnp.tanh(inner)


def poles(rate_ref, half, rows):
    lanes = slice(half * LANES, (half + 1) * LANES)
    return [
        jnp.broadcast_to(jnp.exp(-rate_ref[m : m + 1, lanes]), (rows, LANES)) for m in range(MODES)
    ]


def weights(rate_ref, coef_ref, half, rows):
    lanes = slice(half * LANES, (half + 1) * LANES)
    return [
        jnp.broadcast_to(
            coef_ref[m : m + 1, lanes] * jnp.sqrt(1.0 - jnp.exp(-2.0 * rate_ref[m : m + 1, lanes])),
            (rows, LANES),
        )
        for m in range(MODES)
    ]


def tree(terms):
    while len(terms) > 1:
        terms = [a + b for a, b in zip(terms[::2], terms[1::2])]
    return terms[0]


def edge_kernel(image_ref, rate_hbm_ref, edge_ref, image, rate_ref, arrived):
    def fetch(i):
        cols = pl.ds(pl.multiple_of(i * 16, 16), 16)
        return pltpu.make_async_copy(image_ref.at[:, cols, :], image.at[:, cols, :], arrived.at[i])

    rates = pltpu.make_async_copy(rate_hbm_ref, rate_ref, arrived.at[4])
    rates.start()
    for i in range(4):
        fetch(i).start()
    rates.wait()

    def chunk(i, _):
        fetch(i).wait()
        cols = pl.ds(pl.multiple_of(i * 16, 16), 16)
        for half in range(2):
            lanes = slice(half * LANES, (half + 1) * LANES)
            pole = poles(rate_ref, half, 16)

            def steps(j, states, lanes=lanes, pole=pole):
                for k in range(16):
                    u = image[j * 16 + k, cols, lanes].astype(F32)
                    states = [p * h + u for p, h in zip(pole, states)]
                return states

            states = lax.fori_loop(0, 4, steps, [jnp.zeros((16, LANES), F32)] * MODES)
            for m in range(MODES):
                edge_ref[half, pl.ds(i * 2, 2), m] = states[m].reshape(2, 8, LANES)
        return 0

    lax.fori_loop(0, 4, chunk, 0)


def prefix_kernel(span, edge_ref, rate_ref, out_ref):
    decay = [
        jnp.broadcast_to(jnp.exp(-span * rate_ref[m : m + 1, :]), (8, LANES)) for m in range(MODES)
    ]
    states = [jnp.zeros((8, LANES), F32)] * MODES
    for r in range(edge_ref.shape[0]):
        for m in range(MODES):
            out_ref[r, m] = states[m]
            states[m] = decay[m] * states[m] + edge_ref[r, m]


def local_kernel(scale, image_ref, rate_ref, coef_ref, out_ref):
    for half in range(2):
        lanes = slice(half * LANES, (half + 1) * LANES)
        pole = poles(rate_ref, half, 16)
        weight = [scale * q for q in weights(rate_ref, coef_ref, half, 16)]

        def steps(i, states, lanes=lanes, pole=pole, weight=weight):
            for k in range(8):
                s = i * 8 + k
                u = image_ref[s, :, lanes].astype(F32)
                states = [p * h + u for p, h in zip(pole, states)]
                out_ref[s, :, lanes] = tree([q * h for q, h in zip(weight, states)])
            return states

        lax.fori_loop(0, 8, steps, [jnp.zeros((16, LANES), F32)] * MODES)


def decays(rate_ref, span):
    return [jnp.broadcast_to(jnp.exp(-span * rate_ref[m : m + 1, :]), (8, LANES)) for m in range(MODES)]


def join_kernel(span, core_ref, mine_ref, came_ref, rate_ref, first_ref, joined_ref):
    left_here = core_ref[0] == 0
    decay = decays(rate_ref, span)
    for b in range(8):
        for m in range(MODES):
            mine, came = mine_ref[b, m], came_ref[b, m]
            first = jnp.where(left_here, mine, came)
            first_ref[b, m] = first
            joined_ref[b, m] = decay[m] * first + jnp.where(left_here, came, mine)


def part_kernel(span, core_ref, chain_ref, first_ref, rate_ref, keep_ref, send_ref):
    left_here = core_ref[0] == 0
    decay = decays(rate_ref, span)
    for b in range(8):
        for m in range(MODES):
            chain = chain_ref[b, m]
            after = decay[m] * chain + first_ref[b, m]
            keep_ref[b, m] = jnp.where(left_here, chain, after)
            send_ref[b, m] = jnp.where(left_here, after, chain)


def act_kernel(core_ref, local_ref, in_ref, vr_ref, vc_ref, hr_ref, act_ref, mine_ref, other_ref, tails, field):
    for half in range(2):
        lanes = slice(half * LANES, (half + 1) * LANES)
        pole = poles(vr_ref, half, 16)

        @pl.when(pl.program_id(0) == 0)
        def _(half=half, pole=pole):
            weight = weights(vr_ref, vc_ref, half, 16)
            for m in range(MODES):
                factor = (0.5 * pole[m] * weight[m])[None, :8]
                tails[half, :, m] = in_ref[half, :, m] * factor

        def block(b, _, half=half, lanes=lanes, pole=pole):
            pair = pl.ds(b * 2, 2)
            cols = pl.ds(pl.multiple_of(b * 16, 16), 16)
            tail = [tails[half, pair, m].reshape(16, LANES) for m in range(MODES)]
            for s in range(local_ref.shape[0]):
                y = local_ref[s, cols, lanes] + tree(tail)
                tail = [p * g for p, g in zip(pole, tail)]
                a = gelu_of_half(y).astype(BF16).astype(F32)
                field[half, pl.ds(s * PITCH + b * 16, 16), :] = a
            for m in range(MODES):
                tails[half, pair, m] = tail[m].reshape(2, 8, LANES)
            return 0

        lax.fori_loop(0, 4, block, 0)

    for half in range(2):
        lanes = slice(half * LANES, (half + 1) * LANES)
        pole = poles(hr_ref, half, 16)
        mine = core_ref[0] == half
        for r in range(0, local_ref.shape[0], 16):

            def steps(i, states, half=half, lanes=lanes, pole=pole, r=r):
                for k in range(16):
                    w = i * 16 + k
                    u = field[half, pl.ds(w + r * PITCH, 16, stride=PITCH), :]
                    act_ref[w, r : r + 16, lanes] = u.astype(BF16)
                    states = [p * h + u for p, h in zip(pole, states)]
                return states

            states = lax.fori_loop(0, 4, steps, [jnp.zeros((16, LANES), F32)] * MODES)

            @pl.when(mine)
            def _(states=states, r=r):
                for m in range(MODES):
                    mine_ref[r // 8 : r // 8 + 2, m] = states[m].reshape(2, 8, LANES)

            @pl.when(jnp.logical_not(mine))
            def _(states=states, r=r):
                for m in range(MODES):
                    other_ref[r // 8 : r // 8 + 2, m] = states[m].reshape(2, 8, LANES)


def mix_kernel(core_ref, local_ref, keep_ref, got_ref, hr_ref, hc_ref, w_in_ref, w_out_ref, out_ref, horiz, mixed):
    core = core_ref[0]
    rows = local_ref.shape[1]
    for r in range(0, rows, 16):
        pair = pl.ds(pl.program_id(0) * (rows // 8) + r // 8, 2)
        for half in range(2):
            lanes = slice(half * LANES, (half + 1) * LANES)
            pole = poles(hr_ref, half, 16)
            weight = weights(hr_ref, hc_ref, half, 16)
            mine = core == half
            tail = [
                jnp.where(mine, keep_ref[pair, m], got_ref[pair, m]).reshape(16, LANES)
                * (pole[m] * weight[m])
                for m in range(MODES)
            ]

            def steps(i, tail, lanes=lanes, pole=pole, r=r):
                for k in range(8):
                    w = i * 8 + k
                    y = local_ref[w, r : r + 16, lanes] + tree(tail)
                    tail = [p * g for p, g in zip(pole, tail)]
                    horiz[pl.ds(pl.multiple_of(w * 16, 16), 16), lanes] = y
                return tail

            lax.fori_loop(0, 8, steps, tail)

        y = horiz[...]
        scale = lax.rsqrt(jnp.mean(y * y, axis=-1, keepdims=True) + 1e-06)
        normed = (y * scale).astype(BF16)
        hidden = gelu_packed(jnp.dot(normed, w_in_ref[...], preferred_element_type=F32))
        out = y + jnp.dot(hidden, w_out_ref[...], preferred_element_type=F32)
        for w in range(64):
            for half in range(2):
                lanes = slice(half * LANES, (half + 1) * LANES)
                mixed[half, pl.ds(w, 16, stride=PITCH), :] = out[w * 16 : (w + 1) * 16, lanes]
        for half in range(2):
            lanes = slice(half * LANES, (half + 1) * LANES)
            for h in range(16):
                out_ref[r + h, :, lanes] = mixed[half, h * PITCH : h * PITCH + 64].astype(BF16)


def in_hbm(block):
    return pltpu.with_memory_space_constraint(block, pltpu.HBM)


def whole(shape):
    return pl.BlockSpec(shape, lambda i: (0,) * len(shape))


def params(mib):
    return pltpu.CompilerParams(vmem_limit_bytes=mib * 1024 * 1024)


VMEM = pl.BlockSpec(memory_space=pltpu.VMEM)
HBM = pl.BlockSpec(memory_space=pltpu.HBM)
SMEM = pl.BlockSpec(memory_space=pltpu.SMEM)


def row_edges(image, rate):
    return pl.pallas_call(
        edge_kernel,
        in_specs=[HBM, HBM],
        out_specs=VMEM,
        out_shape=jax.ShapeDtypeStruct((2, 8, 8, 8, LANES), F32),
        scratch_shapes=[
            pltpu.VMEM((64, 64, 256), BF16),
            pltpu.VMEM((8, 256), F32),
            pltpu.SemaphoreType.DMA((5,)),
        ],
        compiler_params=params(24),
        name="row_edges",
    )(in_hbm(image), in_hbm(rate))


def prefix(edges, rate, span):
    def kernel(edge_ref, rate_ref, out_ref):
        prefix_kernel(span, edge_ref, rate_ref, out_ref)

    return pl.pallas_call(
        kernel,
        out_shape=jax.ShapeDtypeStruct(edges.shape, F32),
        compiler_params=params(8),
        name="prefix",
    )(edges, rate)


def local_scan(block, rate, coef, name, scale):
    place = pl.BlockSpec((64, 16, 256), lambda i: (0, i, 0))
    return pl.pallas_call(
        functools.partial(local_kernel, scale),
        grid=(4,),
        in_specs=[place, whole((8, 256)), whole((8, 256))],
        out_specs=place,
        out_shape=pltpu.HBM((64, 64, 256), F32),
        compiler_params=params(56),
        cost_estimate=pl.CostEstimate(flops=5_000_000_000, bytes_accessed=8_000_000, transcendentals=0),
        name=name,
    )(block, rate, coef)


def small(kernel, name, outs, *operands):
    return pl.pallas_call(
        kernel,
        in_specs=[SMEM] + [VMEM] * (len(operands) - 1),
        out_specs=[VMEM] * len(outs),
        out_shape=[jax.ShapeDtypeStruct(shape, F32) for shape in outs],
        compiler_params=params(8),
        name=name,
    )(*operands)


def act_and_edges(core, local, incoming, vert_rate, vert_coef, horiz_rate):
    edge = pl.BlockSpec((ACT_ROWS // 8, 8, 8, LANES), lambda i: (i, 0, 0, 0))
    return pl.pallas_call(
        act_kernel,
        grid=(64 // ACT_ROWS,),
        in_specs=[SMEM, pl.BlockSpec((ACT_ROWS, 64, 256), lambda i: (i, 0, 0)), VMEM, VMEM, VMEM, VMEM],
        out_specs=[pl.BlockSpec((64, ACT_ROWS, 256), lambda i: (0, i, 0)), edge, edge],
        out_shape=[pltpu.HBM((64, 64, 256), BF16)] + [jax.ShapeDtypeStruct((8, 8, 8, LANES), F32)] * 2,
        scratch_shapes=[
            pltpu.VMEM((2, 8, 8, 8, LANES), F32),
            pltpu.VMEM((2, ACT_ROWS * PITCH, LANES), F32),
        ],
        compiler_params=params(24),
        name="act_and_edges",
    )(core, in_hbm(local), incoming, vert_rate, vert_coef, horiz_rate)


def mix(core, local, keep, got, horiz_rate, horiz_coef, w_in, w_out):
    return pl.pallas_call(
        mix_kernel,
        grid=(64 // MIX_ROWS,),
        in_specs=[SMEM, pl.BlockSpec((64, MIX_ROWS, 256), lambda i: (0, i, 0))] + [VMEM] * 6,
        out_specs=pl.BlockSpec((MIX_ROWS, 64, 256), lambda i: (i, 0, 0)),
        out_shape=jax.ShapeDtypeStruct((64, 64, 256), BF16),
        scratch_shapes=[pltpu.VMEM((1024, 256), F32), pltpu.VMEM((2, 16 * PITCH, LANES), F32)],
        compiler_params=params(40),
        name="mix",
    )(core, in_hbm(local), keep, got, horiz_rate, horiz_coef, w_in, w_out)


def swap(block, bits):
    n = lax.axis_size("col")
    return lax.ppermute(block, "col", [(i, i ^ bits) for i in range(n)])


def together(arrived, local):
    return lax.optimization_barrier((arrived, local))


def on_device(image, vert_rate, vert_coef, horiz_rate, horiz_coef, w_in, w_out):
    rows, cols = lax.axis_size("row"), lax.axis_size("col")
    piece = lax.axis_index("row")
    core = (lax.axis_index("col") % 2).reshape(1)

    edges = row_edges(image, vert_rate).reshape(rows, 8, 8, LANES)
    edges = lax.all_to_all(edges, "row", 0, 0, tiled=True)
    rate = lax.dynamic_slice_in_dim(vert_rate, (piece // 8) * LANES, LANES, 1)
    local = local_scan(image, vert_rate, vert_coef, "vert_local", 0.5)
    edges, local = together(edges, local)
    incoming = prefix(edges, rate, 64.0)
    incoming = lax.all_to_all(incoming, "row", 0, 0, tiled=True).reshape(2, 8, 8, 8, LANES)

    act, edge, other = act_and_edges(core, local, incoming, vert_rate, vert_coef, horiz_rate)

    chips = [[2 * z + c for z in range(cols // 2)] for c in range(2)]
    rate = lax.dynamic_slice_in_dim(horiz_rate, core[0] * LANES, LANES, 1)
    tile = [(8, 8, 8, LANES)] * 2
    join = functools.partial(join_kernel, 64.0)
    first, joined = small(join, "join_cores", tile, core, edge, swap(other, 1), rate)
    joined = lax.all_to_all(joined, "col", 0, 0, tiled=True, axis_index_groups=chips)
    local = local_scan(act, horiz_rate, horiz_coef, "horiz_local", 1.0)
    joined, local = together(joined, local)
    chain = prefix(joined, rate, 128.0)
    chain = lax.all_to_all(chain, "col", 0, 0, tiled=True, axis_index_groups=chips)
    part = functools.partial(part_kernel, 64.0)
    keep, send = small(part, "part_cores", tile, core, chain, first, rate)
    got = swap(send, 1)

    return mix(core, local, keep, got, horiz_rate, horiz_coef, w_in, w_out)


def solution(mesh):
    placed = (P("row", "col", None), P(), P(), P(), P(), P(), P())
    return jax.shard_map(
        on_device, mesh=mesh, in_specs=placed, out_specs=P("row", "col", None), check_vma=False
    )
```

time: 99.5 us -> 97.4 us (0.979)
  Pallas kernels: 42 us -> 39.9 us
  starting transfers between devices: 22.8 us -> 24.9 us
  blocking collectives: 14.7 us -> 12.9 us
    pallas_call x5 -> x4, Pallas kernels: 35.9 us -> 33.8 us  [the longest x2 14.6 us: local_scan(): pl.pallas_call(functools.partial(local_kernel, scale), grid=(4,), in_spec...]
    ppermute x2, starting transfers between devices: 3.49 us -> 5.58 us  [swap(): return lax.ppermute(block, 'col', [(i, i ^ bits) for i in range(n)])]
    all_to_all x1, blocking collectives: 14.7 us -> 12.9 us  [on_device(): lax.all_to_all(chain, 'col', 0, 0, tiled=True, axis_index_groups=chips)]
    all_to_all x1, waiting for transfers between devices: 5.04 us -> 3.75 us  [on_device(): lax.all_to_all(joined, 'col', 0, 0, tiled=True, axis_index_groups=chips)]
    ppermute x2, waiting for transfers between devices: 1.16 us -> 2.32 us  [swap(): return lax.ppermute(block, 'col', [(i, i ^ bits) for i in range(n)])]
  transfers between devices with their start and end apart: 5 -> 5, of which waited for: 4 -> 5; matrix products, arithmetic and copies ran while one was open for 0% -> 0% of each run, Pallas kernels for 20% -> 15%
where the time goes in v7:
time: 97.4 us; the launch traced here: 96.8 us
  Pallas kernels  39.9 us (41%)
  starting transfers between devices  24.9 us (26%)
  waiting for transfers between devices  18.9 us (19%)
  blocking collectives  12.9 us (13%)
    pallas_call x2, Pallas kernels, local_scan(): pl.pallas_call(functools.partial(local_kernel, scale), grid=(4,), in_spec...  14.6 us
    all_to_all x1, blocking collectives, on_device(): lax.all_to_all(chain, 'col', 0, 0, tiled=True, axis_index_groups=chips)  12.9 us
    pallas_call x1, Pallas kernels, mix(): pl.pallas_call(mix_kernel, grid=(64 // MIX_ROWS,), in_specs=[SMEM, pl.Blo...  10.7 us
    all_to_all x1, waiting for transfers between devices, on_device(): lax.all_to_all(incoming, 'row', 0, 0, tiled=True).reshape(2, 8, 8, 8, LANES)  9.65 us
    pallas_call x1, Pallas kernels, act_and_edges(): pl.pallas_call(act_kernel, grid=(64 // ACT_ROWS,), in_specs=[SMEM, pl.Blo...  8.52 us
    all_to_all x1, starting transfers between devices, on_device(): lax.all_to_all(joined, 'col', 0, 0, tiled=True, axis_index_groups=chips)  8.19 us
    all_to_all x1, starting transfers between devices, on_device(): edges = lax.all_to_all(edges, 'row', 0, 0, tiled=True)  7.6 us
    ppermute x2, starting transfers between devices, swap(): return lax.ppermute(block, 'col', [(i, i ^ bits) for i in range(n)])  5.58 us
  transfers between devices with their start and end apart: 5, of which 5 were waited for; matrix products, arithmetic and copies ran while one was open for 0% of the time, Pallas kernels for 15%

profile of v7, /device:TPU:1, one launch (start us, length us, event | category | flops | bytes accessed | tf_op | source)
XLA Modules:
  0.0 96.8 jit_solution(11428315364985336051)
XLA Ops:
  0.0 0.0 copy-start.2
  0.0 4.4 %row_edges.1 = f32[2,8,8,8,128]{4,3,2,1,0:T(8,128)} custom-call(bf16[64,64,256]{2,1,0:T(8,128)(2,1)} %image_ref.3, f32[8,256]{1,0:T(8,128)} %vr_ref.1), custom_call_target="tpu_custom_call" | custom-call | tf_op jit(solution)/shard_map/row_edges/pallas_call | solution.py:256
  4.4 7.6 %all-to-all-start = ((f32[16,8,8,128]{3,2,1,0:T(8,128)}), f32[16,8,8,128]{3,2,1,0:T(8,128)S(1)}, u32[]{:S(2)}, u32[]{:S(2)}) async-start(f32[16,8,8,128]{3,2,1,0:T(8,128)} %bitcast.1), calls=%async_computation | async-start | bytes 1048576 | tf_op jit(solution)/shard_map/all_to_all | solution.py:353
  12.1 0.0 copy-done.2
  12.1 7.3 %vert_local.1.local_ref = f32[64,64,256]{2,1,0:T(8,128)} custom-call(bf16[64,64,256]{2,1,0:T(8,128)(2,1)} %image_ref.3, f32[8,256]{1,0:T(8,128)} %vr_ref.1, f32[8,256]{1,0:T(8,128)} %vc_ref.1), custom_call_target="tpu_custom_call" | custom-call | flops 5000000000 | bytes 8000000 | tf_op jit(solution)/shard_map/vert_local/pallas_call | solution.py:285
  19.4 0.0 copy-start.3
  19.4 0.0 copy-start.4
  19.4 0.0 copy-start.6
  19.4 3.2 %all-to-all-done.edge_ref = f32[16,8,8,128]{3,2,1,0:T(8,128)S(1)} async-done(((f32[16,8,8,128]{3,2,1,0:T(8,128)}), f32[16,8,8,128]{3,2,1,0:T(8,128)S(1)}, u32[]{:S(2)}, u32[]{:S(2)}) %all-to-all-start) | async-done | bytes 524320 | tf_op jit(solution)/shard_map/all_to_all | solution.py:353
  22.5 0.8 prefix.2
  23.4 3.6 %all-to-all-start.1 = ((f32[16,8,8,128]{3,2,1,0:T(8,128)}), f32[16,8,8,128]{3,2,1,0:T(8,128)S(1)}, u32[]{:S(2)}, u32[]{:S(2)}) async-start(f32[16,8,8,128]{3,2,1,0:T(8,128)} %prefix.2), calls=%async_computation.1 | async-start | bytes 1048576 | tf_op jit(solution)/shard_map/all_to_all | solution.py:358
  27.0 9.7 %all-to-all-done.1 = f32[16,8,8,128]{3,2,1,0:T(8,128)S(1)} async-done(((f32[16,8,8,128]{3,2,1,0:T(8,128)}), f32[16,8,8,128]{3,2,1,0:T(8,128)S(1)}, u32[]{:S(2)}, u32[]{:S(2)}) %all-to-all-start.1) | async-done | bytes 524320 | tf_op jit(solution)/shard_map/all_to_all | solution.py:358
  36.6 0.0 copy-done.3
  36.6 0.0 copy-done.4
  36.6 0.0 copy-done.6
  36.6 8.5 %act_and_edges.1 = (bf16[64,64,256]{2,1,0:T(8,128)(2,1)}, f32[8,8,8,128]{3,2,1,0:T(8,128)S(1)}, f32[8,8,8,128]{3,2,1,0:T(8,128)S(1)}) custom-call(s32[1]{0:T(128)} %bitcast.core_ref, f32[64,64,256]{2,1,0:T(8,128)} %vert_local.1.local_ref, f32[2,8,8,8,128]{4,3,2,1,0:T(8,128)S(1)} %bitcast.3, f32[8,256]{1,0:T(8,128)S(1)} %copy-done.3, f32[8,256]{1,0:T(8,128)S(1)} %copy-done.6, ...), custom_call_target="tpu_custom_call" | custom-call | tf_op jit(solution)/shard_map/act_and_edges/pallas_call | solution.py:310
  45.2 2.8 %collective-permute-start = (f32[8,8,8,128]{3,2,1,0:T(8,128)S(1)}, f32[8,8,8,128]{3,2,1,0:T(8,128)S(1)}, u32[]{:S(2)}, u32[]{:S(2)}) collective-permute-start(f32[8,8,8,128]{3,2,1,0:T(8,128)S(1)} %get-tuple-element.19), channel_id=1, source_target_pairs={{0,1},{1,0},{2,3},{3,2},{4,5},{5,4},{6,7},{7,6},{8,9},{9,8},{10,11... | collective-permute-start | bytes 786440 | tf_op jit(solution)/shard_map/ppermute | solution.py:340
  48.0 1.2 %collective-permute-done.came_ref = f32[8,8,8,128]{3,2,1,0:T(8,128)S(1)} collective-permute-done((f32[8,8,8,128]{3,2,1,0:T(8,128)S(1)}, f32[8,8,8,128]{3,2,1,0:T(8,128)S(1)}, u32[]{:S(2)}, u32[]{:S(2)}) %collective-permute-start) | collective-permute-done | bytes 262176 | tf_op jit(solution)/shard_map/ppermute | solution.py:340
  49.2 0.8 join_cores.1
  49.9 8.2 %all-to-all-start.2 = ((f32[8,8,8,128]{3,2,1,0:T(8,128)}), f32[8,8,8,128]{3,2,1,0:T(8,128)S(1)}, u32[]{:S(2)}, u32[]{:S(2)}) async-start(f32[8,8,8,128]{3,2,1,0:T(8,128)} %get-tuple-element.20), calls=%async_computation.2 | async-start | bytes 524288 | tf_op jit(solution)/shard_map/all_to_all | solution.py:367
  58.1 0.0 copy-start
  58.1 0.0 copy-start.1
  58.1 0.0 copy-start.5
  58.1 0.0 copy-start.7
  58.1 7.3 %horiz_local.1.local_ref = f32[64,64,256]{2,1,0:T(8,128)} custom-call(bf16[64,64,256]{2,1,0:T(8,128)(2,1)} %get-tuple-element.21.image_ref, f32[8,256]{1,0:T(8,128)} %hr_ref.3, f32[8,256]{1,0:T(8,128)} %hc_ref.1), custom_call_target="tpu_custom_call" | custom-call | flops 5000000000 | bytes 8000000 | tf_op jit(solution)/shard_map/horiz_local/pallas_call | solution.py:285
  65.4 3.7 %all-to-all-done.2.edge_ref = f32[8,8,8,128]{3,2,1,0:T(8,128)S(1)} async-done(((f32[8,8,8,128]{3,2,1,0:T(8,128)}), f32[8,8,8,128]{3,2,1,0:T(8,128)S(1)}, u32[]{:S(2)}, u32[]{:S(2)}) %all-to-all-start.2) | async-done | bytes 262176 | tf_op jit(solution)/shard_map/all_to_all | solution.py:367
  69.2 12.9 %all_to_all.20.chain_ref = f32[8,8,8,128]{3,2,1,0:T(8,128)S(1)} all-to-all(f32[8,8,8,128]{3,2,1,0:T(8,128)S(1)} %prefix.3), channel_id=1, replica_groups={{0,2,4,6,8,10,12,14},{1,3,5,7,9,11,13,15},{16,18,20,22,24,26,28,30},{17..., dimensions={0} | all-to-all | bytes 524288 | tf_op jit(solution)/shard_map/all_to_all | solution.py:371
  82.1 0.1 part_cores.1
  82.1 2.7 %collective-permute-start.1 = (f32[8,8,8,128]{3,2,1,0:T(8,128)S(1)}, f32[8,8,8,128]{3,2,1,0:T(8,128)S(1)}, u32[]{:S(2)}, u32[]{:S(2)}) collective-permute-start(f32[8,8,8,128]{3,2,1,0:T(8,128)S(1)} %get-tuple-element.26), channel_id=1, source_target_pairs={{0,1},{1,0},{2,3},{3,2},{4,5},{5,4},{6,7},{7,6},{8,9},{9,8},{10,11... | collective-permute-start | bytes 786440 | tf_op jit(solution)/shard_map/ppermute | solution.py:340
  84.9 1.2 %collective-permute-done.1.got_ref = f32[8,8,8,128]{3,2,1,0:T(8,128)S(1)} collective-permute-done((f32[8,8,8,128]{3,2,1,0:T(8,128)S(1)}, f32[8,8,8,128]{3,2,1,0:T(8,128)S(1)}, u32[]{:S(2)}, u32[]{:S(2)}) %collective-permute-start.1) | collective-permute-done | bytes 262176 | tf_op jit(solution)/shard_map/ppermute | solution.py:340
  86.0 0.0 copy-done
  86.1 0.0 copy-done.1
  86.1 0.0 copy-done.5
  86.1 0.0 copy-done.7
  86.1 10.7 %mix.1 = bf16[64,64,256]{2,1,0:T(8,128)(2,1)} custom-call(s32[1]{0:T(128)} %bitcast.core_ref, f32[64,64,256]{2,1,0:T(8,128)} %horiz_local.1.local_ref, f32[8,8,8,128]{3,2,1,0:T(8,128)S(1)} %get-tuple-element.25.keep_ref, f32[8,8,8,128]{3,2,1,0:T(8,128)S(1)} %collective-permute-done.1.got_ref, f32[8,256]{1,0:T(8,128)S(1)} %copy-done.5, ...), custom_call_target="tpu_custom_call" | custom-call | tf_op jit(solution)/shard_map/mix/pallas_call | solution.py:326
  (3 shorter events, 0.0 us)
Async XLA Ops:
  0.0 12.1 %copy-start.2 = (f32[8,256]{1,0:T(8,128)S(1)}, f32[8,256]{1,0:T(8,128)}, u32[]{:S(2)}) copy-start(f32[8,256]{1,0:T(8,128)} %vr_ref.1) | copy-start | bytes 24580
  4.4 18.1 %all-to-all-start = ((f32[16,8,8,128]{3,2,1,0:T(8,128)}), f32[16,8,8,128]{3,2,1,0:T(8,128)S(1)}, u32[]{:S(2)}, u32[]{:S(2)}) async-start(f32[16,8,8,128]{3,2,1,0:T(8,128)} %bitcast.1), calls=%async_computation | async-start | bytes 1048576 | tf_op jit(solution)/shard_map/all_to_all | solution.py:353
  19.4 17.3 %copy-start.3 = (f32[8,256]{1,0:T(8,128)S(1)}, f32[8,256]{1,0:T(8,128)}, u32[]{:S(2)}) copy-start(f32[8,256]{1,0:T(8,128)} %vr_ref.1) | copy-start | bytes 24580
  19.4 17.3 %copy-start.4 = (f32[8,256]{1,0:T(8,128)S(1)}, f32[8,256]{1,0:T(8,128)}, u32[]{:S(2)}) copy-start(f32[8,256]{1,0:T(8,128)} %hr_ref.3) | copy-start | bytes 24580
  19.4 17.3 %copy-start.6 = (f32[8,256]{1,0:T(8,128)S(1)}, f32[8,256]{1,0:T(8,128)}, u32[]{:S(2)}) copy-start(f32[8,256]{1,0:T(8,128)} %vc_ref.1) | copy-start | bytes 24580
  23.4 13.2 %all-to-all-start.1 = ((f32[16,8,8,128]{3,2,1,0:T(8,128)}), f32[16,8,8,128]{3,2,1,0:T(8,128)S(1)}, u32[]{:S(2)}, u32[]{:S(2)}) async-start(f32[16,8,8,128]{3,2,1,0:T(8,128)} %prefix.2), calls=%async_computation.1 | async-start | bytes 1048576 | tf_op jit(solution)/shard_map/all_to_all | solution.py:358
  45.2 4.0 %collective-permute-start = (f32[8,8,8,128]{3,2,1,0:T(8,128)S(1)}, f32[8,8,8,128]{3,2,1,0:T(8,128)S(1)}, u32[]{:S(2)}, u32[]{:S(2)}) collective-permute-start(f32[8,8,8,128]{3,2,1,0:T(8,128)S(1)} %get-tuple-element.19), channel_id=1, source_target_pairs={{0,1},{1,0},{2,3},{3,2},{4,5},{5,4},{6,7},{7,6},{8,9},{9,8},{10,11... | collective-permute-start | bytes 786440 | tf_op jit(solution)/shard_map/ppermute | solution.py:340
  49.9 19.3 %all-to-all-start.2 = ((f32[8,8,8,128]{3,2,1,0:T(8,128)}), f32[8,8,8,128]{3,2,1,0:T(8,128)S(1)}, u32[]{:S(2)}, u32[]{:S(2)}) async-start(f32[8,8,8,128]{3,2,1,0:T(8,128)} %get-tuple-element.20), calls=%async_computation.2 | async-start | bytes 524288 | tf_op jit(solution)/shard_map/all_to_all | solution.py:367
  58.1 27.9 %copy-start = (bf16[256,1024]{1,0:T(8,128)(2,1)S(1)}, bf16[256,1024]{1,0:T(8,128)(2,1)}, u32[]{:S(2)}) copy-start(bf16[256,1024]{1,0:T(8,128)(2,1)} %w_in_ref.1) | copy-start | bytes 1572868
  58.1 27.9 %copy-start.1 = (bf16[1024,256]{1,0:T(8,128)(2,1)S(1)}, bf16[1024,256]{1,0:T(8,128)(2,1)}, u32[]{:S(2)}) copy-start(bf16[1024,256]{1,0:T(8,128)(2,1)} %w_out_ref.1) | copy-start | bytes 1572868
  58.1 27.9 %copy-start.5 = (f32[8,256]{1,0:T(8,128)S(1)}, f32[8,256]{1,0:T(8,128)}, u32[]{:S(2)}) copy-start(f32[8,256]{1,0:T(8,128)} %hr_ref.3) | copy-start | bytes 24580
  58.1 27.9 %copy-start.7 = (f32[8,256]{1,0:T(8,128)S(1)}, f32[8,256]{1,0:T(8,128)}, u32[]{:S(2)}) copy-start(f32[8,256]{1,0:T(8,128)} %hc_ref.1) | copy-start | bytes 24580
  82.1 3.9 %collective-permute-start.1 = (f32[8,8,8,128]{3,2,1,0:T(8,128)S(1)}, f32[8,8,8,128]{3,2,1,0:T(8,128)S(1)}, u32[]{:S(2)}, u32[]{:S(2)}) collective-permute-start(f32[8,8,8,128]{3,2,1,0:T(8,128)S(1)} %get-tuple-element.26), channel_id=1, source_target_pairs={{0,1},{1,0},{2,3},{3,2},{4,5},{5,4},{6,7},{7,6},{8,9},{9,8},{10,11... | collective-permute-start | bytes 786440 | tf_op jit(solution)/shard_map/ppermute | solution.py:340

commit v8 on v7

--- a/solution.py
+++ b/solution.py
@@ -97,21 +97,41 @@
             states[m] = decay[m] * states[m] + edge_ref[r, m]
 
 
-def local_kernel(scale, image_ref, rate_ref, coef_ref, out_ref):
-    for half in range(2):
-        lanes = slice(half * LANES, (half + 1) * LANES)
-        pole = poles(rate_ref, half, 16)
-        weight = [scale * q for q in weights(rate_ref, coef_ref, half, 16)]
-
-        def steps(i, states, lanes=lanes, pole=pole, weight=weight):
-            for k in range(8):
-                s = i * 8 + k
-                u = image_ref[s, :, lanes].astype(F32)
-                states = [p * h + u for p, h in zip(pole, states)]
-                out_ref[s, :, lanes] = tree([q * h for q, h in zip(weight, states)])
-            return states
-
-        lax.fori_loop(0, 8, steps, [jnp.zeros((16, LANES), F32)] * MODES)
+def local_kernel(scale, block_ref, rate_ref, coef_ref, out_ref, block, result, arrived, left):
+    def part(i):
+        return pl.ds(pl.multiple_of(i * 16, 16), 16)
+
+    def fetch(i):
+        return pltpu.make_async_copy(block_ref.at[:, part(i), :], block.at[:, part(i), :], arrived.at[i])
+
+    def put(i):
+        return pltpu.make_async_copy(result.at[:, part(i), :], out_ref.at[:, part(i), :], left.at[i])
+
+    for i in range(4):
+        fetch(i).start()
+
+    def chunk(i, _):
+        fetch(i).wait()
+        for half in range(2):
+            lanes = slice(half * LANES, (half + 1) * LANES)
+            pole = poles(rate_ref, half, 16)
+            weight = [scale * q for q in weights(rate_ref, coef_ref, half, 16)]
+
+            def steps(j, states, lanes=lanes, pole=pole, weight=weight):
+                for k in range(16):
+                    s = j * 16 + k
+                    u = block[s, part(i), lanes].astype(F32)
+                    states = [p * h + u for p, h in zip(pole, states)]
+                    result[s, part(i), lanes] = tree([q * h for q, h in zip(weight, states)])
+                return states
+
+            lax.fori_loop(0, 4, steps, [jnp.zeros((16, LANES), F32)] * MODES)
+        put(i).start()
+        return 0
+
+    lax.fori_loop(0, 4, chunk, 0)
+    for i in range(4):
+        put(i).wait()
 
 
 def decays(rate_ref, span):
@@ -281,17 +301,21 @@
 
 
 def local_scan(block, rate, coef, name, scale):
-    place = pl.BlockSpec((64, 16, 256), lambda i: (0, i, 0))
     return pl.pallas_call(
         functools.partial(local_kernel, scale),
-        grid=(4,),
-        in_specs=[place, whole((8, 256)), whole((8, 256))],
-        out_specs=place,
+        in_specs=[HBM, VMEM, VMEM],
+        out_specs=HBM,
         out_shape=pltpu.HBM((64, 64, 256), F32),
-        compiler_params=params(56),
+        scratch_shapes=[
+            pltpu.VMEM((64, 64, 256), BF16),
+            pltpu.VMEM((64, 64, 256), F32),
+            pltpu.SemaphoreType.DMA((4,)),
+            pltpu.SemaphoreType.DMA((4,)),
+        ],
+        compiler_params=params(24),
         cost_estimate=pl.CostEstimate(flops=5_000_000_000, bytes_accessed=8_000_000, transcendentals=0),
         name=name,
-    )(block, rate, coef)
+    )(in_hbm(block), rate, coef)
 
 
 def small(kernel, name, outs, *operands):
@@ -348,29 +372,29 @@
     rows, cols = lax.axis_size("row"), lax.axis_size("col")
     piece = lax.axis_index("row")
     core = (lax.axis_index("col") % 2).reshape(1)
+    rate_along = lax.dynamic_slice_in_dim(horiz_rate, core[0] * LANES, LANES, 1)
 
     edges = row_edges(image, vert_rate).reshape(rows, 8, 8, LANES)
     edges = lax.all_to_all(edges, "row", 0, 0, tiled=True)
     rate = lax.dynamic_slice_in_dim(vert_rate, (piece // 8) * LANES, LANES, 1)
     local = local_scan(image, vert_rate, vert_coef, "vert_local", 0.5)
-    edges, local = together(edges, local)
+    edges, local, core, rate_along = lax.optimization_barrier((edges, local, core, rate_along))
     incoming = prefix(edges, rate, 64.0)
     incoming = lax.all_to_all(incoming, "row", 0, 0, tiled=True).reshape(2, 8, 8, 8, LANES)
 
     act, edge, other = act_and_edges(core, local, incoming, vert_rate, vert_coef, horiz_rate)
 
     chips = [[2 * z + c for z in range(cols // 2)] for c in range(2)]
-    rate = lax.dynamic_slice_in_dim(horiz_rate, core[0] * LANES, LANES, 1)
     tile = [(8, 8, 8, LANES)] * 2
     join = functools.partial(join_kernel, 64.0)
-    first, joined = small(join, "join_cores", tile, core, edge, swap(other, 1), rate)
+    first, joined = small(join, "join_cores", tile, core, edge, swap(other, 1), rate_along)
     joined = lax.all_to_all(joined, "col", 0, 0, tiled=True, axis_index_groups=chips)
     local = local_scan(act, horiz_rate, horiz_coef, "horiz_local", 1.0)
     joined, local = together(joined, local)
-    chain = prefix(joined, rate, 128.0)
+    chain = prefix(joined, rate_along, 128.0)
     chain = lax.all_to_all(chain, "col", 0, 0, tiled=True, axis_index_groups=chips)
     part = functools.partial(part_kernel, 64.0)
-    keep, send = small(part, "part_cores", tile, core, chain, first, rate)
+    keep, send = small(part, "part_cores", tile, core, chain, first, rate_along)
     got = swap(send, 1)
 
     return mix(core, local, keep, got, horiz_rate, horiz_coef, w_in, w_out)

time: 97.4 us -> 95.7 us (0.983)
  blocking collectives: 12.9 us -> 25.2 us
  waiting for transfers between devices: 18.9 us -> 10 us
  starting transfers between devices: 24.9 us -> 21.6 us
  Pallas kernels: 39.9 us -> 38.3 us
    all_to_all x0 -> x1, blocking collectives: none -> 13.1 us  [on_device(): lax.all_to_all(incoming, 'row', 0, 0, tiled=True).reshape(2, 8, 8, 8, LANES)]
    all_to_all x1 -> x0, waiting for transfers between devices: 9.65 us -> none  [on_device(): lax.all_to_all(incoming, 'row', 0, 0, tiled=True).reshape(2, 8, 8, 8, LANES)]
    all_to_all x1 -> x0, starting transfers between devices: 3.57 us -> none  [on_device(): lax.all_to_all(incoming, 'row', 0, 0, tiled=True).reshape(2, 8, 8, 8, LANES)]
  transfers between devices with their start and end apart: 5 -> 4, of which waited for: 5 -> 4; matrix products, arithmetic and copies ran while one was open for 0% -> 0% of each run, Pallas kernels for 15% -> 14%
where the time goes in v8:
time: 95.7 us; the launch traced here: 95.3 us
  Pallas kernels  38.3 us (40%)
  blocking collectives  25.2 us (26%)
  starting transfers between devices  21.6 us (23%)
  waiting for transfers between devices  10 us (10%)
    pallas_call x2, Pallas kernels, local_scan(): pl.pallas_call(functools.partial(local_kernel, scale), in_specs=[HBM, VME...  13.8 us
    all_to_all x1, blocking collectives, on_device(): lax.all_to_all(incoming, 'row', 0, 0, tiled=True).reshape(2, 8, 8, 8, LANES)  13.1 us
    all_to_all x1, blocking collectives, on_device(): lax.all_to_all(chain, 'col', 0, 0, tiled=True, axis_index_groups=chips)  12.1 us
    pallas_call x1, Pallas kernels, mix(): pl.pallas_call(mix_kernel, grid=(64 // MIX_ROWS,), in_specs=[SMEM, pl.Blo...  10.7 us
    pallas_call x1, Pallas kernels, act_and_edges(): pl.pallas_call(act_kernel, grid=(64 // ACT_ROWS,), in_specs=[SMEM, pl.Blo...  8.52 us
    all_to_all x1, starting transfers between devices, on_device(): lax.all_to_all(joined, 'col', 0, 0, tiled=True, axis_index_groups=chips)  8.19 us
    all_to_all x1, starting transfers between devices, on_device(): edges = lax.all_to_all(edges, 'row', 0, 0, tiled=True)  7.6 us
    ppermute x2, starting transfers between devices, swap(): return lax.ppermute(block, 'col', [(i, i ^ bits) for i in range(n)])  5.83 us
  transfers between devices with their start and end apart: 4, of which 4 were waited for; matrix products, arithmetic and copies ran while one was open for 0% of the time, Pallas kernels for 14%

profile of v8, /device:TPU:1, one launch (start us, length us, event | category | flops | bytes accessed | tf_op | source)
XLA Modules:
  0.0 95.3 jit_solution(6165643730260919440)
XLA Ops:
  0.0 0.0 copy-start.2
  0.0 0.0 copy-start.3
  0.0 0.0 copy-start.4
  0.0 4.4 %row_edges.1 = f32[2,8,8,8,128]{4,3,2,1,0:T(8,128)} custom-call(bf16[64,64,256]{2,1,0:T(8,128)(2,1)} %block_ref.1, f32[8,256]{1,0:T(8,128)} %vr_ref.1), custom_call_target="tpu_custom_call" | custom-call | tf_op jit(solution)/shard_map/row_edges/pallas_call | solution.py:276
  4.5 7.6 %all-to-all-start = ((f32[16,8,8,128]{3,2,1,0:T(8,128)}), f32[16,8,8,128]{3,2,1,0:T(8,128)S(1)}, u32[]{:S(2)}, u32[]{:S(2)}) async-start(f32[16,8,8,128]{3,2,1,0:T(8,128)} %bitcast), calls=%async_computation | async-start | bytes 1048576 | tf_op jit(solution)/shard_map/all_to_all | solution.py:378
  12.1 0.0 copy-done.2
  12.1 0.0 copy-done.3
  12.2 0.0 copy-done.4
  12.2 6.9 %vert_local.1.local_ref = f32[64,64,256]{2,1,0:T(8,128)} custom-call(bf16[64,64,256]{2,1,0:T(8,128)(2,1)} %block_ref.1, f32[8,256]{1,0:T(8,128)S(1)} %copy-done.2, f32[8,256]{1,0:T(8,128)S(1)} %copy-done.4), custom_call_target="tpu_custom_call" | custom-call | flops 5000000000 | bytes 8000000 | tf_op jit(solution)/shard_map/vert_local/pallas_call | solution.py:304
  19.0 3.5 %all-to-all-done.edge_ref = f32[16,8,8,128]{3,2,1,0:T(8,128)S(1)} async-done(((f32[16,8,8,128]{3,2,1,0:T(8,128)}), f32[16,8,8,128]{3,2,1,0:T(8,128)S(1)}, u32[]{:S(2)}, u32[]{:S(2)}) %all-to-all-start) | async-done | bytes 524320 | tf_op jit(solution)/shard_map/all_to_all | solution.py:378
  22.6 0.1 prefix.2
  22.6 13.1 %all_to_all.20 = f32[16,8,8,128]{3,2,1,0:T(8,128)S(1)} all-to-all(f32[16,8,8,128]{3,2,1,0:T(8,128)S(1)} %prefix.2), channel_id=1, replica_groups=mesh['row'=16,'col'=16] {'row'}, dimensions={0} | all-to-all | bytes 1048576 | tf_op jit(solution)/shard_map/all_to_all | solution.py:383
  35.7 0.0 copy-start.5
  35.7 8.5 %act_and_edges.1 = (bf16[64,64,256]{2,1,0:T(8,128)(2,1)}, f32[8,8,8,128]{3,2,1,0:T(8,128)S(1)}, f32[8,8,8,128]{3,2,1,0:T(8,128)S(1)}) custom-call(s32[1]{0:T(128)} %bitcast.1.core_ref, f32[64,64,256]{2,1,0:T(8,128)} %vert_local.1.local_ref, f32[2,8,8,8,128]{4,3,2,1,0:T(8,128)S(1)} %bitcast.3, f32[8,256]{1,0:T(8,128)S(1)} %copy-done.2, ...), custom_call_target="tpu_custom_call" | custom-call | tf_op jit(solution)/shard_map/act_and_edges/pallas_call | solution.py:334
  44.2 2.6 %collective-permute-start = (f32[8,8,8,128]{3,2,1,0:T(8,128)S(1)}, f32[8,8,8,128]{3,2,1,0:T(8,128)S(1)}, u32[]{:S(2)}, u32[]{:S(2)}) collective-permute-start(f32[8,8,8,128]{3,2,1,0:T(8,128)S(1)} %get-tuple-element.22), channel_id=1, source_target_pairs={{0,1},{1,0},{2,3},{3,2},{4,5},{5,4},{6,7},{7,6},{8,9},{9,8},{10,11... | collective-permute-start | bytes 786440 | tf_op jit(solution)/shard_map/ppermute | solution.py:364
  46.8 1.2 %collective-permute-done.came_ref = f32[8,8,8,128]{3,2,1,0:T(8,128)S(1)} collective-permute-done((f32[8,8,8,128]{3,2,1,0:T(8,128)S(1)}, f32[8,8,8,128]{3,2,1,0:T(8,128)S(1)}, u32[]{:S(2)}, u32[]{:S(2)}) %collective-permute-start) | collective-permute-done | bytes 262176 | tf_op jit(solution)/shard_map/ppermute | solution.py:364
  48.0 0.8 join_cores.1
  48.7 8.2 %all-to-all-start.2 = ((f32[8,8,8,128]{3,2,1,0:T(8,128)}), f32[8,8,8,128]{3,2,1,0:T(8,128)S(1)}, u32[]{:S(2)}, u32[]{:S(2)}) async-start(f32[8,8,8,128]{3,2,1,0:T(8,128)} %get-tuple-element.24), calls=%async_computation.2 | async-start | bytes 524288 | tf_op jit(solution)/shard_map/all_to_all | solution.py:391
  56.9 0.0 copy-done.5
  56.9 0.0 copy-start
  57.0 0.0 copy-start.1
  57.0 6.9 %horiz_local.1.local_ref = f32[64,64,256]{2,1,0:T(8,128)} custom-call(bf16[64,64,256]{2,1,0:T(8,128)(2,1)} %get-tuple-element.25.block_ref, f32[8,256]{1,0:T(8,128)S(1)} %copy-done.3, f32[8,256]{1,0:T(8,128)S(1)} %copy-done.5), custom_call_target="tpu_custom_call" | custom-call | flops 5000000000 | bytes 8000000 | tf_op jit(solution)/shard_map/horiz_local/pallas_call | solution.py:304
  63.9 4.1 %all-to-all-done.2.edge_ref = f32[8,8,8,128]{3,2,1,0:T(8,128)S(1)} async-done(((f32[8,8,8,128]{3,2,1,0:T(8,128)}), f32[8,8,8,128]{3,2,1,0:T(8,128)S(1)}, u32[]{:S(2)}, u32[]{:S(2)}) %all-to-all-start.2) | async-done | bytes 262176 | tf_op jit(solution)/shard_map/all_to_all | solution.py:391
  68.1 12.1 %all_to_all.21.chain_ref = f32[8,8,8,128]{3,2,1,0:T(8,128)S(1)} all-to-all(f32[8,8,8,128]{3,2,1,0:T(8,128)S(1)} %prefix.3), channel_id=1, replica_groups={{0,2,4,6,8,10,12,14},{1,3,5,7,9,11,13,15},{16,18,20,22,24,26,28,30},{17..., dimensions={0} | all-to-all | bytes 524288 | tf_op jit(solution)/shard_map/all_to_all | solution.py:395
  80.1 0.1 part_cores.1
  80.2 3.3 %collective-permute-start.1 = (f32[8,8,8,128]{3,2,1,0:T(8,128)S(1)}, f32[8,8,8,128]{3,2,1,0:T(8,128)S(1)}, u32[]{:S(2)}, u32[]{:S(2)}) collective-permute-start(f32[8,8,8,128]{3,2,1,0:T(8,128)S(1)} %get-tuple-element.30), channel_id=1, source_target_pairs={{0,1},{1,0},{2,3},{3,2},{4,5},{5,4},{6,7},{7,6},{8,9},{9,8},{10,11... | collective-permute-start | bytes 786440 | tf_op jit(solution)/shard_map/ppermute | solution.py:364
  83.4 1.2 %collective-permute-done.1.got_ref = f32[8,8,8,128]{3,2,1,0:T(8,128)S(1)} collective-permute-done((f32[8,8,8,128]{3,2,1,0:T(8,128)S(1)}, f32[8,8,8,128]{3,2,1,0:T(8,128)S(1)}, u32[]{:S(2)}, u32[]{:S(2)}) %collective-permute-start.1) | collective-permute-done | bytes 262176 | tf_op jit(solution)/shard_map/ppermute | solution.py:364
  84.6 0.0 copy-done
  84.6 0.0 copy-done.1
  84.6 10.7 %mix.1 = bf16[64,64,256]{2,1,0:T(8,128)(2,1)} custom-call(s32[1]{0:T(128)} %bitcast.1.core_ref, f32[64,64,256]{2,1,0:T(8,128)} %horiz_local.1.local_ref, f32[8,8,8,128]{3,2,1,0:T(8,128)S(1)} %get-tuple-element.29.keep_ref, f32[8,8,8,128]{3,2,1,0:T(8,128)S(1)} %collective-permute-done.1.got_ref, f32[8,256]{1,0:T(8,128)S(1)} %copy-done.3, ...), custom_call_target="tpu_custom_call" | custom-call | tf_op jit(solution)/shard_map/mix/pallas_call | solution.py:350
  (3 shorter events, 0.0 us)
Async XLA Ops:
  0.0 12.1 %copy-start.2 = (f32[8,256]{1,0:T(8,128)S(1)}, f32[8,256]{1,0:T(8,128)}, u32[]{:S(2)}) copy-start(f32[8,256]{1,0:T(8,128)} %vr_ref.1) | copy-start | bytes 24580
  0.0 12.1 %copy-start.3 = (f32[8,256]{1,0:T(8,128)S(1)}, f32[8,256]{1,0:T(8,128)}, u32[]{:S(2)}) copy-start(f32[8,256]{1,0:T(8,128)} %hr_ref.3) | copy-start | bytes 24580
  0.0 12.2 %copy-start.4 = (f32[8,256]{1,0:T(8,128)S(1)}, f32[8,256]{1,0:T(8,128)}, u32[]{:S(2)}) copy-start(f32[8,256]{1,0:T(8,128)} %vc_ref.1) | copy-start | bytes 24580
  4.5 18.1 %all-to-all-start = ((f32[16,8,8,128]{3,2,1,0:T(8,128)}), f32[16,8,8,128]{3,2,1,0:T(8,128)S(1)}, u32[]{:S(2)}, u32[]{:S(2)}) async-start(f32[16,8,8,128]{3,2,1,0:T(8,128)} %bitcast), calls=%async_computation | async-start | bytes 1048576 | tf_op jit(solution)/shard_map/all_to_all | solution.py:378
  35.7 21.2 %copy-start.5 = (f32[8,256]{1,0:T(8,128)S(1)}, f32[8,256]{1,0:T(8,128)}, u32[]{:S(2)}) copy-start(f32[8,256]{1,0:T(8,128)} %hc_ref.1) | copy-start | bytes 24580
  44.2 3.7 %collective-permute-start = (f32[8,8,8,128]{3,2,1,0:T(8,128)S(1)}, f32[8,8,8,128]{3,2,1,0:T(8,128)S(1)}, u32[]{:S(2)}, u32[]{:S(2)}) collective-permute-start(f32[8,8,8,128]{3,2,1,0:T(8,128)S(1)} %get-tuple-element.22), channel_id=1, source_target_pairs={{0,1},{1,0},{2,3},{3,2},{4,5},{5,4},{6,7},{7,6},{8,9},{9,8},{10,11... | collective-permute-start | bytes 786440 | tf_op jit(solution)/shard_map/ppermute | solution.py:364
  48.7 19.3 %all-to-all-start.2 = ((f32[8,8,8,128]{3,2,1,0:T(8,128)}), f32[8,8,8,128]{3,2,1,0:T(8,128)S(1)}, u32[]{:S(2)}, u32[]{:S(2)}) async-start(f32[8,8,8,128]{3,2,1,0:T(8,128)} %get-tuple-element.24), calls=%async_computation.2 | async-start | bytes 524288 | tf_op jit(solution)/shard_map/all_to_all | solution.py:391
  56.9 27.7 %copy-start = (bf16[256,1024]{1,0:T(8,128)(2,1)S(1)}, bf16[256,1024]{1,0:T(8,128)(2,1)}, u32[]{:S(2)}) copy-start(bf16[256,1024]{1,0:T(8,128)(2,1)} %w_in_ref.1) | copy-start | bytes 1572868
  57.0 27.7 %copy-start.1 = (bf16[1024,256]{1,0:T(8,128)(2,1)S(1)}, bf16[1024,256]{1,0:T(8,128)(2,1)}, u32[]{:S(2)}) copy-start(bf16[1024,256]{1,0:T(8,128)(2,1)} %w_out_ref.1) | copy-start | bytes 1572868
  80.2 4.4 %collective-permute-start.1 = (f32[8,8,8,128]{3,2,1,0:T(8,128)S(1)}, f32[8,8,8,128]{3,2,1,0:T(8,128)S(1)}, u32[]{:S(2)}, u32[]{:S(2)}) collective-permute-start(f32[8,8,8,128]{3,2,1,0:T(8,128)S(1)} %get-tuple-element.30), channel_id=1, source_target_pairs={{0,1},{1,0},{2,3},{3,2},{4,5},{5,4},{6,7},{7,6},{8,9},{9,8},{10,11... | collective-permute-start | bytes 786440 | tf_op jit(solution)/shard_map/ppermute | solution.py:364

commit v9 on v8

--- a/solution.py
+++ b/solution.py
@@ -97,7 +97,7 @@
             states[m] = decay[m] * states[m] + edge_ref[r, m]
 
 
-def local_kernel(scale, block_ref, rate_ref, coef_ref, out_ref, block, result, arrived, left):
+def local_kernel(scale, block_ref, rate_hbm_ref, coef_hbm_ref, out_ref, block, result, rate_ref, coef_ref, arrived, left):
     def part(i):
         return pl.ds(pl.multiple_of(i * 16, 16), 16)
 
@@ -107,8 +107,16 @@
     def put(i):
         return pltpu.make_async_copy(result.at[:, part(i), :], out_ref.at[:, part(i), :], left.at[i])
 
+    tables = [
+        pltpu.make_async_copy(rate_hbm_ref, rate_ref, arrived.at[4]),
+        pltpu.make_async_copy(coef_hbm_ref, coef_ref, arrived.at[5]),
+    ]
+    for table in tables:
+        table.start()
     for i in range(4):
         fetch(i).start()
+    for table in tables:
+        table.wait()
 
     def chunk(i, _):
         fetch(i).wait()
@@ -138,26 +146,67 @@
     return [jnp.broadcast_to(jnp.exp(-span * rate_ref[m : m + 1, :]), (8, LANES)) for m in range(MODES)]
 
 
-def join_kernel(span, core_ref, mine_ref, came_ref, rate_ref, first_ref, joined_ref):
-    left_here = core_ref[0] == 0
+def join_kernel(span, left_ref, here_ref, keep_ref, came_ref, rate_ref, first_ref, *out_refs):
+    left_here, here = left_ref[0] == 0, here_ref[0]
     decay = decays(rate_ref, span)
-    for b in range(8):
-        for m in range(MODES):
-            mine, came = mine_ref[b, m], came_ref[b, m]
-            first = jnp.where(left_here, mine, came)
-            first_ref[b, m] = first
-            joined_ref[b, m] = decay[m] * first + jnp.where(left_here, came, mine)
-
-
-def part_kernel(span, core_ref, chain_ref, first_ref, rate_ref, keep_ref, send_ref):
-    left_here = core_ref[0] == 0
+    part = keep_ref.shape[0] // len(out_refs)
+    for b in range(part):
+        for k, out_ref in enumerate(out_refs):
+            at = b if len(out_refs) == 1 else (here * part if k == 0 else part - here * part) + b
+            for m in range(MODES):
+                keep, came = keep_ref[at, m], came_ref[at, m]
+                first = jnp.where(left_here, keep, came)
+                first_ref[at, m] = first
+                out_ref[b, m] = decay[m] * first + jnp.where(left_here, came, keep)
+
+
+def part_kernel(span, left_ref, here_ref, *refs):
+    *in_refs, first_ref, rate_ref, keep_ref, send_ref = refs
+    left_here, here = left_ref[0] == 0, here_ref[0]
     decay = decays(rate_ref, span)
-    for b in range(8):
-        for m in range(MODES):
-            chain = chain_ref[b, m]
-            after = decay[m] * chain + first_ref[b, m]
-            keep_ref[b, m] = jnp.where(left_here, chain, after)
-            send_ref[b, m] = jnp.where(left_here, after, chain)
+    part = first_ref.shape[0] // len(in_refs)
+    for b in range(part):
+        for k, in_ref in enumerate(in_refs):
+            at = b if len(in_refs) == 1 else (here * part if k == 0 else part - here * part) + b
+            for m in range(MODES):
+                chain = in_ref[b, m]
+                after = decay[m] * chain + first_ref[at, m]
+                keep_ref[at, m] = jnp.where(left_here, chain, after)
+                send_ref[at, m] = jnp.where(left_here, after, chain)
+
+
+def piece_kernel(part, block_ref, rate_ref, coef_ref, *refs):
+    out_ref, block, result, arrived, left = refs[-5:]
+    rows = pl.ds(part * 16, 16)
+
+    def fetch(half):
+        lanes = pl.ds(half * LANES, LANES)
+        return pltpu.make_async_copy(block_ref.at[:, rows, lanes], block.at[:, :, lanes], arrived.at[half])
+
+    def put(half):
+        lanes = pl.ds(half * LANES, LANES)
+        return pltpu.make_async_copy(result.at[:, :, lanes], out_ref.at[:, rows, lanes], left.at[half])
+
+    for half in range(2):
+        fetch(half).start()
+    for half in range(2):
+        lanes = slice(half * LANES, (half + 1) * LANES)
+        pole = poles(rate_ref, half, 16)
+        weight = weights(rate_ref, coef_ref, half, 16)
+        fetch(half).wait()
+
+        def steps(j, states, lanes=lanes, pole=pole, weight=weight):
+            for k in range(16):
+                s = j * 16 + k
+                u = block[s, :, lanes].astype(F32)
+                states = [p * h + u for p, h in zip(pole, states)]
+                result[s, :, lanes] = tree([q * h for q, h in zip(weight, states)])
+            return states
+
+        lax.fori_loop(0, 4, steps, [jnp.zeros((16, LANES), F32)] * MODES)
+        put(half).start()
+    for half in range(2):
+        put(half).wait()
 
 
 def act_kernel(core_ref, local_ref, in_ref, vr_ref, vc_ref, hr_ref, act_ref, mine_ref, other_ref, tails, field):
@@ -303,25 +352,47 @@
 def local_scan(block, rate, coef, name, scale):
     return pl.pallas_call(
         functools.partial(local_kernel, scale),
-        in_specs=[HBM, VMEM, VMEM],
+        in_specs=[HBM, HBM, HBM],
         out_specs=HBM,
         out_shape=pltpu.HBM((64, 64, 256), F32),
         scratch_shapes=[
             pltpu.VMEM((64, 64, 256), BF16),
             pltpu.VMEM((64, 64, 256), F32),
-            pltpu.SemaphoreType.DMA((4,)),
+            pltpu.VMEM((8, 256), F32),
+            pltpu.VMEM((8, 256), F32),
+            pltpu.SemaphoreType.DMA((6,)),
             pltpu.SemaphoreType.DMA((4,)),
         ],
         compiler_params=params(24),
         cost_estimate=pl.CostEstimate(flops=5_000_000_000, bytes_accessed=8_000_000, transcendentals=0),
         name=name,
-    )(in_hbm(block), rate, coef)
+    )(in_hbm(block), in_hbm(rate), in_hbm(coef))
+
+
+def local_piece(block, rate, coef, part, into):
+    more = [] if into is None else [in_hbm(into)]
+    return pl.pallas_call(
+        functools.partial(piece_kernel, part),
+        in_specs=[HBM, VMEM, VMEM] + [HBM] * len(more),
+        out_specs=HBM,
+        out_shape=pltpu.HBM((64, 64, 256), F32),
+        input_output_aliases={3: 0} if more else {},
+        scratch_shapes=[
+            pltpu.VMEM((64, 16, 256), BF16),
+            pltpu.VMEM((64, 16, 256), F32),
+            pltpu.SemaphoreType.DMA((2,)),
+            pltpu.SemaphoreType.DMA((2,)),
+        ],
+        compiler_params=params(8),
+        cost_estimate=pl.CostEstimate(flops=1_250_000_000, bytes_accessed=2_000_000, transcendentals=0),
+        name=f"horiz_local_{part}",
+    )(in_hbm(block), rate, coef, *more)
 
 
 def small(kernel, name, outs, *operands):
     return pl.pallas_call(
         kernel,
-        in_specs=[SMEM] + [VMEM] * (len(operands) - 1),
+        in_specs=[SMEM] * 2 + [VMEM] * (len(operands) - 2),
         out_specs=[VMEM] * len(outs),
         out_shape=[jax.ShapeDtypeStruct(shape, F32) for shape in outs],
         compiler_params=params(8),
@@ -371,33 +442,50 @@
 def on_device(image, vert_rate, vert_coef, horiz_rate, horiz_coef, w_in, w_out):
     rows, cols = lax.axis_size("row"), lax.axis_size("col")
     piece = lax.axis_index("row")
-    core = (lax.axis_index("col") % 2).reshape(1)
+    col = lax.axis_index("col").reshape(1)
+    core, chip = col % 2, col // 2
+    side = [core, chip % 2, chip // 2 % 2]
+    upper = chip // 4
+    here = [side[1] ^ upper, side[2] ^ upper, upper]
     rate_along = lax.dynamic_slice_in_dim(horiz_rate, core[0] * LANES, LANES, 1)
 
     edges = row_edges(image, vert_rate).reshape(rows, 8, 8, LANES)
     edges = lax.all_to_all(edges, "row", 0, 0, tiled=True)
     rate = lax.dynamic_slice_in_dim(vert_rate, (piece // 8) * LANES, LANES, 1)
     local = local_scan(image, vert_rate, vert_coef, "vert_local", 0.5)
-    edges, local, core, rate_along = lax.optimization_barrier((edges, local, core, rate_along))
+    edges, local, side, here, rate_along = lax.optimization_barrier((edges, local, side, here, rate_along))
     incoming = prefix(edges, rate, 64.0)
     incoming = lax.all_to_all(incoming, "row", 0, 0, tiled=True).reshape(2, 8, 8, 8, LANES)
 
-    act, edge, other = act_and_edges(core, local, incoming, vert_rate, vert_coef, horiz_rate)
-
-    chips = [[2 * z + c for z in range(cols // 2)] for c in range(2)]
-    tile = [(8, 8, 8, LANES)] * 2
-    join = functools.partial(join_kernel, 64.0)
-    first, joined = small(join, "join_cores", tile, core, edge, swap(other, 1), rate_along)
-    joined = lax.all_to_all(joined, "col", 0, 0, tiled=True, axis_index_groups=chips)
-    local = local_scan(act, horiz_rate, horiz_coef, "horiz_local", 1.0)
-    joined, local = together(joined, local)
-    chain = prefix(joined, rate_along, 128.0)
-    chain = lax.all_to_all(chain, "col", 0, 0, tiled=True, axis_index_groups=chips)
-    part = functools.partial(part_kernel, 64.0)
-    keep, send = small(part, "part_cores", tile, core, chain, first, rate_along)
+    act, mine, other = act_and_edges(side[0], local, incoming, vert_rate, vert_coef, horiz_rate)
+
+    eight, four, two = (8, 8, 8, LANES), (4, 8, 8, LANES), (2, 8, 8, LANES)
+
+    def horiz(part, into):
+        return local_piece(act, horiz_rate, horiz_coef, part, into)
+
+    def join(level, outs, keep, came):
+        kernel = functools.partial(join_kernel, 64.0 * 2**level)
+        return small(kernel, f"join_{level}", outs, side[level], here[level], keep, came, rate_along)
+
+    def part(level, shape, chains, first):
+        kernel = functools.partial(part_kernel, 64.0 * 2**level)
+        return small(kernel, f"part_{level}", [shape] * 2, side[level], here[level], *chains, first, rate_along)
+
+    first_tile, keep, send = join(0, [eight, four, four], mine, swap(other, 1))
+    came, local = together(swap(send, 2), horiz(0, None))
+    first_chip, keep, send = join(1, [four, two, two], keep, came)
+    came, local = together(swap(send, 4), horiz(1, local))
+    first_pair, group = join(2, [two, two], keep, came)
+    chain = lax.ppermute(group, "col", [(i, i ^ (cols - 2)) for i in range(cols // 2)])
+    chain, local = together(chain, horiz(2, local))
+    keep, send = part(2, two, [chain], first_pair)
+    came, local = together(swap(send, 4), horiz(3, local))
+    keep, send = part(1, four, [keep, came], first_chip)
+    keep, send = part(0, eight, [keep, swap(send, 2)], first_tile)
     got = swap(send, 1)
 
-    return mix(core, local, keep, got, horiz_rate, horiz_coef, w_in, w_out)
+    return mix(side[0], local, keep, got, horiz_rate, horiz_coef, w_in, w_out)
 
 
 def solution(mesh):

time: 95.7 us -> 95 us (level)
  blocking collectives: 25.2 us -> 14.5 us
  starting transfers between devices: 21.6 us -> 27.3 us
  Pallas kernels: 38.3 us -> 43 us
  waiting for transfers between devices: 10 us -> 8.18 us
  local copies, waits for them, and re-layouts: 0.04 us -> 1.41 us
    all_to_all x1 -> x0, blocking collectives: 12.1 us -> none  [on_device(): lax.all_to_all(chain, 'col', 0, 0, tiled=True, axis_index_groups=chips)]
    all_to_all x1 -> x0, starting transfers between devices: 8.19 us -> none  [on_device(): lax.all_to_all(joined, 'col', 0, 0, tiled=True, axis_index_groups=chips)]
    ppermute x2 -> x6, starting transfers between devices: 5.83 us -> 13.8 us  [swap(): return lax.ppermute(block, 'col', [(i, i ^ bits) for i in range(n)])]
    ppermute x0 -> x1, starting transfers between devices: none -> 5.88 us  [on_device(): lax.ppermute(group, 'col', [(i, i ^ cols - 2) for i in range(cols // 2)])]
    pallas_call x4 -> x11, Pallas kernels: 14.6 us -> 19.2 us  [the longest x4 11.9 us: local_piece(): pl.pallas_call(functools.partial(piece_kernel, part), in_specs=[HBM, VMEM...]
    all_to_all x1 -> x0, waiting for transfers between devices: 4.14 us -> none  [on_device(): lax.all_to_all(joined, 'col', 0, 0, tiled=True, axis_index_groups=chips)]
    ppermute x2 -> x6, waiting for transfers between devices: 2.32 us -> 6.15 us  [swap(): return lax.ppermute(block, 'col', [(i, i ^ bits) for i in range(n)])]
    all_to_all x1, waiting for transfers between devices: 3.54 us -> 2.03 us  [on_device(): edges = lax.all_to_all(edges, 'row', 0, 0, tiled=True)]
  transfers between devices with their start and end apart: 4 -> 8, of which waited for: 4 -> 5; matrix products, arithmetic and copies ran while one was open for 0% -> 1% of each run, Pallas kernels for 14% -> 20%
where the time goes in v9:
time: 95 us; the launch traced here: 94.6 us
  Pallas kernels  43 us (45%)
  starting transfers between devices  27.3 us (29%)
  blocking collectives  14.5 us (15%)
  waiting for transfers between devices  8.18 us (9%)
  local copies, waits for them, and re-layouts  1.41 us (1%)
    all_to_all x1, blocking collectives, on_device(): lax.all_to_all(incoming, 'row', 0, 0, tiled=True).reshape(2, 8, 8, 8, LANES)  14.5 us
    ppermute x6, starting transfers between devices, swap(): return lax.ppermute(block, 'col', [(i, i ^ bits) for i in range(n)])  13.8 us
    pallas_call x4, Pallas kernels, local_piece(): pl.pallas_call(functools.partial(piece_kernel, part), in_specs=[HBM, VMEM...  11.9 us
    pallas_call x1, Pallas kernels, mix(): pl.pallas_call(mix_kernel, grid=(64 // MIX_ROWS,), in_specs=[SMEM, pl.Blo...  10.7 us
    pallas_call x1, Pallas kernels, act_and_edges(): pl.pallas_call(act_kernel, grid=(64 // ACT_ROWS,), in_specs=[SMEM, pl.Blo...  8.52 us
    all_to_all x1, starting transfers between devices, on_device(): edges = lax.all_to_all(edges, 'row', 0, 0, tiled=True)  7.6 us
    pallas_call x1, Pallas kernels, local_scan(): pl.pallas_call(functools.partial(local_kernel, scale), in_specs=[HBM, HBM...  7.04 us
    ppermute x6, waiting for transfers between devices, swap(): return lax.ppermute(block, 'col', [(i, i ^ bits) for i in range(n)])  6.15 us
  transfers between devices with their start and end apart: 8, of which 5 were waited for; matrix products, arithmetic and copies ran while one was open for 1% of the time, Pallas kernels for 20%

profile of v9, /device:TPU:1, one launch (start us, length us, event | category | flops | bytes accessed | tf_op | source)
XLA Modules:
  0.0 94.6 jit_solution(16187766369020630817)
XLA Ops:
  0.0 4.4 %row_edges.1 = f32[2,8,8,8,128]{4,3,2,1,0:T(8,128)} custom-call(bf16[64,64,256]{2,1,0:T(8,128)(2,1)} %block_ref.1, f32[8,256]{1,0:T(8,128)} %vr_ref.1), custom_call_target="tpu_custom_call" | custom-call | tf_op jit(solution)/shard_map/row_edges/pallas_call | solution.py:325
  4.4 7.6 %all-to-all-start = ((f32[16,8,8,128]{3,2,1,0:T(8,128)}), f32[16,8,8,128]{3,2,1,0:T(8,128)S(1)}, u32[]{:S(2)}, u32[]{:S(2)}) async-start(f32[16,8,8,128]{3,2,1,0:T(8,128)} %bitcast), calls=%async_computation | async-start | bytes 1048576 | tf_op jit(solution)/shard_map/all_to_all | solution.py:453
  12.1 0.7 constant_dynamic-slice_fusion.rate_ref
  12.7 0.7 constant_dynamic-slice_fusion.1.rate_ref.refs_2_.refs_3_
  13.4 0.0 copy-start.2
  13.4 0.0 copy-start.4
  13.4 0.0 copy-start.5
  13.4 7.0 %vert_local.1.local_ref = f32[64,64,256]{2,1,0:T(8,128)} custom-call(bf16[64,64,256]{2,1,0:T(8,128)(2,1)} %block_ref.1, f32[8,256]{1,0:T(8,128)} %vr_ref.1, f32[8,256]{1,0:T(8,128)} %vc_ref.1), custom_call_target="tpu_custom_call" | custom-call | flops 5000000000 | bytes 8000000 | tf_op jit(solution)/shard_map/vert_local/pallas_call | solution.py:353
  20.5 0.0 copy-start.3
  20.5 2.0 %all-to-all-done.edge_ref = f32[16,8,8,128]{3,2,1,0:T(8,128)S(1)} async-done(((f32[16,8,8,128]{3,2,1,0:T(8,128)}), f32[16,8,8,128]{3,2,1,0:T(8,128)S(1)}, u32[]{:S(2)}, u32[]{:S(2)}) %all-to-all-start) | async-done | bytes 524320 | tf_op jit(solution)/shard_map/all_to_all | solution.py:453
  22.5 0.1 prefix.1
  22.6 14.5 %all_to_all.10 = f32[16,8,8,128]{3,2,1,0:T(8,128)S(1)} all-to-all(f32[16,8,8,128]{3,2,1,0:T(8,128)S(1)} %prefix.1), channel_id=1, replica_groups=mesh['row'=16,'col'=16] {'row'}, dimensions={0} | all-to-all | bytes 1048576 | tf_op jit(solution)/shard_map/all_to_all | solution.py:458
  37.1 0.0 copy-done.2
  37.1 0.0 copy-done.4
  37.1 0.0 copy-done.5
  37.1 8.5 %act_and_edges.1 = (bf16[64,64,256]{2,1,0:T(8,128)(2,1)}, f32[8,8,8,128]{3,2,1,0:T(8,128)S(1)}, f32[8,8,8,128]{3,2,1,0:T(8,128)S(1)}) custom-call(s32[1]{0:T(128)S(6)} %select_n.36.core_ref.left_ref, f32[64,64,256]{2,1,0:T(8,128)} %vert_local.1.local_ref, f32[2,8,8,8,128]{4,3,2,1,0:T(8,128)S(1)} %bitcast.4, f32[8,256]{1,0:T(8,128)S(1)} %copy-done.4, ...), custom_call_target="tpu_custom_call" | custom-call | tf_op jit(solution)/shard_map/act_and_edges/pallas_call | solution.py:405
  45.7 2.4 %collective-permute-start = (f32[8,8,8,128]{3,2,1,0:T(8,128)S(1)}, f32[8,8,8,128]{3,2,1,0:T(8,128)S(1)}, u32[]{:S(2)}, u32[]{:S(2)}) collective-permute-start(f32[8,8,8,128]{3,2,1,0:T(8,128)S(1)} %get-tuple-element.48), channel_id=1, source_target_pairs={{0,1},{1,0},{2,3},{3,2},{4,5},{5,4},{6,7},{7,6},{8,9},{9,8},{10,11... | collective-permute-start | bytes 786440 | tf_op jit(solution)/shard_map/ppermute | solution.py:435
  48.0 1.2 %collective-permute-done.came_ref = f32[8,8,8,128]{3,2,1,0:T(8,128)S(1)} collective-permute-done((f32[8,8,8,128]{3,2,1,0:T(8,128)S(1)}, f32[8,8,8,128]{3,2,1,0:T(8,128)S(1)}, u32[]{:S(2)}, u32[]{:S(2)}) %collective-permute-start) | collective-permute-done | bytes 262176 | tf_op jit(solution)/shard_map/ppermute | solution.py:435
  49.2 0.1 join_0.1
  49.2 1.7 %collective-permute-start.1 = (f32[4,8,8,128]{3,2,1,0:T(8,128)S(1)}, f32[4,8,8,128]{3,2,1,0:T(8,128)S(1)}, u32[]{:S(2)}, u32[]{:S(2)}) collective-permute-start(f32[4,8,8,128]{3,2,1,0:T(8,128)S(1)} %get-tuple-element.51), channel_id=1, source_target_pairs={{0,2},{1,3},{2,0},{3,1},{4,6},{5,7},{6,4},{7,5},{8,10},{9,11},{10,... | collective-permute-start | bytes 393224 | tf_op jit(solution)/shard_map/ppermute | solution.py:435
  51.0 0.0 copy-done.3
  51.0 2.9 %horiz_local_0.1.refs_0_ = f32[64,64,256]{2,1,0:T(8,128)} custom-call(bf16[64,64,256]{2,1,0:T(8,128)(2,1)} %get-tuple-element.52.block_ref, f32[8,256]{1,0:T(8,128)S(1)} %copy-done.2, f32[8,256]{1,0:T(8,128)S(1)} %copy-done.3), custom_call_target="tpu_custom_call" | custom-call | flops 1250000000 | bytes 2000000 | tf_op jit(solution)/shard_map/horiz_local_0/pallas_call | solution.py:374
  53.9 0.5 collective-permute-done.1.came_ref
  54.5 3.1 %collective-permute-start.2 = (f32[2,8,8,128]{3,2,1,0:T(8,128)S(1)}, f32[2,8,8,128]{3,2,1,0:T(8,128)S(1)}, u32[]{:S(2)}, u32[]{:S(2)}) collective-permute-start(f32[2,8,8,128]{3,2,1,0:T(8,128)S(1)} %get-tuple-element.55), channel_id=1, source_target_pairs={{0,4},{1,5},{2,6},{3,7},{4,0},{5,1},{6,2},{7,3},{8,12},{9,13},{10,... | collective-permute-start | bytes 196616 | tf_op jit(solution)/shard_map/ppermute | solution.py:435
  57.5 2.9 %horiz_local_1.1.refs_0_ = f32[64,64,256]{2,1,0:T(8,128)} custom-call(bf16[64,64,256]{2,1,0:T(8,128)(2,1)} %get-tuple-element.52.block_ref, f32[8,256]{1,0:T(8,128)S(1)} %copy-done.2, f32[8,256]{1,0:T(8,128)S(1)} %copy-done.3, f32[64,64,256]{2,1,0:T(8,128)} %horiz_local_0.1.refs_0_), custom_call_target="tpu_custom_call", output_to_operand_aliasing={{}: (3, {})} | custom-call | flops 1250000000 | bytes 2000000 | tf_op jit(solution)/shard_map/horiz_local_1/pallas_call | solution.py:374
  60.5 0.0 collective-permute-done.2.came_ref
  60.5 5.9 %collective-permute-start.3 = (f32[2,8,8,128]{3,2,1,0:T(8,128)S(1)}, f32[2,8,8,128]{3,2,1,0:T(8,128)S(1)}, u32[]{:S(2)}, u32[]{:S(2)}) collective-permute-start(f32[2,8,8,128]{3,2,1,0:T(8,128)S(1)} %get-tuple-element.58), channel_id=1, source_target_pairs={{0,14},{1,15},{2,12},{3,13},{4,10},{5,11},{6,8},{7,9},{16,30},{17,... | collective-permute-start | bytes 196616 | tf_op jit(solution)/shard_map/ppermute | solution.py:480
  66.4 3.0 %horiz_local_2.1.refs_0_ = f32[64,64,256]{2,1,0:T(8,128)} custom-call(bf16[64,64,256]{2,1,0:T(8,128)(2,1)} %get-tuple-element.52.block_ref, f32[8,256]{1,0:T(8,128)S(1)} %copy-done.2, f32[8,256]{1,0:T(8,128)S(1)} %copy-done.3, f32[64,64,256]{2,1,0:T(8,128)} %horiz_local_1.1.refs_0_), custom_call_target="tpu_custom_call", output_to_operand_aliasing={{}: (3, {})} | custom-call | flops 1250000000 | bytes 2000000 | tf_op jit(solution)/shard_map/horiz_local_2/pallas_call | solution.py:374
  69.5 0.0 collective-permute-done.3.refs_0_
  69.5 0.0 copy-start
  69.5 0.0 copy-start.1
  69.5 1.6 %collective-permute-start.4 = (f32[2,8,8,128]{3,2,1,0:T(8,128)S(1)}, f32[2,8,8,128]{3,2,1,0:T(8,128)S(1)}, u32[]{:S(2)}, u32[]{:S(2)}) collective-permute-start(f32[2,8,8,128]{3,2,1,0:T(8,128)S(1)} %get-tuple-element.62), channel_id=1, source_target_pairs={{0,4},{1,5},{2,6},{3,7},{4,0},{5,1},{6,2},{7,3},{8,12},{9,13},{10,... | collective-permute-start | bytes 196616 | tf_op jit(solution)/shard_map/ppermute | solution.py:435
  71.1 3.0 %horiz_local_3.1.local_ref = f32[64,64,256]{2,1,0:T(8,128)} custom-call(bf16[64,64,256]{2,1,0:T(8,128)(2,1)} %get-tuple-element.52.block_ref, f32[8,256]{1,0:T(8,128)S(1)} %copy-done.2, f32[8,256]{1,0:T(8,128)S(1)} %copy-done.3, f32[64,64,256]{2,1,0:T(8,128)} %horiz_local_2.1.refs_0_), custom_call_target="tpu_custom_call", output_to_operand_aliasing={{}: (3, {})} | custom-call | flops 1250000000 | bytes 2000000 | tf_op jit(solution)/shard_map/horiz_local_3/pallas_call | solution.py:374
  74.1 0.0 collective-permute-done.4.refs_1_
  74.2 0.6 collective-permute-start.5
  74.8 3.3 %collective-permute-done.5.refs_1_ = f32[4,8,8,128]{3,2,1,0:T(8,128)S(1)} collective-permute-done((f32[4,8,8,128]{3,2,1,0:T(8,128)S(1)}, f32[4,8,8,128]{3,2,1,0:T(8,128)S(1)}, u32[]{:S(2)}, u32[]{:S(2)}) %collective-permute-start.5) | collective-permute-done | bytes 131104 | tf_op jit(solution)/shard_map/ppermute | solution.py:435
  78.1 0.1 part_0.1
  78.2 4.5 %collective-permute-start.6 = (f32[8,8,8,128]{3,2,1,0:T(8,128)S(1)}, f32[8,8,8,128]{3,2,1,0:T(8,128)S(1)}, u32[]{:S(2)}, u32[]{:S(2)}) collective-permute-start(f32[8,8,8,128]{3,2,1,0:T(8,128)S(1)} %get-tuple-element.72), channel_id=1, source_target_pairs={{0,1},{1,0},{2,3},{3,2},{4,5},{5,4},{6,7},{7,6},{8,9},{9,8},{10,11... | collective-permute-start | bytes 786440 | tf_op jit(solution)/shard_map/ppermute | solution.py:435
  82.7 1.2 %collective-permute-done.6.got_ref = f32[8,8,8,128]{3,2,1,0:T(8,128)S(1)} collective-permute-done((f32[8,8,8,128]{3,2,1,0:T(8,128)S(1)}, f32[8,8,8,128]{3,2,1,0:T(8,128)S(1)}, u32[]{:S(2)}, u32[]{:S(2)}) %collective-permute-start.6) | collective-permute-done | bytes 262176 | tf_op jit(solution)/shard_map/ppermute | solution.py:435
  83.8 0.0 copy-done
  83.8 0.0 copy-done.1
  83.8 10.7 %mix.1 = bf16[64,64,256]{2,1,0:T(8,128)(2,1)} custom-call(s32[1]{0:T(128)S(6)} %select_n.36.core_ref.left_ref, f32[64,64,256]{2,1,0:T(8,128)} %horiz_local_3.1.local_ref, f32[8,8,8,128]{3,2,1,0:T(8,128)S(1)} %get-tuple-element.71.keep_ref, f32[8,8,8,128]{3,2,1,0:T(8,128)S(1)} %collective-permute-done.6.got_ref, f32[8,256]{1,0:T(8,128)S(1)} %copy-done.2, ...), custom_call_target="tpu_custom_call" | custom-call | tf_op jit(solution)/shard_map/mix/pallas_call | solution.py:421
  (4 shorter events, 0.1 us)
Async XLA Ops:
  4.4 18.1 %all-to-all-start = ((f32[16,8,8,128]{3,2,1,0:T(8,128)}), f32[16,8,8,128]{3,2,1,0:T(8,128)S(1)}, u32[]{:S(2)}, u32[]{:S(2)}) async-start(f32[16,8,8,128]{3,2,1,0:T(8,128)} %bitcast), calls=%async_computation | async-start | bytes 1048576 | tf_op jit(solution)/shard_map/all_to_all | solution.py:453
  13.4 23.7 %copy-start.2 = (f32[8,256]{1,0:T(8,128)S(1)}, f32[8,256]{1,0:T(8,128)}, u32[]{:S(2)}) copy-start(f32[8,256]{1,0:T(8,128)} %hr_ref.3) | copy-start | bytes 24580
  13.4 23.7 %copy-start.4 = (f32[8,256]{1,0:T(8,128)S(1)}, f32[8,256]{1,0:T(8,128)}, u32[]{:S(2)}) copy-start(f32[8,256]{1,0:T(8,128)} %vr_ref.1) | copy-start | bytes 24580
  13.4 23.7 %copy-start.5 = (f32[8,256]{1,0:T(8,128)S(1)}, f32[8,256]{1,0:T(8,128)}, u32[]{:S(2)}) copy-start(f32[8,256]{1,0:T(8,128)} %vc_ref.1) | copy-start | bytes 24580
  20.5 30.5 %copy-start.3 = (f32[8,256]{1,0:T(8,128)S(1)}, f32[8,256]{1,0:T(8,128)}, u32[]{:S(2)}) copy-start(f32[8,256]{1,0:T(8,128)} %hc_ref.1) | copy-start | bytes 24580
  45.7 3.5 %collective-permute-start = (f32[8,8,8,128]{3,2,1,0:T(8,128)S(1)}, f32[8,8,8,128]{3,2,1,0:T(8,128)S(1)}, u32[]{:S(2)}, u32[]{:S(2)}) collective-permute-start(f32[8,8,8,128]{3,2,1,0:T(8,128)S(1)} %get-tuple-element.48), channel_id=1, source_target_pairs={{0,1},{1,0},{2,3},{3,2},{4,5},{5,4},{6,7},{7,6},{8,9},{9,8},{10,11... | collective-permute-start | bytes 786440 | tf_op jit(solution)/shard_map/ppermute | solution.py:435
  49.2 5.2 %collective-permute-start.1 = (f32[4,8,8,128]{3,2,1,0:T(8,128)S(1)}, f32[4,8,8,128]{3,2,1,0:T(8,128)S(1)}, u32[]{:S(2)}, u32[]{:S(2)}) collective-permute-start(f32[4,8,8,128]{3,2,1,0:T(8,128)S(1)} %get-tuple-element.51), channel_id=1, source_target_pairs={{0,2},{1,3},{2,0},{3,1},{4,6},{5,7},{6,4},{7,5},{8,10},{9,11},{10,... | collective-permute-start | bytes 393224 | tf_op jit(solution)/shard_map/ppermute | solution.py:435
  54.5 6.0 %collective-permute-start.2 = (f32[2,8,8,128]{3,2,1,0:T(8,128)S(1)}, f32[2,8,8,128]{3,2,1,0:T(8,128)S(1)}, u32[]{:S(2)}, u32[]{:S(2)}) collective-permute-start(f32[2,8,8,128]{3,2,1,0:T(8,128)S(1)} %get-tuple-element.55), channel_id=1, source_target_pairs={{0,4},{1,5},{2,6},{3,7},{4,0},{5,1},{6,2},{7,3},{8,12},{9,13},{10,... | collective-permute-start | bytes 196616 | tf_op jit(solution)/shard_map/ppermute | solution.py:435
  60.5 8.9 %collective-permute-start.3 = (f32[2,8,8,128]{3,2,1,0:T(8,128)S(1)}, f32[2,8,8,128]{3,2,1,0:T(8,128)S(1)}, u32[]{:S(2)}, u32[]{:S(2)}) collective-permute-start(f32[2,8,8,128]{3,2,1,0:T(8,128)S(1)} %get-tuple-element.58), channel_id=1, source_target_pairs={{0,14},{1,15},{2,12},{3,13},{4,10},{5,11},{6,8},{7,9},{16,30},{17,... | collective-permute-start | bytes 196616 | tf_op jit(solution)/shard_map/ppermute | solution.py:480
  69.5 14.3 %copy-start = (bf16[256,1024]{1,0:T(8,128)(2,1)S(1)}, bf16[256,1024]{1,0:T(8,128)(2,1)}, u32[]{:S(2)}) copy-start(bf16[256,1024]{1,0:T(8,128)(2,1)} %w_in_ref.1) | copy-start | bytes 1572868
  69.5 14.3 %copy-start.1 = (bf16[1024,256]{1,0:T(8,128)(2,1)S(1)}, bf16[1024,256]{1,0:T(8,128)(2,1)}, u32[]{:S(2)}) copy-start(bf16[1024,256]{1,0:T(8,128)(2,1)} %w_out_ref.1) | copy-start | bytes 1572868
  69.5 4.6 %collective-permute-start.4 = (f32[2,8,8,128]{3,2,1,0:T(8,128)S(1)}, f32[2,8,8,128]{3,2,1,0:T(8,128)S(1)}, u32[]{:S(2)}, u32[]{:S(2)}) collective-permute-start(f32[2,8,8,128]{3,2,1,0:T(8,128)S(1)} %get-tuple-element.62), channel_id=1, source_target_pairs={{0,4},{1,5},{2,6},{3,7},{4,0},{5,1},{6,2},{7,3},{8,12},{9,13},{10,... | collective-permute-start | bytes 196616 | tf_op jit(solution)/shard_map/ppermute | solution.py:435
  74.2 3.9 %collective-permute-start.5 = (f32[4,8,8,128]{3,2,1,0:T(8,128)S(1)}, f32[4,8,8,128]{3,2,1,0:T(8,128)S(1)}, u32[]{:S(2)}, u32[]{:S(2)}) collective-permute-start(f32[4,8,8,128]{3,2,1,0:T(8,128)S(1)} %get-tuple-element.69), channel_id=1, source_target_pairs={{0,2},{1,3},{2,0},{3,1},{4,6},{5,7},{6,4},{7,5},{8,10},{9,11},{10,... | collective-permute-start | bytes 393224 | tf_op jit(solution)/shard_map/ppermute | solution.py:435
  78.2 5.6 %collective-permute-start.6 = (f32[8,8,8,128]{3,2,1,0:T(8,128)S(1)}, f32[8,8,8,128]{3,2,1,0:T(8,128)S(1)}, u32[]{:S(2)}, u32[]{:S(2)}) collective-permute-start(f32[8,8,8,128]{3,2,1,0:T(8,128)S(1)} %get-tuple-element.72), channel_id=1, source_target_pairs={{0,1},{1,0},{2,3},{3,2},{4,5},{5,4},{6,7},{7,6},{8,9},{9,8},{10,11... | collective-permute-start | bytes 786440 | tf_op jit(solution)/shard_map/ppermute | solution.py:435

commit v10 on v9

--- a/solution.py
+++ b/solution.py
@@ -86,10 +86,8 @@
     lax.fori_loop(0, 4, chunk, 0)
 
 
-def prefix_kernel(span, edge_ref, rate_ref, out_ref):
-    decay = [
-        jnp.broadcast_to(jnp.exp(-span * rate_ref[m : m + 1, :]), (8, LANES)) for m in range(MODES)
-    ]
+def prefix_kernel(span, half_ref, edge_ref, rate_ref, out_ref):
+    decay = decays(rate_ref, half_ref, span)
     states = [jnp.zeros((8, LANES), F32)] * MODES
     for r in range(edge_ref.shape[0]):
         for m in range(MODES):
@@ -142,13 +140,14 @@
         put(i).wait()
 
 
-def decays(rate_ref, span):
-    return [jnp.broadcast_to(jnp.exp(-span * rate_ref[m : m + 1, :]), (8, LANES)) for m in range(MODES)]
-
-
-def join_kernel(span, left_ref, here_ref, keep_ref, came_ref, rate_ref, first_ref, *out_refs):
+def decays(rate_ref, half_ref, span):
+    lanes = pl.ds(pl.multiple_of(half_ref[0] * LANES, LANES), LANES)
+    return [jnp.broadcast_to(jnp.exp(-span * rate_ref[m : m + 1, lanes]), (8, LANES)) for m in range(MODES)]
+
+
+def join_kernel(span, half_ref, left_ref, here_ref, keep_ref, came_ref, rate_ref, first_ref, *out_refs):
     left_here, here = left_ref[0] == 0, here_ref[0]
-    decay = decays(rate_ref, span)
+    decay = decays(rate_ref, half_ref, span)
     part = keep_ref.shape[0] // len(out_refs)
     for b in range(part):
         for k, out_ref in enumerate(out_refs):
@@ -160,16 +159,18 @@
                 out_ref[b, m] = decay[m] * first + jnp.where(left_here, came, keep)
 
 
-def part_kernel(span, left_ref, here_ref, *refs):
+def part_kernel(span, half_ref, left_ref, here_ref, *refs):
     *in_refs, first_ref, rate_ref, keep_ref, send_ref = refs
     left_here, here = left_ref[0] == 0, here_ref[0]
-    decay = decays(rate_ref, span)
+    decay = decays(rate_ref, half_ref, span)
     part = first_ref.shape[0] // len(in_refs)
     for b in range(part):
         for k, in_ref in enumerate(in_refs):
             at = b if len(in_refs) == 1 else (here * part if k == 0 else part - here * part) + b
             for m in range(MODES):
                 chain = in_ref[b, m]
+                if len(in_refs) == 1:
+                    chain = jnp.where(here == 1, chain, 0.0)
                 after = decay[m] * chain + first_ref[at, m]
                 keep_ref[at, m] = jnp.where(left_here, chain, after)
                 send_ref[at, m] = jnp.where(left_here, after, chain)
@@ -337,16 +338,15 @@
     )(in_hbm(image), in_hbm(rate))
 
 
-def prefix(edges, rate, span):
-    def kernel(edge_ref, rate_ref, out_ref):
-        prefix_kernel(span, edge_ref, rate_ref, out_ref)
-
-    return pl.pallas_call(
-        kernel,
+def prefix(half, edges, rate, span):
+    return pl.pallas_call(
+        functools.partial(prefix_kernel, span),
+        in_specs=[SMEM, VMEM, VMEM],
+        out_specs=VMEM,
         out_shape=jax.ShapeDtypeStruct(edges.shape, F32),
         compiler_params=params(8),
         name="prefix",
-    )(edges, rate)
+    )(half, edges, rate)
 
 
 def local_scan(block, rate, coef, name, scale):
@@ -392,7 +392,7 @@
 def small(kernel, name, outs, *operands):
     return pl.pallas_call(
         kernel,
-        in_specs=[SMEM] * 2 + [VMEM] * (len(operands) - 2),
+        in_specs=[SMEM] * 3 + [VMEM] * (len(operands) - 3),
         out_specs=[VMEM] * len(outs),
         out_shape=[jax.ShapeDtypeStruct(shape, F32) for shape in outs],
         compiler_params=params(8),
@@ -441,23 +441,22 @@
 
 def on_device(image, vert_rate, vert_coef, horiz_rate, horiz_coef, w_in, w_out):
     rows, cols = lax.axis_size("row"), lax.axis_size("col")
-    piece = lax.axis_index("row")
+    piece_half = (lax.axis_index("row") // (rows // 2)).reshape(1)
     col = lax.axis_index("col").reshape(1)
     core, chip = col % 2, col // 2
     side = [core, chip % 2, chip // 2 % 2]
     upper = chip // 4
     here = [side[1] ^ upper, side[2] ^ upper, upper]
-    rate_along = lax.dynamic_slice_in_dim(horiz_rate, core[0] * LANES, LANES, 1)
 
     edges = row_edges(image, vert_rate).reshape(rows, 8, 8, LANES)
     edges = lax.all_to_all(edges, "row", 0, 0, tiled=True)
-    rate = lax.dynamic_slice_in_dim(vert_rate, (piece // 8) * LANES, LANES, 1)
     local = local_scan(image, vert_rate, vert_coef, "vert_local", 0.5)
-    edges, local, side, here, rate_along = lax.optimization_barrier((edges, local, side, here, rate_along))
-    incoming = prefix(edges, rate, 64.0)
+    edges, local, side, here = lax.optimization_barrier((edges, local, side, here))
+    core = side[0]
+    incoming = prefix(piece_half, edges, vert_rate, 64.0)
     incoming = lax.all_to_all(incoming, "row", 0, 0, tiled=True).reshape(2, 8, 8, 8, LANES)
 
-    act, mine, other = act_and_edges(side[0], local, incoming, vert_rate, vert_coef, horiz_rate)
+    act, mine, other = act_and_edges(core, local, incoming, vert_rate, vert_coef, horiz_rate)
 
     eight, four, two = (8, 8, 8, LANES), (4, 8, 8, LANES), (2, 8, 8, LANES)
 
@@ -466,26 +465,25 @@
 
     def join(level, outs, keep, came):
         kernel = functools.partial(join_kernel, 64.0 * 2**level)
-        return small(kernel, f"join_{level}", outs, side[level], here[level], keep, came, rate_along)
+        return small(kernel, f"join_{level}", outs, core, side[level], here[level], keep, came, horiz_rate)
 
     def part(level, shape, chains, first):
         kernel = functools.partial(part_kernel, 64.0 * 2**level)
-        return small(kernel, f"part_{level}", [shape] * 2, side[level], here[level], *chains, first, rate_along)
+        return small(kernel, f"part_{level}", [shape] * 2, core, side[level], here[level], *chains, first, horiz_rate)
 
     first_tile, keep, send = join(0, [eight, four, four], mine, swap(other, 1))
     came, local = together(swap(send, 2), horiz(0, None))
     first_chip, keep, send = join(1, [four, two, two], keep, came)
     came, local = together(swap(send, 4), horiz(1, local))
     first_pair, group = join(2, [two, two], keep, came)
-    chain = lax.ppermute(group, "col", [(i, i ^ (cols - 2)) for i in range(cols // 2)])
-    chain, local = together(chain, horiz(2, local))
+    chain, local = together(swap(group, cols - 2), horiz(2, local))
     keep, send = part(2, two, [chain], first_pair)
     came, local = together(swap(send, 4), horiz(3, local))
     keep, send = part(1, four, [keep, came], first_chip)
     keep, send = part(0, eight, [keep, swap(send, 2)], first_tile)
     got = swap(send, 1)
 
-    return mix(side[0], local, keep, got, horiz_rate, horiz_coef, w_in, w_out)
+    return mix(core, local, keep, got, horiz_rate, horiz_coef, w_in, w_out)
 
 
 def solution(mesh):

time: 95 us -> 91.9 us (0.967)
  starting transfers between devices: 27.3 us -> 25.7 us
  blocking collectives: 14.5 us -> 13.1 us
  local copies, waits for them, and re-layouts: 1.41 us -> 0.04 us
  waiting for transfers between devices: 8.18 us -> 9.5 us
    ppermute x1 -> x0, starting transfers between devices: 5.88 us -> none  [on_device(): lax.ppermute(group, 'col', [(i, i ^ cols - 2) for i in range(cols // 2)])]
    ppermute x6 -> x7, starting transfers between devices: 13.8 us -> 18.1 us  [swap(): return lax.ppermute(block, 'col', [(i, i ^ bits) for i in range(n)])]
    all_to_all x1, blocking collectives: 14.5 us -> 13.1 us  [on_device(): lax.all_to_all(incoming, 'row', 0, 0, tiled=True).reshape(2, 8, 8, 8, LANES)]
    dynamic_slice x2 -> x0, local copies, waits for them, and re-layouts: 1.38 us -> none  [the longest x1 0.69 us: on_device(): rate = lax.dynamic_slice_in_dim(vert_rate, piece // 8 * LANES, LANES, 1)]
    all_to_all x1, waiting for transfers between devices: 2.03 us -> 3.35 us  [on_device(): edges = lax.all_to_all(edges, 'row', 0, 0, tiled=True)]
    ppermute x6 -> x7, waiting for transfers between devices: 6.15 us -> 6.16 us  [swap(): return lax.ppermute(block, 'col', [(i, i ^ bits) for i in range(n)])]
  transfers between devices with their start and end apart: 8 -> 8, of which waited for: 5 -> 5; matrix products, arithmetic and copies ran while one was open for 1% -> 0% of each run, Pallas kernels for 20% -> 21%
where the time goes in v10:
time: 91.9 us; the launch traced here: 91.5 us
  Pallas kernels  42.9 us (47%)
  starting transfers between devices  25.7 us (28%)
  blocking collectives  13.1 us (14%)
  waiting for transfers between devices  9.5 us (10%)
    ppermute x7, starting transfers between devices, swap(): return lax.ppermute(block, 'col', [(i, i ^ bits) for i in range(n)])  18.1 us
    all_to_all x1, blocking collectives, on_device(): lax.all_to_all(incoming, 'row', 0, 0, tiled=True).reshape(2, 8, 8, 8, LANES)  13.1 us
    pallas_call x4, Pallas kernels, local_piece(): pl.pallas_call(functools.partial(piece_kernel, part), in_specs=[HBM, VMEM...  11.9 us
    pallas_call x1, Pallas kernels, mix(): pl.pallas_call(mix_kernel, grid=(64 // MIX_ROWS,), in_specs=[SMEM, pl.Blo...  10.7 us
    pallas_call x1, Pallas kernels, act_and_edges(): pl.pallas_call(act_kernel, grid=(64 // ACT_ROWS,), in_specs=[SMEM, pl.Blo...  8.51 us
    all_to_all x1, starting transfers between devices, on_device(): edges = lax.all_to_all(edges, 'row', 0, 0, tiled=True)  7.6 us
    pallas_call x1, Pallas kernels, local_scan(): pl.pallas_call(functools.partial(local_kernel, scale), in_specs=[HBM, HBM...  7.02 us
    ppermute x7, waiting for transfers between devices, swap(): return lax.ppermute(block, 'col', [(i, i ^ bits) for i in range(n)])  6.16 us
  transfers between devices with their start and end apart: 8, of which 5 were waited for; matrix products, arithmetic and copies ran while one was open for 0% of the time, Pallas kernels for 21%

profile of v10, /device:TPU:1, one launch (start us, length us, event | category | flops | bytes accessed | tf_op | source)
XLA Modules:
  0.0 91.5 jit_solution(10553555950000026495)
XLA Ops:
  0.0 4.4 %row_edges.1 = f32[2,8,8,8,128]{4,3,2,1,0:T(8,128)} custom-call(bf16[64,64,256]{2,1,0:T(8,128)(2,1)} %block_ref.1, f32[8,256]{1,0:T(8,128)} %vr_ref.1), custom_call_target="tpu_custom_call" | custom-call | tf_op jit(solution)/shard_map/row_edges/pallas_call | solution.py:326
  4.4 7.6 %all-to-all-start = ((f32[16,8,8,128]{3,2,1,0:T(8,128)}), f32[16,8,8,128]{3,2,1,0:T(8,128)S(1)}, u32[]{:S(2)}, u32[]{:S(2)}) async-start(f32[16,8,8,128]{3,2,1,0:T(8,128)} %bitcast), calls=%async_computation | async-start | bytes 1048576 | tf_op jit(solution)/shard_map/all_to_all | solution.py:452
  12.1 0.0 copy-start.4
  12.1 0.0 copy-start
  12.1 0.0 copy-start.5
  12.1 7.0 %vert_local.1.local_ref = f32[64,64,256]{2,1,0:T(8,128)} custom-call(bf16[64,64,256]{2,1,0:T(8,128)(2,1)} %block_ref.1, f32[8,256]{1,0:T(8,128)} %vr_ref.1, f32[8,256]{1,0:T(8,128)} %vc_ref.1), custom_call_target="tpu_custom_call" | custom-call | flops 5000000000 | bytes 8000000 | tf_op jit(solution)/shard_map/vert_local/pallas_call | solution.py:353
  19.2 0.0 copy-start.3
  19.2 3.3 %all-to-all-done.edge_ref = f32[16,8,8,128]{3,2,1,0:T(8,128)S(1)} async-done(((f32[16,8,8,128]{3,2,1,0:T(8,128)}), f32[16,8,8,128]{3,2,1,0:T(8,128)S(1)}, u32[]{:S(2)}, u32[]{:S(2)}) %all-to-all-start) | async-done | bytes 524320 | tf_op jit(solution)/shard_map/all_to_all | solution.py:452
  22.5 0.0 copy-done.4
  22.5 0.1 prefix.1
  22.6 13.1 %all_to_all.10 = f32[16,8,8,128]{3,2,1,0:T(8,128)S(1)} all-to-all(f32[16,8,8,128]{3,2,1,0:T(8,128)S(1)} %prefix.1), channel_id=1, replica_groups=mesh['row'=16,'col'=16] {'row'}, dimensions={0} | all-to-all | bytes 1048576 | tf_op jit(solution)/shard_map/all_to_all | solution.py:457
  35.7 0.0 copy-done
  35.7 0.0 copy-done.5
  35.7 8.5 %act_and_edges.1 = (bf16[64,64,256]{2,1,0:T(8,128)(2,1)}, f32[8,8,8,128]{3,2,1,0:T(8,128)S(1)}, f32[8,8,8,128]{3,2,1,0:T(8,128)S(1)}) custom-call(s32[1]{0:T(128)S(6)} %select_n.30.core_ref.half_ref.left_ref, f32[64,64,256]{2,1,0:T(8,128)} %vert_local.1.local_ref, f32[2,8,8,8,128]{4,3,2,1,0:T(8,128)S(1)} %bitcast.4, f32[8,256]{1,0:T(8,128)S(1)} %copy-done.4, ...), custom_call_target="tpu_custom_call" | custom-call | tf_op jit(solution)/shard_map/act_and_edges/pallas_call | solution.py:405
  44.2 2.6 %collective-permute-start = (f32[8,8,8,128]{3,2,1,0:T(8,128)S(1)}, f32[8,8,8,128]{3,2,1,0:T(8,128)S(1)}, u32[]{:S(2)}, u32[]{:S(2)}) collective-permute-start(f32[8,8,8,128]{3,2,1,0:T(8,128)S(1)} %get-tuple-element.47), channel_id=1, source_target_pairs={{0,1},{1,0},{2,3},{3,2},{4,5},{5,4},{6,7},{7,6},{8,9},{9,8},{10,11... | collective-permute-start | bytes 786440 | tf_op jit(solution)/shard_map/ppermute | solution.py:435
  46.8 1.2 %collective-permute-done.came_ref = f32[8,8,8,128]{3,2,1,0:T(8,128)S(1)} collective-permute-done((f32[8,8,8,128]{3,2,1,0:T(8,128)S(1)}, f32[8,8,8,128]{3,2,1,0:T(8,128)S(1)}, u32[]{:S(2)}, u32[]{:S(2)}) %collective-permute-start) | collective-permute-done | bytes 262176 | tf_op jit(solution)/shard_map/ppermute | solution.py:435
  47.9 0.1 join_0.1
  48.0 1.7 %collective-permute-start.1 = (f32[4,8,8,128]{3,2,1,0:T(8,128)S(1)}, f32[4,8,8,128]{3,2,1,0:T(8,128)S(1)}, u32[]{:S(2)}, u32[]{:S(2)}) collective-permute-start(f32[4,8,8,128]{3,2,1,0:T(8,128)S(1)} %get-tuple-element.49), channel_id=1, source_target_pairs={{0,2},{1,3},{2,0},{3,1},{4,6},{5,7},{6,4},{7,5},{8,10},{9,11},{10,... | collective-permute-start | bytes 393224 | tf_op jit(solution)/shard_map/ppermute | solution.py:435
  49.7 0.0 copy-done.3
  49.7 2.9 %horiz_local_0.1.refs_0_ = f32[64,64,256]{2,1,0:T(8,128)} custom-call(bf16[64,64,256]{2,1,0:T(8,128)(2,1)} %get-tuple-element.50.block_ref, f32[8,256]{1,0:T(8,128)S(1)} %copy-done, f32[8,256]{1,0:T(8,128)S(1)} %copy-done.3), custom_call_target="tpu_custom_call" | custom-call | flops 1250000000 | bytes 2000000 | tf_op jit(solution)/shard_map/horiz_local_0/pallas_call | solution.py:374
  52.7 0.5 collective-permute-done.1.came_ref
  53.2 3.1 %collective-permute-start.2 = (f32[2,8,8,128]{3,2,1,0:T(8,128)S(1)}, f32[2,8,8,128]{3,2,1,0:T(8,128)S(1)}, u32[]{:S(2)}, u32[]{:S(2)}) collective-permute-start(f32[2,8,8,128]{3,2,1,0:T(8,128)S(1)} %get-tuple-element.53), channel_id=1, source_target_pairs={{0,4},{1,5},{2,6},{3,7},{4,0},{5,1},{6,2},{7,3},{8,12},{9,13},{10,... | collective-permute-start | bytes 196616 | tf_op jit(solution)/shard_map/ppermute | solution.py:435
  56.3 2.9 %horiz_local_1.1.refs_0_ = f32[64,64,256]{2,1,0:T(8,128)} custom-call(bf16[64,64,256]{2,1,0:T(8,128)(2,1)} %get-tuple-element.50.block_ref, f32[8,256]{1,0:T(8,128)S(1)} %copy-done, f32[8,256]{1,0:T(8,128)S(1)} %copy-done.3, f32[64,64,256]{2,1,0:T(8,128)} %horiz_local_0.1.refs_0_), custom_call_target="tpu_custom_call", output_to_operand_aliasing={{}: (3, {})} | custom-call | flops 1250000000 | bytes 2000000 | tf_op jit(solution)/shard_map/horiz_local_1/pallas_call | solution.py:374
  59.2 0.0 collective-permute-done.2.came_ref
  59.3 4.1 %collective-permute-start.3 = (f32[2,8,8,128]{3,2,1,0:T(8,128)S(1)}, f32[2,8,8,128]{3,2,1,0:T(8,128)S(1)}, u32[]{:S(2)}, u32[]{:S(2)}) collective-permute-start(f32[2,8,8,128]{3,2,1,0:T(8,128)S(1)} %get-tuple-element.56), channel_id=1, source_target_pairs={{0,14},{1,15},{2,12},{3,13},{4,10},{5,11},{6,8},{7,9},{8,6},{9,7},... | collective-permute-start | bytes 196616 | tf_op jit(solution)/shard_map/ppermute | solution.py:435
  63.3 3.0 %horiz_local_2.1.refs_0_ = f32[64,64,256]{2,1,0:T(8,128)} custom-call(bf16[64,64,256]{2,1,0:T(8,128)(2,1)} %get-tuple-element.50.block_ref, f32[8,256]{1,0:T(8,128)S(1)} %copy-done, f32[8,256]{1,0:T(8,128)S(1)} %copy-done.3, f32[64,64,256]{2,1,0:T(8,128)} %horiz_local_1.1.refs_0_), custom_call_target="tpu_custom_call", output_to_operand_aliasing={{}: (3, {})} | custom-call | flops 1250000000 | bytes 2000000 | tf_op jit(solution)/shard_map/horiz_local_2/pallas_call | solution.py:374
  66.4 0.0 collective-permute-done.3.refs_0_
  66.4 0.0 copy-start.1
  66.4 0.0 copy-start.2
  66.4 1.6 %collective-permute-start.4 = (f32[2,8,8,128]{3,2,1,0:T(8,128)S(1)}, f32[2,8,8,128]{3,2,1,0:T(8,128)S(1)}, u32[]{:S(2)}, u32[]{:S(2)}) collective-permute-start(f32[2,8,8,128]{3,2,1,0:T(8,128)S(1)} %get-tuple-element.60), channel_id=1, source_target_pairs={{0,4},{1,5},{2,6},{3,7},{4,0},{5,1},{6,2},{7,3},{8,12},{9,13},{10,... | collective-permute-start | bytes 196616 | tf_op jit(solution)/shard_map/ppermute | solution.py:435
  68.0 3.0 %horiz_local_3.1.local_ref = f32[64,64,256]{2,1,0:T(8,128)} custom-call(bf16[64,64,256]{2,1,0:T(8,128)(2,1)} %get-tuple-element.50.block_ref, f32[8,256]{1,0:T(8,128)S(1)} %copy-done, f32[8,256]{1,0:T(8,128)S(1)} %copy-done.3, f32[64,64,256]{2,1,0:T(8,128)} %horiz_local_2.1.refs_0_), custom_call_target="tpu_custom_call", output_to_operand_aliasing={{}: (3, {})} | custom-call | flops 1250000000 | bytes 2000000 | tf_op jit(solution)/shard_map/horiz_local_3/pallas_call | solution.py:374
  71.1 0.0 collective-permute-done.4.refs_1_
  71.1 0.6 collective-permute-start.5
  71.7 3.3 %collective-permute-done.5.refs_1_ = f32[4,8,8,128]{3,2,1,0:T(8,128)S(1)} collective-permute-done((f32[4,8,8,128]{3,2,1,0:T(8,128)S(1)}, f32[4,8,8,128]{3,2,1,0:T(8,128)S(1)}, u32[]{:S(2)}, u32[]{:S(2)}) %collective-permute-start.5) | collective-permute-done | bytes 131104 | tf_op jit(solution)/shard_map/ppermute | solution.py:435
  75.0 0.1 part_0.1
  75.1 4.5 %collective-permute-start.6 = (f32[8,8,8,128]{3,2,1,0:T(8,128)S(1)}, f32[8,8,8,128]{3,2,1,0:T(8,128)S(1)}, u32[]{:S(2)}, u32[]{:S(2)}) collective-permute-start(f32[8,8,8,128]{3,2,1,0:T(8,128)S(1)} %get-tuple-element.70), channel_id=1, source_target_pairs={{0,1},{1,0},{2,3},{3,2},{4,5},{5,4},{6,7},{7,6},{8,9},{9,8},{10,11... | collective-permute-start | bytes 786440 | tf_op jit(solution)/shard_map/ppermute | solution.py:435
  79.6 1.2 %collective-permute-done.6.got_ref = f32[8,8,8,128]{3,2,1,0:T(8,128)S(1)} collective-permute-done((f32[8,8,8,128]{3,2,1,0:T(8,128)S(1)}, f32[8,8,8,128]{3,2,1,0:T(8,128)S(1)}, u32[]{:S(2)}, u32[]{:S(2)}) %collective-permute-start.6) | collective-permute-done | bytes 262176 | tf_op jit(solution)/shard_map/ppermute | solution.py:435
  80.7 0.0 copy-done.1
  80.7 0.0 copy-done.2
  80.7 10.7 %mix.1 = bf16[64,64,256]{2,1,0:T(8,128)(2,1)} custom-call(s32[1]{0:T(128)S(6)} %select_n.30.core_ref.half_ref.left_ref, f32[64,64,256]{2,1,0:T(8,128)} %horiz_local_3.1.local_ref, f32[8,8,8,128]{3,2,1,0:T(8,128)S(1)} %get-tuple-element.69.keep_ref, f32[8,8,8,128]{3,2,1,0:T(8,128)S(1)} %collective-permute-done.6.got_ref, f32[8,256]{1,0:T(8,128)S(1)} %copy-done, ...), custom_call_target="tpu_custom_call" | custom-call | tf_op jit(solution)/shard_map/mix/pallas_call | solution.py:421
  (4 shorter events, 0.1 us)
Async XLA Ops:
  4.4 18.1 %all-to-all-start = ((f32[16,8,8,128]{3,2,1,0:T(8,128)}), f32[16,8,8,128]{3,2,1,0:T(8,128)S(1)}, u32[]{:S(2)}, u32[]{:S(2)}) async-start(f32[16,8,8,128]{3,2,1,0:T(8,128)} %bitcast), calls=%async_computation | async-start | bytes 1048576 | tf_op jit(solution)/shard_map/all_to_all | solution.py:452
  12.1 10.4 %copy-start.4 = (f32[8,256]{1,0:T(8,128)S(1)}, f32[8,256]{1,0:T(8,128)}, u32[]{:S(2)}) copy-start(f32[8,256]{1,0:T(8,128)} %vr_ref.1) | copy-start | bytes 24580
  12.1 23.6 %copy-start = (f32[8,256]{1,0:T(8,128)S(1)}, f32[8,256]{1,0:T(8,128)}, u32[]{:S(2)}) copy-start(f32[8,256]{1,0:T(8,128)} %hr_ref.3) | copy-start | bytes 24580
  12.1 23.6 %copy-start.5 = (f32[8,256]{1,0:T(8,128)S(1)}, f32[8,256]{1,0:T(8,128)}, u32[]{:S(2)}) copy-start(f32[8,256]{1,0:T(8,128)} %vc_ref.1) | copy-start | bytes 24580
  19.2 30.6 %copy-start.3 = (f32[8,256]{1,0:T(8,128)S(1)}, f32[8,256]{1,0:T(8,128)}, u32[]{:S(2)}) copy-start(f32[8,256]{1,0:T(8,128)} %hc_ref.1) | copy-start | bytes 24580
  44.2 3.7 %collective-permute-start = (f32[8,8,8,128]{3,2,1,0:T(8,128)S(1)}, f32[8,8,8,128]{3,2,1,0:T(8,128)S(1)}, u32[]{:S(2)}, u32[]{:S(2)}) collective-permute-start(f32[8,8,8,128]{3,2,1,0:T(8,128)S(1)} %get-tuple-element.47), channel_id=1, source_target_pairs={{0,1},{1,0},{2,3},{3,2},{4,5},{5,4},{6,7},{7,6},{8,9},{9,8},{10,11... | collective-permute-start | bytes 786440 | tf_op jit(solution)/shard_map/ppermute | solution.py:435
  48.0 5.2 %collective-permute-start.1 = (f32[4,8,8,128]{3,2,1,0:T(8,128)S(1)}, f32[4,8,8,128]{3,2,1,0:T(8,128)S(1)}, u32[]{:S(2)}, u32[]{:S(2)}) collective-permute-start(f32[4,8,8,128]{3,2,1,0:T(8,128)S(1)} %get-tuple-element.49), channel_id=1, source_target_pairs={{0,2},{1,3},{2,0},{3,1},{4,6},{5,7},{6,4},{7,5},{8,10},{9,11},{10,... | collective-permute-start | bytes 393224 | tf_op jit(solution)/shard_map/ppermute | solution.py:435
  53.2 6.0 %collective-permute-start.2 = (f32[2,8,8,128]{3,2,1,0:T(8,128)S(1)}, f32[2,8,8,128]{3,2,1,0:T(8,128)S(1)}, u32[]{:S(2)}, u32[]{:S(2)}) collective-permute-start(f32[2,8,8,128]{3,2,1,0:T(8,128)S(1)} %get-tuple-element.53), channel_id=1, source_target_pairs={{0,4},{1,5},{2,6},{3,7},{4,0},{5,1},{6,2},{7,3},{8,12},{9,13},{10,... | collective-permute-start | bytes 196616 | tf_op jit(solution)/shard_map/ppermute | solution.py:435
  59.3 7.1 %collective-permute-start.3 = (f32[2,8,8,128]{3,2,1,0:T(8,128)S(1)}, f32[2,8,8,128]{3,2,1,0:T(8,128)S(1)}, u32[]{:S(2)}, u32[]{:S(2)}) collective-permute-start(f32[2,8,8,128]{3,2,1,0:T(8,128)S(1)} %get-tuple-element.56), channel_id=1, source_target_pairs={{0,14},{1,15},{2,12},{3,13},{4,10},{5,11},{6,8},{7,9},{8,6},{9,7},... | collective-permute-start | bytes 196616 | tf_op jit(solution)/shard_map/ppermute | solution.py:435
  66.4 14.3 %copy-start.1 = (bf16[256,1024]{1,0:T(8,128)(2,1)S(1)}, bf16[256,1024]{1,0:T(8,128)(2,1)}, u32[]{:S(2)}) copy-start(bf16[256,1024]{1,0:T(8,128)(2,1)} %w_in_ref.1) | copy-start | bytes 1572868
  66.4 14.3 %copy-start.2 = (bf16[1024,256]{1,0:T(8,128)(2,1)S(1)}, bf16[1024,256]{1,0:T(8,128)(2,1)}, u32[]{:S(2)}) copy-start(bf16[1024,256]{1,0:T(8,128)(2,1)} %w_out_ref.1) | copy-start | bytes 1572868
  66.4 4.6 %collective-permute-start.4 = (f32[2,8,8,128]{3,2,1,0:T(8,128)S(1)}, f32[2,8,8,128]{3,2,1,0:T(8,128)S(1)}, u32[]{:S(2)}, u32[]{:S(2)}) collective-permute-start(f32[2,8,8,128]{3,2,1,0:T(8,128)S(1)} %get-tuple-element.60), channel_id=1, source_target_pairs={{0,4},{1,5},{2,6},{3,7},{4,0},{5,1},{6,2},{7,3},{8,12},{9,13},{10,... | collective-permute-start | bytes 196616 | tf_op jit(solution)/shard_map/ppermute | solution.py:435
  71.1 3.9 %collective-permute-start.5 = (f32[4,8,8,128]{3,2,1,0:T(8,128)S(1)}, f32[4,8,8,128]{3,2,1,0:T(8,128)S(1)}, u32[]{:S(2)}, u32[]{:S(2)}) collective-permute-start(f32[4,8,8,128]{3,2,1,0:T(8,128)S(1)} %get-tuple-element.67), channel_id=1, source_target_pairs={{0,2},{1,3},{2,0},{3,1},{4,6},{5,7},{6,4},{7,5},{8,10},{9,11},{10,... | collective-permute-start | bytes 393224 | tf_op jit(solution)/shard_map/ppermute | solution.py:435
  75.1 5.6 %collective-permute-start.6 = (f32[8,8,8,128]{3,2,1,0:T(8,128)S(1)}, f32[8,8,8,128]{3,2,1,0:T(8,128)S(1)}, u32[]{:S(2)}, u32[]{:S(2)}) collective-permute-start(f32[8,8,8,128]{3,2,1,0:T(8,128)S(1)} %get-tuple-element.70), channel_id=1, source_target_pairs={{0,1},{1,0},{2,3},{3,2},{4,5},{5,4},{6,7},{7,6},{8,9},{9,8},{10,11... | collective-permute-start | bytes 786440 | tf_op jit(solution)/shard_map/ppermute | solution.py:435

commit v11 on v10

--- a/solution.py
+++ b/solution.py
@@ -180,34 +180,34 @@
     out_ref, block, result, arrived, left = refs[-5:]
     rows = pl.ds(part * 16, 16)
 
-    def fetch(half):
-        lanes = pl.ds(half * LANES, LANES)
-        return pltpu.make_async_copy(block_ref.at[:, rows, lanes], block.at[:, :, lanes], arrived.at[half])
-
-    def put(half):
-        lanes = pl.ds(half * LANES, LANES)
-        return pltpu.make_async_copy(result.at[:, :, lanes], out_ref.at[:, rows, lanes], left.at[half])
-
-    for half in range(2):
-        fetch(half).start()
+    def fetch(q):
+        cols = pl.ds(q * 16, 16)
+        return pltpu.make_async_copy(block_ref.at[cols, rows, :], block.at[cols], arrived.at[q])
+
+    def put(half, q):
+        cols, lanes = pl.ds(q * 16, 16), pl.ds(half * LANES, LANES)
+        return pltpu.make_async_copy(
+            result.at[cols, :, lanes], out_ref.at[cols, rows, lanes], left.at[half * 4 + q]
+        )
+
+    for q in range(4):
+        fetch(q).start()
     for half in range(2):
         lanes = slice(half * LANES, (half + 1) * LANES)
         pole = poles(rate_ref, half, 16)
         weight = weights(rate_ref, coef_ref, half, 16)
-        fetch(half).wait()
-
-        def steps(j, states, lanes=lanes, pole=pole, weight=weight):
-            for k in range(16):
-                s = j * 16 + k
+        states = [jnp.zeros((16, LANES), F32)] * MODES
+        for q in range(4):
+            if half == 0:
+                fetch(q).wait()
+            for s in range(q * 16, q * 16 + 16):
                 u = block[s, :, lanes].astype(F32)
                 states = [p * h + u for p, h in zip(pole, states)]
                 result[s, :, lanes] = tree([q * h for q, h in zip(weight, states)])
-            return states
-
-        lax.fori_loop(0, 4, steps, [jnp.zeros((16, LANES), F32)] * MODES)
-        put(half).start()
+            put(half, q).start()
     for half in range(2):
-        put(half).wait()
+        for q in range(4):
+            put(half, q).wait()
 
 
 def act_kernel(core_ref, local_ref, in_ref, vr_ref, vc_ref, hr_ref, act_ref, mine_ref, other_ref, tails, field):
@@ -380,8 +380,8 @@
         scratch_shapes=[
             pltpu.VMEM((64, 16, 256), BF16),
             pltpu.VMEM((64, 16, 256), F32),
-            pltpu.SemaphoreType.DMA((2,)),
-            pltpu.SemaphoreType.DMA((2,)),
+            pltpu.SemaphoreType.DMA((4,)),
+            pltpu.SemaphoreType.DMA((8,)),
         ],
         compiler_params=params(8),
         cost_estimate=pl.CostEstimate(flops=1_250_000_000, bytes_accessed=2_000_000, transcendentals=0),

time: 91.9 us -> 91.7 us (level)
  transfers between devices with their start and end apart: 8 -> 8, of which waited for: 5 -> 5; matrix products, arithmetic and copies ran while one was open for 0% -> 0% of each run, Pallas kernels for 21% -> 20%
where the time goes in v11:
time: 91.7 us; the launch traced here: 91.3 us
  Pallas kernels  42.2 us (46%)
  starting transfers between devices  26 us (28%)
  blocking collectives  13.1 us (14%)
  waiting for transfers between devices  9.67 us (11%)
    ppermute x7, starting transfers between devices, swap(): return lax.ppermute(block, 'col', [(i, i ^ bits) for i in range(n)])  18.4 us
    all_to_all x1, blocking collectives, on_device(): lax.all_to_all(incoming, 'row', 0, 0, tiled=True).reshape(2, 8, 8, 8, LANES)  13.1 us
    pallas_call x4, Pallas kernels, local_piece(): pl.pallas_call(functools.partial(piece_kernel, part), in_specs=[HBM, VMEM...  11.2 us
    pallas_call x1, Pallas kernels, mix(): pl.pallas_call(mix_kernel, grid=(64 // MIX_ROWS,), in_specs=[SMEM, pl.Blo...  10.7 us
    pallas_call x1, Pallas kernels, act_and_edges(): pl.pallas_call(act_kernel, grid=(64 // ACT_ROWS,), in_specs=[SMEM, pl.Blo...  8.51 us
    all_to_all x1, starting transfers between devices, on_device(): edges = lax.all_to_all(edges, 'row', 0, 0, tiled=True)  7.6 us
    pallas_call x1, Pallas kernels, local_scan(): pl.pallas_call(functools.partial(local_kernel, scale), in_specs=[HBM, HBM...  7.02 us
    ppermute x7, waiting for transfers between devices, swap(): return lax.ppermute(block, 'col', [(i, i ^ bits) for i in range(n)])  6.32 us
  transfers between devices with their start and end apart: 8, of which 5 were waited for; matrix products, arithmetic and copies ran while one was open for 0% of the time, Pallas kernels for 20%

profile of v11, /device:TPU:1, one launch (start us, length us, event | category | flops | bytes accessed | tf_op | source)
XLA Modules:
  0.0 91.3 jit_solution(16244836810316833577)
XLA Ops:
  0.0 4.4 %row_edges.1 = f32[2,8,8,8,128]{4,3,2,1,0:T(8,128)} custom-call(bf16[64,64,256]{2,1,0:T(8,128)(2,1)} %block_ref.1, f32[8,256]{1,0:T(8,128)} %vr_ref.1), custom_call_target="tpu_custom_call" | custom-call | tf_op jit(solution)/shard_map/row_edges/pallas_call | solution.py:326
  4.4 7.6 %all-to-all-start = ((f32[16,8,8,128]{3,2,1,0:T(8,128)}), f32[16,8,8,128]{3,2,1,0:T(8,128)S(1)}, u32[]{:S(2)}, u32[]{:S(2)}) async-start(f32[16,8,8,128]{3,2,1,0:T(8,128)} %bitcast), calls=%async_computation | async-start | bytes 1048576 | tf_op jit(solution)/shard_map/all_to_all | solution.py:452
  12.1 0.0 copy-start.4
  12.1 0.0 copy-start
  12.1 0.0 copy-start.5
  12.1 7.0 %vert_local.1.local_ref = f32[64,64,256]{2,1,0:T(8,128)} custom-call(bf16[64,64,256]{2,1,0:T(8,128)(2,1)} %block_ref.1, f32[8,256]{1,0:T(8,128)} %vr_ref.1, f32[8,256]{1,0:T(8,128)} %vc_ref.1), custom_call_target="tpu_custom_call" | custom-call | flops 5000000000 | bytes 8000000 | tf_op jit(solution)/shard_map/vert_local/pallas_call | solution.py:353
  19.2 0.0 copy-start.3
  19.2 3.3 %all-to-all-done.edge_ref = f32[16,8,8,128]{3,2,1,0:T(8,128)S(1)} async-done(((f32[16,8,8,128]{3,2,1,0:T(8,128)}), f32[16,8,8,128]{3,2,1,0:T(8,128)S(1)}, u32[]{:S(2)}, u32[]{:S(2)}) %all-to-all-start) | async-done | bytes 524320 | tf_op jit(solution)/shard_map/all_to_all | solution.py:452
  22.5 0.0 copy-done.4
  22.5 0.1 prefix.1
  22.6 13.1 %all_to_all.10 = f32[16,8,8,128]{3,2,1,0:T(8,128)S(1)} all-to-all(f32[16,8,8,128]{3,2,1,0:T(8,128)S(1)} %prefix.1), channel_id=1, replica_groups=mesh['row'=16,'col'=16] {'row'}, dimensions={0} | all-to-all | bytes 1048576 | tf_op jit(solution)/shard_map/all_to_all | solution.py:457
  35.7 0.0 copy-done
  35.7 0.0 copy-done.5
  35.7 8.5 %act_and_edges.1 = (bf16[64,64,256]{2,1,0:T(8,128)(2,1)}, f32[8,8,8,128]{3,2,1,0:T(8,128)S(1)}, f32[8,8,8,128]{3,2,1,0:T(8,128)S(1)}) custom-call(s32[1]{0:T(128)S(6)} %select_n.30.core_ref.half_ref.left_ref, f32[64,64,256]{2,1,0:T(8,128)} %vert_local.1.local_ref, f32[2,8,8,8,128]{4,3,2,1,0:T(8,128)S(1)} %bitcast.4, f32[8,256]{1,0:T(8,128)S(1)} %copy-done.4, ...), custom_call_target="tpu_custom_call" | custom-call | tf_op jit(solution)/shard_map/act_and_edges/pallas_call | solution.py:405
  44.2 2.6 %collective-permute-start = (f32[8,8,8,128]{3,2,1,0:T(8,128)S(1)}, f32[8,8,8,128]{3,2,1,0:T(8,128)S(1)}, u32[]{:S(2)}, u32[]{:S(2)}) collective-permute-start(f32[8,8,8,128]{3,2,1,0:T(8,128)S(1)} %get-tuple-element.47), channel_id=1, source_target_pairs={{0,1},{1,0},{2,3},{3,2},{4,5},{5,4},{6,7},{7,6},{8,9},{9,8},{10,11... | collective-permute-start | bytes 786440 | tf_op jit(solution)/shard_map/ppermute | solution.py:435
  46.8 1.2 %collective-permute-done.came_ref = f32[8,8,8,128]{3,2,1,0:T(8,128)S(1)} collective-permute-done((f32[8,8,8,128]{3,2,1,0:T(8,128)S(1)}, f32[8,8,8,128]{3,2,1,0:T(8,128)S(1)}, u32[]{:S(2)}, u32[]{:S(2)}) %collective-permute-start) | collective-permute-done | bytes 262176 | tf_op jit(solution)/shard_map/ppermute | solution.py:435
  47.9 0.1 join_0.1
  48.0 1.7 %collective-permute-start.1 = (f32[4,8,8,128]{3,2,1,0:T(8,128)S(1)}, f32[4,8,8,128]{3,2,1,0:T(8,128)S(1)}, u32[]{:S(2)}, u32[]{:S(2)}) collective-permute-start(f32[4,8,8,128]{3,2,1,0:T(8,128)S(1)} %get-tuple-element.49), channel_id=1, source_target_pairs={{0,2},{1,3},{2,0},{3,1},{4,6},{5,7},{6,4},{7,5},{8,10},{9,11},{10,... | collective-permute-start | bytes 393224 | tf_op jit(solution)/shard_map/ppermute | solution.py:435
  49.7 0.0 copy-done.3
  49.7 2.8 %horiz_local_0.1.refs_0_ = f32[64,64,256]{2,1,0:T(8,128)} custom-call(bf16[64,64,256]{2,1,0:T(8,128)(2,1)} %get-tuple-element.50.block_ref, f32[8,256]{1,0:T(8,128)S(1)} %copy-done, f32[8,256]{1,0:T(8,128)S(1)} %copy-done.3), custom_call_target="tpu_custom_call" | custom-call | flops 1250000000 | bytes 2000000 | tf_op jit(solution)/shard_map/horiz_local_0/pallas_call | solution.py:374
  52.5 0.7 collective-permute-done.1.came_ref
  53.2 3.1 %collective-permute-start.2 = (f32[2,8,8,128]{3,2,1,0:T(8,128)S(1)}, f32[2,8,8,128]{3,2,1,0:T(8,128)S(1)}, u32[]{:S(2)}, u32[]{:S(2)}) collective-permute-start(f32[2,8,8,128]{3,2,1,0:T(8,128)S(1)} %get-tuple-element.53), channel_id=1, source_target_pairs={{0,4},{1,5},{2,6},{3,7},{4,0},{5,1},{6,2},{7,3},{8,12},{9,13},{10,... | collective-permute-start | bytes 196616 | tf_op jit(solution)/shard_map/ppermute | solution.py:435
  56.3 2.8 %horiz_local_1.1.refs_0_ = f32[64,64,256]{2,1,0:T(8,128)} custom-call(bf16[64,64,256]{2,1,0:T(8,128)(2,1)} %get-tuple-element.50.block_ref, f32[8,256]{1,0:T(8,128)S(1)} %copy-done, f32[8,256]{1,0:T(8,128)S(1)} %copy-done.3, f32[64,64,256]{2,1,0:T(8,128)} %horiz_local_0.1.refs_0_), custom_call_target="tpu_custom_call", output_to_operand_aliasing={{}: (3, {})} | custom-call | flops 1250000000 | bytes 2000000 | tf_op jit(solution)/shard_map/horiz_local_1/pallas_call | solution.py:374
  59.1 0.0 collective-permute-done.2.came_ref
  59.2 4.2 %collective-permute-start.3 = (f32[2,8,8,128]{3,2,1,0:T(8,128)S(1)}, f32[2,8,8,128]{3,2,1,0:T(8,128)S(1)}, u32[]{:S(2)}, u32[]{:S(2)}) collective-permute-start(f32[2,8,8,128]{3,2,1,0:T(8,128)S(1)} %get-tuple-element.56), channel_id=1, source_target_pairs={{0,14},{1,15},{2,12},{3,13},{4,10},{5,11},{6,8},{7,9},{8,6},{9,7},... | collective-permute-start | bytes 196616 | tf_op jit(solution)/shard_map/ppermute | solution.py:435
  63.3 2.8 %horiz_local_2.1.refs_0_ = f32[64,64,256]{2,1,0:T(8,128)} custom-call(bf16[64,64,256]{2,1,0:T(8,128)(2,1)} %get-tuple-element.50.block_ref, f32[8,256]{1,0:T(8,128)S(1)} %copy-done, f32[8,256]{1,0:T(8,128)S(1)} %copy-done.3, f32[64,64,256]{2,1,0:T(8,128)} %horiz_local_1.1.refs_0_), custom_call_target="tpu_custom_call", output_to_operand_aliasing={{}: (3, {})} | custom-call | flops 1250000000 | bytes 2000000 | tf_op jit(solution)/shard_map/horiz_local_2/pallas_call | solution.py:374
  66.2 0.0 collective-permute-done.3.refs_0_
  66.2 0.0 copy-start.1
  66.2 0.0 copy-start.2
  66.2 1.6 %collective-permute-start.4 = (f32[2,8,8,128]{3,2,1,0:T(8,128)S(1)}, f32[2,8,8,128]{3,2,1,0:T(8,128)S(1)}, u32[]{:S(2)}, u32[]{:S(2)}) collective-permute-start(f32[2,8,8,128]{3,2,1,0:T(8,128)S(1)} %get-tuple-element.60), channel_id=1, source_target_pairs={{0,4},{1,5},{2,6},{3,7},{4,0},{5,1},{6,2},{7,3},{8,12},{9,13},{10,... | collective-permute-start | bytes 196616 | tf_op jit(solution)/shard_map/ppermute | solution.py:435
  67.8 2.8 %horiz_local_3.1.local_ref = f32[64,64,256]{2,1,0:T(8,128)} custom-call(bf16[64,64,256]{2,1,0:T(8,128)(2,1)} %get-tuple-element.50.block_ref, f32[8,256]{1,0:T(8,128)S(1)} %copy-done, f32[8,256]{1,0:T(8,128)S(1)} %copy-done.3, f32[64,64,256]{2,1,0:T(8,128)} %horiz_local_2.1.refs_0_), custom_call_target="tpu_custom_call", output_to_operand_aliasing={{}: (3, {})} | custom-call | flops 1250000000 | bytes 2000000 | tf_op jit(solution)/shard_map/horiz_local_3/pallas_call | solution.py:374
  70.6 0.0 collective-permute-done.4.refs_1_
  70.6 0.8 collective-permute-start.5
  71.5 3.3 %collective-permute-done.5.refs_1_ = f32[4,8,8,128]{3,2,1,0:T(8,128)S(1)} collective-permute-done((f32[4,8,8,128]{3,2,1,0:T(8,128)S(1)}, f32[4,8,8,128]{3,2,1,0:T(8,128)S(1)}, u32[]{:S(2)}, u32[]{:S(2)}) %collective-permute-start.5) | collective-permute-done | bytes 131104 | tf_op jit(solution)/shard_map/ppermute | solution.py:435
  74.8 0.1 part_0.1
  74.9 4.5 %collective-permute-start.6 = (f32[8,8,8,128]{3,2,1,0:T(8,128)S(1)}, f32[8,8,8,128]{3,2,1,0:T(8,128)S(1)}, u32[]{:S(2)}, u32[]{:S(2)}) collective-permute-start(f32[8,8,8,128]{3,2,1,0:T(8,128)S(1)} %get-tuple-element.70), channel_id=1, source_target_pairs={{0,1},{1,0},{2,3},{3,2},{4,5},{5,4},{6,7},{7,6},{8,9},{9,8},{10,11... | collective-permute-start | bytes 786440 | tf_op jit(solution)/shard_map/ppermute | solution.py:435
  79.4 1.2 %collective-permute-done.6.got_ref = f32[8,8,8,128]{3,2,1,0:T(8,128)S(1)} collective-permute-done((f32[8,8,8,128]{3,2,1,0:T(8,128)S(1)}, f32[8,8,8,128]{3,2,1,0:T(8,128)S(1)}, u32[]{:S(2)}, u32[]{:S(2)}) %collective-permute-start.6) | collective-permute-done | bytes 262176 | tf_op jit(solution)/shard_map/ppermute | solution.py:435
  80.5 0.0 copy-done.1
  80.5 0.0 copy-done.2
  80.5 10.7 %mix.1 = bf16[64,64,256]{2,1,0:T(8,128)(2,1)} custom-call(s32[1]{0:T(128)S(6)} %select_n.30.core_ref.half_ref.left_ref, f32[64,64,256]{2,1,0:T(8,128)} %horiz_local_3.1.local_ref, f32[8,8,8,128]{3,2,1,0:T(8,128)S(1)} %get-tuple-element.69.keep_ref, f32[8,8,8,128]{3,2,1,0:T(8,128)S(1)} %collective-permute-done.6.got_ref, f32[8,256]{1,0:T(8,128)S(1)} %copy-done, ...), custom_call_target="tpu_custom_call" | custom-call | tf_op jit(solution)/shard_map/mix/pallas_call | solution.py:421
  (4 shorter events, 0.1 us)
Async XLA Ops:
  4.4 18.1 %all-to-all-start = ((f32[16,8,8,128]{3,2,1,0:T(8,128)}), f32[16,8,8,128]{3,2,1,0:T(8,128)S(1)}, u32[]{:S(2)}, u32[]{:S(2)}) async-start(f32[16,8,8,128]{3,2,1,0:T(8,128)} %bitcast), calls=%async_computation | async-start | bytes 1048576 | tf_op jit(solution)/shard_map/all_to_all | solution.py:452
  12.1 10.4 %copy-start.4 = (f32[8,256]{1,0:T(8,128)S(1)}, f32[8,256]{1,0:T(8,128)}, u32[]{:S(2)}) copy-start(f32[8,256]{1,0:T(8,128)} %vr_ref.1) | copy-start | bytes 24580
  12.1 23.6 %copy-start = (f32[8,256]{1,0:T(8,128)S(1)}, f32[8,256]{1,0:T(8,128)}, u32[]{:S(2)}) copy-start(f32[8,256]{1,0:T(8,128)} %hr_ref.3) | copy-start | bytes 24580
  12.1 23.6 %copy-start.5 = (f32[8,256]{1,0:T(8,128)S(1)}, f32[8,256]{1,0:T(8,128)}, u32[]{:S(2)}) copy-start(f32[8,256]{1,0:T(8,128)} %vc_ref.1) | copy-start | bytes 24580
  19.2 30.6 %copy-start.3 = (f32[8,256]{1,0:T(8,128)S(1)}, f32[8,256]{1,0:T(8,128)}, u32[]{:S(2)}) copy-start(f32[8,256]{1,0:T(8,128)} %hc_ref.1) | copy-start | bytes 24580
  44.2 3.7 %collective-permute-start = (f32[8,8,8,128]{3,2,1,0:T(8,128)S(1)}, f32[8,8,8,128]{3,2,1,0:T(8,128)S(1)}, u32[]{:S(2)}, u32[]{:S(2)}) collective-permute-start(f32[8,8,8,128]{3,2,1,0:T(8,128)S(1)} %get-tuple-element.47), channel_id=1, source_target_pairs={{0,1},{1,0},{2,3},{3,2},{4,5},{5,4},{6,7},{7,6},{8,9},{9,8},{10,11... | collective-permute-start | bytes 786440 | tf_op jit(solution)/shard_map/ppermute | solution.py:435
  48.0 5.2 %collective-permute-start.1 = (f32[4,8,8,128]{3,2,1,0:T(8,128)S(1)}, f32[4,8,8,128]{3,2,1,0:T(8,128)S(1)}, u32[]{:S(2)}, u32[]{:S(2)}) collective-permute-start(f32[4,8,8,128]{3,2,1,0:T(8,128)S(1)} %get-tuple-element.49), channel_id=1, source_target_pairs={{0,2},{1,3},{2,0},{3,1},{4,6},{5,7},{6,4},{7,5},{8,10},{9,11},{10,... | collective-permute-start | bytes 393224 | tf_op jit(solution)/shard_map/ppermute | solution.py:435
  53.2 5.9 %collective-permute-start.2 = (f32[2,8,8,128]{3,2,1,0:T(8,128)S(1)}, f32[2,8,8,128]{3,2,1,0:T(8,128)S(1)}, u32[]{:S(2)}, u32[]{:S(2)}) collective-permute-start(f32[2,8,8,128]{3,2,1,0:T(8,128)S(1)} %get-tuple-element.53), channel_id=1, source_target_pairs={{0,4},{1,5},{2,6},{3,7},{4,0},{5,1},{6,2},{7,3},{8,12},{9,13},{10,... | collective-permute-start | bytes 196616 | tf_op jit(solution)/shard_map/ppermute | solution.py:435
  59.2 7.0 %collective-permute-start.3 = (f32[2,8,8,128]{3,2,1,0:T(8,128)S(1)}, f32[2,8,8,128]{3,2,1,0:T(8,128)S(1)}, u32[]{:S(2)}, u32[]{:S(2)}) collective-permute-start(f32[2,8,8,128]{3,2,1,0:T(8,128)S(1)} %get-tuple-element.56), channel_id=1, source_target_pairs={{0,14},{1,15},{2,12},{3,13},{4,10},{5,11},{6,8},{7,9},{8,6},{9,7},... | collective-permute-start | bytes 196616 | tf_op jit(solution)/shard_map/ppermute | solution.py:435
  66.2 14.3 %copy-start.1 = (bf16[256,1024]{1,0:T(8,128)(2,1)S(1)}, bf16[256,1024]{1,0:T(8,128)(2,1)}, u32[]{:S(2)}) copy-start(bf16[256,1024]{1,0:T(8,128)(2,1)} %w_in_ref.1) | copy-start | bytes 1572868
  66.2 14.3 %copy-start.2 = (bf16[1024,256]{1,0:T(8,128)(2,1)S(1)}, bf16[1024,256]{1,0:T(8,128)(2,1)}, u32[]{:S(2)}) copy-start(bf16[1024,256]{1,0:T(8,128)(2,1)} %w_out_ref.1) | copy-start | bytes 1572868
  66.2 4.4 %collective-permute-start.4 = (f32[2,8,8,128]{3,2,1,0:T(8,128)S(1)}, f32[2,8,8,128]{3,2,1,0:T(8,128)S(1)}, u32[]{:S(2)}, u32[]{:S(2)}) collective-permute-start(f32[2,8,8,128]{3,2,1,0:T(8,128)S(1)} %get-tuple-element.60), channel_id=1, source_target_pairs={{0,4},{1,5},{2,6},{3,7},{4,0},{5,1},{6,2},{7,3},{8,12},{9,13},{10,... | collective-permute-start | bytes 196616 | tf_op jit(solution)/shard_map/ppermute | solution.py:435
  70.6 4.2 %collective-permute-start.5 = (f32[4,8,8,128]{3,2,1,0:T(8,128)S(1)}, f32[4,8,8,128]{3,2,1,0:T(8,128)S(1)}, u32[]{:S(2)}, u32[]{:S(2)}) collective-permute-start(f32[4,8,8,128]{3,2,1,0:T(8,128)S(1)} %get-tuple-element.67), channel_id=1, source_target_pairs={{0,2},{1,3},{2,0},{3,1},{4,6},{5,7},{6,4},{7,5},{8,10},{9,11},{10,... | collective-permute-start | bytes 393224 | tf_op jit(solution)/shard_map/ppermute | solution.py:435
  74.9 5.7 %collective-permute-start.6 = (f32[8,8,8,128]{3,2,1,0:T(8,128)S(1)}, f32[8,8,8,128]{3,2,1,0:T(8,128)S(1)}, u32[]{:S(2)}, u32[]{:S(2)}) collective-permute-start(f32[8,8,8,128]{3,2,1,0:T(8,128)S(1)} %get-tuple-element.70), channel_id=1, source_target_pairs={{0,1},{1,0},{2,3},{3,2},{4,5},{5,4},{6,7},{7,6},{8,9},{9,8},{10,11... | collective-permute-start | bytes 786440 | tf_op jit(solution)/shard_map/ppermute | solution.py:435

commit v12 on v11

--- a/solution.py
+++ b/solution.py
@@ -410,7 +410,7 @@
         out_shape=[pltpu.HBM((64, 64, 256), BF16)] + [jax.ShapeDtypeStruct((8, 8, 8, LANES), F32)] * 2,
         scratch_shapes=[
             pltpu.VMEM((2, 8, 8, 8, LANES), F32),
-            pltpu.VMEM((2, ACT_ROWS * PITCH, LANES), F32),
+            pltpu.VMEM((2, (ACT_ROWS + 1) * PITCH, LANES), F32),
         ],
         compiler_params=params(24),
         name="act_and_edges",
@@ -424,7 +424,7 @@
         in_specs=[SMEM, pl.BlockSpec((64, MIX_ROWS, 256), lambda i: (0, i, 0))] + [VMEM] * 6,
         out_specs=pl.BlockSpec((MIX_ROWS, 64, 256), lambda i: (i, 0, 0)),
         out_shape=jax.ShapeDtypeStruct((64, 64, 256), BF16),
-        scratch_shapes=[pltpu.VMEM((1024, 256), F32), pltpu.VMEM((2, 16 * PITCH, LANES), F32)],
+        scratch_shapes=[pltpu.VMEM((1024, 256), F32), pltpu.VMEM((2, 17 * PITCH, LANES), F32)],
         compiler_params=params(40),
         name="mix",
     )(core, in_hbm(local), keep, got, horiz_rate, horiz_coef, w_in, w_out)

time: 91.7 us -> 91.7 us (level)
  no operation moved by 1% of the time
where the time goes in v12:
time: 91.7 us; the launch traced here: 91.3 us
  Pallas kernels  42.2 us (46%)
  starting transfers between devices  26 us (28%)
  blocking collectives  13.1 us (14%)
  waiting for transfers between devices  9.67 us (11%)
    ppermute x7, starting transfers between devices, swap(): return lax.ppermute(block, 'col', [(i, i ^ bits) for i in range(n)])  18.4 us
    all_to_all x1, blocking collectives, on_device(): lax.all_to_all(incoming, 'row', 0, 0, tiled=True).reshape(2, 8, 8, 8, LANES)  13.1 us
    pallas_call x4, Pallas kernels, local_piece(): pl.pallas_call(functools.partial(piece_kernel, part), in_specs=[HBM, VMEM...  11.2 us
    pallas_call x1, Pallas kernels, mix(): pl.pallas_call(mix_kernel, grid=(64 // MIX_ROWS,), in_specs=[SMEM, pl.Blo...  10.7 us
    pallas_call x1, Pallas kernels, act_and_edges(): pl.pallas_call(act_kernel, grid=(64 // ACT_ROWS,), in_specs=[SMEM, pl.Blo...  8.51 us
    all_to_all x1, starting transfers between devices, on_device(): edges = lax.all_to_all(edges, 'row', 0, 0, tiled=True)  7.6 us
    pallas_call x1, Pallas kernels, local_scan(): pl.pallas_call(functools.partial(local_kernel, scale), in_specs=[HBM, HBM...  7.02 us
    ppermute x7, waiting for transfers between devices, swap(): return lax.ppermute(block, 'col', [(i, i ^ bits) for i in range(n)])  6.32 us
  transfers between devices with their start and end apart: 8, of which 5 were waited for; matrix products, arithmetic and copies ran while one was open for 0% of the time, Pallas kernels for 20%

profile of v12, /device:TPU:1, one launch (start us, length us, event | category | flops | bytes accessed | tf_op | source)
XLA Modules:
  0.0 91.3 jit_solution(1104009054792763512)
XLA Ops:
  0.0 4.4 %row_edges.1 = f32[2,8,8,8,128]{4,3,2,1,0:T(8,128)} custom-call(bf16[64,64,256]{2,1,0:T(8,128)(2,1)} %block_ref.1, f32[8,256]{1,0:T(8,128)} %vr_ref.1), custom_call_target="tpu_custom_call" | custom-call | tf_op jit(solution)/shard_map/row_edges/pallas_call | solution.py:326
  4.4 7.6 %all-to-all-start = ((f32[16,8,8,128]{3,2,1,0:T(8,128)}), f32[16,8,8,128]{3,2,1,0:T(8,128)S(1)}, u32[]{:S(2)}, u32[]{:S(2)}) async-start(f32[16,8,8,128]{3,2,1,0:T(8,128)} %bitcast), calls=%async_computation | async-start | bytes 1048576 | tf_op jit(solution)/shard_map/all_to_all | solution.py:452
  12.1 0.0 copy-start.4
  12.1 0.0 copy-start
  12.1 0.0 copy-start.5
  12.1 7.0 %vert_local.1.local_ref = f32[64,64,256]{2,1,0:T(8,128)} custom-call(bf16[64,64,256]{2,1,0:T(8,128)(2,1)} %block_ref.1, f32[8,256]{1,0:T(8,128)} %vr_ref.1, f32[8,256]{1,0:T(8,128)} %vc_ref.1), custom_call_target="tpu_custom_call" | custom-call | flops 5000000000 | bytes 8000000 | tf_op jit(solution)/shard_map/vert_local/pallas_call | solution.py:353
  19.2 0.0 copy-start.3
  19.2 3.3 %all-to-all-done.edge_ref = f32[16,8,8,128]{3,2,1,0:T(8,128)S(1)} async-done(((f32[16,8,8,128]{3,2,1,0:T(8,128)}), f32[16,8,8,128]{3,2,1,0:T(8,128)S(1)}, u32[]{:S(2)}, u32[]{:S(2)}) %all-to-all-start) | async-done | bytes 524320 | tf_op jit(solution)/shard_map/all_to_all | solution.py:452
  22.5 0.0 copy-done.4
  22.5 0.1 prefix.1
  22.6 13.1 %all_to_all.10 = f32[16,8,8,128]{3,2,1,0:T(8,128)S(1)} all-to-all(f32[16,8,8,128]{3,2,1,0:T(8,128)S(1)} %prefix.1), channel_id=1, replica_groups=mesh['row'=16,'col'=16] {'row'}, dimensions={0} | all-to-all | bytes 1048576 | tf_op jit(solution)/shard_map/all_to_all | solution.py:457
  35.7 0.0 copy-done
  35.7 0.0 copy-done.5
  35.7 8.5 %act_and_edges.1 = (bf16[64,64,256]{2,1,0:T(8,128)(2,1)}, f32[8,8,8,128]{3,2,1,0:T(8,128)S(1)}, f32[8,8,8,128]{3,2,1,0:T(8,128)S(1)}) custom-call(s32[1]{0:T(128)S(6)} %select_n.30.core_ref.half_ref.left_ref, f32[64,64,256]{2,1,0:T(8,128)} %vert_local.1.local_ref, f32[2,8,8,8,128]{4,3,2,1,0:T(8,128)S(1)} %bitcast.4, f32[8,256]{1,0:T(8,128)S(1)} %copy-done.4, ...), custom_call_target="tpu_custom_call" | custom-call | tf_op jit(solution)/shard_map/act_and_edges/pallas_call | solution.py:405
  44.2 2.6 %collective-permute-start = (f32[8,8,8,128]{3,2,1,0:T(8,128)S(1)}, f32[8,8,8,128]{3,2,1,0:T(8,128)S(1)}, u32[]{:S(2)}, u32[]{:S(2)}) collective-permute-start(f32[8,8,8,128]{3,2,1,0:T(8,128)S(1)} %get-tuple-element.47), channel_id=1, source_target_pairs={{0,1},{1,0},{2,3},{3,2},{4,5},{5,4},{6,7},{7,6},{8,9},{9,8},{10,11... | collective-permute-start | bytes 786440 | tf_op jit(solution)/shard_map/ppermute | solution.py:435
  46.8 1.2 %collective-permute-done.came_ref = f32[8,8,8,128]{3,2,1,0:T(8,128)S(1)} collective-permute-done((f32[8,8,8,128]{3,2,1,0:T(8,128)S(1)}, f32[8,8,8,128]{3,2,1,0:T(8,128)S(1)}, u32[]{:S(2)}, u32[]{:S(2)}) %collective-permute-start) | collective-permute-done | bytes 262176 | tf_op jit(solution)/shard_map/ppermute | solution.py:435
  47.9 0.1 join_0.1
  48.0 1.7 %collective-permute-start.1 = (f32[4,8,8,128]{3,2,1,0:T(8,128)S(1)}, f32[4,8,8,128]{3,2,1,0:T(8,128)S(1)}, u32[]{:S(2)}, u32[]{:S(2)}) collective-permute-start(f32[4,8,8,128]{3,2,1,0:T(8,128)S(1)} %get-tuple-element.49), channel_id=1, source_target_pairs={{0,2},{1,3},{2,0},{3,1},{4,6},{5,7},{6,4},{7,5},{8,10},{9,11},{10,... | collective-permute-start | bytes 393224 | tf_op jit(solution)/shard_map/ppermute | solution.py:435
  49.7 0.0 copy-done.3
  49.7 2.8 %horiz_local_0.1.refs_0_ = f32[64,64,256]{2,1,0:T(8,128)} custom-call(bf16[64,64,256]{2,1,0:T(8,128)(2,1)} %get-tuple-element.50.block_ref, f32[8,256]{1,0:T(8,128)S(1)} %copy-done, f32[8,256]{1,0:T(8,128)S(1)} %copy-done.3), custom_call_target="tpu_custom_call" | custom-call | flops 1250000000 | bytes 2000000 | tf_op jit(solution)/shard_map/horiz_local_0/pallas_call | solution.py:374
  52.5 0.7 collective-permute-done.1.came_ref
  53.2 3.1 %collective-permute-start.2 = (f32[2,8,8,128]{3,2,1,0:T(8,128)S(1)}, f32[2,8,8,128]{3,2,1,0:T(8,128)S(1)}, u32[]{:S(2)}, u32[]{:S(2)}) collective-permute-start(f32[2,8,8,128]{3,2,1,0:T(8,128)S(1)} %get-tuple-element.53), channel_id=1, source_target_pairs={{0,4},{1,5},{2,6},{3,7},{4,0},{5,1},{6,2},{7,3},{8,12},{9,13},{10,... | collective-permute-start | bytes 196616 | tf_op jit(solution)/shard_map/ppermute | solution.py:435
  56.3 2.8 %horiz_local_1.1.refs_0_ = f32[64,64,256]{2,1,0:T(8,128)} custom-call(bf16[64,64,256]{2,1,0:T(8,128)(2,1)} %get-tuple-element.50.block_ref, f32[8,256]{1,0:T(8,128)S(1)} %copy-done, f32[8,256]{1,0:T(8,128)S(1)} %copy-done.3, f32[64,64,256]{2,1,0:T(8,128)} %horiz_local_0.1.refs_0_), custom_call_target="tpu_custom_call", output_to_operand_aliasing={{}: (3, {})} | custom-call | flops 1250000000 | bytes 2000000 | tf_op jit(solution)/shard_map/horiz_local_1/pallas_call | solution.py:374
  59.1 0.0 collective-permute-done.2.came_ref
  59.2 4.2 %collective-permute-start.3 = (f32[2,8,8,128]{3,2,1,0:T(8,128)S(1)}, f32[2,8,8,128]{3,2,1,0:T(8,128)S(1)}, u32[]{:S(2)}, u32[]{:S(2)}) collective-permute-start(f32[2,8,8,128]{3,2,1,0:T(8,128)S(1)} %get-tuple-element.56), channel_id=1, source_target_pairs={{0,14},{1,15},{2,12},{3,13},{4,10},{5,11},{6,8},{7,9},{8,6},{9,7},... | collective-permute-start | bytes 196616 | tf_op jit(solution)/shard_map/ppermute | solution.py:435
  63.3 2.8 %horiz_local_2.1.refs_0_ = f32[64,64,256]{2,1,0:T(8,128)} custom-call(bf16[64,64,256]{2,1,0:T(8,128)(2,1)} %get-tuple-element.50.block_ref, f32[8,256]{1,0:T(8,128)S(1)} %copy-done, f32[8,256]{1,0:T(8,128)S(1)} %copy-done.3, f32[64,64,256]{2,1,0:T(8,128)} %horiz_local_1.1.refs_0_), custom_call_target="tpu_custom_call", output_to_operand_aliasing={{}: (3, {})} | custom-call | flops 1250000000 | bytes 2000000 | tf_op jit(solution)/shard_map/horiz_local_2/pallas_call | solution.py:374
  66.2 0.0 collective-permute-done.3.refs_0_
  66.2 0.0 copy-start.1
  66.2 0.0 copy-start.2
  66.2 1.6 %collective-permute-start.4 = (f32[2,8,8,128]{3,2,1,0:T(8,128)S(1)}, f32[2,8,8,128]{3,2,1,0:T(8,128)S(1)}, u32[]{:S(2)}, u32[]{:S(2)}) collective-permute-start(f32[2,8,8,128]{3,2,1,0:T(8,128)S(1)} %get-tuple-element.60), channel_id=1, source_target_pairs={{0,4},{1,5},{2,6},{3,7},{4,0},{5,1},{6,2},{7,3},{8,12},{9,13},{10,... | collective-permute-start | bytes 196616 | tf_op jit(solution)/shard_map/ppermute | solution.py:435
  67.8 2.8 %horiz_local_3.1.local_ref = f32[64,64,256]{2,1,0:T(8,128)} custom-call(bf16[64,64,256]{2,1,0:T(8,128)(2,1)} %get-tuple-element.50.block_ref, f32[8,256]{1,0:T(8,128)S(1)} %copy-done, f32[8,256]{1,0:T(8,128)S(1)} %copy-done.3, f32[64,64,256]{2,1,0:T(8,128)} %horiz_local_2.1.refs_0_), custom_call_target="tpu_custom_call", output_to_operand_aliasing={{}: (3, {})} | custom-call | flops 1250000000 | bytes 2000000 | tf_op jit(solution)/shard_map/horiz_local_3/pallas_call | solution.py:374
  70.6 0.0 collective-permute-done.4.refs_1_
  70.6 0.8 collective-permute-start.5
  71.5 3.3 %collective-permute-done.5.refs_1_ = f32[4,8,8,128]{3,2,1,0:T(8,128)S(1)} collective-permute-done((f32[4,8,8,128]{3,2,1,0:T(8,128)S(1)}, f32[4,8,8,128]{3,2,1,0:T(8,128)S(1)}, u32[]{:S(2)}, u32[]{:S(2)}) %collective-permute-start.5) | collective-permute-done | bytes 131104 | tf_op jit(solution)/shard_map/ppermute | solution.py:435
  74.8 0.1 part_0.1
  74.9 4.5 %collective-permute-start.6 = (f32[8,8,8,128]{3,2,1,0:T(8,128)S(1)}, f32[8,8,8,128]{3,2,1,0:T(8,128)S(1)}, u32[]{:S(2)}, u32[]{:S(2)}) collective-permute-start(f32[8,8,8,128]{3,2,1,0:T(8,128)S(1)} %get-tuple-element.70), channel_id=1, source_target_pairs={{0,1},{1,0},{2,3},{3,2},{4,5},{5,4},{6,7},{7,6},{8,9},{9,8},{10,11... | collective-permute-start | bytes 786440 | tf_op jit(solution)/shard_map/ppermute | solution.py:435
  79.4 1.2 %collective-permute-done.6.got_ref = f32[8,8,8,128]{3,2,1,0:T(8,128)S(1)} collective-permute-done((f32[8,8,8,128]{3,2,1,0:T(8,128)S(1)}, f32[8,8,8,128]{3,2,1,0:T(8,128)S(1)}, u32[]{:S(2)}, u32[]{:S(2)}) %collective-permute-start.6) | collective-permute-done | bytes 262176 | tf_op jit(solution)/shard_map/ppermute | solution.py:435
  80.5 0.0 copy-done.1
  80.5 0.0 copy-done.2
  80.5 10.7 %mix.1 = bf16[64,64,256]{2,1,0:T(8,128)(2,1)} custom-call(s32[1]{0:T(128)S(6)} %select_n.30.core_ref.half_ref.left_ref, f32[64,64,256]{2,1,0:T(8,128)} %horiz_local_3.1.local_ref, f32[8,8,8,128]{3,2,1,0:T(8,128)S(1)} %get-tuple-element.69.keep_ref, f32[8,8,8,128]{3,2,1,0:T(8,128)S(1)} %collective-permute-done.6.got_ref, f32[8,256]{1,0:T(8,128)S(1)} %copy-done, ...), custom_call_target="tpu_custom_call" | custom-call | tf_op jit(solution)/shard_map/mix/pallas_call | solution.py:421
  (4 shorter events, 0.1 us)
Async XLA Ops:
  4.4 18.1 %all-to-all-start = ((f32[16,8,8,128]{3,2,1,0:T(8,128)}), f32[16,8,8,128]{3,2,1,0:T(8,128)S(1)}, u32[]{:S(2)}, u32[]{:S(2)}) async-start(f32[16,8,8,128]{3,2,1,0:T(8,128)} %bitcast), calls=%async_computation | async-start | bytes 1048576 | tf_op jit(solution)/shard_map/all_to_all | solution.py:452
  12.1 10.4 %copy-start.4 = (f32[8,256]{1,0:T(8,128)S(1)}, f32[8,256]{1,0:T(8,128)}, u32[]{:S(2)}) copy-start(f32[8,256]{1,0:T(8,128)} %vr_ref.1) | copy-start | bytes 24580
  12.1 23.6 %copy-start = (f32[8,256]{1,0:T(8,128)S(1)}, f32[8,256]{1,0:T(8,128)}, u32[]{:S(2)}) copy-start(f32[8,256]{1,0:T(8,128)} %hr_ref.3) | copy-start | bytes 24580
  12.1 23.6 %copy-start.5 = (f32[8,256]{1,0:T(8,128)S(1)}, f32[8,256]{1,0:T(8,128)}, u32[]{:S(2)}) copy-start(f32[8,256]{1,0:T(8,128)} %vc_ref.1) | copy-start | bytes 24580
  19.2 30.6 %copy-start.3 = (f32[8,256]{1,0:T(8,128)S(1)}, f32[8,256]{1,0:T(8,128)}, u32[]{:S(2)}) copy-start(f32[8,256]{1,0:T(8,128)} %hc_ref.1) | copy-start | bytes 24580
  44.2 3.7 %collective-permute-start = (f32[8,8,8,128]{3,2,1,0:T(8,128)S(1)}, f32[8,8,8,128]{3,2,1,0:T(8,128)S(1)}, u32[]{:S(2)}, u32[]{:S(2)}) collective-permute-start(f32[8,8,8,128]{3,2,1,0:T(8,128)S(1)} %get-tuple-element.47), channel_id=1, source_target_pairs={{0,1},{1,0},{2,3},{3,2},{4,5},{5,4},{6,7},{7,6},{8,9},{9,8},{10,11... | collective-permute-start | bytes 786440 | tf_op jit(solution)/shard_map/ppermute | solution.py:435
  48.0 5.2 %collective-permute-start.1 = (f32[4,8,8,128]{3,2,1,0:T(8,128)S(1)}, f32[4,8,8,128]{3,2,1,0:T(8,128)S(1)}, u32[]{:S(2)}, u32[]{:S(2)}) collective-permute-start(f32[4,8,8,128]{3,2,1,0:T(8,128)S(1)} %get-tuple-element.49), channel_id=1, source_target_pairs={{0,2},{1,3},{2,0},{3,1},{4,6},{5,7},{6,4},{7,5},{8,10},{9,11},{10,... | collective-permute-start | bytes 393224 | tf_op jit(solution)/shard_map/ppermute | solution.py:435
  53.2 5.9 %collective-permute-start.2 = (f32[2,8,8,128]{3,2,1,0:T(8,128)S(1)}, f32[2,8,8,128]{3,2,1,0:T(8,128)S(1)}, u32[]{:S(2)}, u32[]{:S(2)}) collective-permute-start(f32[2,8,8,128]{3,2,1,0:T(8,128)S(1)} %get-tuple-element.53), channel_id=1, source_target_pairs={{0,4},{1,5},{2,6},{3,7},{4,0},{5,1},{6,2},{7,3},{8,12},{9,13},{10,... | collective-permute-start | bytes 196616 | tf_op jit(solution)/shard_map/ppermute | solution.py:435
  59.2 7.0 %collective-permute-start.3 = (f32[2,8,8,128]{3,2,1,0:T(8,128)S(1)}, f32[2,8,8,128]{3,2,1,0:T(8,128)S(1)}, u32[]{:S(2)}, u32[]{:S(2)}) collective-permute-start(f32[2,8,8,128]{3,2,1,0:T(8,128)S(1)} %get-tuple-element.56), channel_id=1, source_target_pairs={{0,14},{1,15},{2,12},{3,13},{4,10},{5,11},{6,8},{7,9},{8,6},{9,7},... | collective-permute-start | bytes 196616 | tf_op jit(solution)/shard_map/ppermute | solution.py:435
  66.2 14.3 %copy-start.1 = (bf16[256,1024]{1,0:T(8,128)(2,1)S(1)}, bf16[256,1024]{1,0:T(8,128)(2,1)}, u32[]{:S(2)}) copy-start(bf16[256,1024]{1,0:T(8,128)(2,1)} %w_in_ref.1) | copy-start | bytes 1572868
  66.2 14.3 %copy-start.2 = (bf16[1024,256]{1,0:T(8,128)(2,1)S(1)}, bf16[1024,256]{1,0:T(8,128)(2,1)}, u32[]{:S(2)}) copy-start(bf16[1024,256]{1,0:T(8,128)(2,1)} %w_out_ref.1) | copy-start | bytes 1572868
  66.2 4.4 %collective-permute-start.4 = (f32[2,8,8,128]{3,2,1,0:T(8,128)S(1)}, f32[2,8,8,128]{3,2,1,0:T(8,128)S(1)}, u32[]{:S(2)}, u32[]{:S(2)}) collective-permute-start(f32[2,8,8,128]{3,2,1,0:T(8,128)S(1)} %get-tuple-element.60), channel_id=1, source_target_pairs={{0,4},{1,5},{2,6},{3,7},{4,0},{5,1},{6,2},{7,3},{8,12},{9,13},{10,... | collective-permute-start | bytes 196616 | tf_op jit(solution)/shard_map/ppermute | solution.py:435
  70.6 4.2 %collective-permute-start.5 = (f32[4,8,8,128]{3,2,1,0:T(8,128)S(1)}, f32[4,8,8,128]{3,2,1,0:T(8,128)S(1)}, u32[]{:S(2)}, u32[]{:S(2)}) collective-permute-start(f32[4,8,8,128]{3,2,1,0:T(8,128)S(1)} %get-tuple-element.67), channel_id=1, source_target_pairs={{0,2},{1,3},{2,0},{3,1},{4,6},{5,7},{6,4},{7,5},{8,10},{9,11},{10,... | collective-permute-start | bytes 393224 | tf_op jit(solution)/shard_map/ppermute | solution.py:435
  74.9 5.7 %collective-permute-start.6 = (f32[8,8,8,128]{3,2,1,0:T(8,128)S(1)}, f32[8,8,8,128]{3,2,1,0:T(8,128)S(1)}, u32[]{:S(2)}, u32[]{:S(2)}) collective-permute-start(f32[8,8,8,128]{3,2,1,0:T(8,128)S(1)} %get-tuple-element.70), channel_id=1, source_target_pairs={{0,1},{1,0},{2,3},{3,2},{4,5},{5,4},{6,7},{7,6},{8,9},{9,8},{10,11... | collective-permute-start | bytes 786440 | tf_op jit(solution)/shard_map/ppermute | solution.py:435
